TPU v7x, 32 devices: a whole 2x2x4 slice. The times are simulated.
32 devices in a mesh: enc: 4 (over z), seq: 2 (over x), req: 4 (over y, core).
Axes of the slice: x: 2, y: 2, z: 4, core: 2. Of those that a mesh axis runs over, the one named last changes fastest.
Arguments:
- encoder_hidden: bfloat16 [2, 128, 4096], P('seq', None, ('enc', 'req'))
- prompt_token_ids: int32 [2, 128], replicated, may hold values from 0 to 32127, as said below
- context_weight: bfloat16 [4096, 3072], P(('enc', 'req'))
- context_bias: bfloat16 [3072], P(('enc', 'req')), may hold values from -16 to 16
- modulation_shift: bfloat16 [2, 3072], P('seq', ('enc', 'req')), may hold values from -6 to 6
- modulation_scale: bfloat16 [2, 3072], P('seq', ('enc', 'req')), may hold values from -3 to 3
- key_value_weight: bfloat16 [3072, 6144], P(('enc', 'req')), may hold values from -0.109375 to 0.109375
- key_value_bias: bfloat16 [6144], replicated, may hold values from -6 to 6
- request_prompt: int32 [4, 4], P('enc', 'req'), may hold values from 0 to 1
- adapter_of_request: int32 [4, 4], P('enc', 'req'), may hold values from 0 to 3
- adapter_down_maps: bfloat16 [4, 3072, 64], P('req'), may hold values from -0.109375 to 0.109375
- adapter_up_maps: bfloat16 [4, 64, 3072], P('req'), may hold values from -0.75 to 0.75
- image_stream_input: bfloat16 [4, 4, 128, 3072], P('enc', 'req', 'seq'), may hold values from -6 to 6
- image_query_key: bfloat16 [4, 4, 128, 6144], P('enc', 'req', 'seq'), may hold values from -4.5 to 4.5
- image_value_rows: bfloat16 [4, 4, 128, 3072], P('enc', 'req', 'seq'), may hold values from -6 to 6
Outputs:
- attended: bfloat16 [4, 4, 128, 3072], P('enc', 'req', 'seq')
Inputs may be any that keep to these rules, and one draw needn't show every extreme that they name: `prompt_token_ids`: id 0 marks padding; in each prompt the live tokens come first, end with id 1 and number at least 32; some prompt has no padding. `request_prompt`: a prompt index below 2. `adapter_of_request`: an adapter index below 4.
All inputs are finite; a program needn't handle non-finite values.
Results may differ from a plain program's by a relative error of at most 0.0039.
Values may be sent and summed in bfloat16 or wider, within the bound.
No kernel may reach another device: no remote copies, remote signals or barrier semaphores. Data moves between devices by JAX's collectives and lax.ppermute only.
A program may use at most 64 MiB of HBM per device.

v0:
```python
import jax
import jax.numpy as jnp
from jax import lax
from jax.sharding import PartitionSpec as P

HDIM = 128


epsilon_norm = 1e-06


def from_root(block, axis, source):
    block = jnp.where(lax.axis_index(axis) == source, block, jnp.zeros_like(block))
    return lax.psum(block, axis)


def finish_rows(projected):
    row_count = projected.shape[0]
    inner_width = projected.shape[1] // 2
    key_part = projected[:, :inner_width].reshape(row_count, inner_width // HDIM, HDIM)
    key_part = key_part * lax.rsqrt(
        jnp.mean(key_part * key_part, axis=2, keepdims=True) + epsilon_norm
    )
    return jnp.concatenate(
        [key_part.reshape(row_count, inner_width), projected[:, inner_width:]], axis=1
    ).astype(jnp.bfloat16)


def attend(queries, key_rows, value_rows, live_keys):
    query_count = queries.shape[0]
    head_count = queries.shape[1]
    per_block = 1
    while per_block * query_count < 512 and head_count % (2 * per_block) == 0:
        per_block = per_block * 2

    def heads_first(tensor):
        return jnp.swapaxes(tensor, 0, 1).reshape(
            head_count // per_block, per_block, tensor.shape[0], HDIM
        )

    def block_attend(pieces):
        block_queries, block_keys, block_values = pieces
        scores = jnp.einsum(
            "hqd,hkd->hqk", block_queries, block_keys, preferred_element_type=jnp.float32
        ) * HDIM ** (-0.5)
        scores = jnp.where(live_keys[None, None, :], scores, -jnp.inf)
        largest = jnp.max(scores, axis=2, keepdims=True)
        weights = jnp.exp(scores - largest)
        totals = jnp.sum(weights, axis=2, keepdims=True)
        rounded = weights.astype(jnp.bfloat16)
        mixed = (
            jnp.einsum("hqk,hkd->hqd", rounded, block_values, preferred_element_type=jnp.float32)
            / totals
        )
        return mixed.astype(jnp.bfloat16)

    outputs = lax.map(
        block_attend, (heads_first(queries), heads_first(key_rows), heads_first(value_rows))
    )
    return jnp.swapaxes(outputs.reshape(head_count, query_count, HDIM), 0, 1)


def per_device(
    encoder_hidden,
    prompt_token_ids,
    context_weight,
    context_bias,
    modulation_shift,
    modulation_scale,
    key_value_weight,
    key_value_bias,
    request_prompt,
    adapter_of_request,
    adapter_down_maps,
    adapter_up_maps,
    image_stream_input,
    image_query_key,
    image_value_rows,
):
    partial_value = jnp.dot(encoder_hidden[0], context_weight, preferred_element_type=jnp.float32)
    embedded = lax.psum_scatter(
        partial_value, ("enc", "req"), scatter_dimension=1, tiled=True
    ) + context_bias.astype(jnp.float32)
    full_width = embedded.shape[1] * lax.axis_size(("enc", "req"))
    row_sums, row_squares = lax.psum(
        (jnp.sum(embedded, axis=1), jnp.sum(embedded * embedded, axis=1)), ("enc", "req")
    )
    average = row_sums / full_width
    spread = row_squares / full_width - average * average
    normed = (embedded - average[:, None]) * lax.rsqrt(spread + epsilon_norm)[:, None]
    modulated = (
        (1.0 + modulation_scale[0].astype(jnp.float32)) * normed
        + modulation_shift[0].astype(jnp.float32)
    ).astype(jnp.bfloat16)
    bias_rows = key_value_bias.astype(jnp.float32)
    summed = lax.psum(
        jnp.dot(modulated, key_value_weight, preferred_element_type=jnp.float32), ("enc", "req")
    )
    text_kv = finish_rows(summed + bias_rows)
    chosen = request_prompt[0, 0]
    request_adapter = adapter_of_request[0, 0]
    down_all, up_all = (
        lax.all_gather(adapter_down_maps, "req", axis=0, tiled=True),
        lax.all_gather(adapter_up_maps, "req", axis=0, tiled=True),
    )
    down_pick = lax.dynamic_index_in_dim(down_all, request_adapter, 0, keepdims=False)
    up_pick = lax.dynamic_index_in_dim(up_all, request_adapter, 0, keepdims=False)
    adapter_delta = jnp.dot(
        image_stream_input[0, 0], down_pick, preferred_element_type=jnp.float32
    ).astype(jnp.bfloat16)
    image_value_base = (
        image_value_rows[0, 0].astype(jnp.float32)
        + jnp.dot(adapter_delta, up_pick, preferred_element_type=jnp.float32)
    ).astype(jnp.bfloat16)
    inner_width = image_value_base.shape[1]
    text_count = text_kv.shape[0]
    qk_rows = image_query_key[0, 0]
    queries_local = qk_rows[:, :inner_width]
    keys_local = qk_rows[:, inner_width:]
    live_text = lax.dynamic_index_in_dim(prompt_token_ids, chosen, 0, keepdims=False) != 0
    text_all = from_root(text_kv, "seq", chosen)
    keys_all, values_all = (
        lax.all_gather(keys_local, "seq", axis=0, tiled=True),
        lax.all_gather(image_value_base, "seq", axis=0, tiled=True),
    )
    token_total = keys_all.shape[0]
    head_count = inner_width // HDIM
    queries = queries_local.reshape(-1, head_count, HDIM)
    key_rows = jnp.concatenate([text_all[:, :inner_width], keys_all], axis=0).reshape(
        text_count + token_total, head_count, HDIM
    )
    value_rows = jnp.concatenate([text_all[:, inner_width:], values_all], axis=0).reshape(
        text_count + token_total, head_count, HDIM
    )
    live_keys = jnp.concatenate([live_text, jnp.ones((token_total,), dtype=jnp.bool_)])
    result = attend(queries, key_rows, value_rows, live_keys).reshape(-1, inner_width)
    return result[None, None]


def solution(mesh):
    return jax.shard_map(
        per_device,
        mesh=mesh,
        in_specs=(
            P("seq", None, ("enc", "req")),
            P(),
            P(("enc", "req"), None),
            P(("enc", "req")),
            P("seq", ("enc", "req")),
            P("seq", ("enc", "req")),
            P(("enc", "req"), None),
            P(),
            P("enc", "req"),
            P("enc", "req"),
            P("req", None, None),
            P("req", None, None),
            P("enc", "req", "seq", None),
            P("enc", "req", "seq", None),
            P("enc", "req", "seq", None),
        ),
        out_specs=P("enc", "req", "seq", None),
        check_vma=False,
    )
```

profile of v0, /device:TPU:0, one launch (start us, length us, event | category | flops | bytes accessed | tf_op | source)
XLA Modules:
  0.0 309.8 jit_solution(9182830563528276853)
XLA Ops:
  7.4 3.5 %fusion.26 = f32[128,3072]{0,1:T(8,128)} fusion(bf16[256,3072]{1,0:T(8,128)(2,1)} %param.19, bf16[1,128,256]{2,1,0:T(8,128)(2,1)} %param.17), kind=kOutput, calls=%fused_computation.39 | convolution fusion | flops 201326592 | bytes 3211264 | tf_op jit(solution)/shard_map/dot_general | solution.py:80
  10.9 0.6 copy-done.9
  11.6 62.5 %reduce-scatter.2.cloned.1.call-done = f32[128,192]{0,1:T(8,128)} async-done(((f32[128,3072]{0,1:T(8,128)}), f32[128,192]{0,1:T(8,128)}) %reduce-scatter.2.cloned.1.call-update) | async-done | bytes 98320 | tf_op jit(solution)/shard_map/reduce_scatter | solution.py:81
  74.1 1.0 add_reduce_fusion
  75.1 29.6 %all-reduce.1 = (f32[128]{0:T(128)S(1)}, f32[128]{0:T(128)S(1)}) all-reduce(f32[128]{0:T(128)S(1)} %get-tuple-element.39, f32[128]{0:T(128)S(1)} %get-tuple-element.38), channel_id=1, replica_groups=mesh['enc'=4,'seq'=2,'req'=4] {'enc','req'}, use_global_device_ids=true, to_apply=%region_4.0 | all-reduce | flops 256 | bytes 2048 | tf_op jit(solution)/shard_map/psum | solution.py:85
  104.6 3.3 %fusion.28 = f32[128,6144]{1,0:T(8,128)} fusion(bf16[192,6144]{1,0:T(8,128)(2,1)S(1)} %copy-done, f32[128,192]{0,1:T(8,128)} %reduce-scatter.2.cloned.1.call-done, f32[192]{0:T(256)S(1)} %bitcast.99, f32[128]{0:T(128)S(1)} %get-tuple-element.61, f32[128]{0:T(128)S(1)} %get-tuple-element.60, f32[192]{0:T(256)S(1)} %convert_element_type.36, f32[192]{0:T(256)S(1)} %bitcast.100), kind=kOutput, calls=%fused_computation.41 | convolution fusion | flops 302137344 | bytes 5606656 | tf_op jit(solution)/shard_map/dot_general | solution.py:97
  108.0 0.5 all-gather.3.cloned.1.call-update
  108.6 0.5 all-gather.5.cloned.1.call-update
  109.8 104.1 %all-reduce.5.cloned.1.call-done = f32[128,6144]{1,0:T(8,128)} async-done(((f32[128,6144]{1,0:T(8,128)}), f32[128,6144]{1,0:T(8,128)}) %all-reduce.5.cloned.1.call-update) | async-done | bytes 3145744 | tf_op jit(solution)/shard_map/psum | solution.py:96
  213.9 2.2 broadcast_add_fusion
  216.4 1.4 copy-done.1
  217.8 1.4 copy.36
  219.2 1.9 reduce_sum.38
  221.3 0.5 mul.53
  221.8 1.7 fusion.17
  223.5 1.5 maximum_select_fusion
  226.1 0.8 fusion.38
  227.1 18.7 %all_gather.12 = bf16[128,3072]{1,0:T(8,128)(2,1)S(1)} all-gather(bf16[64,3072]{1,0:T(8,128)(2,1)} %get-tuple-element.58), channel_id=1, replica_groups=mesh['enc'=4,'seq'=2,'req'=4] {'seq'}, dimensions={0}, use_global_device_ids=true | all-gather | bytes 1179648 | tf_op jit(solution)/shard_map/all_gather | solution.py:123
  245.8 2.8 fusion.16
  248.6 14.2 %all_gather.15 = bf16[128,3072]{1,0:T(8,128)(2,1)} all-gather(bf16[64,3072]{1,0:T(8,128)(2,1)} %fusion.16), channel_id=1, replica_groups=mesh['enc'=4,'seq'=2,'req'=4] {'seq'}, dimensions={0}, use_global_device_ids=true | all-gather | bytes 1179648 | tf_op jit(solution)/shard_map/all_gather | solution.py:124
  262.8 24.0 %all-reduce.7.cloned.1.call-done = bf16[128,6144]{1,0:T(8,128)(2,1)} async-done(((bf16[128,6144]{1,0:T(8,128)(2,1)}), bf16[128,6144]{1,0:T(8,128)(2,1)}) %all-reduce.7.cloned.1.call-update) | async-done | bytes 1572880 | tf_op jit(solution)/shard_map/psum | solution.py:14
  286.8 1.5 fusion.37
  288.9 1.5 copy.32
  290.7 1.5 copy.33
  292.3 9.2 %while.10 = (s32[]{:T(128)}, bf16[3,8,64,128]{3,2,1,0:T(8,128)(2,1)S(1)}, pred[256]{0:T(512)(128)(4,1)S(1)}, bf16[3,8,64,128]{3,2,1,0:T(8,128)(2,1)S(1)}, bf16[3...) while((s32[]{:T(128)}, bf16[3,8,64,128]{3,2,1,0:T(8,128)(2,1)S(1)}, ...), condition=%wide.region_11.12_spmd, body=%wide.region_8.11_spmd.sunk | while | flops 68156416 | bytes 2900557 | solution.py:57
  292.3 1.4 fusion.48
  294.0 1.4 fusion.50
  295.3 1.4 fusion.48
  297.1 1.4 fusion.50
  298.4 1.4 fusion.48
  300.1 1.4 fusion.50
  301.8 0.9 broadcast_in_dim_reshape.3
  (50 shorter events, 3.2 us)
Async XLA Ops:
  7.4 97.3 %copy-start = (bf16[192,6144]{1,0:T(8,128)(2,1)S(1)}, bf16[192,6144]{1,0:T(8,128)(2,1)}, u32[]{:S(2)}) copy-start(bf16[192,6144]{1,0:T(8,128)(2,1)} %param.23) | copy-start | bytes 7077892
  7.4 66.7 %reduce-scatter.2.cloned.1.call-start = ((), (), s32[]{:S(2)}) async-start(), calls=%async_computation.1 | async-start | bytes 1671168 | tf_op jit(solution)/shard_map/reduce_scatter | solution.py:81
  10.9 0.7 copy-start.9
  10.9 0.7 copy-start.6
  10.9 0.7 copy-start.7
  10.9 203.0 %all-reduce.5.cloned.1.call-start = ((), (), s32[]{:S(2)}) async-start(), calls=%async_computation.2 | async-start | bytes 6291456 | tf_op jit(solution)/shard_map/psum | solution.py:96
  107.9 1.3 copy-start.5
  107.9 137.8 %all-gather.3.cloned.1.call-start = ((), (), s32[]{:S(2)}) async-start(), calls=%async_computation.4 | async-start | bytes 1966080 | tf_op jit(solution)/shard_map/all_gather | solution.py:103
  108.5 137.3 %all-gather.5.cloned.1.call-start = ((), (), s32[]{:S(2)}) async-start(), calls=%async_computation.5 | async-start | bytes 1966080 | tf_op jit(solution)/shard_map/all_gather | solution.py:104
  109.1 177.7 %all-reduce.7.cloned.1.call-start = ((), (), s32[]{:S(2)}) async-start(), calls=%async_computation.3 | async-start | bytes 3145728 | tf_op jit(solution)/shard_map/psum | solution.py:14
  216.1 1.7 copy-start.1
  224.9 1.1 copy-start.3
  226.1 1.0 copy-start.8
  286.8 1.6 copy-start.2
  290.7 1.5 copy-start.4
Sparse Core Ops, SparseCore 0:
  11.9 62.1 reduce-scatter.1
  108.1 105.8 all-reduce.4
  225.1 61.6 all-reduce.6
Sparse Core Ops, SparseCore 1:
  110.0 17.5 all-gather.2
  129.0 19.5 all-gather.4
where the time goes:
time: 311 us; the launch traced here: 310 us
  waiting for transfers between devices  192 us (62%)
  blocking collectives  62.4 us (20%)
  matrix products  17.9 us (6%)
  between operations  16.1 us (5%)
  local copies, waits for them, and re-layouts  12 us (4%)
  other arithmetic  9.42 us (3%)
    psum x1, waiting for transfers between devices, per_device(): lax.psum(jnp.dot(modulated, key_value_weight, preferred_element_type=jnp....  104 us
    reduce_scatter x1, waiting for transfers between devices, per_device(): lax.psum_scatter(partial_value, ('enc', 'req'), scatter_dimension=1, tile...  62.5 us
    psum x1, blocking collectives, per_device(): lax.psum((jnp.sum(embedded, axis=1), jnp.sum(embedded * embedded, axis=1)...  29.6 us
    psum x1, waiting for transfers between devices, from_root(): return lax.psum(block, axis)  24 us
    all_gather x1, blocking collectives, per_device(): lax.all_gather(keys_local, 'seq', axis=0, tiled=True)  18.7 us
    all_gather x1, blocking collectives, per_device(): lax.all_gather(image_value_base, 'seq', axis=0, tiled=True)  14.2 us
  transfers between devices with their start and end apart: 5, of which 3 were waited for; matrix products, arithmetic and copies ran while one was open for 4% of the time, Pallas kernels for 0%

commit v1 on v0

v1 whole, which is shorter than its diff:
```python
import functools

import jax
import jax.numpy as jnp
from jax import lax
from jax.experimental import pallas as pl
from jax.experimental.pallas import tpu as pltpu
from jax.sharding import PartitionSpec as P

HDIM = 128
ROWS = 16

epsilon_norm = 1e-06


def swap(block, axis, size, step):
    return lax.ppermute(block, axis, [(i, i ^ step) for i in range(size)])


def pick(array, index, dim):
    return lax.dynamic_index_in_dim(array, index, dim, keepdims=False)


def split_two(value):
    high = lax.reduce_precision(value, 8, 7)
    return high.astype(jnp.bfloat16), (value - high).astype(jnp.bfloat16)


def bits_of(size):
    return [1 << b for b in range(size.bit_length() - 1)]


def with_stat_rows(data, stat):
    high, low = split_two(stat)
    rows = jnp.concatenate(
        [high[None], low[None], jnp.zeros((ROWS - 2, stat.shape[0]), jnp.bfloat16)], axis=0
    )
    rows = jnp.broadcast_to(rows, data.shape[:-2] + rows.shape)
    return jnp.concatenate([data.astype(jnp.bfloat16), rows], axis=-2)


def attention_kernel(heads, inner, scale, mask_ref, q_ref, kt_ref, vt_ref, ki_ref, vi_ref, o_ref):
    live = mask_ref[...] != 0
    for h in range(heads):
        cols = slice(h * HDIM, (h + 1) * HDIM)
        q = q_ref[:, cols]
        dims = (((1,), (1,)), ((), ()))
        st = lax.dot_general(q, kt_ref[:, cols], dims, preferred_element_type=jnp.float32) * scale
        si = lax.dot_general(q, ki_ref[:, cols], dims, preferred_element_type=jnp.float32) * scale
        st = jnp.where(live, st, -jnp.inf)
        top = jnp.maximum(
            jnp.max(st, axis=1, keepdims=True), jnp.max(si, axis=1, keepdims=True)
        )
        wt = jnp.exp(st - top)
        wi = jnp.exp(si - top)
        total = jnp.sum(wt, axis=1, keepdims=True) + jnp.sum(wi, axis=1, keepdims=True)
        mixed = jnp.dot(
            wt.astype(jnp.bfloat16), vt_ref[:, cols], preferred_element_type=jnp.float32
        ) + jnp.dot(wi.astype(jnp.bfloat16), vi_ref[:, cols], preferred_element_type=jnp.float32)
        o_ref[:, cols] = (mixed / total).astype(o_ref.dtype)


def attention(queries, text_keys, text_values, image_keys, image_values, live):
    width = queries.shape[1]
    heads = width // HDIM
    rows = queries.shape[0]
    mask = jnp.broadcast_to(live.astype(jnp.int32)[None, :], (8, live.shape[0]))[:1]
    return pl.pallas_call(
        functools.partial(attention_kernel, heads, width, HDIM ** (-0.5)),
        out_shape=jax.ShapeDtypeStruct((rows, width), jnp.bfloat16),
        compiler_params=pltpu.CompilerParams(vmem_limit_bytes=48 * 1024 * 1024),
        name="attention",
    )(mask, queries, text_keys, text_values, image_keys, image_values)


def per_device(
    n_enc,
    n_req,
    n_seq,
    encoder_hidden,
    prompt_token_ids,
    context_weight,
    context_bias,
    modulation_shift,
    modulation_scale,
    key_value_weight,
    key_value_bias,
    request_prompt,
    adapter_of_request,
    adapter_down_maps,
    adapter_up_maps,
    image_stream_input,
    image_query_key,
    image_value_rows,
):
    f32, bf16 = jnp.float32, jnp.bfloat16
    e, r, s = lax.axis_index("enc"), lax.axis_index("req"), lax.axis_index("seq")
    req_bits = bits_of(n_req)
    model_width = context_weight.shape[1]
    features = context_bias.shape[0]
    tokens = encoder_hidden.shape[1]
    inner = key_value_weight.shape[1] // 2
    part = inner // n_seq

    def heads_of(array, share):
        return lax.dynamic_slice_in_dim(array, share * part, part, 1)

    qk = image_query_key[0, 0]
    sources = [qk[:, :inner], qk[:, inner:], image_value_rows[0, 0], image_stream_input[0, 0]]
    image_parts = [
        jnp.stack([heads_of(a, s ^ k) for a in sources]) for k in range(n_seq)
    ]
    image_parts = [image_parts[0]] + [
        swap(image_parts[k], "seq", n_seq, k) for k in range(1, n_seq)
    ]
    image_all = jnp.concatenate(image_parts, axis=1)
    queries, image_keys, base_values, stream = [image_all[i] for i in range(4)]

    partial_value = lax.dot_general(
        context_weight, encoder_hidden[0], (((0,), (1,)), ((), ())), preferred_element_type=f32
    )
    stat = jnp.sum(partial_value, axis=0) + jnp.sum(context_bias.astype(f32))
    acc = partial_value.reshape((n_enc,) + (2,) * len(req_bits) + (features, tokens))
    for i, bit in enumerate(req_bits):
        mine = (r // bit) % 2
        dim = len(req_bits) - i
        got = swap(with_stat_rows(pick(acc, 1 - mine, dim), stat), "req", n_req, bit).astype(f32)
        acc = pick(acc, mine, dim) + got[..., :features, :]
        got_stat = got.reshape((-1,) + got.shape[-2:])[0, features:]
        stat = stat + got_stat[0] + got_stat[1]
    arrived = [
        swap(with_stat_rows(pick(acc, e ^ k, 0), stat), "enc", n_enc, k).astype(f32)
        for k in range(1, n_enc)
    ]
    embedded = pick(acc, e, 0)
    for got in arrived:
        embedded = embedded + got[:features]
        stat = stat + got[features] + got[features + 1]
    embedded = embedded + context_bias.astype(f32)[:, None]
    centred = embedded - (stat / model_width)[None, :]
    squares = jnp.sum(centred * centred, axis=0)
    scaled = (1.0 + modulation_scale[0].astype(f32))[:, None] * centred

    own = with_stat_rows(scaled, squares)
    blocks = [own] + [swap(own, "seq", n_seq, k) for k in range(1, n_seq)]
    scaled_all = jnp.concatenate([b[:features] for b in blocks], axis=1)
    squares_all = jnp.concatenate(
        [b[features].astype(f32) + b[features + 1].astype(f32) for b in blocks]
    )
    weight_own = jnp.concatenate(
        [heads_of(key_value_weight[:, :inner], s), heads_of(key_value_weight[:, inner:], s)], axis=1
    )
    width = 2 * part
    projected = lax.dot_general(
        scaled_all, weight_own, (((0,), (0,)), ((), ())), preferred_element_type=f32
    )

    shift_part = jnp.dot(modulation_shift, key_value_weight, preferred_element_type=f32)
    for bit in req_bits:
        shift_part = shift_part + swap(shift_part, "req", n_req, bit)
    for bit in bits_of(n_enc):
        shift_part = shift_part + swap(shift_part, "enc", n_enc, bit)
    shift_part = shift_part + key_value_bias.astype(f32)[None]

    def columns_of(row, share):
        return jnp.concatenate(
            [heads_of(row[:, :inner], share), heads_of(row[:, inner:], share)], axis=1
        )

    shift_rows = jnp.concatenate(
        [columns_of(shift_part, s)]
        + [swap(columns_of(shift_part, s ^ k), "seq", n_seq, k) for k in range(1, n_seq)],
        axis=0,
    )

    halves = tokens // n_req // ROWS
    split = (n_seq,) + (2,) * len(req_bits) + (halves, ROWS)
    acc = projected.reshape(split + (width,))
    acc_stat = squares_all.reshape(split)

    def with_stat_columns(data, stat):
        high, low = split_two(stat)
        lane = lax.broadcasted_iota(jnp.int32, stat.shape + (HDIM,), stat.ndim)
        columns = jnp.where(
            lane == 0, high[..., None], jnp.where(lane == 1, low[..., None], jnp.zeros((), bf16))
        )
        return jnp.concatenate([data.astype(bf16), columns], axis=-1)

    for i, bit in enumerate(req_bits):
        mine = (r // bit) % 2
        dim = len(req_bits) - i
        got = swap(
            with_stat_columns(pick(acc, 1 - mine, dim), pick(acc_stat, 1 - mine, dim)),
            "req", n_req, bit,
        ).astype(f32)
        acc = pick(acc, mine, dim) + got[..., :width]
        acc_stat = pick(acc_stat, mine, dim) + got[..., width] + got[..., width + 1]
    acc = acc.reshape(n_enc, ROWS, width)
    acc_stat = acc_stat.reshape(n_enc, ROWS)
    arrived = [
        swap(with_stat_columns(pick(acc, e ^ k, 0), pick(acc_stat, e ^ k, 0)), "enc", n_enc, k)
        .astype(f32)
        for k in range(1, n_enc)
    ]
    rows = pick(acc, e, 0)
    row_squares = pick(acc_stat, e, 0)
    for got in arrived:
        rows = rows + got[:, :width]
        row_squares = row_squares + got[:, width] + got[:, width + 1]
    rows = rows * lax.rsqrt(row_squares / model_width + epsilon_norm)[:, None]
    rows = rows + pick(shift_rows, e // halves, 0)[None]
    keys = rows[:, :part].reshape(ROWS, part // HDIM, HDIM)
    keys = keys * lax.rsqrt(jnp.mean(keys * keys, axis=2, keepdims=True) + epsilon_norm)
    text = jnp.concatenate([keys.reshape(ROWS, part), rows[:, part:]], axis=1).astype(bf16)

    chosen = request_prompt[0, 0]
    relative = s ^ chosen
    by_enc = [text] + [swap(text, "enc", n_enc, k) for k in range(1, n_enc)]
    by_enc = jnp.stack(by_enc)
    by_enc = jnp.stack([pick(by_enc, k ^ e, 0) for k in range(n_enc)])
    held = by_enc.reshape(1, n_seq, halves, ROWS, width)
    first = req_bits[0]
    held = jnp.concatenate([held, swap(held, "req", n_req, first)], axis=0)
    groups = [pick(held, relative, 1)]
    for step in range(2, n_req, 2):
        wanted = swap(relative, "req", n_req, step)
        groups.append(swap(pick(held, wanted, 1), "req", n_req, step))
    text_rows = jnp.concatenate(groups, axis=0).reshape(-1, width)
    live = pick(prompt_token_ids, chosen, 0) != 0
    live = live.reshape(n_req, halves * ROWS)
    live = jnp.concatenate([pick(live, r ^ k, 0) for k in range(n_req)])

    down = lax.dynamic_slice_in_dim(adapter_down_maps[0], s * part, part, 0).T
    up = heads_of(adapter_up_maps[0], s)
    maps = jnp.concatenate([down, up], axis=0)[None]
    for bit in reversed(req_bits):
        maps = jnp.concatenate([maps, swap(maps, "req", n_req, bit)], axis=0)
    other = adapter_of_request[0, 0] ^ r
    index = 0
    for bit in req_bits:
        index = index * 2 + (other // bit) % 2
    chosen_maps = pick(maps, index, 0)
    rank = up.shape[0]
    lowrank = lax.dot_general(
        stream, chosen_maps[:rank], (((1,), (1,)), ((), ())), preferred_element_type=f32
    ).reshape(n_seq, -1, rank)
    for bit in bits_of(n_seq):
        got = swap(lowrank, "seq", n_seq, bit)
        lowrank = lowrank + jnp.stack([got[k ^ bit] for k in range(n_seq)])
    lowrank = lowrank.reshape(-1, rank).astype(bf16)
    image_values = (
        base_values.astype(f32) + jnp.dot(lowrank, chosen_maps[rank:], preferred_element_type=f32)
    ).astype(bf16)

    mixed = attention(
        queries, text_rows[:, :part], text_rows[:, part:], image_keys, image_values, live
    ).reshape(n_seq, -1, part)
    pieces = jnp.stack([mixed[0]] + [swap(mixed[k], "seq", n_seq, k) for k in range(1, n_seq)])
    result = jnp.concatenate([pick(pieces, s ^ k, 0) for k in range(n_seq)], axis=1)
    return result[None, None]


def solution(mesh):
    sizes = mesh.shape
    return jax.shard_map(
        functools.partial(per_device, sizes["enc"], sizes["req"], sizes["seq"]),
        mesh=mesh,
        in_specs=(
            P("seq", None, ("enc", "req")),
            P(),
            P(("enc", "req"), None),
            P(("enc", "req")),
            P("seq", ("enc", "req")),
            P("seq", ("enc", "req")),
            P(("enc", "req"), None),
            P(),
            P("enc", "req"),
            P("enc", "req"),
            P("req", None, None),
            P("req", None, None),
            P("enc", "req", "seq", None),
            P("enc", "req", "seq", None),
            P("enc", "req", "seq", None),
        ),
        out_specs=P("enc", "req", "seq", None),
        check_vma=False,
    )
```

time: 311 us -> 141 us (0.45)
  waiting for transfers between devices: 192 us -> 35.6 us
  blocking collectives: 62.4 us -> 0 us
  starting transfers between devices: 0.17 us -> 35.2 us
  other arithmetic: 9.42 us -> 33.2 us
  matrix products: 17.9 us -> 5.19 us
  between operations: 16.1 us -> 4.02 us
  local copies, waits for them, and re-layouts: 12 us -> 23.6 us
  Pallas kernels: 0 us -> 3.26 us
    psum x2 -> x0, waiting for transfers between devices: 128 us -> none  [the longest x1 104 us: per_device(): lax.psum(jnp.dot(modulated, key_value_weight, preferred_element_type=jnp....]
    reduce_scatter x1 -> x0, waiting for transfers between devices: 62.5 us -> none  [per_device(): lax.psum_scatter(partial_value, ('enc', 'req'), scatter_dimension=1, tile...]
    ppermute x0 -> x27, waiting for transfers between devices: none -> 35.6 us  [swap(): return lax.ppermute(block, axis, [(i, i ^ step) for i in range(size)])]
    ppermute x0 -> x27, starting transfers between devices: none -> 35.2 us  [swap(): return lax.ppermute(block, axis, [(i, i ^ step) for i in range(size)])]
    all_gather x2 -> x0, blocking collectives: 32.9 us -> none  [the longest x1 18.7 us: per_device(): lax.all_gather(keys_local, 'seq', axis=0, tiled=True)]
    psum x1 -> x0, blocking collectives: 29.6 us -> none  [per_device(): lax.psum((jnp.sum(embedded, axis=1), jnp.sum(embedded * embedded, axis=1)...]
    dot_general x9 -> x5, matrix products: 17.9 us -> 5.19 us  [the longest x1 1.79 us: per_device(): lax.dot_general(context_weight, encoder_hidden[0], (((0,), (1,)), ((), ()...]
    concatenate x0 -> x18, other arithmetic: none -> 8.6 us  [the longest x2 2.03 us: per_device(): maps = jnp.concatenate([maps, swap(maps, 'req', n_req, bit)], axis=0)]
  transfers between devices with their start and end apart: 5 -> 27, of which waited for: 3 -> 10; matrix products, arithmetic and copies ran while one was open for 4% -> 37% of each run, Pallas kernels for 0% -> 0%
where the time goes in v1:
time: 141 us; the launch traced here: 140 us
  waiting for transfers between devices  35.6 us (25%)
  starting transfers between devices  35.2 us (25%)
  other arithmetic  33.2 us (24%)
  local copies, waits for them, and re-layouts  23.6 us (17%)
  matrix products  5.19 us (4%)
  between operations  4.02 us (3%)
  Pallas kernels  3.26 us (2%)
    ppermute x27, waiting for transfers between devices, swap(): return lax.ppermute(block, axis, [(i, i ^ step) for i in range(size)])  35.6 us
    ppermute x27, starting transfers between devices, swap(): return lax.ppermute(block, axis, [(i, i ^ step) for i in range(size)])  35.2 us
    unnamed x74, local copies, waits for them, and re-layouts  5.25 us
    pallas_call x1, Pallas kernels, attention(): pl.pallas_call(functools.partial(attention_kernel, heads, width, HDIM **...  3.26 us
    dynamic_slice x5, local copies, waits for them, and re-layouts, pick(): return lax.dynamic_index_in_dim(array, index, dim, keepdims=False)  3.13 us
    add x1, other arithmetic, per_device(): rows = rows + pick(shift_rows, e // halves, 0)[None]  2.96 us
    another operation x2, local copies, waits for them, and re-layouts, per_device(): jnp.stack([heads_of(a, s ^ k) for a in sources])  2.85 us
    dynamic_slice x3, local copies, waits for them, and re-layouts, heads_of(): return lax.dynamic_slice_in_dim(array, share * part, part, 1)  2.85 us
  transfers between devices with their start and end apart: 27, of which 10 were waited for; matrix products, arithmetic and copies ran while one was open for 37% of the time, Pallas kernels for 0%

profile of v1, /device:TPU:0, one launch (start us, length us, event | category | flops | bytes accessed | tf_op | source)
XLA Modules:
  0.0 140.1 jit_solution(11190187260969208308)
XLA Ops:
  2.1 3.0 %collective-permute-start.23 = (bf16[1,128,1536]{2,1,0:T(8,128)(2,1)S(1)}, bf16[1,128,1536]{2,1,0:T(8,128)(2,1)}, u32[]{:S(2)}, u32[]{:S(2)}) collective-permute-start(bf16[1,128,1536]{2,1,0:T(8,128)(2,1)S(1)} %maximum_bitcast_fusion), channel_id=1, source_target_pairs={{0,2},{1,3},{2,0},{3,1},{4,6},{5,7},{6,4},{7,5},{8,10},{9,11},{10,... | collective-permute-start | bytes 1179656 | tf_op jit(solution)/shard_map/ppermute | solution.py:17
  6.0 2.0 %dynamic-slice_bitcast_fusion.6 = (bf16[1,64,1536]{2,1,0:T(8,128)(2,1)}, bf16[1,64,1536]{2,1,0:T(8,128)(2,1)S(1)}, bf16[1,64,1536]{2,1,0:T(8,128)(2,1)S(1)}, bf16[1,64,1536]{2,1,0:T(8,128)(2,1)}) fusion(bf16[1,1,64,3072]{3,2,1,0:T(8,128)(2,1)} %param.27, s32[]{:T(128)S(6)} %select_n.191, s32[]{:T(128)S(6)} %select_n.192, bf16[1,1,64,3072]{3,2,1,0:T(8,128)(2,1)} %param.29), kind=kLoop, calls=%fused_computation.77 | loop fusion | bytes 1572872 | tf_op jit(solution)/shard_map/stack | solution.py:111
  9.0 1.5 %collective-permute-start = (bf16[4,64,1536]{2,1,0:T(8,128)(2,1)}, bf16[4,64,1536]{2,1,0:T(8,128)(2,1)}, u32[]{:S(2)}, u32[]{:S(2)}) collective-permute-start(bf16[4,64,1536]{2,1,0:T(8,128)(2,1)} %pad_maximum_fusion.2), channel_id=1, source_target_pairs={{0,4},{4,0},{1,5},{5,1},{2,6},{6,2},{3,7},{7,3},{8,12},{12,8},{9,1... | collective-permute-start | bytes 2359304 | tf_op jit(solution)/shard_map/ppermute | solution.py:17
  11.2 1.8 %fusion.87 = (f32[128]{0:T(128)S(1)}, f32[3072,128]{1,0:T(8,128)S(1)}) fusion(bf16[256,3072]{1,0:T(8,128)(2,1)S(1)} %copy-done, bf16[1,128,256]{2,1,0:T(8,128)(2,1)} %param.15), kind=kOutput, calls=%fused_computation.253 | convolution fusion | flops 201719680 | bytes 3211776 | tf_op jit(solution)/shard_map/dot_general | solution.py:119
  22.5 1.6 %collective-permute-start.14 = (f32[1,6144]{1,0:T(1,128)S(1)}, f32[1,6144]{1,0:T(1,128)S(1)}, u32[]{:S(2)}, u32[]{:S(2)}) collective-permute-start(f32[1,6144]{1,0:T(1,128)S(1)} %add.508), channel_id=1, source_target_pairs={{0,8},{8,0},{16,24},{24,16},{1,9},{9,1},{17,25},{25,17},{2,10},{10... | collective-permute-start | bytes 73736 | tf_op jit(solution)/shard_map/ppermute | solution.py:17
  24.2 1.4 %constant_dynamic-slice_fusion.26 = (pred[1,32]{1,0:T(4,128)(4,1)}, pred[1,32]{1,0:T(4,128)(4,1)}, pred[1,32]{1,0:T(4,128)(4,1)}, pred[1,32]{1,0:T(4,128)(4,1)}) fusion(pred[4,32]{1,0:T(4,128)(4,1)} %ne.58, s32[]{:T(128)S(6)} %select_n.187, s32[]{:T(128)S(6)} %select_n.190, s32[]{:T(128)S(6)} %select_n.189, s32[]{:T(128)S(6)} %select_n.188), kind=kLoop, calls=%fused_computation.153 | loop fusion | bytes 272 | tf_op jit(solution)/shard_map/jit(dynamic_index_in_dim)/dynamic_slice | solution.py:21
  27.0 2.6 %collective-permute-start.15 = (f32[1,6144]{1,0:T(1,128)}, f32[1,6144]{1,0:T(1,128)}, u32[]{:S(2)}, u32[]{:S(2)}) collective-permute-start(f32[1,6144]{1,0:T(1,128)} %add.509), channel_id=1, source_target_pairs={{0,16},{8,24},{16,0},{24,8},{1,17},{9,25},{17,1},{25,9},{2,18},{10... | collective-permute-start | bytes 73736 | tf_op jit(solution)/shard_map/ppermute | solution.py:17
  37.3 1.6 %collective-permute-start.2 = (bf16[4,208,128]{2,1,0:T(8,128)(2,1)S(1)}, bf16[4,208,128]{2,1,0:T(8,128)(2,1)S(1)}, u32[]{:S(2)}, u32[]{:S(2)}) collective-permute-start(bf16[4,208,128]{2,1,0:T(8,128)(2,1)S(1)} %pad_maximum_fusion.9), channel_id=1, source_target_pairs={{0,2},{1,3},{2,0},{3,1},{4,6},{5,7},{6,4},{7,5},{8,10},{9,11},{10,... | collective-permute-start | bytes 638984 | tf_op jit(solution)/shard_map/ppermute | solution.py:17
  39.5 3.7 %collective-permute-done.2 = bf16[4,208,128]{2,1,0:T(8,128)(2,1)S(1)} collective-permute-done((bf16[4,208,128]{2,1,0:T(8,128)(2,1)S(1)}, bf16[4,208,128]{2,1,0:T(8,128)(2,1)S(1)}, u32[]{:S(2)}, u32[]{:S(2)}) %collective-permute-start.2) | collective-permute-done | bytes 213024 | tf_op jit(solution)/shard_map/ppermute | solution.py:17
  43.5 1.6 %collective-permute-start.3 = (bf16[208,128]{1,0:T(8,128)(2,1)S(1)}, bf16[208,128]{1,0:T(8,128)(2,1)S(1)}, u32[]{:S(2)}, u32[]{:S(2)}) collective-permute-start(bf16[208,128]{1,0:T(8,128)(2,1)S(1)} %get-tuple-element.58), channel_id=1, source_target_pairs={{0,8},{8,0},{16,24},{24,16},{1,9},{9,1},{17,25},{25,17},{2,10},{10... | collective-permute-start | bytes 159752 | tf_op jit(solution)/shard_map/ppermute | solution.py:17
  45.1 2.0 %collective-permute-start.4 = (bf16[208,128]{1,0:T(8,128)(2,1)S(1)}, bf16[208,128]{1,0:T(8,128)(2,1)S(1)}, u32[]{:S(2)}, u32[]{:S(2)}) collective-permute-start(bf16[208,128]{1,0:T(8,128)(2,1)S(1)} %get-tuple-element.59), channel_id=1, source_target_pairs={{0,16},{8,24},{16,0},{24,8},{1,17},{9,25},{17,1},{25,9},{2,18},{10... | collective-permute-start | bytes 159752 | tf_op jit(solution)/shard_map/ppermute | solution.py:17
  48.5 2.8 %collective-permute-start.21 = (s32[]{:T(128)}, s32[]{:T(128)}, u32[]{:S(2)}, u32[]{:S(2)}) collective-permute-start(s32[]{:T(128)} %xor.48), channel_id=1, source_target_pairs={{0,2},{1,3},{2,0},{3,1},{4,6},{5,7},{6,4},{7,5},{8,10},{9,11},{10,... | collective-permute-start | bytes 20 | tf_op jit(solution)/shard_map/ppermute | solution.py:17
  55.4 3.6 %collective-permute-done.6 = bf16[208,128]{1,0:T(8,128)(2,1)S(1)} collective-permute-done((bf16[208,128]{1,0:T(8,128)(2,1)S(1)}, bf16[208,128]{1,0:T(8,128)(2,1)S(1)}, u32[]{:S(2)}, u32[]{:S(2)}) %collective-permute-start.6) | collective-permute-done | bytes 53280 | tf_op jit(solution)/shard_map/ppermute | solution.py:17
  59.0 1.4 fusion.2
  60.4 1.6 %copy-done.2 = f32[256,3072]{1,0:T(8,128)} copy-done((f32[256,3072]{1,0:T(8,128)}, f32[256,3072]{1,0:T(8,128)S(1)}, u32[]{:S(2)}) %copy-start.2) | copy-done | bytes 3145752
  65.1 1.4 %pad_maximum_fusion = bf16[4,128,1536]{2,1,0:T(8,128)(2,1)S(1)} fusion(bf16[4,64,1536]{2,1,0:T(8,128)(2,1)} %collective-permute-done, bf16[1,64,1536]{2,1,0:T(8,128)(2,1)S(1)} %copy-done.14, bf16[1,64,1536]{2,1,0:T(8,128)(2,1)S(1)} %copy-done.15, bf16[1,64,1536]{2,1,0:T(8,128)(2,1)S(1)} %copy-done.12, bf16[1,64,1536]{2,1,0:T(8,128)(2,1)S(1)} %copy-done.13), kind=kLoop, calls=%fused_computation.6 | loop fusion | flops 7864320 | bytes 3145728 | tf_op jit(solution)/shard_map/concatenate | solution.py:116
  68.1 1.6 %collective-permute-start.8 = (bf16[2,2,16,3200]{3,2,1,0:T(8,128)(2,1)S(1)}, bf16[2,2,16,3200]{3,2,1,0:T(8,128)(2,1)S(1)}, u32[]{:S(2)}, u32[]{:S(2)}) collective-permute-start(bf16[2,2,16,3200]{3,2,1,0:T(8,128)(2,1)S(1)} %pad_maximum_fusion.6), channel_id=1, source_target_pairs={{0,2},{1,3},{2,0},{3,1},{4,6},{5,7},{6,4},{7,5},{8,10},{9,11},{10,... | collective-permute-start | bytes 1228808 | tf_op jit(solution)/shard_map/ppermute | solution.py:17
  71.5 8.3 %collective-permute-done.8 = bf16[2,2,16,3200]{3,2,1,0:T(8,128)(2,1)S(1)} collective-permute-done((bf16[2,2,16,3200]{3,2,1,0:T(8,128)(2,1)S(1)}, bf16[2,2,16,3200]{3,2,1,0:T(8,128)(2,1)S(1)}, u32[]{:S(2)}, u32[]{:S(2)}) %collective-permute-start.8) | collective-permute-done | bytes 409632 | tf_op jit(solution)/shard_map/ppermute | solution.py:17
  81.0 2.5 %collective-permute-start.10 = (bf16[16,3200]{1,0:T(8,128)(2,1)}, bf16[16,3200]{1,0:T(8,128)(2,1)S(1)}, u32[]{:S(2)}, u32[]{:S(2)}) collective-permute-start(bf16[16,3200]{1,0:T(8,128)(2,1)} %pad_maximum_fusion.15), channel_id=1, source_target_pairs={{0,16},{8,24},{16,0},{24,8},{1,17},{9,25},{17,1},{25,9},{2,18},{10... | collective-permute-start | bytes 307208 | tf_op jit(solution)/shard_map/ppermute | solution.py:17
  84.1 1.9 %collective-permute-start.11 = (bf16[16,3200]{1,0:T(8,128)(2,1)}, bf16[16,3200]{1,0:T(8,128)(2,1)S(1)}, u32[]{:S(2)}, u32[]{:S(2)}) collective-permute-start(bf16[16,3200]{1,0:T(8,128)(2,1)} %pad_maximum_fusion.16), channel_id=1, source_target_pairs={{0,24},{8,16},{16,8},{24,0},{1,25},{9,17},{17,9},{25,1},{2,26},{10... | collective-permute-start | bytes 307208 | tf_op jit(solution)/shard_map/ppermute | solution.py:17
  86.0 1.7 %copy.55 = f32[1,16,3072]{1,2,0:T(8,128)} copy(f32[1,16,3072]{2,1,0:T(8,128)S(1)} %constant_dynamic-slice_fusion.15) | data formatting | bytes 393216 | tf_op jit(solution)/shard_map/jit(dynamic_index_in_dim)/dynamic_slice | solution.py:21
  89.4 2.5 %collective-permute-done.10 = bf16[16,3200]{1,0:T(8,128)(2,1)S(1)} collective-permute-done((bf16[16,3200]{1,0:T(8,128)(2,1)}, bf16[16,3200]{1,0:T(8,128)(2,1)S(1)}, u32[]{:S(2)}, u32[]{:S(2)}) %collective-permute-start.10) | collective-permute-done | bytes 102432 | tf_op jit(solution)/shard_map/ppermute | solution.py:17
  96.2 3.0 %fusion.1 = f32[16,3072]{0,1:T(8,128)S(1)} fusion(f32[16,3200]{0,1:T(8,128)S(1)} %convert_element_type.410, f32[16,3200]{0,1:T(8,128)} %convert_element_type.405, f32[16,3200]{0,1:T(8,128)S(1)} %copy-done.5, f32[1,16,3072]{1,2,0:T(8,128)} %copy.55, f32[3072]{0:T(1024)S(1)} %bitcast.236, f32[16]{0:T(128)S(1)} %rsqrt_bitcast_fusion), kind=kLoop, calls=%fused_computation.2 | loop fusion | flops 245760 | bytes 995392 | tf_op jit(solution)/shard_map/add | solution.py:211
  102.7 2.5 %collective-permute-start.18 = (bf16[16,3072]{1,0:T(8,128)(2,1)}, bf16[16,3072]{1,0:T(8,128)(2,1)}, u32[]{:S(2)}, u32[]{:S(2)}) collective-permute-start(bf16[16,3072]{1,0:T(8,128)(2,1)} %pad_maximum_fusion.17), channel_id=1, source_target_pairs={{0,16},{8,24},{16,0},{24,8},{1,17},{9,25},{17,1},{25,9},{2,18},{10... | collective-permute-start | bytes 294920 | tf_op jit(solution)/shard_map/ppermute | solution.py:17
  105.2 1.9 %collective-permute-start.19 = (bf16[16,3072]{1,0:T(8,128)(2,1)}, bf16[16,3072]{1,0:T(8,128)(2,1)}, u32[]{:S(2)}, u32[]{:S(2)}) collective-permute-start(bf16[16,3072]{1,0:T(8,128)(2,1)} %pad_maximum_fusion.17), channel_id=1, source_target_pairs={{0,24},{8,16},{16,8},{24,0},{1,25},{9,17},{17,9},{25,1},{2,26},{10... | collective-permute-start | bytes 294920 | tf_op jit(solution)/shard_map/ppermute | solution.py:17
  109.8 2.3 %collective-permute-done.18 = bf16[16,3072]{1,0:T(8,128)(2,1)} collective-permute-done((bf16[16,3072]{1,0:T(8,128)(2,1)}, bf16[16,3072]{1,0:T(8,128)(2,1)}, u32[]{:S(2)}, u32[]{:S(2)}) %collective-permute-start.18) | collective-permute-done | bytes 98336 | tf_op jit(solution)/shard_map/ppermute | solution.py:17
  113.6 1.5 %collective-permute-start.25 = (f32[2,64,64]{2,1,0:T(8,128)S(1)}, f32[2,64,64]{2,1,0:T(8,128)S(1)}, u32[]{:S(2)}, u32[]{:S(2)}) collective-permute-start(f32[2,64,64]{2,1,0:T(8,128)S(1)} %fusion.23), channel_id=1, source_target_pairs={{0,4},{4,0},{1,5},{5,1},{2,6},{6,2},{3,7},{7,3},{8,12},{12,8},{9,1... | collective-permute-start | bytes 98312 | tf_op jit(solution)/shard_map/ppermute | solution.py:17
  119.3 1.5 %collective-permute-start.22 = (bf16[2,2,16,3072]{3,2,1,0:T(8,128)(2,1)S(1)}, bf16[2,2,16,3072]{3,2,1,0:T(8,128)(2,1)S(1)}, u32[]{:S(2)}, u32[]{:S(2)}) collective-permute-start(bf16[2,2,16,3072]{3,2,1,0:T(8,128)(2,1)S(1)} %get-tuple-element.25), channel_id=1, source_target_pairs={{0,2},{1,3},{2,0},{3,1},{4,6},{5,7},{6,4},{7,5},{8,10},{9,11},{10,... | collective-permute-start | bytes 1179656 | tf_op jit(solution)/shard_map/ppermute | solution.py:17
  122.1 7.9 %collective-permute-done.22 = bf16[2,2,16,3072]{3,2,1,0:T(8,128)(2,1)S(1)} collective-permute-done((bf16[2,2,16,3072]{3,2,1,0:T(8,128)(2,1)S(1)}, bf16[2,2,16,3072]{3,2,1,0:T(8,128)(2,1)S(1)}, u32[]{:S(2)}, u32[]{:S(2)}) %collective-permute-start.22) | collective-permute-done | bytes 393248 | tf_op jit(solution)/shard_map/ppermute | solution.py:17
  130.2 3.3 %attention.1 = bf16[128,1536]{1,0:T(8,128)(2,1)S(1)} custom-call(s32[1,128]{1,0:T(1,128)S(1)} %add_convert_fusion.mask_ref, bf16[128,1536]{1,0:T(8,128)(2,1)S(1)} %get-tuple-element.21.q_ref, bf16[128,1536]{1,0:T(8,128)(2,1)S(1)} %get-tuple-element.23.kt_ref, bf16[128,1536]{1,0:T(8,128)(2,1)S(1)} %get-tuple-element.22.vt_ref, ...), custom_call_target="tpu_custom_call" | custom-call | tf_op jit(solution)/shard_map/attention/pallas_call | solution.py:68
  133.5 1.5 %collective-permute-start.26 = (bf16[64,1536]{1,0:T(8,128)(2,1)S(1)}, bf16[64,1536]{1,0:T(8,128)(2,1)S(1)}, u32[]{:S(2)}, u32[]{:S(2)}) collective-permute-start(bf16[64,1536]{1,0:T(8,128)(2,1)S(1)} %get-tuple-element.33), channel_id=1, source_target_pairs={{0,4},{4,0},{1,5},{5,1},{2,6},{6,2},{3,7},{7,3},{8,12},{12,8},{9,1... | collective-permute-start | bytes 589832 | tf_op jit(solution)/shard_map/ppermute | solution.py:17
  135.0 4.2 %collective-permute-done.26 = bf16[64,1536]{1,0:T(8,128)(2,1)S(1)} collective-permute-done((bf16[64,1536]{1,0:T(8,128)(2,1)S(1)}, bf16[64,1536]{1,0:T(8,128)(2,1)S(1)}, u32[]{:S(2)}, u32[]{:S(2)}) %collective-permute-start.26) | collective-permute-done | bytes 196640 | tf_op jit(solution)/shard_map/ppermute | solution.py:17
  (222 shorter events, 54.5 us)
Async XLA Ops:
  2.1 61.5 %collective-permute-start.23 = (bf16[1,128,1536]{2,1,0:T(8,128)(2,1)S(1)}, bf16[1,128,1536]{2,1,0:T(8,128)(2,1)}, u32[]{:S(2)}, u32[]{:S(2)}) collective-permute-start(bf16[1,128,1536]{2,1,0:T(8,128)(2,1)S(1)} %maximum_bitcast_fusion), channel_id=1, source_target_pairs={{0,2},{1,3},{2,0},{3,1},{4,6},{5,7},{6,4},{7,5},{8,10},{9,11},{10,... | collective-permute-start | bytes 1179656 | tf_op jit(solution)/shard_map/ppermute | solution.py:17
  9.0 56.0 %collective-permute-start = (bf16[4,64,1536]{2,1,0:T(8,128)(2,1)}, bf16[4,64,1536]{2,1,0:T(8,128)(2,1)}, u32[]{:S(2)}, u32[]{:S(2)}) collective-permute-start(bf16[4,64,1536]{2,1,0:T(8,128)(2,1)} %pad_maximum_fusion.2), channel_id=1, source_target_pairs={{0,4},{4,0},{1,5},{5,1},{2,6},{6,2},{3,7},{7,3},{8,12},{12,8},{9,1... | collective-permute-start | bytes 2359304 | tf_op jit(solution)/shard_map/ppermute | solution.py:17
  14.7 19.0 %collective-permute-start.1 = (bf16[4,2,208,128]{3,2,0,1:T(8,128)(2,1)}, bf16[4,2,208,128]{3,2,0,1:T(8,128)(2,1)}, u32[]{:S(2)}, u32[]{:S(2)}) collective-permute-start(bf16[4,2,208,128]{3,2,0,1:T(8,128)(2,1)} %pad_maximum_fusion.5), channel_id=1, source_target_pairs={{0,1},{1,0},{2,3},{3,2},{4,5},{5,4},{6,7},{7,6},{8,9},{9,8},{10,11... | collective-permute-start | bytes 1277960 | tf_op jit(solution)/shard_map/ppermute | solution.py:17
  15.1 1.9 %collective-permute-start.12 = (f32[1,6144]{1,0:T(1,128)S(1)}, f32[1,6144]{1,0:T(1,128)S(1)}, u32[]{:S(2)}, u32[]{:S(2)}) collective-permute-start(f32[1,6144]{1,0:T(1,128)S(1)} %fusion.50), channel_id=1, source_target_pairs={{0,1},{1,0},{2,3},{3,2},{4,5},{5,4},{6,7},{7,6},{8,9},{9,8},{10,11... | collective-permute-start | bytes 73736 | tf_op jit(solution)/shard_map/ppermute | solution.py:17
  15.8 16.4 %copy-start.22 = (bf16[6144]{0:T(1024)(128)(2,1)S(1)}, bf16[6144]{0:T(1024)(128)(2,1)}, u32[]{:S(2)}) copy-start(bf16[6144]{0:T(1024)(128)(2,1)} %param.22) | copy-start | bytes 36868
  17.6 4.2 %collective-permute-start.13 = (f32[1,6144]{1,0:T(1,128)}, f32[1,6144]{1,0:T(1,128)}, u32[]{:S(2)}, u32[]{:S(2)}) collective-permute-start(f32[1,6144]{1,0:T(1,128)} %add.507), channel_id=1, source_target_pairs={{0,2},{1,3},{2,0},{3,1},{4,6},{5,7},{6,4},{7,5},{8,10},{9,11},{10,... | collective-permute-start | bytes 73736 | tf_op jit(solution)/shard_map/ppermute | solution.py:17
  22.5 3.9 %collective-permute-start.14 = (f32[1,6144]{1,0:T(1,128)S(1)}, f32[1,6144]{1,0:T(1,128)S(1)}, u32[]{:S(2)}, u32[]{:S(2)}) collective-permute-start(f32[1,6144]{1,0:T(1,128)S(1)} %add.508), channel_id=1, source_target_pairs={{0,8},{8,0},{16,24},{24,16},{1,9},{9,1},{17,25},{25,17},{2,10},{10... | collective-permute-start | bytes 73736 | tf_op jit(solution)/shard_map/ppermute | solution.py:17
  27.0 5.7 %collective-permute-start.15 = (f32[1,6144]{1,0:T(1,128)}, f32[1,6144]{1,0:T(1,128)}, u32[]{:S(2)}, u32[]{:S(2)}) collective-permute-start(f32[1,6144]{1,0:T(1,128)} %add.509), channel_id=1, source_target_pairs={{0,16},{8,24},{16,0},{24,8},{1,17},{9,25},{17,1},{25,9},{2,18},{10... | collective-permute-start | bytes 73736 | tf_op jit(solution)/shard_map/ppermute | solution.py:17
  37.3 15.8 %copy-start.28 = (f32[1,192]{1,0:T(1,128)S(1)}, f32[1,192]{1,0:T(1,128)}, u32[]{:S(2)}) copy-start(f32[1,192]{1,0:T(1,128)} %convert_add_fusion.2) | copy-start | bytes 2308
  37.3 15.8 %copy-start.34 = (f32[192]{0:T(256)S(1)}, f32[192]{0:T(256)}, u32[]{:S(2)}) copy-start(f32[192]{0:T(256)} %convert_element_type.357) | copy-start | bytes 2308
  37.3 5.9 %collective-permute-start.2 = (bf16[4,208,128]{2,1,0:T(8,128)(2,1)S(1)}, bf16[4,208,128]{2,1,0:T(8,128)(2,1)S(1)}, u32[]{:S(2)}, u32[]{:S(2)}) collective-permute-start(bf16[4,208,128]{2,1,0:T(8,128)(2,1)S(1)} %pad_maximum_fusion.9), channel_id=1, source_target_pairs={{0,2},{1,3},{2,0},{3,1},{4,6},{5,7},{6,4},{7,5},{8,10},{9,11},{10,... | collective-permute-start | bytes 638984 | tf_op jit(solution)/shard_map/ppermute | solution.py:17
  43.3 15.7 %copy-start.7 = (bf16[192,1536]{1,0:T(8,128)(2,1)S(1)}, bf16[192,1536]{1,0:T(8,128)(2,1)}, u32[]{:S(2)}) copy-start(bf16[192,1536]{1,0:T(8,128)(2,1)} %get-tuple-element.84) | copy-start | bytes 1769476
  43.3 15.7 %copy-start.8 = (bf16[192,1536]{1,0:T(8,128)(2,1)S(1)}, bf16[192,1536]{1,0:T(8,128)(2,1)}, u32[]{:S(2)}) copy-start(bf16[192,1536]{1,0:T(8,128)(2,1)} %get-tuple-element.85) | copy-start | bytes 1769476
  43.5 5.1 %collective-permute-start.3 = (bf16[208,128]{1,0:T(8,128)(2,1)S(1)}, bf16[208,128]{1,0:T(8,128)(2,1)S(1)}, u32[]{:S(2)}, u32[]{:S(2)}) collective-permute-start(bf16[208,128]{1,0:T(8,128)(2,1)S(1)} %get-tuple-element.58), channel_id=1, source_target_pairs={{0,8},{8,0},{16,24},{24,16},{1,9},{9,1},{17,25},{25,17},{2,10},{10... | collective-permute-start | bytes 159752 | tf_op jit(solution)/shard_map/ppermute | solution.py:17
  45.1 6.3 %collective-permute-start.4 = (bf16[208,128]{1,0:T(8,128)(2,1)S(1)}, bf16[208,128]{1,0:T(8,128)(2,1)S(1)}, u32[]{:S(2)}, u32[]{:S(2)}) collective-permute-start(bf16[208,128]{1,0:T(8,128)(2,1)S(1)} %get-tuple-element.59), channel_id=1, source_target_pairs={{0,16},{8,24},{16,0},{24,8},{1,17},{9,25},{17,1},{25,9},{2,18},{10... | collective-permute-start | bytes 159752 | tf_op jit(solution)/shard_map/ppermute | solution.py:17
  47.1 5.9 %collective-permute-start.5 = (bf16[208,128]{1,0:T(8,128)(2,1)S(1)}, bf16[208,128]{1,0:T(8,128)(2,1)S(1)}, u32[]{:S(2)}, u32[]{:S(2)}) collective-permute-start(bf16[208,128]{1,0:T(8,128)(2,1)S(1)} %get-tuple-element.60), channel_id=1, source_target_pairs={{0,24},{8,16},{16,8},{24,0},{1,25},{9,17},{17,9},{25,1},{2,26},{10... | collective-permute-start | bytes 159752 | tf_op jit(solution)/shard_map/ppermute | solution.py:17
  48.5 66.6 %collective-permute-start.21 = (s32[]{:T(128)}, s32[]{:T(128)}, u32[]{:S(2)}, u32[]{:S(2)}) collective-permute-start(s32[]{:T(128)} %xor.48), channel_id=1, source_target_pairs={{0,2},{1,3},{2,0},{3,1},{4,6},{5,7},{6,4},{7,5},{8,10},{9,11},{10,... | collective-permute-start | bytes 20 | tf_op jit(solution)/shard_map/ppermute | solution.py:17
  51.4 11.2 %collective-permute-start.16 = (f32[1,3072]{1,0:T(1,128)}, f32[1,3072]{1,0:T(1,128)}, u32[]{:S(2)}, u32[]{:S(2)}) collective-permute-start(f32[1,3072]{1,0:T(1,128)} %pad_maximum_fusion.24), channel_id=1, source_target_pairs={{0,4},{4,0},{1,5},{5,1},{2,6},{6,2},{3,7},{7,3},{8,12},{12,8},{9,1... | collective-permute-start | bytes 36872 | tf_op jit(solution)/shard_map/ppermute | solution.py:17
  54.8 4.2 %collective-permute-start.6 = (bf16[208,128]{1,0:T(8,128)(2,1)S(1)}, bf16[208,128]{1,0:T(8,128)(2,1)S(1)}, u32[]{:S(2)}, u32[]{:S(2)}) collective-permute-start(bf16[208,128]{1,0:T(8,128)(2,1)S(1)} %pad_maximum_fusion.10), channel_id=1, source_target_pairs={{0,4},{4,0},{1,5},{5,1},{2,6},{6,2},{3,7},{7,3},{8,12},{12,8},{9,1... | collective-permute-start | bytes 159752 | tf_op jit(solution)/shard_map/ppermute | solution.py:17
  62.5 4.0 %collective-permute-start.7 = (bf16[2,2,2,16,3200]{4,3,2,1,0:T(8,128)(2,1)S(1)}, bf16[2,2,2,16,3200]{4,3,2,1,0:T(8,128)(2,1)S(1)}, u32[]{:S(2)}, u32[]{:S(2)}) collective-permute-start(bf16[2,2,2,16,3200]{4,3,2,1,0:T(8,128)(2,1)S(1)} %pad_maximum_fusion.1), channel_id=1, source_target_pairs={{0,1},{1,0},{2,3},{3,2},{4,5},{5,4},{6,7},{7,6},{8,9},{9,8},{10,11... | collective-permute-start | bytes 2457608 | tf_op jit(solution)/shard_map/ppermute | solution.py:17
  64.7 5.8 %collective-permute-start.24 = (bf16[2,128,1536]{2,1,0:T(8,128)(2,1)S(1)}, bf16[2,128,1536]{2,1,0:T(8,128)(2,1)S(1)}, u32[]{:S(2)}, u32[]{:S(2)}) collective-permute-start(bf16[2,128,1536]{2,1,0:T(8,128)(2,1)S(1)} %pad_maximum_fusion.4), channel_id=1, source_target_pairs={{0,1},{1,0},{2,3},{3,2},{4,5},{5,4},{6,7},{7,6},{8,9},{9,8},{10,11... | collective-permute-start | bytes 2359304 | tf_op jit(solution)/shard_map/ppermute | solution.py:17
  68.1 11.7 %collective-permute-start.8 = (bf16[2,2,16,3200]{3,2,1,0:T(8,128)(2,1)S(1)}, bf16[2,2,16,3200]{3,2,1,0:T(8,128)(2,1)S(1)}, u32[]{:S(2)}, u32[]{:S(2)}) collective-permute-start(bf16[2,2,16,3200]{3,2,1,0:T(8,128)(2,1)S(1)} %pad_maximum_fusion.6), channel_id=1, source_target_pairs={{0,2},{1,3},{2,0},{3,1},{4,6},{5,7},{6,4},{7,5},{8,10},{9,11},{10,... | collective-permute-start | bytes 1228808 | tf_op jit(solution)/shard_map/ppermute | solution.py:17
  80.3 7.4 %collective-permute-start.9 = (bf16[16,3200]{1,0:T(8,128)(2,1)S(1)}, bf16[16,3200]{1,0:T(8,128)(2,1)S(1)}, u32[]{:S(2)}, u32[]{:S(2)}) collective-permute-start(bf16[16,3200]{1,0:T(8,128)(2,1)S(1)} %pad_maximum_fusion.14), channel_id=1, source_target_pairs={{0,8},{8,0},{16,24},{24,16},{1,9},{9,1},{17,25},{25,17},{2,10},{10... | collective-permute-start | bytes 307208 | tf_op jit(solution)/shard_map/ppermute | solution.py:17
  81.0 10.9 %collective-permute-start.10 = (bf16[16,3200]{1,0:T(8,128)(2,1)}, bf16[16,3200]{1,0:T(8,128)(2,1)S(1)}, u32[]{:S(2)}, u32[]{:S(2)}) collective-permute-start(bf16[16,3200]{1,0:T(8,128)(2,1)} %pad_maximum_fusion.15), channel_id=1, source_target_pairs={{0,16},{8,24},{16,0},{24,8},{1,17},{9,25},{17,1},{25,9},{2,18},{10... | collective-permute-start | bytes 307208 | tf_op jit(solution)/shard_map/ppermute | solution.py:17
  84.1 9.5 %collective-permute-start.11 = (bf16[16,3200]{1,0:T(8,128)(2,1)}, bf16[16,3200]{1,0:T(8,128)(2,1)S(1)}, u32[]{:S(2)}, u32[]{:S(2)}) collective-permute-start(bf16[16,3200]{1,0:T(8,128)(2,1)} %pad_maximum_fusion.16), channel_id=1, source_target_pairs={{0,24},{8,16},{16,8},{24,0},{1,25},{9,17},{17,9},{25,1},{2,26},{10... | collective-permute-start | bytes 307208 | tf_op jit(solution)/shard_map/ppermute | solution.py:17
  102.7 7.1 %collective-permute-start.17 = (bf16[16,3072]{1,0:T(8,128)(2,1)}, bf16[16,3072]{1,0:T(8,128)(2,1)}, u32[]{:S(2)}, u32[]{:S(2)}) collective-permute-start(bf16[16,3072]{1,0:T(8,128)(2,1)} %pad_maximum_fusion.17), channel_id=1, source_target_pairs={{0,8},{8,0},{16,24},{24,16},{1,9},{9,1},{17,25},{25,17},{2,10},{10... | collective-permute-start | bytes 294920 | tf_op jit(solution)/shard_map/ppermute | solution.py:17
  102.7 9.4 %collective-permute-start.18 = (bf16[16,3072]{1,0:T(8,128)(2,1)}, bf16[16,3072]{1,0:T(8,128)(2,1)}, u32[]{:S(2)}, u32[]{:S(2)}) collective-permute-start(bf16[16,3072]{1,0:T(8,128)(2,1)} %pad_maximum_fusion.17), channel_id=1, source_target_pairs={{0,16},{8,24},{16,0},{24,8},{1,17},{9,25},{17,1},{25,9},{2,18},{10... | collective-permute-start | bytes 294920 | tf_op jit(solution)/shard_map/ppermute | solution.py:17
  105.2 6.9 %collective-permute-start.19 = (bf16[16,3072]{1,0:T(8,128)(2,1)}, bf16[16,3072]{1,0:T(8,128)(2,1)}, u32[]{:S(2)}, u32[]{:S(2)}) collective-permute-start(bf16[16,3072]{1,0:T(8,128)(2,1)} %pad_maximum_fusion.17), channel_id=1, source_target_pairs={{0,24},{8,16},{16,8},{24,0},{1,25},{9,17},{17,9},{25,1},{2,26},{10... | collective-permute-start | bytes 294920 | tf_op jit(solution)/shard_map/ppermute | solution.py:17
  113.2 4.9 %collective-permute-start.20 = (bf16[1,2,2,16,3072]{4,3,2,1,0:T(8,128)(2,1)S(1)}, bf16[1,2,2,16,3072]{4,3,2,1,0:T(8,128)(2,1)}, u32[]{:S(2)}, u32[]{:S(2)}) collective-permute-start(bf16[1,2,2,16,3072]{4,3,2,1,0:T(8,128)(2,1)S(1)} %bitcast.229), channel_id=1, source_target_pairs={{0,1},{1,0},{2,3},{3,2},{4,5},{5,4},{6,7},{7,6},{8,9},{9,8},{10,11... | collective-permute-start | bytes 1179656 | tf_op jit(solution)/shard_map/ppermute | solution.py:17
  113.6 4.5 %collective-permute-start.25 = (f32[2,64,64]{2,1,0:T(8,128)S(1)}, f32[2,64,64]{2,1,0:T(8,128)S(1)}, u32[]{:S(2)}, u32[]{:S(2)}) collective-permute-start(f32[2,64,64]{2,1,0:T(8,128)S(1)} %fusion.23), channel_id=1, source_target_pairs={{0,4},{4,0},{1,5},{5,1},{2,6},{6,2},{3,7},{7,3},{8,12},{12,8},{9,1... | collective-permute-start | bytes 98312 | tf_op jit(solution)/shard_map/ppermute | solution.py:17
  119.3 10.8 %collective-permute-start.22 = (bf16[2,2,16,3072]{3,2,1,0:T(8,128)(2,1)S(1)}, bf16[2,2,16,3072]{3,2,1,0:T(8,128)(2,1)S(1)}, u32[]{:S(2)}, u32[]{:S(2)}) collective-permute-start(bf16[2,2,16,3072]{3,2,1,0:T(8,128)(2,1)S(1)} %get-tuple-element.25), channel_id=1, source_target_pairs={{0,2},{1,3},{2,0},{3,1},{4,6},{5,7},{6,4},{7,5},{8,10},{9,11},{10,... | collective-permute-start | bytes 1179656 | tf_op jit(solution)/shard_map/ppermute | solution.py:17
  133.5 5.7 %collective-permute-start.26 = (bf16[64,1536]{1,0:T(8,128)(2,1)S(1)}, bf16[64,1536]{1,0:T(8,128)(2,1)S(1)}, u32[]{:S(2)}, u32[]{:S(2)}) collective-permute-start(bf16[64,1536]{1,0:T(8,128)(2,1)S(1)} %get-tuple-element.33), channel_id=1, source_target_pairs={{0,4},{4,0},{1,5},{5,1},{2,6},{6,2},{3,7},{7,3},{8,12},{12,8},{9,1... | collective-permute-start | bytes 589832 | tf_op jit(solution)/shard_map/ppermute | solution.py:17
  (32 other events, 94.1 us)

commit v2 on v1

--- a/solution.py
+++ b/solution.py
@@ -260,10 +260,537 @@
     return result[None, None]
 
 
+F32, BF16 = jnp.float32, jnp.bfloat16
+ANY = pl.BlockSpec(memory_space=pl.ANY)
+VMEM = pl.BlockSpec(memory_space=pltpu.VMEM)
+SMEM = pl.BlockSpec(memory_space=pltpu.SMEM)
+NT = (((1,), (1,)), ((), ()))
+TN = (((0,), (0,)), ((), ()))
+
+
+def call(kernel, outs, ins, specs=None, scratch=(), name=None):
+    return pl.pallas_call(
+        kernel,
+        out_shape=outs,
+        in_specs=specs if specs is not None else [VMEM] * len(ins),
+        out_specs=jax.tree.map(lambda _: VMEM, outs),
+        scratch_shapes=list(scratch),
+        compiler_params=pltpu.CompilerParams(vmem_limit_bytes=40 * 1024 * 1024),
+        name=name,
+    )(*ins)
+
+
+def struct(shape, dtype=BF16):
+    return jax.ShapeDtypeStruct(shape, dtype)
+
+
+def at(index, size):
+    return pl.ds(pl.multiple_of(index * size, size), size)
+
+
+def stat_rows(stat):
+    high = stat.astype(BF16).astype(F32)
+    row = lax.broadcasted_iota(jnp.int32, (ROWS, stat.shape[1]), 0)
+    return jnp.where(row == 0, high, jnp.where(row == 1, stat - high, 0.0)).astype(BF16)
+
+
+def stat_of(rows):
+    rows = rows.astype(F32)
+    return rows[0:1] + rows[1:2]
+
+
+def context_kernel(h_ref, w_ref, b_ref, send_ref, keep_ref, stat_ref):
+    mine = lax.rem(lax.axis_index("req"), 2)
+    features = b_ref.shape[1]
+    pairs = w_ref.shape[1] // (2 * features)
+    total = jnp.zeros((1, h_ref.shape[0]), F32)
+    for p in range(pairs):
+        product = jnp.dot(
+            h_ref[...], w_ref[:, p * 2 * features : (p + 1) * 2 * features],
+            preferred_element_type=F32,
+        ).T
+        total = total + jnp.sum(product, axis=0, keepdims=True)
+        low, high = product[:features], product[features:]
+        rows = slice(p * features, (p + 1) * features)
+        keep_ref[rows] = jnp.where(mine == 0, low, high)
+        send_ref[rows] = jnp.where(mine == 0, high, low).astype(BF16)
+    stat = total + jnp.sum(b_ref[...].astype(F32))
+    send_ref[pairs * features :] = stat_rows(stat)
+    stat_ref[...] = jnp.broadcast_to(stat, stat_ref.shape)
+
+
+def halve_kernel(features, got_ref, keep_ref, stat_ref, send_ref, kept_ref, out_stat_ref):
+    mine = lax.rem(lax.axis_index("req") // 2, 2)
+    count = keep_ref.shape[0] // (2 * features)
+    for i in range(count):
+        rows = slice(i * features, (i + 1) * features)
+        own, other = at(2 * i + mine, features), at(2 * i + 1 - mine, features)
+        kept_ref[rows] = keep_ref[own] + got_ref[own].astype(F32)
+        send_ref[rows] = (keep_ref[other] + got_ref[other].astype(F32)).astype(BF16)
+    stat = stat_ref[0:1] + stat_of(got_ref[2 * count * features :])
+    send_ref[count * features :] = stat_rows(stat)
+    out_stat_ref[...] = jnp.broadcast_to(stat, out_stat_ref.shape)
+
+
+def scatter_kernel(features, got_ref, keep_ref, stat_ref, kept_ref, out_stat_ref, *send_refs):
+    e = lax.axis_index("enc")
+    count = keep_ref.shape[0] // features
+    stat = stat_ref[0:1] + stat_of(got_ref[count * features :])
+    own = at(e, features)
+    for k, send_ref in enumerate(send_refs):
+        other = at(e ^ (k + 1), features)
+        send_ref[:features] = (keep_ref[other] + got_ref[other].astype(F32)).astype(BF16)
+        send_ref[features:] = stat_rows(stat)
+    kept_ref[...] = keep_ref[own] + got_ref[own].astype(F32)
+    out_stat_ref[...] = jnp.broadcast_to(stat, out_stat_ref.shape)
+
+
+def centre_kernel(width, keep_ref, stat_ref, bias_ref, scale_ref, *refs):
+    got_refs, out_ref = refs[:-1], refs[-1]
+    features = keep_ref.shape[0]
+    total = keep_ref[...] + bias_ref[...]
+    stat = stat_ref[0:1]
+    for got_ref in got_refs:
+        total = total + got_ref[:features].astype(F32)
+        stat = stat + stat_of(got_ref[features:])
+    centred = total - stat * (1.0 / width)
+    out_ref[:features] = (scale_ref[...] * centred).astype(BF16)
+    out_ref[features:] = stat_rows(jnp.sum(centred * centred, axis=0, keepdims=True))
+
+
+def project_kernel(n_seq, n_req, n_enc, *refs):
+    payload_refs = refs[: n_seq * n_req]
+    weight_refs = refs[n_seq * n_req : n_seq * n_req + n_req]
+    keep_ref = refs[n_seq * n_req + n_req]
+    send_refs = refs[n_seq * n_req + n_req + 1 : -1]
+    rows_ref = refs[-1]
+    features, width = weight_refs[0].shape
+    tokens = payload_refs[0].shape[1]
+    lane = lax.broadcasted_iota(jnp.int32, (tokens, HDIM), 1)
+    for p in range(n_seq):
+        total, squares = None, None
+        for k in range(n_req):
+            payload = payload_refs[p * n_req + k]
+            term = lax.dot_general(
+                payload[:features], weight_refs[k][...], TN, preferred_element_type=F32
+            )
+            part = stat_of(payload[features:])
+            total = term if total is None else total + term
+            squares = part if squares is None else squares + part
+        rows = slice(p * tokens, (p + 1) * tokens)
+        rows_ref[rows, :width] = total
+        column = jnp.broadcast_to(squares, (HDIM, tokens)).T
+        high = column.astype(BF16).astype(F32)
+        rows_ref[rows, width:] = jnp.where(
+            lane == 0, high, jnp.where(lane == 1, column - high, 0.0)
+        )
+    e = lax.axis_index("enc")
+    size = n_seq * tokens // n_enc
+    keep_ref[...] = rows_ref[at(e, size)]
+    for k, send_ref in enumerate(send_refs):
+        send_ref[...] = rows_ref[at(e ^ (k + 1), size)].astype(BF16)
+
+
+def finish_kernel(n_seq, n_enc, n_req, model_width, keep_ref, shift_ref, bias_ref, *refs):
+    got_refs, out_ref = refs[:-1], refs[-1]
+    e, r, s = lax.axis_index("enc"), lax.axis_index("req"), lax.axis_index("seq")
+    width = out_ref.shape[1]
+    half = width // 2
+    inner = shift_ref.shape[1] // 2
+    total = keep_ref[...]
+    for got_ref in got_refs:
+        total = total + got_ref[...].astype(F32)
+    squares = total[:, width : width + 1] + total[:, width + 1 : width + 2]
+    factor = lax.rsqrt(squares * (1.0 / model_width) + epsilon_norm)
+    prompt = s ^ (e // (n_enc // n_seq))
+    for part in range(2):
+        columns = pl.ds(
+            pl.multiple_of(part * inner + (s * n_req + r) * half, HDIM), half
+        )
+        shift = shift_ref[pl.ds(prompt, 1), columns] + bias_ref[:, columns].astype(F32)
+        rows = total[:, part * half : (part + 1) * half] * factor + shift
+        for h in range(half // HDIM):
+            head = rows[:, h * HDIM : (h + 1) * HDIM]
+            if part == 0:
+                head = head * lax.rsqrt(
+                    jnp.mean(head * head, axis=1, keepdims=True) + epsilon_norm
+                )
+            place = part * half + h * HDIM
+            out_ref[:, place : place + HDIM] = head.astype(BF16)
+
+
+def choose_kernel(n_seq, n_enc, chosen_ref, *refs):
+    part_refs, out_refs = refs[:n_enc], refs[n_enc:]
+    e, r, s = lax.axis_index("enc"), lax.axis_index("req"), lax.axis_index("seq")
+    halves = n_enc // n_seq
+    size = part_refs[0].shape[0]
+    for k, out_ref in enumerate(out_refs):
+        prompt = s ^ chosen_ref[r ^ k]
+        for h in range(halves):
+            place = e ^ (prompt * halves + h)
+            for j in range(n_enc):
+                @pl.when(place == j)
+                def _():
+                    out_ref[h * size : (h + 1) * size] = part_refs[j][...]
+
+
+def weight_kernel(n_req, part, inner, *refs):
+    w_ref, out_refs, sems = refs[0], refs[2:-1], refs[-1]
+    r, s = lax.axis_index("req"), lax.axis_index("seq")
+    half = part // n_req
+    copies = []
+    for k, out_ref in enumerate(out_refs):
+        for side in range(2):
+            columns = pl.ds(
+                pl.multiple_of(side * inner + (s * n_req + (r ^ k)) * half, HDIM), half
+            )
+            copies.append(
+                pltpu.make_async_copy(
+                    w_ref.at[:, columns],
+                    out_ref.at[:, pl.ds(side * half, half)],
+                    sems.at[2 * k + side],
+                )
+            )
+    for copy in copies:
+        copy.start()
+    for copy in copies:
+        copy.wait()
+
+
+def image_kernel(part, inner, step, qk_ref, v_ref, x_ref, dep_ref, out_ref, sems):
+    start = (lax.axis_index("seq") ^ step) * part
+    copies = []
+    for i, (ref, base) in enumerate(((qk_ref, 0), (qk_ref, inner), (v_ref, 0), (x_ref, 0))):
+        columns = pl.ds(pl.multiple_of(base + start, HDIM), part)
+        copies.append(pltpu.make_async_copy(ref.at[:, columns], out_ref.at[i], sems.at[i]))
+    for copy in copies:
+        copy.start()
+    for copy in copies:
+        copy.wait()
+
+
+def maps_kernel(part, down_ref, up_ref, dep_ref, out_ref, sems):
+    rank = down_ref.shape[0]
+    columns = pl.ds(pl.multiple_of(lax.axis_index("seq") * part, HDIM), part)
+    copies = [
+        pltpu.make_async_copy(down_ref.at[:, columns], out_ref.at[pl.ds(0, rank)], sems.at[0]),
+        pltpu.make_async_copy(up_ref.at[:, columns], out_ref.at[pl.ds(rank, rank)], sems.at[1]),
+    ]
+    for copy in copies:
+        copy.start()
+    for copy in copies:
+        copy.wait()
+
+
+def lowrank_kernel(n_req, part, adapter_ref, x_ref, *refs):
+    out_ref, chosen_ref = refs[-2:]
+    map_refs = refs[:n_req]
+    got_refs = refs[n_req:-2]
+    place = adapter_ref[0, 0] ^ lax.axis_index("req")
+    for k in range(n_req):
+        @pl.when(place == k)
+        def _():
+            chosen_ref[...] = map_refs[k][...]
+    rank = out_ref.shape[-1]
+    down = chosen_ref[:rank]
+    own = x_ref[:, pl.ds(pl.multiple_of(lax.axis_index("seq") * part, HDIM), part)]
+    out_ref[0] = lax.dot_general(own, down, NT, preferred_element_type=F32)
+    for k, got_ref in enumerate(got_refs):
+        out_ref[k + 1] = lax.dot_general(got_ref[3], down, NT, preferred_element_type=F32)
+
+
+def arrange_kernel(n_req, part, inner, low_ref, maps_ref, qk_ref, v_ref, *refs):
+    got_refs, (q_out, k_out, v_out) = refs[:-3], refs[-3:]
+    r, s = lax.axis_index("req"), lax.axis_index("seq")
+    rank = maps_ref.shape[0] // 2
+    half = part // n_req
+    tokens = qk_ref.shape[0]
+    low = low_ref[...].astype(BF16)
+    for k in range(n_req):
+        place = (r ^ k) * half
+        up = maps_ref[rank:, pl.ds(pl.multiple_of(place, HDIM), half)]
+        for i in range(len(got_refs) + 1):
+            rows = slice(i * tokens, (i + 1) * tokens)
+            if i == 0:
+                own = s * part + place
+                q = qk_ref[:, pl.ds(pl.multiple_of(own, HDIM), half)]
+                key = qk_ref[:, pl.ds(pl.multiple_of(inner + own, HDIM), half)]
+                base = v_ref[:, pl.ds(pl.multiple_of(own, HDIM), half)]
+            else:
+                columns = pl.ds(pl.multiple_of(place, HDIM), half)
+                q = got_refs[i - 1][0, :, columns]
+                key = got_refs[i - 1][1, :, columns]
+                base = got_refs[i - 1][2, :, columns]
+            q_out[k, rows] = q
+            k_out[k, rows] = key
+            v_out[k, rows] = (
+                base.astype(F32) + jnp.dot(low[i], up, preferred_element_type=F32)
+            ).astype(BF16)
+
+
+def heads_kernel(scale, live_ref, text_ref, q_ref, k_ref, v_ref, *out_refs):
+    live = live_ref[...] != 0
+    half = q_ref.shape[2]
+    size = out_refs[0].shape[0]
+    for h in range(half // HDIM):
+        cols = slice(h * HDIM, (h + 1) * HDIM)
+        vals = slice(half + h * HDIM, half + (h + 1) * HDIM)
+        q = q_ref[0, :, cols]
+        st = lax.dot_general(q, text_ref[:, cols], NT, preferred_element_type=F32) * scale
+        si = lax.dot_general(q, k_ref[0, :, cols], NT, preferred_element_type=F32) * scale
+        st = jnp.where(live, st, -jnp.inf)
+        top = jnp.maximum(
+            jnp.max(st, axis=1, keepdims=True), jnp.max(si, axis=1, keepdims=True)
+        )
+        wt = jnp.exp(st - top)
+        wi = jnp.exp(si - top)
+        total = jnp.sum(wt, axis=1, keepdims=True) + jnp.sum(wi, axis=1, keepdims=True)
+        mixed = jnp.dot(
+            wt.astype(BF16), text_ref[:, vals], preferred_element_type=F32
+        ) + jnp.dot(wi.astype(BF16), v_ref[0, :, cols], preferred_element_type=F32)
+        mixed = (mixed / total).astype(BF16)
+        for i, out_ref in enumerate(out_refs):
+            out_ref[:, cols] = mixed[i * size : (i + 1) * size]
+
+
+def assemble_kernel(n_req, n_seq, *refs):
+    out_ref = refs[-1]
+    r, s = lax.axis_index("req"), lax.axis_index("seq")
+    half = refs[0].shape[1]
+    for k in range(n_req):
+        for i in range(n_seq):
+            start = ((s ^ i) * n_req + (r ^ k)) * half
+            out_ref[:, pl.ds(pl.multiple_of(start, HDIM), half)] = refs[k * n_seq + i][...]
+
+
+def per_device_heads(
+    n_enc,
+    n_req,
+    n_seq,
+    encoder_hidden,
+    prompt_token_ids,
+    context_weight,
+    context_bias,
+    modulation_shift,
+    modulation_scale,
+    key_value_weight,
+    key_value_bias,
+    request_prompt,
+    adapter_of_request,
+    adapter_down_maps,
+    adapter_up_maps,
+    image_stream_input,
+    image_query_key,
+    image_value_rows,
+):
+    e, r, s = lax.axis_index("enc"), lax.axis_index("req"), lax.axis_index("seq")
+    model_width = context_weight.shape[1]
+    features = context_bias.shape[0]
+    tokens = encoder_hidden.shape[1]
+    inner = key_value_weight.shape[1] // 2
+    part = inner // n_seq
+    half = part // n_req
+    image_rows = image_query_key.shape[2]
+    rank = adapter_up_maps.shape[1]
+    qk, base, stream = image_query_key[0, 0], image_value_rows[0, 0], image_stream_input[0, 0]
+    dma = pltpu.SemaphoreType.DMA
+    stat = struct((8, tokens), F32)
+
+    send, keep, sums = call(
+        context_kernel,
+        (
+            struct((model_width // 2 + ROWS, tokens)),
+            struct((model_width // 2, tokens), F32),
+            stat,
+        ),
+        (encoder_hidden[0], context_weight, context_bias[None]),
+        name="context",
+    )
+    got = swap(send, "req", n_req, 1)
+
+    packed = [
+        call(
+            functools.partial(image_kernel, part, inner, k),
+            struct((4, image_rows, part)),
+            (qk, base, stream, keep),
+            [ANY] * 4,
+            [dma((4,))],
+            name="image_pack",
+        )
+        for k in range(1, n_seq)
+    ]
+    image_got = [swap(packed[k - 1], "seq", n_seq, k) for k in range(1, n_seq)]
+    weights = call(
+        functools.partial(weight_kernel, n_req, part, inner),
+        tuple(struct((features, 2 * half)) for _ in range(n_req)),
+        (key_value_weight, keep),
+        [ANY] * 2,
+        [dma((2 * n_req,))],
+        name="weight_pack",
+    )
+
+    send, keep, sums = call(
+        functools.partial(halve_kernel, features),
+        (
+            struct((n_enc * features + ROWS, tokens)),
+            struct((n_enc * features, tokens), F32),
+            stat,
+        ),
+        (got, keep, sums),
+        name="halve",
+    )
+    got = swap(send, "req", n_req, 2)
+    keep, sums, *sends = call(
+        functools.partial(scatter_kernel, features),
+        (struct((features, tokens), F32), stat)
+        + tuple(struct((features + ROWS, tokens)) for _ in range(1, n_enc)),
+        (got, keep, sums),
+        name="scatter",
+    )
+    arrived = [swap(sends[k - 1], "enc", n_enc, k) for k in range(1, n_enc)]
+    weights = lax.optimization_barrier((weights, keep))[0]
+    weights = [weights[0]] + [swap(weights[k], "req", n_req, k) for k in range(1, n_req)]
+
+    bias_columns = jnp.broadcast_to(context_bias.astype(F32)[:, None], (features, tokens))
+    scale_columns = jnp.broadcast_to(
+        1.0 + modulation_scale[0].astype(F32)[:, None], (features, tokens)
+    )
+    own = call(
+        functools.partial(centre_kernel, model_width),
+        struct((features + ROWS, tokens)),
+        (keep, sums, bias_columns, scale_columns, *arrived),
+        name="centre",
+    )
+    payloads = []
+    for i in range(n_seq):
+        for k in range(n_req):
+            block = own
+            if i or k:
+                block = lax.ppermute(
+                    own,
+                    ("seq", "req"),
+                    [
+                        (a * n_req + b, (a ^ i) * n_req + (b ^ k))
+                        for a in range(n_seq)
+                        for b in range(n_req)
+                    ],
+                )
+            payloads.append(block)
+
+    shift_part = jnp.dot(modulation_shift, key_value_weight, preferred_element_type=F32)
+    wide = 2 * inner
+    index = jnp.arange(n_seq + 1)[:, None]
+    lane = jnp.arange(wide)[None, :]
+    asked = jnp.where(
+        (lane == e * n_req + r) & (s == 0), request_prompt[0, 0].astype(F32), 0.0
+    )
+    table = jnp.where(
+        index == s, shift_part, jnp.where(index == n_seq, asked, jnp.zeros((), F32))
+    )
+    table = lax.psum(table, ("enc", "seq", "req"))
+    prompts = lax.dynamic_slice_in_dim(table[n_seq], e * n_req, n_req, 0).astype(jnp.int32)
+
+    size = n_seq * tokens // n_enc
+    wide_rows = 2 * half + HDIM
+    keep, *sends = call(
+        functools.partial(project_kernel, n_seq, n_req, n_enc),
+        (struct((size, wide_rows), F32),)
+        + tuple(struct((size, wide_rows)) for _ in range(1, n_enc)),
+        (*payloads, *weights),
+        scratch=[pltpu.VMEM((n_seq * tokens, wide_rows), F32)],
+        name="project",
+    )
+    arrived = [swap(sends[k - 1], "enc", n_enc, k) for k in range(1, n_enc)]
+
+    maps = call(
+        functools.partial(maps_kernel, part),
+        struct((2 * rank, part)),
+        (adapter_down_maps[0].T, adapter_up_maps[0], keep),
+        [ANY] * 3,
+        [dma((2,))],
+        name="maps_pack",
+    )
+    maps = [maps]
+    step = n_req // 2
+    while step:
+        maps = maps + [swap(m, "req", n_req, step) for m in maps]
+        step //= 2
+    ordered = [None] * n_req
+    place = [0]
+    step = n_req // 2
+    while step:
+        place = place + [p ^ step for p in place]
+        step //= 2
+    for p, m in zip(place, maps):
+        ordered[p] = m
+    low, chosen_maps = call(
+        functools.partial(lowrank_kernel, n_req, part),
+        (struct((n_seq, image_rows, rank), F32), struct((2 * rank, part))),
+        (adapter_of_request, stream, *ordered, *image_got),
+        [SMEM] + [VMEM] * (1 + n_req + len(image_got)),
+        name="lowrank",
+    )
+    for bit in bits_of(n_seq):
+        other = swap(low, "seq", n_seq, bit)
+        low = low + jnp.stack([other[k ^ bit] for k in range(n_seq)])
+    arranged = struct((n_req, n_seq * image_rows, half))
+    queries, image_keys, image_values = call(
+        functools.partial(arrange_kernel, n_req, part, inner),
+        (arranged, arranged, arranged),
+        (low, chosen_maps, qk, base, *image_got),
+        name="arrange",
+    )
+
+    text = call(
+        functools.partial(finish_kernel, n_seq, n_enc, n_req, model_width),
+        struct((size, 2 * half)),
+        (keep, table, key_value_bias[None], *arrived),
+        name="finish",
+    )
+    parts = [text] + [swap(text, "enc", n_enc, k) for k in range(1, n_enc)]
+    rows = call(
+        functools.partial(choose_kernel, n_seq, n_enc),
+        tuple(struct((tokens, 2 * half)) for _ in range(n_req)),
+        (prompts, *parts),
+        [SMEM] + [VMEM] * n_enc,
+        name="choose",
+    )
+    rows = [rows[0]] + [swap(rows[k], "req", n_req, k) for k in range(1, n_req)]
+    live = lax.dynamic_slice_in_dim(prompt_token_ids, request_prompt[0, 0], 1, 0)
+    pieces = [None] * n_req
+    for k in range(n_req):
+        block = pl.BlockSpec((1, n_seq * image_rows, half), lambda i, k=k: (k, 0, 0))
+        whole = lambda shape: pl.BlockSpec(shape, lambda i: (0, 0))
+        mixed = pl.pallas_call(
+            functools.partial(heads_kernel, HDIM ** (-0.5)),
+            grid=(1,),
+            out_shape=[struct((image_rows, half)) for _ in range(n_seq)],
+            in_specs=[whole((1, tokens)), whole((tokens, 2 * half)), block, block, block],
+            out_specs=[whole((image_rows, half)) for _ in range(n_seq)],
+            compiler_params=pltpu.CompilerParams(vmem_limit_bytes=40 * 1024 * 1024),
+            name="heads",
+        )(live, rows[k], queries, image_keys, image_values)
+        pieces[k] = [mixed[0]] + [swap(mixed[i], "seq", n_seq, i) for i in range(1, n_seq)]
+    result = call(
+        functools.partial(assemble_kernel, n_req, n_seq),
+        struct((image_rows, inner)),
+        tuple(p for group in pieces for p in group),
+        name="assemble",
+    )
+    return result[None, None]
+
+
 def solution(mesh):
     sizes = mesh.shape
+    n_enc, n_req, n_seq = sizes["enc"], sizes["req"], sizes["seq"]
+
+    def run(*arrays):
+        heads = arrays[6].shape[1] // (2 * HDIM)
+        pick_body = per_device_heads if heads % (n_seq * n_req) == 0 else per_device
+        return pick_body(n_enc, n_req, n_seq, *arrays)
+
     return jax.shard_map(
-        functools.partial(per_device, sizes["enc"], sizes["req"], sizes["seq"]),
+        run,
         mesh=mesh,
         in_specs=(
             P("seq", None, ("enc", "req")),

time: 141 us -> 237 us (1.68)
  waiting for transfers between devices: 35.6 us -> 150 us
  other arithmetic: 33.2 us -> 1.57 us
  Pallas kernels: 3.26 us -> 14.4 us
  between operations: 4.02 us -> 15.1 us
  local copies, waits for them, and re-layouts: 23.6 us -> 13.7 us
  starting transfers between devices: 35.2 us -> 41 us
  matrix products: 5.19 us -> 1.03 us
    psum x0 -> x1, waiting for transfers between devices: none -> 119 us  [per_device_heads(): table = lax.psum(table, ('enc', 'seq', 'req'))]
    ppermute x27 -> x26, waiting for transfers between devices: 35.6 us -> 23.3 us  [swap(): return lax.ppermute(block, axis, [(i, i ^ step) for i in range(size)])]
    pallas_call x1 -> x17, Pallas kernels: 3.26 us -> 14.4 us  [the longest x13 10.7 us: call(): pl.pallas_call(kernel, out_shape=outs, in_specs=specs if specs is not Non...]
    concatenate x18 -> x0, other arithmetic: 8.6 us -> none  [the longest x2 2.03 us: per_device(): maps = jnp.concatenate([maps, swap(maps, 'req', n_req, bit)], axis=0)]
    convert_element_type x24 -> x1, other arithmetic: 8.21 us -> 0.07 us  [per_device_heads(): lax.dynamic_slice_in_dim(table[n_seq], e * n_req, n_req, 0)]
    ppermute x0 -> x7, waiting for transfers between devices: none -> 7.47 us  [per_device_heads(): lax.ppermute(own, ('seq', 'req'), [(a * n_req + b, (a ^ i) * n_req + (b ^...]
    add x14 -> x2, other arithmetic: 6.8 us -> 0.02 us  [the longest x1 0.01 us: per_device_heads(): low = low + jnp.stack([other[k ^ bit] for k in range(n_seq)])]
    unnamed x74 -> x62, local copies, waits for them, and re-layouts: 5.25 us -> 11.1 us
  transfers between devices with their start and end apart: 27 -> 34, of which waited for: 10 -> 14; matrix products, arithmetic and copies ran while one was open for 37% -> 2% of each run, Pallas kernels for 0% -> 5%
where the time goes in v2:
time: 237 us; the launch traced here: 236 us
  waiting for transfers between devices  150 us (63%)
  starting transfers between devices  41 us (17%)
  between operations  15.1 us (6%)
  Pallas kernels  14.4 us (6%)
  local copies, waits for them, and re-layouts  13.7 us (6%)
    psum x1, waiting for transfers between devices, per_device_heads(): table = lax.psum(table, ('enc', 'seq', 'req'))  119 us
    ppermute x26, starting transfers between devices, swap(): return lax.ppermute(block, axis, [(i, i ^ step) for i in range(size)])  35.7 us
    ppermute x26, waiting for transfers between devices, swap(): return lax.ppermute(block, axis, [(i, i ^ step) for i in range(size)])  23.3 us
    unnamed x62, local copies, waits for them, and re-layouts  11.1 us
    pallas_call x13, Pallas kernels, call(): pl.pallas_call(kernel, out_shape=outs, in_specs=specs if specs is not Non...  10.7 us
    ppermute x7, waiting for transfers between devices, per_device_heads(): lax.ppermute(own, ('seq', 'req'), [(a * n_req + b, (a ^ i) * n_req + (b ^...  7.47 us
    ppermute x7, starting transfers between devices, per_device_heads(): lax.ppermute(own, ('seq', 'req'), [(a * n_req + b, (a ^ i) * n_req + (b ^...  5.28 us
  transfers between devices with their start and end apart: 34, of which 14 were waited for; matrix products, arithmetic and copies ran while one was open for 2% of the time, Pallas kernels for 5%

profile of v2, /device:TPU:0, one launch (start us, length us, event | category | flops | bytes accessed | tf_op | source)
XLA Modules:
  0.0 236.4 jit_solution(2213610637598320776)
XLA Ops:
  7.4 1.4 copy-done.5
  10.8 1.4 collective-permute-done.got_ref
  12.3 3.0 %collective-permute-start.1 = (bf16[784,128]{1,0:T(8,128)(2,1)S(1)}, bf16[784,128]{1,0:T(8,128)(2,1)S(1)}, u32[]{:S(2)}, u32[]{:S(2)}) collective-permute-start(bf16[784,128]{1,0:T(8,128)(2,1)S(1)} %get-tuple-element.48), channel_id=1, source_target_pairs={{0,2},{1,3},{2,0},{3,1},{4,6},{5,7},{6,4},{7,5},{8,10},{9,11},{10,... | collective-permute-start | bytes 602120 | tf_op jit(solution)/shard_map/ppermute | solution.py:17
  15.2 5.3 %collective-permute-done.1.got_ref = bf16[784,128]{1,0:T(8,128)(2,1)S(1)} collective-permute-done((bf16[784,128]{1,0:T(8,128)(2,1)S(1)}, bf16[784,128]{1,0:T(8,128)(2,1)S(1)}, u32[]{:S(2)}, u32[]{:S(2)}) %collective-permute-start.1) | collective-permute-done | bytes 200736 | tf_op jit(solution)/shard_map/ppermute | solution.py:17
  20.6 1.9 collective-permute-start.2
  22.4 1.2 weight_pack.1
  24.3 2.6 %collective-permute-start.3 = (bf16[208,128]{1,0:T(8,128)(2,1)S(1)}, bf16[208,128]{1,0:T(8,128)(2,1)S(1)}, u32[]{:S(2)}, u32[]{:S(2)}) collective-permute-start(bf16[208,128]{1,0:T(8,128)(2,1)S(1)} %get-tuple-element.54), channel_id=1, source_target_pairs={{0,16},{8,24},{16,0},{24,8},{1,17},{9,25},{17,1},{25,9},{2,18},{10... | collective-permute-start | bytes 159752 | tf_op jit(solution)/shard_map/ppermute | solution.py:17
  26.9 1.7 collective-permute-start.13
  29.9 3.0 %collective-permute-done.4.refs_2_ = bf16[208,128]{1,0:T(8,128)(2,1)S(1)} collective-permute-done((bf16[208,128]{1,0:T(8,128)(2,1)S(1)}, bf16[208,128]{1,0:T(8,128)(2,1)S(1)}, u32[]{:S(2)}, u32[]{:S(2)}) %collective-permute-start.4) | collective-permute-done | bytes 53280 | tf_op jit(solution)/shard_map/ppermute | solution.py:17
  33.7 2.4 %collective-permute-start.10 = (bf16[208,128]{1,0:T(8,128)(2,1)}, bf16[208,128]{1,0:T(8,128)(2,1)S(1)}, u32[]{:S(2)}, u32[]{:S(2)}) collective-permute-start(bf16[208,128]{1,0:T(8,128)(2,1)} %centre.1.refs_0_), channel_id=1, source_target_pairs={{0,6},{1,7},{2,4},{3,5},{4,2},{5,3},{6,0},{7,1},{8,14},{9,15},{10,... | collective-permute-start | bytes 159752 | tf_op jit(solution)/shard_map/ppermute | solution.py:669
  36.2 2.9 %collective-permute-done.10.refs_6_ = bf16[208,128]{1,0:T(8,128)(2,1)S(1)} collective-permute-done((bf16[208,128]{1,0:T(8,128)(2,1)}, bf16[208,128]{1,0:T(8,128)(2,1)S(1)}, u32[]{:S(2)}, u32[]{:S(2)}) %collective-permute-start.10) | collective-permute-done | bytes 53280 | tf_op jit(solution)/shard_map/ppermute | solution.py:669
  39.7 1.3 collective-permute-done.11.refs_7_
  43.0 3.3 %collective-permute-done.6.refs_2_ = bf16[208,128]{1,0:T(8,128)(2,1)S(1)} collective-permute-done((bf16[208,128]{1,0:T(8,128)(2,1)}, bf16[208,128]{1,0:T(8,128)(2,1)S(1)}, u32[]{:S(2)}, u32[]{:S(2)}) %collective-permute-start.6) | collective-permute-done | bytes 53280 | tf_op jit(solution)/shard_map/ppermute | solution.py:669
  47.0 2.0 collective-permute-start.8
  49.6 1.1 copy-done.2
  54.0 2.6 %project.1 = (f32[64,896]{1,0:T(8,128)S(1)}, bf16[64,896]{1,0:T(8,128)(2,1)}, bf16[64,896]{1,0:T(8,128)(2,1)S(1)}, bf16[64,896]{1,0:T(8,128)(2,1)S(1)}) custom-call(bf16[208,128]{1,0:T(8,128)(2,1)} %centre.1.refs_0_, bf16[208,128]{1,0:T(8,128)(2,1)S(1)} %copy-done.21, bf16[208,128]{1,0:T(8,128)(2,1)S(1)} %copy-done.23, bf16[208,128]{1,0:T(8,128)(2,1)S(1)} %copy-done.25, ...), custom_call_target="tpu_custom_call" | custom-call | tf_op jit(solution)/shard_map/project/pallas_call | solution.py:272
  57.5 1.4 collective-permute-start.22
  62.0 3.5 %collective-permute-start.16 = (bf16[64,896]{1,0:T(8,128)(2,1)}, bf16[64,896]{1,0:T(8,128)(2,1)S(1)}, u32[]{:S(2)}, u32[]{:S(2)}) collective-permute-start(bf16[64,896]{1,0:T(8,128)(2,1)} %copy-done.27), channel_id=1, source_target_pairs={{0,16},{8,24},{16,0},{24,8},{1,17},{9,25},{17,1},{25,9},{2,18},{10... | collective-permute-start | bytes 344072 | tf_op jit(solution)/shard_map/ppermute | solution.py:17
  66.1 4.7 %collective-permute-start.17 = (bf16[64,896]{1,0:T(8,128)(2,1)}, bf16[64,896]{1,0:T(8,128)(2,1)S(1)}, u32[]{:S(2)}, u32[]{:S(2)}) collective-permute-start(bf16[64,896]{1,0:T(8,128)(2,1)} %copy-done.26), channel_id=1, source_target_pairs={{0,24},{8,16},{16,8},{24,0},{1,25},{9,17},{17,9},{25,1},{2,26},{10... | collective-permute-start | bytes 344072 | tf_op jit(solution)/shard_map/ppermute | solution.py:17
  70.8 1.5 select_select_fusion
  73.7 118.8 %all-reduce.2.cloned.1.call-done.shift_ref = f32[3,6144]{1,0:T(4,128)} async-done(((f32[3,6144]{1,0:T(4,128)}), f32[3,6144]{1,0:T(4,128)}) %all-reduce.2.cloned.1.call-update) | async-done | bytes 73744 | tf_op jit(solution)/shard_map/psum | solution.py:690
  195.6 3.3 %collective-permute-start.18 = (bf16[64,768]{1,0:T(8,128)(2,1)S(1)}, bf16[64,768]{1,0:T(8,128)(2,1)S(1)}, u32[]{:S(2)}, u32[]{:S(2)}) collective-permute-start(bf16[64,768]{1,0:T(8,128)(2,1)S(1)} %finish.1.refs_0_), channel_id=1, source_target_pairs={{0,8},{8,0},{16,24},{24,16},{1,9},{9,1},{17,25},{25,17},{2,10},{10... | collective-permute-start | bytes 294920 | tf_op jit(solution)/shard_map/ppermute | solution.py:17
  198.9 1.4 collective-permute-start.19
  202.3 1.4 lowrank.1
  203.7 1.6 collective-permute-start.25
  205.4 2.0 collective-permute-done.19.refs_2_
  208.3 1.6 collective-permute-start.29
  210.4 4.9 %collective-permute-done.31.text_ref = bf16[128,768]{1,0:T(8,128)(2,1)S(1)} collective-permute-done((bf16[128,768]{1,0:T(8,128)(2,1)S(1)}, bf16[128,768]{1,0:T(8,128)(2,1)S(1)}, u32[]{:S(2)}, u32[]{:S(2)}) %collective-permute-start.31) | collective-permute-done | bytes 196640 | tf_op jit(solution)/shard_map/ppermute | solution.py:17
  216.3 1.6 collective-permute-start.32
  217.9 1.7 collective-permute-done.29.text_ref
  222.4 1.3 collective-permute-start.28
  226.6 2.2 collective-permute-done.26.refs_1_
  (130 shorter events, 31.4 us)
Async XLA Ops:
  6.5 186.0 %all-reduce.2.cloned.1.call-start = ((), (), s32[]{:S(2)}) async-start(), calls=%async_computation | async-start | bytes 196608 | tf_op jit(solution)/shard_map/psum | solution.py:690
  12.3 8.2 %collective-permute-start.1 = (bf16[784,128]{1,0:T(8,128)(2,1)S(1)}, bf16[784,128]{1,0:T(8,128)(2,1)S(1)}, u32[]{:S(2)}, u32[]{:S(2)}) collective-permute-start(bf16[784,128]{1,0:T(8,128)(2,1)S(1)} %get-tuple-element.48), channel_id=1, source_target_pairs={{0,2},{1,3},{2,0},{3,1},{4,6},{5,7},{6,4},{7,5},{8,10},{9,11},{10,... | collective-permute-start | bytes 602120 | tf_op jit(solution)/shard_map/ppermute | solution.py:17
  20.6 8.1 %collective-permute-start.2 = (bf16[208,128]{1,0:T(8,128)(2,1)S(1)}, bf16[208,128]{1,0:T(8,128)(2,1)S(1)}, u32[]{:S(2)}, u32[]{:S(2)}) collective-permute-start(bf16[208,128]{1,0:T(8,128)(2,1)S(1)} %get-tuple-element.53), channel_id=1, source_target_pairs={{0,8},{8,0},{16,24},{24,16},{1,9},{9,1},{17,25},{25,17},{2,10},{10... | collective-permute-start | bytes 159752 | tf_op jit(solution)/shard_map/ppermute | solution.py:17
  24.3 5.5 %collective-permute-start.3 = (bf16[208,128]{1,0:T(8,128)(2,1)S(1)}, bf16[208,128]{1,0:T(8,128)(2,1)S(1)}, u32[]{:S(2)}, u32[]{:S(2)}) collective-permute-start(bf16[208,128]{1,0:T(8,128)(2,1)S(1)} %get-tuple-element.54), channel_id=1, source_target_pairs={{0,16},{8,24},{16,0},{24,8},{1,17},{9,25},{17,1},{25,9},{2,18},{10... | collective-permute-start | bytes 159752 | tf_op jit(solution)/shard_map/ppermute | solution.py:17
  26.9 5.9 %collective-permute-start.4 = (bf16[208,128]{1,0:T(8,128)(2,1)S(1)}, bf16[208,128]{1,0:T(8,128)(2,1)S(1)}, u32[]{:S(2)}, u32[]{:S(2)}) collective-permute-start(bf16[208,128]{1,0:T(8,128)(2,1)S(1)} %get-tuple-element.55), channel_id=1, source_target_pairs={{0,24},{8,16},{16,8},{24,0},{1,25},{9,17},{17,9},{25,1},{2,26},{10... | collective-permute-start | bytes 159752 | tf_op jit(solution)/shard_map/ppermute | solution.py:17
  26.9 27.0 %collective-permute-start.12 = (bf16[192,768]{1,0:T(8,128)(2,1)}, bf16[192,768]{1,0:T(8,128)(2,1)}, u32[]{:S(2)}, u32[]{:S(2)}) collective-permute-start(bf16[192,768]{1,0:T(8,128)(2,1)} %get-tuple-element.61), channel_id=1, source_target_pairs={{0,1},{1,0},{2,3},{3,2},{4,5},{5,4},{6,7},{7,6},{8,9},{9,8},{10,11... | collective-permute-start | bytes 884744 | tf_op jit(solution)/shard_map/ppermute | solution.py:17
  26.9 27.0 %collective-permute-start.13 = (bf16[192,768]{1,0:T(8,128)(2,1)}, bf16[192,768]{1,0:T(8,128)(2,1)}, u32[]{:S(2)}, u32[]{:S(2)}) collective-permute-start(bf16[192,768]{1,0:T(8,128)(2,1)} %get-tuple-element.62), channel_id=1, source_target_pairs={{0,2},{1,3},{2,0},{3,1},{4,6},{5,7},{6,4},{7,5},{8,10},{9,11},{10,... | collective-permute-start | bytes 884744 | tf_op jit(solution)/shard_map/ppermute | solution.py:17
  28.7 25.2 %collective-permute-start.14 = (bf16[192,768]{1,0:T(8,128)(2,1)}, bf16[192,768]{1,0:T(8,128)(2,1)}, u32[]{:S(2)}, u32[]{:S(2)}) collective-permute-start(bf16[192,768]{1,0:T(8,128)(2,1)} %get-tuple-element.63), channel_id=1, source_target_pairs={{0,3},{1,2},{2,1},{3,0},{4,7},{5,6},{6,5},{7,4},{8,11},{9,10},{10,... | collective-permute-start | bytes 884744 | tf_op jit(solution)/shard_map/ppermute | solution.py:17
  33.7 5.3 %collective-permute-start.10 = (bf16[208,128]{1,0:T(8,128)(2,1)}, bf16[208,128]{1,0:T(8,128)(2,1)S(1)}, u32[]{:S(2)}, u32[]{:S(2)}) collective-permute-start(bf16[208,128]{1,0:T(8,128)(2,1)} %centre.1.refs_0_), channel_id=1, source_target_pairs={{0,6},{1,7},{2,4},{3,5},{4,2},{5,3},{6,0},{7,1},{8,14},{9,15},{10,... | collective-permute-start | bytes 159752 | tf_op jit(solution)/shard_map/ppermute | solution.py:669
  36.2 4.8 %collective-permute-start.11 = (bf16[208,128]{1,0:T(8,128)(2,1)}, bf16[208,128]{1,0:T(8,128)(2,1)S(1)}, u32[]{:S(2)}, u32[]{:S(2)}) collective-permute-start(bf16[208,128]{1,0:T(8,128)(2,1)} %centre.1.refs_0_), channel_id=1, source_target_pairs={{0,7},{1,6},{2,5},{3,4},{4,3},{5,2},{6,1},{7,0},{8,15},{9,14},{10,... | collective-permute-start | bytes 159752 | tf_op jit(solution)/shard_map/ppermute | solution.py:669
  41.6 4.8 %collective-permute-start.6 = (bf16[208,128]{1,0:T(8,128)(2,1)}, bf16[208,128]{1,0:T(8,128)(2,1)S(1)}, u32[]{:S(2)}, u32[]{:S(2)}) collective-permute-start(bf16[208,128]{1,0:T(8,128)(2,1)} %centre.1.refs_0_), channel_id=1, source_target_pairs={{0,2},{1,3},{2,0},{3,1},{4,6},{5,7},{6,4},{7,5},{8,10},{9,11},{10,... | collective-permute-start | bytes 159752 | tf_op jit(solution)/shard_map/ppermute | solution.py:669
  43.0 6.0 %collective-permute-start.7 = (bf16[208,128]{1,0:T(8,128)(2,1)}, bf16[208,128]{1,0:T(8,128)(2,1)S(1)}, u32[]{:S(2)}, u32[]{:S(2)}) collective-permute-start(bf16[208,128]{1,0:T(8,128)(2,1)} %centre.1.refs_0_), channel_id=1, source_target_pairs={{0,3},{1,2},{2,1},{3,0},{4,7},{5,6},{6,5},{7,4},{8,11},{9,10},{10,... | collective-permute-start | bytes 159752 | tf_op jit(solution)/shard_map/ppermute | solution.py:669
  47.0 5.9 %collective-permute-start.8 = (bf16[208,128]{1,0:T(8,128)(2,1)}, bf16[208,128]{1,0:T(8,128)(2,1)}, u32[]{:S(2)}, u32[]{:S(2)}) collective-permute-start(bf16[208,128]{1,0:T(8,128)(2,1)} %centre.1.refs_0_), channel_id=1, source_target_pairs={{0,4},{1,5},{2,6},{3,7},{4,0},{5,1},{6,2},{7,3},{8,12},{9,13},{10,... | collective-permute-start | bytes 159752 | tf_op jit(solution)/shard_map/ppermute | solution.py:669
  49.6 4.3 %collective-permute-start.9 = (bf16[208,128]{1,0:T(8,128)(2,1)}, bf16[208,128]{1,0:T(8,128)(2,1)}, u32[]{:S(2)}, u32[]{:S(2)}) collective-permute-start(bf16[208,128]{1,0:T(8,128)(2,1)} %centre.1.refs_0_), channel_id=1, source_target_pairs={{0,5},{1,4},{2,7},{3,6},{4,1},{5,0},{6,3},{7,2},{8,13},{9,12},{10,... | collective-permute-start | bytes 159752 | tf_op jit(solution)/shard_map/ppermute | solution.py:669
  52.9 147.4 %collective-permute-start.24 = (bf16[4,64,1536]{2,1,0:T(8,128)(2,1)}, bf16[4,64,1536]{2,1,0:T(8,128)(2,1)S(1)}, u32[]{:S(2)}, u32[]{:S(2)}) collective-permute-start(bf16[4,64,1536]{2,1,0:T(8,128)(2,1)} %image_pack.1), channel_id=1, source_target_pairs={{0,4},{4,0},{1,5},{5,1},{2,6},{6,2},{3,7},{7,3},{8,12},{12,8},{9,1... | collective-permute-start | bytes 2359304 | tf_op jit(solution)/shard_map/ppermute | solution.py:17
  57.5 13.4 %collective-permute-start.22 = (bf16[128,1536]{1,0:T(8,128)(2,1)}, bf16[128,1536]{1,0:T(8,128)(2,1)}, u32[]{:S(2)}, u32[]{:S(2)}) collective-permute-start(bf16[128,1536]{1,0:T(8,128)(2,1)} %maps_pack.1.refs_0_), channel_id=1, source_target_pairs={{0,2},{1,3},{2,0},{3,1},{4,6},{5,7},{6,4},{7,5},{8,10},{9,11},{10,... | collective-permute-start | bytes 1179656 | tf_op jit(solution)/shard_map/ppermute | solution.py:17
  59.9 6.2 %collective-permute-start.15 = (bf16[64,896]{1,0:T(8,128)(2,1)}, bf16[64,896]{1,0:T(8,128)(2,1)S(1)}, u32[]{:S(2)}, u32[]{:S(2)}) collective-permute-start(bf16[64,896]{1,0:T(8,128)(2,1)} %get-tuple-element.65), channel_id=1, source_target_pairs={{0,8},{8,0},{16,24},{24,16},{1,9},{9,1},{17,25},{25,17},{2,10},{10... | collective-permute-start | bytes 344072 | tf_op jit(solution)/shard_map/ppermute | solution.py:17
  61.3 140.1 %collective-permute-start.21 = (bf16[128,1536]{1,0:T(8,128)(2,1)}, bf16[128,1536]{1,0:T(8,128)(2,1)S(1)}, u32[]{:S(2)}, u32[]{:S(2)}) collective-permute-start(bf16[128,1536]{1,0:T(8,128)(2,1)} %maps_pack.1.refs_0_), channel_id=1, source_target_pairs={{0,1},{1,0},{2,3},{3,2},{4,5},{5,4},{6,7},{7,6},{8,9},{9,8},{10,11... | collective-permute-start | bytes 1179656 | tf_op jit(solution)/shard_map/ppermute | solution.py:17
  62.0 131.5 %collective-permute-start.16 = (bf16[64,896]{1,0:T(8,128)(2,1)}, bf16[64,896]{1,0:T(8,128)(2,1)S(1)}, u32[]{:S(2)}, u32[]{:S(2)}) collective-permute-start(bf16[64,896]{1,0:T(8,128)(2,1)} %copy-done.27), channel_id=1, source_target_pairs={{0,16},{8,24},{16,0},{24,8},{1,17},{9,25},{17,1},{25,9},{2,18},{10... | collective-permute-start | bytes 344072 | tf_op jit(solution)/shard_map/ppermute | solution.py:17
  66.1 127.4 %collective-permute-start.17 = (bf16[64,896]{1,0:T(8,128)(2,1)}, bf16[64,896]{1,0:T(8,128)(2,1)S(1)}, u32[]{:S(2)}, u32[]{:S(2)}) collective-permute-start(bf16[64,896]{1,0:T(8,128)(2,1)} %copy-done.26), channel_id=1, source_target_pairs={{0,24},{8,16},{16,8},{24,0},{1,25},{9,17},{17,9},{25,1},{2,26},{10... | collective-permute-start | bytes 344072 | tf_op jit(solution)/shard_map/ppermute | solution.py:17
  70.8 130.5 %collective-permute-start.23 = (bf16[128,1536]{1,0:T(8,128)(2,1)}, bf16[128,1536]{1,0:T(8,128)(2,1)S(1)}, u32[]{:S(2)}, u32[]{:S(2)}) collective-permute-start(bf16[128,1536]{1,0:T(8,128)(2,1)} %collective-permute-done.22.refs_2_), channel_id=1, source_target_pairs={{0,1},{1,0},{2,3},{3,2},{4,5},{5,4},{6,7},{7,6},{8,9},{9,8},{10,11... | collective-permute-start | bytes 1179656 | tf_op jit(solution)/shard_map/ppermute | solution.py:17
  195.6 9.8 %collective-permute-start.18 = (bf16[64,768]{1,0:T(8,128)(2,1)S(1)}, bf16[64,768]{1,0:T(8,128)(2,1)S(1)}, u32[]{:S(2)}, u32[]{:S(2)}) collective-permute-start(bf16[64,768]{1,0:T(8,128)(2,1)S(1)} %finish.1.refs_0_), channel_id=1, source_target_pairs={{0,8},{8,0},{16,24},{24,16},{1,9},{9,1},{17,25},{25,17},{2,10},{10... | collective-permute-start | bytes 294920 | tf_op jit(solution)/shard_map/ppermute | solution.py:17
  198.9 8.5 %collective-permute-start.19 = (bf16[64,768]{1,0:T(8,128)(2,1)S(1)}, bf16[64,768]{1,0:T(8,128)(2,1)S(1)}, u32[]{:S(2)}, u32[]{:S(2)}) collective-permute-start(bf16[64,768]{1,0:T(8,128)(2,1)S(1)} %finish.1.refs_0_), channel_id=1, source_target_pairs={{0,16},{8,24},{16,0},{24,8},{1,17},{9,25},{17,1},{25,9},{2,18},{10... | collective-permute-start | bytes 294920 | tf_op jit(solution)/shard_map/ppermute | solution.py:17
  200.3 7.1 %collective-permute-start.20 = (bf16[64,768]{1,0:T(8,128)(2,1)S(1)}, bf16[64,768]{1,0:T(8,128)(2,1)S(1)}, u32[]{:S(2)}, u32[]{:S(2)}) collective-permute-start(bf16[64,768]{1,0:T(8,128)(2,1)S(1)} %finish.1.refs_0_), channel_id=1, source_target_pairs={{0,24},{8,16},{16,8},{24,0},{1,25},{9,17},{17,9},{25,1},{2,26},{10... | collective-permute-start | bytes 294920 | tf_op jit(solution)/shard_map/ppermute | solution.py:17
  203.7 6.4 %collective-permute-start.25 = (f32[2,64,64]{2,1,0:T(8,128)S(1)}, f32[2,64,64]{2,1,0:T(8,128)S(1)}, u32[]{:S(2)}, u32[]{:S(2)}) collective-permute-start(f32[2,64,64]{2,1,0:T(8,128)S(1)} %get-tuple-element.69), channel_id=1, source_target_pairs={{0,4},{4,0},{1,5},{5,1},{2,6},{6,2},{3,7},{7,3},{8,12},{12,8},{9,1... | collective-permute-start | bytes 98312 | tf_op jit(solution)/shard_map/ppermute | solution.py:17
  208.2 7.2 %collective-permute-start.31 = (bf16[128,768]{1,0:T(8,128)(2,1)S(1)}, bf16[128,768]{1,0:T(8,128)(2,1)S(1)}, u32[]{:S(2)}, u32[]{:S(2)}) collective-permute-start(bf16[128,768]{1,0:T(8,128)(2,1)S(1)} %get-tuple-element.82), channel_id=1, source_target_pairs={{0,3},{1,2},{2,1},{3,0},{4,7},{5,6},{6,5},{7,4},{8,11},{9,10},{10,... | collective-permute-start | bytes 589832 | tf_op jit(solution)/shard_map/ppermute | solution.py:17
  208.3 11.4 %collective-permute-start.29 = (bf16[128,768]{1,0:T(8,128)(2,1)S(1)}, bf16[128,768]{1,0:T(8,128)(2,1)S(1)}, u32[]{:S(2)}, u32[]{:S(2)}) collective-permute-start(bf16[128,768]{1,0:T(8,128)(2,1)S(1)} %get-tuple-element.79), channel_id=1, source_target_pairs={{0,2},{1,3},{2,0},{3,1},{4,6},{5,7},{6,4},{7,5},{8,10},{9,11},{10,... | collective-permute-start | bytes 589832 | tf_op jit(solution)/shard_map/ppermute | solution.py:17
  209.8 11.7 %collective-permute-start.27 = (bf16[128,768]{1,0:T(8,128)(2,1)S(1)}, bf16[128,768]{1,0:T(8,128)(2,1)S(1)}, u32[]{:S(2)}, u32[]{:S(2)}) collective-permute-start(bf16[128,768]{1,0:T(8,128)(2,1)S(1)} %get-tuple-element.76), channel_id=1, source_target_pairs={{0,1},{1,0},{2,3},{3,2},{4,5},{5,4},{6,7},{7,6},{8,9},{9,8},{10,11... | collective-permute-start | bytes 589832 | tf_op jit(solution)/shard_map/ppermute | solution.py:17
  216.3 9.2 %collective-permute-start.32 = (bf16[64,384]{1,0:T(8,128)(2,1)S(1)}, bf16[64,384]{1,0:T(8,128)(2,1)S(1)}, u32[]{:S(2)}, u32[]{:S(2)}) collective-permute-start(bf16[64,384]{1,0:T(8,128)(2,1)S(1)} %get-tuple-element.84), channel_id=1, source_target_pairs={{0,4},{4,0},{1,5},{5,1},{2,6},{6,2},{3,7},{7,3},{8,12},{12,8},{9,1... | collective-permute-start | bytes 147464 | tf_op jit(solution)/shard_map/ppermute | solution.py:17
  220.6 4.9 %collective-permute-start.30 = (bf16[64,384]{1,0:T(8,128)(2,1)S(1)}, bf16[64,384]{1,0:T(8,128)(2,1)S(1)}, u32[]{:S(2)}, u32[]{:S(2)}) collective-permute-start(bf16[64,384]{1,0:T(8,128)(2,1)S(1)} %get-tuple-element.81), channel_id=1, source_target_pairs={{0,4},{4,0},{1,5},{5,1},{2,6},{6,2},{3,7},{7,3},{8,12},{12,8},{9,1... | collective-permute-start | bytes 147464 | tf_op jit(solution)/shard_map/ppermute | solution.py:17
  222.4 4.2 %collective-permute-start.28 = (bf16[64,384]{1,0:T(8,128)(2,1)S(1)}, bf16[64,384]{1,0:T(8,128)(2,1)S(1)}, u32[]{:S(2)}, u32[]{:S(2)}) collective-permute-start(bf16[64,384]{1,0:T(8,128)(2,1)S(1)} %get-tuple-element.78), channel_id=1, source_target_pairs={{0,4},{4,0},{1,5},{5,1},{2,6},{6,2},{3,7},{7,3},{8,12},{12,8},{9,1... | collective-permute-start | bytes 147464 | tf_op jit(solution)/shard_map/ppermute | solution.py:17
  224.6 4.2 %collective-permute-start.26 = (bf16[64,384]{1,0:T(8,128)(2,1)S(1)}, bf16[64,384]{1,0:T(8,128)(2,1)S(1)}, u32[]{:S(2)}, u32[]{:S(2)}) collective-permute-start(bf16[64,384]{1,0:T(8,128)(2,1)S(1)} %get-tuple-element.75), channel_id=1, source_target_pairs={{0,4},{4,0},{1,5},{5,1},{2,6},{6,2},{3,7},{7,3},{8,12},{12,8},{9,1... | collective-permute-start | bytes 147464 | tf_op jit(solution)/shard_map/ppermute | solution.py:17
  (33 other events, 359.7 us)
Sparse Core Ops, SparseCore 0:
  72.5 120.0 all-reduce.1

commit v3 on v2

--- a/solution.py
+++ b/solution.py
@@ -268,14 +268,14 @@
 TN = (((0,), (0,)), ((), ()))
 
 
-def call(kernel, outs, ins, specs=None, scratch=(), name=None):
+def call(kernel, outs, ins, specs=None, scratch=(), name=None, out_specs=None):
     return pl.pallas_call(
         kernel,
         out_shape=outs,
         in_specs=specs if specs is not None else [VMEM] * len(ins),
-        out_specs=jax.tree.map(lambda _: VMEM, outs),
+        out_specs=out_specs if out_specs is not None else jax.tree.map(lambda _: VMEM, outs),
         scratch_shapes=list(scratch),
-        compiler_params=pltpu.CompilerParams(vmem_limit_bytes=40 * 1024 * 1024),
+        compiler_params=pltpu.CompilerParams(vmem_limit_bytes=16 * 1024 * 1024),
         name=name,
     )(*ins)
 
@@ -332,7 +332,8 @@
     out_stat_ref[...] = jnp.broadcast_to(stat, out_stat_ref.shape)
 
 
-def scatter_kernel(features, got_ref, keep_ref, stat_ref, kept_ref, out_stat_ref, *send_refs):
+def scatter_kernel(features, deps, got_ref, keep_ref, stat_ref, *refs):
+    kept_ref, out_stat_ref, *send_refs = refs[deps:]
     e = lax.axis_index("enc")
     count = keep_ref.shape[0] // features
     stat = stat_ref[0:1] + stat_of(got_ref[count * features :])
@@ -345,9 +346,9 @@
     out_stat_ref[...] = jnp.broadcast_to(stat, out_stat_ref.shape)
 
 
-def centre_kernel(width, keep_ref, stat_ref, bias_ref, scale_ref, *refs):
+def centre_kernel(width, prompt_ref, keep_ref, stat_ref, bias_ref, scale_ref, shift_ref, *refs):
     got_refs, out_ref = refs[:-1], refs[-1]
-    features = keep_ref.shape[0]
+    features, tokens = keep_ref.shape
     total = keep_ref[...] + bias_ref[...]
     stat = stat_ref[0:1]
     for got_ref in got_refs:
@@ -355,68 +356,106 @@
         stat = stat + stat_of(got_ref[features:])
     centred = total - stat * (1.0 / width)
     out_ref[:features] = (scale_ref[...] * centred).astype(BF16)
-    out_ref[features:] = stat_rows(jnp.sum(centred * centred, axis=0, keepdims=True))
+    squares = jnp.sum(centred * centred, axis=0, keepdims=True)
+    high = squares.astype(BF16).astype(F32)
+    row = lax.broadcasted_iota(jnp.int32, (ROWS, tokens), 0)
+    extra = jnp.where(row == 0, high, jnp.where(row == 1, squares - high, 0.0))
+    for j in range(pl.cdiv(features, tokens)):
+        piece = shift_ref[:, j * tokens : min((j + 1) * tokens, features)].astype(F32)
+        gap = tokens - piece.shape[1]
+        if gap:
+            piece = jnp.concatenate([piece, jnp.zeros((1, gap), F32)], axis=1)
+        extra = jnp.where(row == 2 + j, piece, extra)
+    extra = jnp.where(row == ROWS - 1, prompt_ref[0, 0].astype(F32), extra)
+    out_ref[features:] = extra.astype(BF16)
+
+
+def join_kernel(own_ref, got_ref, out_ref):
+    size = own_ref.shape[0]
+    out_ref[:size] = own_ref[...]
+    out_ref[size:] = got_ref[...]
 
 
 def project_kernel(n_seq, n_req, n_enc, *refs):
-    payload_refs = refs[: n_seq * n_req]
-    weight_refs = refs[n_seq * n_req : n_seq * n_req + n_req]
-    keep_ref = refs[n_seq * n_req + n_req]
-    send_refs = refs[n_seq * n_req + n_req + 1 : -1]
+    payload_refs = refs[:n_req]
+    weight_refs = refs[n_req : 2 * n_req]
+    prompts_ref, keep_ref = refs[2 * n_req : 2 * n_req + 2]
+    send_refs = refs[2 * n_req + 2 : -1]
     rows_ref = refs[-1]
     features, width = weight_refs[0].shape
     tokens = payload_refs[0].shape[1]
-    lane = lax.broadcasted_iota(jnp.int32, (tokens, HDIM), 1)
-    for p in range(n_seq):
-        total, squares = None, None
-        for k in range(n_req):
-            payload = payload_refs[p * n_req + k]
-            term = lax.dot_general(
-                payload[:features], weight_refs[k][...], TN, preferred_element_type=F32
+    stride = features + ROWS
+    total = None
+    squares = [jnp.zeros((1, tokens), F32) for _ in range(n_seq)]
+    for k in range(n_req):
+        left = []
+        shifts = []
+        for p in range(n_seq):
+            payload = payload_refs[k]
+            left.append(payload[p * stride : p * stride + features].T)
+            extra = payload[p * stride + features : (p + 1) * stride].astype(F32)
+            squares[p] = squares[p] + extra[0:1] + extra[1:2]
+            pieces = [extra[2 + j : 3 + j] for j in range(pl.cdiv(features, tokens))]
+            shifts.append(jnp.concatenate(pieces, axis=1)[:, :features])
+            if p == 0:
+                prompts_ref[k] = jnp.max(extra[ROWS - 1 : ROWS]).astype(jnp.int32)
+        shifts.append(jnp.zeros((ROWS - n_seq, features), F32))
+        left.append(jnp.concatenate(shifts, axis=0).astype(BF16))
+        term = jnp.dot(
+            jnp.concatenate(left, axis=0), weight_refs[k][...], preferred_element_type=F32
+        )
+        total = term if total is None else total + term
+    size = n_seq * tokens // n_enc
+    heads = width // HDIM
+    step = heads * size + ROWS
+    row = lax.broadcasted_iota(jnp.int32, (ROWS, HDIM), 0)
+    for z in range(n_enc):
+        p, first = divmod(z * size, tokens)
+        shift = total[n_seq * tokens + p : n_seq * tokens + p + 1]
+        square = squares[p][:, first : first + size]
+        square = jnp.concatenate([square, jnp.zeros((1, HDIM - size), F32)], axis=1)
+        high = square.astype(BF16).astype(F32)
+        extra = jnp.where(
+            row == 2 * heads, high, jnp.where(row == 2 * heads + 1, square - high, 0.0)
+        )
+        for h in range(heads):
+            cols = slice(h * HDIM, (h + 1) * HDIM)
+            rows_ref[z * step + h * size : z * step + (h + 1) * size] = total[
+                z * size : (z + 1) * size, cols
+            ]
+            high = shift[:, cols].astype(BF16).astype(F32)
+            extra = jnp.where(
+                row == h, high, jnp.where(row == heads + h, shift[:, cols] - high, extra)
             )
-            part = stat_of(payload[features:])
-            total = term if total is None else total + term
-            squares = part if squares is None else squares + part
-        rows = slice(p * tokens, (p + 1) * tokens)
-        rows_ref[rows, :width] = total
-        column = jnp.broadcast_to(squares, (HDIM, tokens)).T
-        high = column.astype(BF16).astype(F32)
-        rows_ref[rows, width:] = jnp.where(
-            lane == 0, high, jnp.where(lane == 1, column - high, 0.0)
-        )
+        rows_ref[z * step + heads * size : (z + 1) * step] = extra
     e = lax.axis_index("enc")
-    size = n_seq * tokens // n_enc
-    keep_ref[...] = rows_ref[at(e, size)]
+    keep_ref[...] = rows_ref[at(e, step)]
     for k, send_ref in enumerate(send_refs):
-        send_ref[...] = rows_ref[at(e ^ (k + 1), size)].astype(BF16)
-
-
-def finish_kernel(n_seq, n_enc, n_req, model_width, keep_ref, shift_ref, bias_ref, *refs):
+        send_ref[...] = rows_ref[at(e ^ (k + 1), step)].astype(BF16)
+
+
+def finish_kernel(n_req, model_width, keep_ref, bias_ref, *refs):
     got_refs, out_ref = refs[:-1], refs[-1]
-    e, r, s = lax.axis_index("enc"), lax.axis_index("req"), lax.axis_index("seq")
-    width = out_ref.shape[1]
+    r, s = lax.axis_index("req"), lax.axis_index("seq")
+    size, width = out_ref.shape
+    heads = width // HDIM
     half = width // 2
-    inner = shift_ref.shape[1] // 2
+    inner = bias_ref.shape[1] // 2
     total = keep_ref[...]
     for got_ref in got_refs:
         total = total + got_ref[...].astype(F32)
-    squares = total[:, width : width + 1] + total[:, width + 1 : width + 2]
+    extra = total[heads * size :]
+    squares = extra[2 * heads : 2 * heads + 1] + extra[2 * heads + 1 : 2 * heads + 2]
+    squares = jnp.broadcast_to(squares, (HDIM, HDIM)).T[:size]
     factor = lax.rsqrt(squares * (1.0 / model_width) + epsilon_norm)
-    prompt = s ^ (e // (n_enc // n_seq))
-    for part in range(2):
-        columns = pl.ds(
-            pl.multiple_of(part * inner + (s * n_req + r) * half, HDIM), half
-        )
-        shift = shift_ref[pl.ds(prompt, 1), columns] + bias_ref[:, columns].astype(F32)
-        rows = total[:, part * half : (part + 1) * half] * factor + shift
-        for h in range(half // HDIM):
-            head = rows[:, h * HDIM : (h + 1) * HDIM]
-            if part == 0:
-                head = head * lax.rsqrt(
-                    jnp.mean(head * head, axis=1, keepdims=True) + epsilon_norm
-                )
-            place = part * half + h * HDIM
-            out_ref[:, place : place + HDIM] = head.astype(BF16)
+    for h in range(heads):
+        start = (h * HDIM // half) * inner + (s * n_req + r) * half + h * HDIM % half
+        bias = bias_ref[:, pl.ds(pl.multiple_of(start, HDIM), HDIM)].astype(F32)
+        shift = extra[h : h + 1] + extra[heads + h : heads + h + 1] + bias
+        head = total[h * size : (h + 1) * size] * factor + shift
+        if h * HDIM < half:
+            head = head * lax.rsqrt(jnp.mean(head * head, axis=1, keepdims=True) + epsilon_norm)
+        out_ref[:, h * HDIM : (h + 1) * HDIM] = head.astype(BF16)
 
 
 def choose_kernel(n_seq, n_enc, chosen_ref, *refs):
@@ -425,7 +464,7 @@
     halves = n_enc // n_seq
     size = part_refs[0].shape[0]
     for k, out_ref in enumerate(out_refs):
-        prompt = s ^ chosen_ref[r ^ k]
+        prompt = s ^ chosen_ref[k]
         for h in range(halves):
             place = e ^ (prompt * halves + h)
             for j in range(n_enc):
@@ -434,12 +473,11 @@
                     out_ref[h * size : (h + 1) * size] = part_refs[j][...]
 
 
-def weight_kernel(n_req, part, inner, *refs):
-    w_ref, out_refs, sems = refs[0], refs[2:-1], refs[-1]
+def weight_kernel(n_req, part, inner, w_ref, dep_ref, own_ref, core_ref, pair_ref, sems):
     r, s = lax.axis_index("req"), lax.axis_index("seq")
     half = part // n_req
     copies = []
-    for k, out_ref in enumerate(out_refs):
+    for k, out_ref in enumerate((own_ref, core_ref, pair_ref.at[0], pair_ref.at[1])):
         for side in range(2):
             columns = pl.ds(
                 pl.multiple_of(side * inner + (s * n_req + (r ^ k)) * half, HDIM), half
@@ -528,7 +566,7 @@
             ).astype(BF16)
 
 
-def heads_kernel(scale, live_ref, text_ref, q_ref, k_ref, v_ref, *out_refs):
+def heads_kernel(scale, live_ref, text_ref, q_ref, k_ref, v_ref, dep_ref, *out_refs):
     live = live_ref[...] != 0
     half = q_ref.shape[2]
     size = out_refs[0].shape[0]
@@ -620,14 +658,16 @@
         for k in range(1, n_seq)
     ]
     image_got = [swap(packed[k - 1], "seq", n_seq, k) for k in range(1, n_seq)]
-    weights = call(
+    weight = struct((features, 2 * half))
+    weight_own, weight_core, weight_pair = call(
         functools.partial(weight_kernel, n_req, part, inner),
-        tuple(struct((features, 2 * half)) for _ in range(n_req)),
+        (weight, weight, struct((2, features, 2 * half))),
         (key_value_weight, keep),
         [ANY] * 2,
         [dma((2 * n_req,))],
         name="weight_pack",
     )
+    weight_core_got = swap(weight_core, "req", n_req, 1)
 
     send, keep, sums = call(
         functools.partial(halve_kernel, features),
@@ -641,15 +681,22 @@
     )
     got = swap(send, "req", n_req, 2)
     keep, sums, *sends = call(
-        functools.partial(scatter_kernel, features),
+        functools.partial(scatter_kernel, features, 2),
         (struct((features, tokens), F32), stat)
         + tuple(struct((features + ROWS, tokens)) for _ in range(1, n_enc)),
-        (got, keep, sums),
+        (got, keep, sums, weight_pair, packed[0]),
+        [VMEM] * 3 + [ANY] * 2,
         name="scatter",
     )
     arrived = [swap(sends[k - 1], "enc", n_enc, k) for k in range(1, n_enc)]
-    weights = lax.optimization_barrier((weights, keep))[0]
-    weights = [weights[0]] + [swap(weights[k], "req", n_req, k) for k in range(1, n_req)]
+    weight_pair = lax.optimization_barrier((weight_pair, keep))[0]
+    weight_pair_got = swap(weight_pair, "req", n_req, 2)
+    weights = (
+        weight_own,
+        weight_core_got,
+        weight_pair_got[0],
+        swap(weight_pair_got[1], "req", n_req, 1),
+    )
 
     bias_columns = jnp.broadcast_to(context_bias.astype(F32)[:, None], (features, tokens))
     scale_columns = jnp.broadcast_to(
@@ -658,46 +705,27 @@
     own = call(
         functools.partial(centre_kernel, model_width),
         struct((features + ROWS, tokens)),
-        (keep, sums, bias_columns, scale_columns, *arrived),
+        (request_prompt, keep, sums, bias_columns, scale_columns, modulation_shift, *arrived),
+        [SMEM] + [VMEM] * (5 + len(arrived)),
         name="centre",
     )
-    payloads = []
-    for i in range(n_seq):
-        for k in range(n_req):
-            block = own
-            if i or k:
-                block = lax.ppermute(
-                    own,
-                    ("seq", "req"),
-                    [
-                        (a * n_req + b, (a ^ i) * n_req + (b ^ k))
-                        for a in range(n_seq)
-                        for b in range(n_req)
-                    ],
-                )
-            payloads.append(block)
-
-    shift_part = jnp.dot(modulation_shift, key_value_weight, preferred_element_type=F32)
-    wide = 2 * inner
-    index = jnp.arange(n_seq + 1)[:, None]
-    lane = jnp.arange(wide)[None, :]
-    asked = jnp.where(
-        (lane == e * n_req + r) & (s == 0), request_prompt[0, 0].astype(F32), 0.0
-    )
-    table = jnp.where(
-        index == s, shift_part, jnp.where(index == n_seq, asked, jnp.zeros((), F32))
-    )
-    table = lax.psum(table, ("enc", "seq", "req"))
-    prompts = lax.dynamic_slice_in_dim(table[n_seq], e * n_req, n_req, 0).astype(jnp.int32)
+    joined = call(
+        join_kernel,
+        struct((n_seq * (features + ROWS), tokens)),
+        (own, swap(own, "seq", n_seq, 1)),
+        name="join",
+    )
+    payloads = [joined] + [swap(joined, "req", n_req, k) for k in range(1, n_req)]
 
     size = n_seq * tokens // n_enc
-    wide_rows = 2 * half + HDIM
-    keep, *sends = call(
+    step = 2 * half // HDIM * size + ROWS
+    prompts, keep, *sends = call(
         functools.partial(project_kernel, n_seq, n_req, n_enc),
-        (struct((size, wide_rows), F32),)
-        + tuple(struct((size, wide_rows)) for _ in range(1, n_enc)),
+        (struct((n_req,), jnp.int32), struct((step, HDIM), F32))
+        + tuple(struct((step, HDIM)) for _ in range(1, n_enc)),
         (*payloads, *weights),
-        scratch=[pltpu.VMEM((n_seq * tokens, wide_rows), F32)],
+        scratch=[pltpu.VMEM((n_enc * step, HDIM), F32)],
+        out_specs=(SMEM,) + (VMEM,) * n_enc,
         name="project",
     )
     arrived = [swap(sends[k - 1], "enc", n_enc, k) for k in range(1, n_enc)]
@@ -705,7 +733,7 @@
     maps = call(
         functools.partial(maps_kernel, part),
         struct((2 * rank, part)),
-        (adapter_down_maps[0].T, adapter_up_maps[0], keep),
+        (adapter_down_maps[0].T, adapter_up_maps[0], arrived[0]),
         [ANY] * 3,
         [dma((2,))],
         name="maps_pack",
@@ -742,9 +770,9 @@
     )
 
     text = call(
-        functools.partial(finish_kernel, n_seq, n_enc, n_req, model_width),
+        functools.partial(finish_kernel, n_req, model_width),
         struct((size, 2 * half)),
-        (keep, table, key_value_bias[None], *arrived),
+        (keep, key_value_bias[None], *arrived),
         name="finish",
     )
     parts = [text] + [swap(text, "enc", n_enc, k) for k in range(1, n_enc)]
@@ -758,6 +786,7 @@
     rows = [rows[0]] + [swap(rows[k], "req", n_req, k) for k in range(1, n_req)]
     live = lax.dynamic_slice_in_dim(prompt_token_ids, request_prompt[0, 0], 1, 0)
     pieces = [None] * n_req
+    last = live
     for k in range(n_req):
         block = pl.BlockSpec((1, n_seq * image_rows, half), lambda i, k=k: (k, 0, 0))
         whole = lambda shape: pl.BlockSpec(shape, lambda i: (0, 0))
@@ -765,11 +794,12 @@
             functools.partial(heads_kernel, HDIM ** (-0.5)),
             grid=(1,),
             out_shape=[struct((image_rows, half)) for _ in range(n_seq)],
-            in_specs=[whole((1, tokens)), whole((tokens, 2 * half)), block, block, block],
+            in_specs=[whole((1, tokens)), whole((tokens, 2 * half)), block, block, block, ANY],
             out_specs=[whole((image_rows, half)) for _ in range(n_seq)],
-            compiler_params=pltpu.CompilerParams(vmem_limit_bytes=40 * 1024 * 1024),
+            compiler_params=pltpu.CompilerParams(vmem_limit_bytes=16 * 1024 * 1024),
             name="heads",
-        )(live, rows[k], queries, image_keys, image_values)
+        )(live, rows[k], queries, image_keys, image_values, last)
+        last = mixed[0]
         pieces[k] = [mixed[0]] + [swap(mixed[i], "seq", n_seq, i) for i in range(1, n_seq)]
     result = call(
         functools.partial(assemble_kernel, n_req, n_seq),
@@ -786,8 +816,8 @@
 
     def run(*arrays):
         heads = arrays[6].shape[1] // (2 * HDIM)
-        pick_body = per_device_heads if heads % (n_seq * n_req) == 0 else per_device
-        return pick_body(n_enc, n_req, n_seq, *arrays)
+        fits = n_seq == 2 and n_req == 4 and heads % (n_seq * n_req) == 0
+        return (per_device_heads if fits else per_device)(n_enc, n_req, n_seq, *arrays)
 
     return jax.shard_map(
         run,

time: 237 us -> 109 us (0.46)
  waiting for transfers between devices: 150 us -> 54.1 us
  between operations: 15.1 us -> 1.68 us
  local copies, waits for them, and re-layouts: 13.7 us -> 6.52 us
  starting transfers between devices: 41 us -> 34.9 us
  Pallas kernels: 14.4 us -> 11 us
    psum x1 -> x0, waiting for transfers between devices: 119 us -> none  [per_device_heads(): table = lax.psum(table, ('enc', 'seq', 'req'))]
    ppermute x26 -> x30, waiting for transfers between devices: 23.3 us -> 54.1 us  [swap(): return lax.ppermute(block, axis, [(i, i ^ step) for i in range(size)])]
    ppermute x7 -> x0, waiting for transfers between devices: 7.47 us -> none  [per_device_heads(): lax.ppermute(own, ('seq', 'req'), [(a * n_req + b, (a ^ i) * n_req + (b ^...]
    unnamed x62 -> x36, local copies, waits for them, and re-layouts: 11.1 us -> 4.88 us
    ppermute x7 -> x0, starting transfers between devices: 5.28 us -> none  [per_device_heads(): lax.ppermute(own, ('seq', 'req'), [(a * n_req + b, (a ^ i) * n_req + (b ^...]
    pallas_call x13 -> x14, Pallas kernels: 10.7 us -> 7.29 us  [call(): pl.pallas_call(kernel, out_shape=outs, in_specs=specs if specs is not Non...]
    ppermute x26 -> x30, starting transfers between devices: 35.7 us -> 34.9 us  [swap(): return lax.ppermute(block, axis, [(i, i ^ step) for i in range(size)])]
  transfers between devices with their start and end apart: 34 -> 30, of which waited for: 14 -> 16; matrix products, arithmetic and copies ran while one was open for 2% -> 1% of each run, Pallas kernels for 5% -> 6%
where the time goes in v3:
time: 109 us; the launch traced here: 108 us
  waiting for transfers between devices  54.1 us (50%)
  starting transfers between devices  34.9 us (32%)
  Pallas kernels  11 us (10%)
  local copies, waits for them, and re-layouts  6.52 us (6%)
  between operations  1.68 us (2%)
    ppermute x30, waiting for transfers between devices, swap(): return lax.ppermute(block, axis, [(i, i ^ step) for i in range(size)])  54.1 us
    ppermute x30, starting transfers between devices, swap(): return lax.ppermute(block, axis, [(i, i ^ step) for i in range(size)])  34.9 us
    pallas_call x14, Pallas kernels, call(): pl.pallas_call(kernel, out_shape=outs, in_specs=specs if specs is not Non...  7.29 us
    unnamed x36, local copies, waits for them, and re-layouts  4.88 us
    pallas_call x4, Pallas kernels, per_device_heads(): pl.pallas_call(functools.partial(heads_kernel, HDIM ** (-0.5)), grid=(1,)...  3.66 us
  transfers between devices with their start and end apart: 30, of which 16 were waited for; matrix products, arithmetic and copies ran while one was open for 1% of the time, Pallas kernels for 6%

profile of v3, /device:TPU:0, one launch (start us, length us, event | category | flops | bytes accessed | tf_op | source)
XLA Modules:
  0.0 108.2 jit_solution(16191086746058189855)
XLA Ops:
  0.8 1.4 %copy-done.4 = bf16[256,3072]{1,0:T(8,128)(2,1)S(1)} copy-done((bf16[256,3072]{1,0:T(8,128)(2,1)S(1)}, bf16[256,3072]{1,0:T(8,128)(2,1)}, u32[]{:S(2)}) %copy-start.4) | copy-done | bytes 1572888
  5.7 3.0 %collective-permute-start.1 = (bf16[784,128]{1,0:T(8,128)(2,1)S(1)}, bf16[784,128]{1,0:T(8,128)(2,1)S(1)}, u32[]{:S(2)}, u32[]{:S(2)}) collective-permute-start(bf16[784,128]{1,0:T(8,128)(2,1)S(1)} %get-tuple-element.45), channel_id=1, source_target_pairs={{0,2},{1,3},{2,0},{3,1},{4,6},{5,7},{6,4},{7,5},{8,10},{9,11},{10,... | collective-permute-start | bytes 602120 | tf_op jit(solution)/shard_map/ppermute | solution.py:17
  9.2 4.8 %collective-permute-done.1.got_ref = bf16[784,128]{1,0:T(8,128)(2,1)S(1)} collective-permute-done((bf16[784,128]{1,0:T(8,128)(2,1)S(1)}, bf16[784,128]{1,0:T(8,128)(2,1)S(1)}, u32[]{:S(2)}, u32[]{:S(2)}) %collective-permute-start.1) | collective-permute-done | bytes 200736 | tf_op jit(solution)/shard_map/ppermute | solution.py:17
  14.1 1.8 %collective-permute-start.10 = (bf16[2,192,768]{2,1,0:T(8,128)(2,1)S(1)}, bf16[2,192,768]{2,1,0:T(8,128)(2,1)S(1)}, u32[]{:S(2)}, u32[]{:S(2)}) collective-permute-start(bf16[2,192,768]{2,1,0:T(8,128)(2,1)S(1)} %get-tuple-element.56.refs_0_), channel_id=1, source_target_pairs={{0,2},{1,3},{2,0},{3,1},{4,6},{5,7},{6,4},{7,5},{8,10},{9,11},{10,... | collective-permute-start | bytes 1769480 | tf_op jit(solution)/shard_map/ppermute | solution.py:17
  15.9 1.6 %collective-permute-start.2 = (bf16[208,128]{1,0:T(8,128)(2,1)S(1)}, bf16[208,128]{1,0:T(8,128)(2,1)S(1)}, u32[]{:S(2)}, u32[]{:S(2)}) collective-permute-start(bf16[208,128]{1,0:T(8,128)(2,1)S(1)} %get-tuple-element.51), channel_id=1, source_target_pairs={{0,8},{8,0},{16,24},{24,16},{1,9},{9,1},{17,25},{25,17},{2,10},{10... | collective-permute-start | bytes 159752 | tf_op jit(solution)/shard_map/ppermute | solution.py:17
  17.4 2.6 %collective-permute-start.3 = (bf16[208,128]{1,0:T(8,128)(2,1)S(1)}, bf16[208,128]{1,0:T(8,128)(2,1)S(1)}, u32[]{:S(2)}, u32[]{:S(2)}) collective-permute-start(bf16[208,128]{1,0:T(8,128)(2,1)S(1)} %get-tuple-element.52), channel_id=1, source_target_pairs={{0,16},{8,24},{16,0},{24,8},{1,17},{9,25},{17,1},{25,9},{2,18},{10... | collective-permute-start | bytes 159752 | tf_op jit(solution)/shard_map/ppermute | solution.py:17
  20.3 8.7 %collective-permute-done.10 = bf16[2,192,768]{2,1,0:T(8,128)(2,1)S(1)} collective-permute-done((bf16[2,192,768]{2,1,0:T(8,128)(2,1)S(1)}, bf16[2,192,768]{2,1,0:T(8,128)(2,1)S(1)}, u32[]{:S(2)}, u32[]{:S(2)}) %collective-permute-start.10) | collective-permute-done | bytes 589856 | tf_op jit(solution)/shard_map/ppermute | solution.py:17
  30.1 1.5 %collective-permute-start.5 = (bf16[208,128]{1,0:T(8,128)(2,1)S(1)}, bf16[208,128]{1,0:T(8,128)(2,1)S(1)}, u32[]{:S(2)}, u32[]{:S(2)}) collective-permute-start(bf16[208,128]{1,0:T(8,128)(2,1)S(1)} %centre.1.own_ref), channel_id=1, source_target_pairs={{0,4},{4,0},{1,5},{5,1},{2,6},{6,2},{3,7},{7,3},{8,12},{12,8},{9,1... | collective-permute-start | bytes 159752 | tf_op jit(solution)/shard_map/ppermute | solution.py:17
  31.5 2.8 %collective-permute-done.5.got_ref = bf16[208,128]{1,0:T(8,128)(2,1)S(1)} collective-permute-done((bf16[208,128]{1,0:T(8,128)(2,1)S(1)}, bf16[208,128]{1,0:T(8,128)(2,1)S(1)}, u32[]{:S(2)}, u32[]{:S(2)}) %collective-permute-start.5) | collective-permute-done | bytes 53280 | tf_op jit(solution)/shard_map/ppermute | solution.py:17
  34.5 1.5 %collective-permute-start.7 = (bf16[416,128]{1,0:T(8,128)(2,1)S(1)}, bf16[416,128]{1,0:T(8,128)(2,1)S(1)}, u32[]{:S(2)}, u32[]{:S(2)}) collective-permute-start(bf16[416,128]{1,0:T(8,128)(2,1)S(1)} %join.1.refs_0_), channel_id=1, source_target_pairs={{0,2},{1,3},{2,0},{3,1},{4,6},{5,7},{6,4},{7,5},{8,10},{9,11},{10,... | collective-permute-start | bytes 319496 | tf_op jit(solution)/shard_map/ppermute | solution.py:17
  36.3 4.0 %collective-permute-done.7.refs_2_ = bf16[416,128]{1,0:T(8,128)(2,1)S(1)} collective-permute-done((bf16[416,128]{1,0:T(8,128)(2,1)S(1)}, bf16[416,128]{1,0:T(8,128)(2,1)S(1)}, u32[]{:S(2)}, u32[]{:S(2)}) %collective-permute-start.7) | collective-permute-done | bytes 106528 | tf_op jit(solution)/shard_map/ppermute | solution.py:17
  40.3 1.4 %collective-permute-done.8.refs_3_ = bf16[416,128]{1,0:T(8,128)(2,1)S(1)} collective-permute-done((bf16[416,128]{1,0:T(8,128)(2,1)S(1)}, bf16[416,128]{1,0:T(8,128)(2,1)S(1)}, u32[]{:S(2)}, u32[]{:S(2)}) %collective-permute-start.8) | collective-permute-done | bytes 106528 | tf_op jit(solution)/shard_map/ppermute | solution.py:17
  41.7 1.4 %project.1 = (s32[4]{0:T(128)S(1)}, f32[400,128]{1,0:T(8,128)S(1)}, bf16[400,128]{1,0:T(8,128)(2,1)S(1)}, bf16[400,128]{1,0:T(8,128)(2,1)}, bf16[400,128]{1,0:T(8,128)(2,1)}) custom-call(bf16[416,128]{1,0:T(8,128)(2,1)S(1)} %join.1.refs_0_, bf16[416,128]{1,0:T(8,128)(2,1)S(1)} %collective-permute-done.6.refs_1_, ...), custom_call_target="tpu_custom_call" | custom-call | tf_op jit(solution)/shard_map/project/pallas_call | solution.py:272
  43.1 1.5 %collective-permute-start.12 = (bf16[400,128]{1,0:T(8,128)(2,1)S(1)}, bf16[400,128]{1,0:T(8,128)(2,1)S(1)}, u32[]{:S(2)}, u32[]{:S(2)}) collective-permute-start(bf16[400,128]{1,0:T(8,128)(2,1)S(1)} %get-tuple-element.59), channel_id=1, source_target_pairs={{0,8},{8,0},{16,24},{24,16},{1,9},{9,1},{17,25},{25,17},{2,10},{10... | collective-permute-start | bytes 307208 | tf_op jit(solution)/shard_map/ppermute | solution.py:17
  44.6 1.5 %collective-permute-start.21 = (bf16[4,64,1536]{2,1,0:T(8,128)(2,1)S(1)}, bf16[4,64,1536]{2,1,0:T(8,128)(2,1)S(1)}, u32[]{:S(2)}, u32[]{:S(2)}) collective-permute-start(bf16[4,64,1536]{2,1,0:T(8,128)(2,1)S(1)} %image_pack.1.refs_1_), channel_id=1, source_target_pairs={{0,4},{4,0},{1,5},{5,1},{2,6},{6,2},{3,7},{7,3},{8,12},{12,8},{9,1... | collective-permute-start | bytes 2359304 | tf_op jit(solution)/shard_map/ppermute | solution.py:17
  46.1 2.1 %collective-permute-done.12.refs_0_.dep_ref = bf16[400,128]{1,0:T(8,128)(2,1)S(1)} collective-permute-done((bf16[400,128]{1,0:T(8,128)(2,1)S(1)}, bf16[400,128]{1,0:T(8,128)(2,1)S(1)}, u32[]{:S(2)}, u32[]{:S(2)}) %collective-permute-start.12) | collective-permute-done | bytes 102432 | tf_op jit(solution)/shard_map/ppermute | solution.py:17
  48.3 1.5 %collective-permute-start.19 = (bf16[128,1536]{1,0:T(8,128)(2,1)S(1)}, bf16[128,1536]{1,0:T(8,128)(2,1)}, u32[]{:S(2)}, u32[]{:S(2)}) collective-permute-start(bf16[128,1536]{1,0:T(8,128)(2,1)S(1)} %maps_pack.1.refs_0_), channel_id=1, source_target_pairs={{0,2},{1,3},{2,0},{3,1},{4,6},{5,7},{6,4},{7,5},{8,10},{9,11},{10,... | collective-permute-start | bytes 1179656 | tf_op jit(solution)/shard_map/ppermute | solution.py:17
  49.8 9.2 %collective-permute-done.19.refs_2_ = bf16[128,1536]{1,0:T(8,128)(2,1)} collective-permute-done((bf16[128,1536]{1,0:T(8,128)(2,1)S(1)}, bf16[128,1536]{1,0:T(8,128)(2,1)}, u32[]{:S(2)}, u32[]{:S(2)}) %collective-permute-start.19) | collective-permute-done | bytes 393248 | tf_op jit(solution)/shard_map/ppermute | solution.py:17
  59.0 2.6 %collective-permute-start.13 = (bf16[400,128]{1,0:T(8,128)(2,1)}, bf16[400,128]{1,0:T(8,128)(2,1)}, u32[]{:S(2)}, u32[]{:S(2)}) collective-permute-start(bf16[400,128]{1,0:T(8,128)(2,1)} %get-tuple-element.60), channel_id=1, source_target_pairs={{0,16},{8,24},{16,0},{24,8},{1,17},{9,25},{17,1},{25,9},{2,18},{10... | collective-permute-start | bytes 307208 | tf_op jit(solution)/shard_map/ppermute | solution.py:17
  64.2 6.2 %collective-permute-done.13.refs_1_ = bf16[400,128]{1,0:T(8,128)(2,1)} collective-permute-done((bf16[400,128]{1,0:T(8,128)(2,1)}, bf16[400,128]{1,0:T(8,128)(2,1)}, u32[]{:S(2)}, u32[]{:S(2)}) %collective-permute-start.13) | collective-permute-done | bytes 102432 | tf_op jit(solution)/shard_map/ppermute | solution.py:17
  74.1 2.4 %collective-permute-start.15 = (bf16[64,768]{1,0:T(8,128)(2,1)S(1)}, bf16[64,768]{1,0:T(8,128)(2,1)S(1)}, u32[]{:S(2)}, u32[]{:S(2)}) collective-permute-start(bf16[64,768]{1,0:T(8,128)(2,1)S(1)} %finish.1.refs_0_), channel_id=1, source_target_pairs={{0,8},{8,0},{16,24},{24,16},{1,9},{9,1},{17,25},{25,17},{2,10},{10... | collective-permute-start | bytes 294920 | tf_op jit(solution)/shard_map/ppermute | solution.py:17
  76.5 2.0 %collective-permute-start.16 = (bf16[64,768]{1,0:T(8,128)(2,1)S(1)}, bf16[64,768]{1,0:T(8,128)(2,1)S(1)}, u32[]{:S(2)}, u32[]{:S(2)}) collective-permute-start(bf16[64,768]{1,0:T(8,128)(2,1)S(1)} %finish.1.refs_0_), channel_id=1, source_target_pairs={{0,16},{8,24},{16,0},{24,8},{1,17},{9,25},{17,1},{25,9},{2,18},{10... | collective-permute-start | bytes 294920 | tf_op jit(solution)/shard_map/ppermute | solution.py:17
  78.5 1.4 %collective-permute-start.17 = (bf16[64,768]{1,0:T(8,128)(2,1)S(1)}, bf16[64,768]{1,0:T(8,128)(2,1)S(1)}, u32[]{:S(2)}, u32[]{:S(2)}) collective-permute-start(bf16[64,768]{1,0:T(8,128)(2,1)S(1)} %finish.1.refs_0_), channel_id=1, source_target_pairs={{0,24},{8,16},{16,8},{24,0},{1,25},{9,17},{17,9},{25,1},{2,26},{10... | collective-permute-start | bytes 294920 | tf_op jit(solution)/shard_map/ppermute | solution.py:17
  79.8 1.5 %lowrank.1 = (f32[2,64,64]{2,1,0:T(8,128)S(1)}, bf16[128,1536]{1,0:T(8,128)(2,1)S(1)}) custom-call(s32[1,1]{1,0:T(1,128)S(6)} %copy.17.adapter_ref, bf16[64,3072]{1,0:T(8,128)(2,1)S(1)} %bitcast.23, bf16[128,1536]{1,0:T(8,128)(2,1)S(1)} %maps_pack.1.refs_0_, bf16[128,1536]{1,0:T(8,128)(2,1)} %collective-permute-done.18.refs_1_, ...), custom_call_target="tpu_custom_call" | custom-call | tf_op jit(solution)/shard_map/lowrank/pallas_call | solution.py:272
  81.4 1.6 %collective-permute-start.22 = (f32[2,64,64]{2,1,0:T(8,128)S(1)}, f32[2,64,64]{2,1,0:T(8,128)S(1)}, u32[]{:S(2)}, u32[]{:S(2)}) collective-permute-start(f32[2,64,64]{2,1,0:T(8,128)S(1)} %get-tuple-element.63), channel_id=1, source_target_pairs={{0,4},{4,0},{1,5},{5,1},{2,6},{6,2},{3,7},{7,3},{8,12},{12,8},{9,1... | collective-permute-start | bytes 98312 | tf_op jit(solution)/shard_map/ppermute | solution.py:17
  82.9 4.0 %collective-permute-done.17.refs_3_ = bf16[64,768]{1,0:T(8,128)(2,1)S(1)} collective-permute-done((bf16[64,768]{1,0:T(8,128)(2,1)S(1)}, bf16[64,768]{1,0:T(8,128)(2,1)S(1)}, u32[]{:S(2)}, u32[]{:S(2)}) %collective-permute-start.17) | collective-permute-done | bytes 98336 | tf_op jit(solution)/shard_map/ppermute | solution.py:17
  87.7 1.6 %collective-permute-start.26 = (bf16[128,768]{1,0:T(8,128)(2,1)S(1)}, bf16[128,768]{1,0:T(8,128)(2,1)S(1)}, u32[]{:S(2)}, u32[]{:S(2)}) collective-permute-start(bf16[128,768]{1,0:T(8,128)(2,1)S(1)} %get-tuple-element.73), channel_id=1, source_target_pairs={{0,2},{1,3},{2,0},{3,1},{4,6},{5,7},{6,4},{7,5},{8,10},{9,11},{10,... | collective-permute-start | bytes 589832 | tf_op jit(solution)/shard_map/ppermute | solution.py:17
  91.8 3.7 %collective-permute-done.26.text_ref = bf16[128,768]{1,0:T(8,128)(2,1)S(1)} collective-permute-done((bf16[128,768]{1,0:T(8,128)(2,1)S(1)}, bf16[128,768]{1,0:T(8,128)(2,1)S(1)}, u32[]{:S(2)}, u32[]{:S(2)}) %collective-permute-start.26) | collective-permute-done | bytes 196640 | tf_op jit(solution)/shard_map/ppermute | solution.py:17
  96.4 2.4 %collective-permute-done.28.text_ref = bf16[128,768]{1,0:T(8,128)(2,1)S(1)} collective-permute-done((bf16[128,768]{1,0:T(8,128)(2,1)S(1)}, bf16[128,768]{1,0:T(8,128)(2,1)S(1)}, u32[]{:S(2)}, u32[]{:S(2)}) %collective-permute-start.28) | collective-permute-done | bytes 196640 | tf_op jit(solution)/shard_map/ppermute | solution.py:17
  99.7 1.6 %collective-permute-start.29 = (bf16[64,384]{1,0:T(8,128)(2,1)S(1)}, bf16[64,384]{1,0:T(8,128)(2,1)S(1)}, u32[]{:S(2)}, u32[]{:S(2)}) collective-permute-start(bf16[64,384]{1,0:T(8,128)(2,1)S(1)} %get-tuple-element.78), channel_id=1, source_target_pairs={{0,4},{4,0},{1,5},{5,1},{2,6},{6,2},{3,7},{7,3},{8,12},{12,8},{9,1... | collective-permute-start | bytes 147464 | tf_op jit(solution)/shard_map/ppermute | solution.py:17
  101.8 1.5 %collective-permute-start.25 = (bf16[64,384]{1,0:T(8,128)(2,1)S(1)}, bf16[64,384]{1,0:T(8,128)(2,1)S(1)}, u32[]{:S(2)}, u32[]{:S(2)}) collective-permute-start(bf16[64,384]{1,0:T(8,128)(2,1)S(1)} %get-tuple-element.72), channel_id=1, source_target_pairs={{0,4},{4,0},{1,5},{5,1},{2,6},{6,2},{3,7},{7,3},{8,12},{12,8},{9,1... | collective-permute-start | bytes 147464 | tf_op jit(solution)/shard_map/ppermute | solution.py:17
  104.0 1.7 %collective-permute-done.27.refs_5_ = bf16[64,384]{1,0:T(8,128)(2,1)S(1)} collective-permute-done((bf16[64,384]{1,0:T(8,128)(2,1)S(1)}, bf16[64,384]{1,0:T(8,128)(2,1)S(1)}, u32[]{:S(2)}, u32[]{:S(2)}) %collective-permute-start.27) | collective-permute-done | bytes 49184 | tf_op jit(solution)/shard_map/ppermute | solution.py:17
  (91 shorter events, 20.5 us)
Async XLA Ops:
  0.0 82.9 %copy-start = (s32[2,128]{1,0:T(2,128)S(1)}, s32[2,128]{1,0:T(2,128)}, u32[]{:S(2)}) copy-start(s32[2,128]{1,0:T(2,128)} %param.16) | copy-start | bytes 3076
  3.8 1.9 %collective-permute-start = (bf16[1552,128]{1,0:T(8,128)(2,1)S(1)}, bf16[1552,128]{1,0:T(8,128)(2,1)S(1)}, u32[]{:S(2)}, u32[]{:S(2)}) collective-permute-start(bf16[1552,128]{1,0:T(8,128)(2,1)S(1)} %get-tuple-element.42), channel_id=1, source_target_pairs={{0,1},{1,0},{2,3},{3,2},{4,5},{5,4},{6,7},{7,6},{8,9},{9,8},{10,11... | collective-permute-start | bytes 1191944 | tf_op jit(solution)/shard_map/ppermute | solution.py:17
  5.7 8.2 %collective-permute-start.1 = (bf16[784,128]{1,0:T(8,128)(2,1)S(1)}, bf16[784,128]{1,0:T(8,128)(2,1)S(1)}, u32[]{:S(2)}, u32[]{:S(2)}) collective-permute-start(bf16[784,128]{1,0:T(8,128)(2,1)S(1)} %get-tuple-element.45), channel_id=1, source_target_pairs={{0,2},{1,3},{2,0},{3,1},{4,6},{5,7},{6,4},{7,5},{8,10},{9,11},{10,... | collective-permute-start | bytes 602120 | tf_op jit(solution)/shard_map/ppermute | solution.py:17
  14.1 14.9 %collective-permute-start.10 = (bf16[2,192,768]{2,1,0:T(8,128)(2,1)S(1)}, bf16[2,192,768]{2,1,0:T(8,128)(2,1)S(1)}, u32[]{:S(2)}, u32[]{:S(2)}) collective-permute-start(bf16[2,192,768]{2,1,0:T(8,128)(2,1)S(1)} %get-tuple-element.56.refs_0_), channel_id=1, source_target_pairs={{0,2},{1,3},{2,0},{3,1},{4,6},{5,7},{6,4},{7,5},{8,10},{9,11},{10,... | collective-permute-start | bytes 1769480 | tf_op jit(solution)/shard_map/ppermute | solution.py:17
  15.9 20.4 %collective-permute-start.9 = (bf16[192,768]{1,0:T(8,128)(2,1)S(1)}, bf16[192,768]{1,0:T(8,128)(2,1)S(1)}, u32[]{:S(2)}, u32[]{:S(2)}) collective-permute-start(bf16[192,768]{1,0:T(8,128)(2,1)S(1)} %get-tuple-element.55), channel_id=1, source_target_pairs={{0,1},{1,0},{2,3},{3,2},{4,5},{5,4},{6,7},{7,6},{8,9},{9,8},{10,11... | collective-permute-start | bytes 884744 | tf_op jit(solution)/shard_map/ppermute | solution.py:17
  15.9 13.9 %collective-permute-start.2 = (bf16[208,128]{1,0:T(8,128)(2,1)S(1)}, bf16[208,128]{1,0:T(8,128)(2,1)S(1)}, u32[]{:S(2)}, u32[]{:S(2)}) collective-permute-start(bf16[208,128]{1,0:T(8,128)(2,1)S(1)} %get-tuple-element.51), channel_id=1, source_target_pairs={{0,8},{8,0},{16,24},{24,16},{1,9},{9,1},{17,25},{25,17},{2,10},{10... | collective-permute-start | bytes 159752 | tf_op jit(solution)/shard_map/ppermute | solution.py:17
  17.4 12.3 %collective-permute-start.3 = (bf16[208,128]{1,0:T(8,128)(2,1)S(1)}, bf16[208,128]{1,0:T(8,128)(2,1)S(1)}, u32[]{:S(2)}, u32[]{:S(2)}) collective-permute-start(bf16[208,128]{1,0:T(8,128)(2,1)S(1)} %get-tuple-element.52), channel_id=1, source_target_pairs={{0,16},{8,24},{16,0},{24,8},{1,17},{9,25},{17,1},{25,9},{2,18},{10... | collective-permute-start | bytes 159752 | tf_op jit(solution)/shard_map/ppermute | solution.py:17
  20.0 43.5 %copy-start.15 = (bf16[6144]{0:T(1024)(128)(2,1)S(1)}, bf16[6144]{0:T(1024)(128)(2,1)}, u32[]{:S(2)}) copy-start(bf16[6144]{0:T(1024)(128)(2,1)} %param.22) | copy-start | bytes 36868
  20.0 9.8 %collective-permute-start.4 = (bf16[208,128]{1,0:T(8,128)(2,1)S(1)}, bf16[208,128]{1,0:T(8,128)(2,1)S(1)}, u32[]{:S(2)}, u32[]{:S(2)}) collective-permute-start(bf16[208,128]{1,0:T(8,128)(2,1)S(1)} %get-tuple-element.53), channel_id=1, source_target_pairs={{0,24},{8,16},{16,8},{24,0},{1,25},{9,17},{17,9},{25,1},{2,26},{10... | collective-permute-start | bytes 159752 | tf_op jit(solution)/shard_map/ppermute | solution.py:17
  29.0 12.6 %collective-permute-start.11 = (bf16[192,768]{1,0:T(8,128)(2,1)S(1)}, bf16[192,768]{1,0:T(8,128)(2,1)S(1)}, u32[]{:S(2)}, u32[]{:S(2)}) collective-permute-start(bf16[192,768]{1,0:T(8,128)(2,1)S(1)} %get-tuple-element.79), channel_id=1, source_target_pairs={{0,1},{1,0},{2,3},{3,2},{4,5},{5,4},{6,7},{7,6},{8,9},{9,8},{10,11... | collective-permute-start | bytes 884744 | tf_op jit(solution)/shard_map/ppermute | solution.py:17
  30.1 4.3 %collective-permute-start.5 = (bf16[208,128]{1,0:T(8,128)(2,1)S(1)}, bf16[208,128]{1,0:T(8,128)(2,1)S(1)}, u32[]{:S(2)}, u32[]{:S(2)}) collective-permute-start(bf16[208,128]{1,0:T(8,128)(2,1)S(1)} %centre.1.own_ref), channel_id=1, source_target_pairs={{0,4},{4,0},{1,5},{5,1},{2,6},{6,2},{3,7},{7,3},{8,12},{12,8},{9,1... | collective-permute-start | bytes 159752 | tf_op jit(solution)/shard_map/ppermute | solution.py:17
  34.4 1.9 %collective-permute-start.6 = (bf16[416,128]{1,0:T(8,128)(2,1)S(1)}, bf16[416,128]{1,0:T(8,128)(2,1)S(1)}, u32[]{:S(2)}, u32[]{:S(2)}) collective-permute-start(bf16[416,128]{1,0:T(8,128)(2,1)S(1)} %join.1.refs_0_), channel_id=1, source_target_pairs={{0,1},{1,0},{2,3},{3,2},{4,5},{5,4},{6,7},{7,6},{8,9},{9,8},{10,11... | collective-permute-start | bytes 319496 | tf_op jit(solution)/shard_map/ppermute | solution.py:17
  34.5 5.8 %collective-permute-start.7 = (bf16[416,128]{1,0:T(8,128)(2,1)S(1)}, bf16[416,128]{1,0:T(8,128)(2,1)S(1)}, u32[]{:S(2)}, u32[]{:S(2)}) collective-permute-start(bf16[416,128]{1,0:T(8,128)(2,1)S(1)} %join.1.refs_0_), channel_id=1, source_target_pairs={{0,2},{1,3},{2,0},{3,1},{4,6},{5,7},{6,4},{7,5},{8,10},{9,11},{10,... | collective-permute-start | bytes 319496 | tf_op jit(solution)/shard_map/ppermute | solution.py:17
  35.9 5.7 %collective-permute-start.8 = (bf16[416,128]{1,0:T(8,128)(2,1)S(1)}, bf16[416,128]{1,0:T(8,128)(2,1)S(1)}, u32[]{:S(2)}, u32[]{:S(2)}) collective-permute-start(bf16[416,128]{1,0:T(8,128)(2,1)S(1)} %join.1.refs_0_), channel_id=1, source_target_pairs={{0,3},{1,2},{2,1},{3,0},{4,7},{5,6},{6,5},{7,4},{8,11},{9,10},{10,... | collective-permute-start | bytes 319496 | tf_op jit(solution)/shard_map/ppermute | solution.py:17
  43.1 5.1 %collective-permute-start.12 = (bf16[400,128]{1,0:T(8,128)(2,1)S(1)}, bf16[400,128]{1,0:T(8,128)(2,1)S(1)}, u32[]{:S(2)}, u32[]{:S(2)}) collective-permute-start(bf16[400,128]{1,0:T(8,128)(2,1)S(1)} %get-tuple-element.59), channel_id=1, source_target_pairs={{0,8},{8,0},{16,24},{24,16},{1,9},{9,1},{17,25},{25,17},{2,10},{10... | collective-permute-start | bytes 307208 | tf_op jit(solution)/shard_map/ppermute | solution.py:17
  44.6 33.8 %collective-permute-start.21 = (bf16[4,64,1536]{2,1,0:T(8,128)(2,1)S(1)}, bf16[4,64,1536]{2,1,0:T(8,128)(2,1)S(1)}, u32[]{:S(2)}, u32[]{:S(2)}) collective-permute-start(bf16[4,64,1536]{2,1,0:T(8,128)(2,1)S(1)} %image_pack.1.refs_1_), channel_id=1, source_target_pairs={{0,4},{4,0},{1,5},{5,1},{2,6},{6,2},{3,7},{7,3},{8,12},{12,8},{9,1... | collective-permute-start | bytes 2359304 | tf_op jit(solution)/shard_map/ppermute | solution.py:17
  48.3 10.7 %collective-permute-start.19 = (bf16[128,1536]{1,0:T(8,128)(2,1)S(1)}, bf16[128,1536]{1,0:T(8,128)(2,1)}, u32[]{:S(2)}, u32[]{:S(2)}) collective-permute-start(bf16[128,1536]{1,0:T(8,128)(2,1)S(1)} %maps_pack.1.refs_0_), channel_id=1, source_target_pairs={{0,2},{1,3},{2,0},{3,1},{4,6},{5,7},{6,4},{7,5},{8,10},{9,11},{10,... | collective-permute-start | bytes 1179656 | tf_op jit(solution)/shard_map/ppermute | solution.py:17
  49.8 30.0 %collective-permute-start.18 = (bf16[128,1536]{1,0:T(8,128)(2,1)S(1)}, bf16[128,1536]{1,0:T(8,128)(2,1)}, u32[]{:S(2)}, u32[]{:S(2)}) collective-permute-start(bf16[128,1536]{1,0:T(8,128)(2,1)S(1)} %maps_pack.1.refs_0_), channel_id=1, source_target_pairs={{0,1},{1,0},{2,3},{3,2},{4,5},{5,4},{6,7},{7,6},{8,9},{9,8},{10,11... | collective-permute-start | bytes 1179656 | tf_op jit(solution)/shard_map/ppermute | solution.py:17
  59.0 20.9 %collective-permute-start.20 = (bf16[128,1536]{1,0:T(8,128)(2,1)}, bf16[128,1536]{1,0:T(8,128)(2,1)}, u32[]{:S(2)}, u32[]{:S(2)}) collective-permute-start(bf16[128,1536]{1,0:T(8,128)(2,1)} %collective-permute-done.19.refs_2_), channel_id=1, source_target_pairs={{0,1},{1,0},{2,3},{3,2},{4,5},{5,4},{6,7},{7,6},{8,9},{9,8},{10,11... | collective-permute-start | bytes 1179656 | tf_op jit(solution)/shard_map/ppermute | solution.py:17
  59.0 11.4 %collective-permute-start.13 = (bf16[400,128]{1,0:T(8,128)(2,1)}, bf16[400,128]{1,0:T(8,128)(2,1)}, u32[]{:S(2)}, u32[]{:S(2)}) collective-permute-start(bf16[400,128]{1,0:T(8,128)(2,1)} %get-tuple-element.60), channel_id=1, source_target_pairs={{0,16},{8,24},{16,0},{24,8},{1,17},{9,25},{17,1},{25,9},{2,18},{10... | collective-permute-start | bytes 307208 | tf_op jit(solution)/shard_map/ppermute | solution.py:17
  61.6 8.8 %collective-permute-start.14 = (bf16[400,128]{1,0:T(8,128)(2,1)}, bf16[400,128]{1,0:T(8,128)(2,1)}, u32[]{:S(2)}, u32[]{:S(2)}) collective-permute-start(bf16[400,128]{1,0:T(8,128)(2,1)} %get-tuple-element.61), channel_id=1, source_target_pairs={{0,24},{8,16},{16,8},{24,0},{1,25},{9,17},{17,9},{25,1},{2,26},{10... | collective-permute-start | bytes 307208 | tf_op jit(solution)/shard_map/ppermute | solution.py:17
  74.1 8.8 %collective-permute-start.15 = (bf16[64,768]{1,0:T(8,128)(2,1)S(1)}, bf16[64,768]{1,0:T(8,128)(2,1)S(1)}, u32[]{:S(2)}, u32[]{:S(2)}) collective-permute-start(bf16[64,768]{1,0:T(8,128)(2,1)S(1)} %finish.1.refs_0_), channel_id=1, source_target_pairs={{0,8},{8,0},{16,24},{24,16},{1,9},{9,1},{17,25},{25,17},{2,10},{10... | collective-permute-start | bytes 294920 | tf_op jit(solution)/shard_map/ppermute | solution.py:17
  76.5 6.5 %collective-permute-start.16 = (bf16[64,768]{1,0:T(8,128)(2,1)S(1)}, bf16[64,768]{1,0:T(8,128)(2,1)S(1)}, u32[]{:S(2)}, u32[]{:S(2)}) collective-permute-start(bf16[64,768]{1,0:T(8,128)(2,1)S(1)} %finish.1.refs_0_), channel_id=1, source_target_pairs={{0,16},{8,24},{16,0},{24,8},{1,17},{9,25},{17,1},{25,9},{2,18},{10... | collective-permute-start | bytes 294920 | tf_op jit(solution)/shard_map/ppermute | solution.py:17
  78.5 8.4 %collective-permute-start.17 = (bf16[64,768]{1,0:T(8,128)(2,1)S(1)}, bf16[64,768]{1,0:T(8,128)(2,1)S(1)}, u32[]{:S(2)}, u32[]{:S(2)}) collective-permute-start(bf16[64,768]{1,0:T(8,128)(2,1)S(1)} %finish.1.refs_0_), channel_id=1, source_target_pairs={{0,24},{8,16},{16,8},{24,0},{1,25},{9,17},{17,9},{25,1},{2,26},{10... | collective-permute-start | bytes 294920 | tf_op jit(solution)/shard_map/ppermute | solution.py:17
  81.4 8.2 %collective-permute-start.22 = (f32[2,64,64]{2,1,0:T(8,128)S(1)}, f32[2,64,64]{2,1,0:T(8,128)S(1)}, u32[]{:S(2)}, u32[]{:S(2)}) collective-permute-start(f32[2,64,64]{2,1,0:T(8,128)S(1)} %get-tuple-element.63), channel_id=1, source_target_pairs={{0,4},{4,0},{1,5},{5,1},{2,6},{6,2},{3,7},{7,3},{8,12},{12,8},{9,1... | collective-permute-start | bytes 98312 | tf_op jit(solution)/shard_map/ppermute | solution.py:17
  87.6 3.2 %collective-permute-start.24 = (bf16[128,768]{1,0:T(8,128)(2,1)S(1)}, bf16[128,768]{1,0:T(8,128)(2,1)S(1)}, u32[]{:S(2)}, u32[]{:S(2)}) collective-permute-start(bf16[128,768]{1,0:T(8,128)(2,1)S(1)} %get-tuple-element.70), channel_id=1, source_target_pairs={{0,1},{1,0},{2,3},{3,2},{4,5},{5,4},{6,7},{7,6},{8,9},{9,8},{10,11... | collective-permute-start | bytes 589832 | tf_op jit(solution)/shard_map/ppermute | solution.py:17
  87.7 7.8 %collective-permute-start.26 = (bf16[128,768]{1,0:T(8,128)(2,1)S(1)}, bf16[128,768]{1,0:T(8,128)(2,1)S(1)}, u32[]{:S(2)}, u32[]{:S(2)}) collective-permute-start(bf16[128,768]{1,0:T(8,128)(2,1)S(1)} %get-tuple-element.73), channel_id=1, source_target_pairs={{0,2},{1,3},{2,0},{3,1},{4,6},{5,7},{6,4},{7,5},{8,10},{9,11},{10,... | collective-permute-start | bytes 589832 | tf_op jit(solution)/shard_map/ppermute | solution.py:17
  89.3 9.5 %collective-permute-start.28 = (bf16[128,768]{1,0:T(8,128)(2,1)S(1)}, bf16[128,768]{1,0:T(8,128)(2,1)S(1)}, u32[]{:S(2)}, u32[]{:S(2)}) collective-permute-start(bf16[128,768]{1,0:T(8,128)(2,1)S(1)} %get-tuple-element.76), channel_id=1, source_target_pairs={{0,3},{1,2},{2,1},{3,0},{4,7},{5,6},{6,5},{7,4},{8,11},{9,10},{10,... | collective-permute-start | bytes 589832 | tf_op jit(solution)/shard_map/ppermute | solution.py:17
  99.7 4.2 %collective-permute-start.29 = (bf16[64,384]{1,0:T(8,128)(2,1)S(1)}, bf16[64,384]{1,0:T(8,128)(2,1)S(1)}, u32[]{:S(2)}, u32[]{:S(2)}) collective-permute-start(bf16[64,384]{1,0:T(8,128)(2,1)S(1)} %get-tuple-element.78), channel_id=1, source_target_pairs={{0,4},{4,0},{1,5},{5,1},{2,6},{6,2},{3,7},{7,3},{8,12},{12,8},{9,1... | collective-permute-start | bytes 147464 | tf_op jit(solution)/shard_map/ppermute | solution.py:17
  101.3 4.4 %collective-permute-start.27 = (bf16[64,384]{1,0:T(8,128)(2,1)S(1)}, bf16[64,384]{1,0:T(8,128)(2,1)S(1)}, u32[]{:S(2)}, u32[]{:S(2)}) collective-permute-start(bf16[64,384]{1,0:T(8,128)(2,1)S(1)} %get-tuple-element.75), channel_id=1, source_target_pairs={{0,4},{4,0},{1,5},{5,1},{2,6},{6,2},{3,7},{7,3},{8,12},{12,8},{9,1... | collective-permute-start | bytes 147464 | tf_op jit(solution)/shard_map/ppermute | solution.py:17
  101.8 4.7 %collective-permute-start.25 = (bf16[64,384]{1,0:T(8,128)(2,1)S(1)}, bf16[64,384]{1,0:T(8,128)(2,1)S(1)}, u32[]{:S(2)}, u32[]{:S(2)}) collective-permute-start(bf16[64,384]{1,0:T(8,128)(2,1)S(1)} %get-tuple-element.72), channel_id=1, source_target_pairs={{0,4},{4,0},{1,5},{5,1},{2,6},{6,2},{3,7},{7,3},{8,12},{12,8},{9,1... | collective-permute-start | bytes 147464 | tf_op jit(solution)/shard_map/ppermute | solution.py:17
  103.3 4.1 %collective-permute-start.23 = (bf16[64,384]{1,0:T(8,128)(2,1)S(1)}, bf16[64,384]{1,0:T(8,128)(2,1)S(1)}, u32[]{:S(2)}, u32[]{:S(2)}) collective-permute-start(bf16[64,384]{1,0:T(8,128)(2,1)S(1)} %get-tuple-element.69), channel_id=1, source_target_pairs={{0,4},{4,0},{1,5},{5,1},{2,6},{6,2},{3,7},{7,3},{8,12},{12,8},{9,1... | collective-permute-start | bytes 147464 | tf_op jit(solution)/shard_map/ppermute | solution.py:17
  (16 other events, 185.6 us)

commit v4 on v3

--- a/solution.py
+++ b/solution.py
@@ -264,6 +264,7 @@
 ANY = pl.BlockSpec(memory_space=pl.ANY)
 VMEM = pl.BlockSpec(memory_space=pltpu.VMEM)
 SMEM = pl.BlockSpec(memory_space=pltpu.SMEM)
+HBM = pl.BlockSpec(memory_space=pltpu.HBM)
 NT = (((1,), (1,)), ((), ()))
 TN = (((0,), (0,)), ((), ()))
 
@@ -299,12 +300,30 @@
     return rows[0:1] + rows[1:2]
 
 
-def context_kernel(h_ref, w_ref, b_ref, send_ref, keep_ref, stat_ref):
+def context_kernel(
+    h_hbm, w_hbm, b_hbm, send_ref, keep_ref, stat_ref, h_ref, w_ref, b_ref, sems
+):
     mine = lax.rem(lax.axis_index("req"), 2)
-    features = b_ref.shape[1]
+    features = b_ref.shape[0]
     pairs = w_ref.shape[1] // (2 * features)
+    count = sems.shape[0] - 2
+    chunk = w_ref.shape[1] // count
+    copies = [pltpu.make_async_copy(h_hbm, h_ref, sems.at[0])]
+    for i in range(count):
+        columns = pl.ds(i * chunk, chunk)
+        copies.append(
+            pltpu.make_async_copy(w_hbm.at[:, columns], w_ref.at[:, columns], sems.at[i + 1])
+        )
+    copies.append(pltpu.make_async_copy(b_hbm, b_ref, sems.at[count + 1]))
+    for copy in copies:
+        copy.start()
+    copies[0].wait()
+    arrived = 0
     total = jnp.zeros((1, h_ref.shape[0]), F32)
     for p in range(pairs):
+        while arrived * chunk < (p + 1) * 2 * features:
+            arrived += 1
+            copies[arrived].wait()
         product = jnp.dot(
             h_ref[...], w_ref[:, p * 2 * features : (p + 1) * 2 * features],
             preferred_element_type=F32,
@@ -314,6 +333,7 @@
         rows = slice(p * features, (p + 1) * features)
         keep_ref[rows] = jnp.where(mine == 0, low, high)
         send_ref[rows] = jnp.where(mine == 0, high, low).astype(BF16)
+    copies[-1].wait()
     stat = total + jnp.sum(b_ref[...].astype(F32))
     send_ref[pairs * features :] = stat_rows(stat)
     stat_ref[...] = jnp.broadcast_to(stat, stat_ref.shape)
@@ -346,7 +366,7 @@
     out_stat_ref[...] = jnp.broadcast_to(stat, out_stat_ref.shape)
 
 
-def centre_kernel(width, prompt_ref, keep_ref, stat_ref, bias_ref, scale_ref, shift_ref, *refs):
+def centre_kernel(width, prompt_ref, adapter_ref, keep_ref, stat_ref, bias_ref, scale_ref, shift_ref, *refs):
     got_refs, out_ref = refs[:-1], refs[-1]
     features, tokens = keep_ref.shape
     total = keep_ref[...] + bias_ref[...]
@@ -367,7 +387,13 @@
             piece = jnp.concatenate([piece, jnp.zeros((1, gap), F32)], axis=1)
         extra = jnp.where(row == 2 + j, piece, extra)
     extra = jnp.where(row == ROWS - 1, prompt_ref[0, 0].astype(F32), extra)
+    extra = jnp.where(row == ROWS - 2, adapter_ref[0, 0].astype(F32), extra)
     out_ref[features:] = extra.astype(BF16)
+
+
+def pass_on_kernel(got_ref, dep_ref, own_ref, next_ref):
+    own_ref[...] = got_ref[0]
+    next_ref[...] = got_ref[1]
 
 
 def join_kernel(own_ref, got_ref, out_ref):
@@ -376,7 +402,7 @@
     out_ref[size:] = got_ref[...]
 
 
-def project_kernel(n_seq, n_req, n_enc, *refs):
+def project_kernel(n_seq, n_req, n_enc, dep_ref, *refs):
     payload_refs = refs[:n_req]
     weight_refs = refs[n_req : 2 * n_req]
     prompts_ref, keep_ref = refs[2 * n_req : 2 * n_req + 2]
@@ -399,6 +425,7 @@
             shifts.append(jnp.concatenate(pieces, axis=1)[:, :features])
             if p == 0:
                 prompts_ref[k] = jnp.max(extra[ROWS - 1 : ROWS]).astype(jnp.int32)
+                prompts_ref[n_req + k] = jnp.max(extra[ROWS - 2 : ROWS - 1]).astype(jnp.int32)
         shifts.append(jnp.zeros((ROWS - n_seq, features), F32))
         left.append(jnp.concatenate(shifts, axis=0).astype(BF16))
         term = jnp.dot(
@@ -434,7 +461,7 @@
         send_ref[...] = rows_ref[at(e ^ (k + 1), step)].astype(BF16)
 
 
-def finish_kernel(n_req, model_width, keep_ref, bias_ref, *refs):
+def finish_kernel(n_req, model_width, dep_ref, keep_ref, bias_ref, *refs):
     got_refs, out_ref = refs[:-1], refs[-1]
     r, s = lax.axis_index("req"), lax.axis_index("seq")
     size, width = out_ref.shape
@@ -458,7 +485,7 @@
         out_ref[:, h * HDIM : (h + 1) * HDIM] = head.astype(BF16)
 
 
-def choose_kernel(n_seq, n_enc, chosen_ref, *refs):
+def choose_kernel(n_seq, n_enc, chosen_ref, dep_ref, *refs):
     part_refs, out_refs = refs[:n_enc], refs[n_enc:]
     e, r, s = lax.axis_index("enc"), lax.axis_index("req"), lax.axis_index("seq")
     halves = n_enc // n_seq
@@ -520,33 +547,43 @@
         copy.wait()
 
 
-def lowrank_kernel(n_req, part, adapter_ref, x_ref, *refs):
-    out_ref, chosen_ref = refs[-2:]
-    map_refs = refs[:n_req]
-    got_refs = refs[n_req:-2]
-    place = adapter_ref[0, 0] ^ lax.axis_index("req")
-    for k in range(n_req):
-        @pl.when(place == k)
+def select_kernel(ids_ref, own_ref, pair_ref, dep_ref, mine_ref, core_ref):
+    r = lax.axis_index("req")
+    for out_ref, adapter in ((mine_ref, ids_ref[4]), (core_ref, ids_ref[5])):
+        other = lax.rem((adapter ^ r) // 2, 2)
+
+        @pl.when(other == 0)
         def _():
-            chosen_ref[...] = map_refs[k][...]
+            out_ref[...] = own_ref[...]
+
+        @pl.when(other == 1)
+        def _():
+            out_ref[...] = pair_ref[...]
+
+
+def lowrank_kernel(part, adapter_ref, x_ref, mine_ref, core_ref, got_ref, out_ref, chosen_ref):
+    other = lax.rem(adapter_ref[0, 0] ^ lax.axis_index("req"), 2)
     rank = out_ref.shape[-1]
-    down = chosen_ref[:rank]
-    own = x_ref[:, pl.ds(pl.multiple_of(lax.axis_index("seq") * part, HDIM), part)]
-    out_ref[0] = lax.dot_general(own, down, NT, preferred_element_type=F32)
-    for k, got_ref in enumerate(got_refs):
-        out_ref[k + 1] = lax.dot_general(got_ref[3], down, NT, preferred_element_type=F32)
-
-
-def arrange_kernel(n_req, part, inner, low_ref, maps_ref, qk_ref, v_ref, *refs):
+    for k, ref in enumerate((mine_ref, core_ref)):
+        @pl.when(other == k)
+        def _():
+            chosen_ref[...] = ref[rank:]
+            own = x_ref[:, pl.ds(pl.multiple_of(lax.axis_index("seq") * part, HDIM), part)]
+            for i, rows in enumerate((own, got_ref[3])):
+                out_ref[i] = lax.dot_general(
+                    rows, ref[:rank], NT, preferred_element_type=F32
+                )
+
+
+def arrange_kernel(n_req, part, inner, low_ref, other_ref, maps_ref, qk_ref, v_ref, *refs):
     got_refs, (q_out, k_out, v_out) = refs[:-3], refs[-3:]
     r, s = lax.axis_index("req"), lax.axis_index("seq")
-    rank = maps_ref.shape[0] // 2
     half = part // n_req
     tokens = qk_ref.shape[0]
-    low = low_ref[...].astype(BF16)
+    low = [(low_ref[i] + other_ref[i ^ 1]).astype(BF16) for i in range(2)]
     for k in range(n_req):
         place = (r ^ k) * half
-        up = maps_ref[rank:, pl.ds(pl.multiple_of(place, HDIM), half)]
+        up = maps_ref[:, pl.ds(pl.multiple_of(place, HDIM), half)]
         for i in range(len(got_refs) + 1):
             rows = slice(i * tokens, (i + 1) * tokens)
             if i == 0:
@@ -566,7 +603,8 @@
             ).astype(BF16)
 
 
-def heads_kernel(scale, live_ref, text_ref, q_ref, k_ref, v_ref, dep_ref, *out_refs):
+def heads_kernel(scale, live_ref, text_ref, q_ref, k_ref, v_ref, *refs):
+    out_refs = refs[2:]
     live = live_ref[...] != 0
     half = q_ref.shape[2]
     size = out_refs[0].shape[0]
@@ -641,7 +679,14 @@
             struct((model_width // 2, tokens), F32),
             stat,
         ),
-        (encoder_hidden[0], context_weight, context_bias[None]),
+        (encoder_hidden[0], context_weight, context_bias),
+        [HBM] * 3,
+        [
+            pltpu.VMEM(encoder_hidden.shape[1:], BF16),
+            pltpu.VMEM(context_weight.shape, BF16),
+            pltpu.VMEM(context_bias.shape, BF16),
+            dma((2 + n_enc,)),
+        ],
         name="context",
     )
     got = swap(send, "req", n_req, 1)
@@ -681,22 +726,16 @@
     )
     got = swap(send, "req", n_req, 2)
     keep, sums, *sends = call(
-        functools.partial(scatter_kernel, features, 2),
+        functools.partial(scatter_kernel, features, 3),
         (struct((features, tokens), F32), stat)
         + tuple(struct((features + ROWS, tokens)) for _ in range(1, n_enc)),
-        (got, keep, sums, weight_pair, packed[0]),
-        [VMEM] * 3 + [ANY] * 2,
+        (got, keep, sums, weight_pair, packed[0], weight_core_got),
+        [VMEM] * 3 + [ANY] * 3,
         name="scatter",
     )
     arrived = [swap(sends[k - 1], "enc", n_enc, k) for k in range(1, n_enc)]
     weight_pair = lax.optimization_barrier((weight_pair, keep))[0]
     weight_pair_got = swap(weight_pair, "req", n_req, 2)
-    weights = (
-        weight_own,
-        weight_core_got,
-        weight_pair_got[0],
-        swap(weight_pair_got[1], "req", n_req, 1),
-    )
 
     bias_columns = jnp.broadcast_to(context_bias.astype(F32)[:, None], (features, tokens))
     scale_columns = jnp.broadcast_to(
@@ -705,8 +744,17 @@
     own = call(
         functools.partial(centre_kernel, model_width),
         struct((features + ROWS, tokens)),
-        (request_prompt, keep, sums, bias_columns, scale_columns, modulation_shift, *arrived),
-        [SMEM] + [VMEM] * (5 + len(arrived)),
+        (
+            request_prompt,
+            adapter_of_request,
+            keep,
+            sums,
+            bias_columns,
+            scale_columns,
+            modulation_shift,
+            *arrived,
+        ),
+        [SMEM] * 2 + [VMEM] * (5 + len(arrived)),
         name="centre",
     )
     joined = call(
@@ -716,14 +764,23 @@
         name="join",
     )
     payloads = [joined] + [swap(joined, "req", n_req, k) for k in range(1, n_req)]
+    weight_own_pair, weight_next = call(
+        pass_on_kernel,
+        (weight, weight),
+        (weight_pair_got, joined),
+        [VMEM, ANY],
+        name="pass_on",
+    )
+    weights = (weight_own, weight_core_got, weight_own_pair, swap(weight_next, "req", n_req, 1))
 
     size = n_seq * tokens // n_enc
     step = 2 * half // HDIM * size + ROWS
-    prompts, keep, *sends = call(
+    ids, keep, *sends = call(
         functools.partial(project_kernel, n_seq, n_req, n_enc),
-        (struct((n_req,), jnp.int32), struct((step, HDIM), F32))
+        (struct((2 * n_req,), jnp.int32), struct((step, HDIM), F32))
         + tuple(struct((step, HDIM)) for _ in range(1, n_enc)),
-        (*payloads, *weights),
+        (image_got[0], *payloads, *weights),
+        [ANY] + [VMEM] * (2 * n_req),
         scratch=[pltpu.VMEM((n_enc * step, HDIM), F32)],
         out_specs=(SMEM,) + (VMEM,) * n_enc,
         name="project",
@@ -733,60 +790,53 @@
     maps = call(
         functools.partial(maps_kernel, part),
         struct((2 * rank, part)),
-        (adapter_down_maps[0].T, adapter_up_maps[0], arrived[0]),
+        (adapter_down_maps[0].T, adapter_up_maps[0], keep),
         [ANY] * 3,
         [dma((2,))],
         name="maps_pack",
     )
-    maps = [maps]
-    step = n_req // 2
-    while step:
-        maps = maps + [swap(m, "req", n_req, step) for m in maps]
-        step //= 2
-    ordered = [None] * n_req
-    place = [0]
-    step = n_req // 2
-    while step:
-        place = place + [p ^ step for p in place]
-        step //= 2
-    for p, m in zip(place, maps):
-        ordered[p] = m
+    maps_pair = swap(maps, "req", n_req, 2)
+
+    text = call(
+        functools.partial(finish_kernel, n_req, model_width),
+        struct((size, 2 * half)),
+        (maps_pair, keep, key_value_bias[None], *arrived),
+        [ANY] + [VMEM] * (2 + len(arrived)),
+        name="finish",
+    )
+    maps_mine, maps_core = call(
+        select_kernel,
+        (struct((2 * rank, part)), struct((2 * rank, part))),
+        (ids, maps, maps_pair, text),
+        [SMEM, VMEM, VMEM, ANY],
+        name="select",
+    )
     low, chosen_maps = call(
-        functools.partial(lowrank_kernel, n_req, part),
-        (struct((n_seq, image_rows, rank), F32), struct((2 * rank, part))),
-        (adapter_of_request, stream, *ordered, *image_got),
-        [SMEM] + [VMEM] * (1 + n_req + len(image_got)),
+        functools.partial(lowrank_kernel, part),
+        (struct((n_seq, image_rows, rank), F32), struct((rank, part))),
+        (adapter_of_request, stream, maps_mine, swap(maps_core, "req", n_req, 1), image_got[0]),
+        [SMEM] + [VMEM] * 4,
         name="lowrank",
     )
-    for bit in bits_of(n_seq):
-        other = swap(low, "seq", n_seq, bit)
-        low = low + jnp.stack([other[k ^ bit] for k in range(n_seq)])
     arranged = struct((n_req, n_seq * image_rows, half))
     queries, image_keys, image_values = call(
         functools.partial(arrange_kernel, n_req, part, inner),
         (arranged, arranged, arranged),
-        (low, chosen_maps, qk, base, *image_got),
+        (low, swap(low, "seq", n_seq, 1), chosen_maps, qk, base, *image_got),
         name="arrange",
-    )
-
-    text = call(
-        functools.partial(finish_kernel, n_req, model_width),
-        struct((size, 2 * half)),
-        (keep, key_value_bias[None], *arrived),
-        name="finish",
     )
     parts = [text] + [swap(text, "enc", n_enc, k) for k in range(1, n_enc)]
     rows = call(
         functools.partial(choose_kernel, n_seq, n_enc),
         tuple(struct((tokens, 2 * half)) for _ in range(n_req)),
-        (prompts, *parts),
-        [SMEM] + [VMEM] * n_enc,
+        (ids, image_values, *parts),
+        [SMEM, ANY] + [VMEM] * n_enc,
         name="choose",
     )
     rows = [rows[0]] + [swap(rows[k], "req", n_req, k) for k in range(1, n_req)]
     live = lax.dynamic_slice_in_dim(prompt_token_ids, request_prompt[0, 0], 1, 0)
     pieces = [None] * n_req
-    last = live
+    last = (live, live)
     for k in range(n_req):
         block = pl.BlockSpec((1, n_seq * image_rows, half), lambda i, k=k: (k, 0, 0))
         whole = lambda shape: pl.BlockSpec(shape, lambda i: (0, 0))
@@ -794,13 +844,13 @@
             functools.partial(heads_kernel, HDIM ** (-0.5)),
             grid=(1,),
             out_shape=[struct((image_rows, half)) for _ in range(n_seq)],
-            in_specs=[whole((1, tokens)), whole((tokens, 2 * half)), block, block, block, ANY],
+            in_specs=[whole((1, tokens)), whole((tokens, 2 * half)), block, block, block, ANY, ANY],
             out_specs=[whole((image_rows, half)) for _ in range(n_seq)],
             compiler_params=pltpu.CompilerParams(vmem_limit_bytes=16 * 1024 * 1024),
             name="heads",
-        )(live, rows[k], queries, image_keys, image_values, last)
-        last = mixed[0]
-        pieces[k] = [mixed[0]] + [swap(mixed[i], "seq", n_seq, i) for i in range(1, n_seq)]
+        )(live, rows[k], queries, image_keys, image_values, *last)
+        pieces[k] = [mixed[0], swap(mixed[1], "seq", n_seq, 1)]
+        last = (mixed[0], pieces[k - 1][1] if k else live)
     result = call(
         functools.partial(assemble_kernel, n_req, n_seq),
         struct((image_rows, inner)),

time: 109 us -> 89.9 us (0.82)
  waiting for transfers between devices: 54.1 us -> 40.4 us
  starting transfers between devices: 34.9 us -> 32.5 us
  local copies, waits for them, and re-layouts: 6.52 us -> 4.81 us
    ppermute x30 -> x29, waiting for transfers between devices: 54.1 us -> 40.4 us  [swap(): return lax.ppermute(block, axis, [(i, i ^ step) for i in range(size)])]
    ppermute x30 -> x29, starting transfers between devices: 34.9 us -> 32.5 us  [swap(): return lax.ppermute(block, axis, [(i, i ^ step) for i in range(size)])]
    pallas_call x14 -> x16, Pallas kernels: 7.29 us -> 6.61 us  [call(): pl.pallas_call(kernel, out_shape=outs, in_specs=specs if specs is not Non...]
    unnamed x36 -> x28, local copies, waits for them, and re-layouts: 4.88 us -> 4.63 us
  transfers between devices with their start and end apart: 30 -> 29, of which waited for: 16 -> 14; matrix products, arithmetic and copies ran while one was open for 1% -> 0% of each run, Pallas kernels for 6% -> 5%
where the time goes in v4:
time: 89.9 us; the launch traced here: 89.6 us
  waiting for transfers between devices  40.4 us (45%)
  starting transfers between devices  32.5 us (36%)
  Pallas kernels  10.3 us (11%)
  local copies, waits for them, and re-layouts  4.81 us (5%)
  between operations  1.62 us (2%)
    ppermute x29, waiting for transfers between devices, swap(): return lax.ppermute(block, axis, [(i, i ^ step) for i in range(size)])  40.4 us
    ppermute x29, starting transfers between devices, swap(): return lax.ppermute(block, axis, [(i, i ^ step) for i in range(size)])  32.5 us
    pallas_call x16, Pallas kernels, call(): pl.pallas_call(kernel, out_shape=outs, in_specs=specs if specs is not Non...  6.61 us
    unnamed x28, local copies, waits for them, and re-layouts  4.63 us
    pallas_call x4, Pallas kernels, per_device_heads(): pl.pallas_call(functools.partial(heads_kernel, HDIM ** (-0.5)), grid=(1,)...  3.66 us
  transfers between devices with their start and end apart: 29, of which 14 were waited for; matrix products, arithmetic and copies ran while one was open for 0% of the time, Pallas kernels for 5%

profile of v4, /device:TPU:0, one launch (start us, length us, event | category | flops | bytes accessed | tf_op | source)
XLA Modules:
  0.0 89.6 jit_solution(13353812253668674431)
XLA Ops:
  0.0 1.4 %copy-done.4 = bf16[256,3072]{1,0:T(8,128)(2,1)S(1)} copy-done((bf16[256,3072]{1,0:T(8,128)(2,1)S(1)}, bf16[256,3072]{1,0:T(8,128)(2,1)}, u32[]{:S(2)}) %copy-start.4) | copy-done | bytes 1572888
  2.9 1.7 %context.1 = (bf16[1552,128]{1,0:T(8,128)(2,1)S(1)}, f32[1536,128]{1,0:T(8,128)S(1)}, f32[8,128]{1,0:T(8,128)S(1)}) custom-call(bf16[128,256]{1,0:T(8,128)(2,1)S(1)} %bitcast.22, bf16[256,3072]{1,0:T(8,128)(2,1)S(1)} %copy-done.4, bf16[192]{0:T(256)(128)(2,1)S(1)} %copy-done.9), custom_call_target="tpu_custom_call" | custom-call | tf_op jit(solution)/shard_map/context/pallas_call | solution.py:273
  5.2 1.7 %copy-done.2 = bf16[192,6144]{1,0:T(8,128)(2,1)S(1)} copy-done((bf16[192,6144]{1,0:T(8,128)(2,1)S(1)}, bf16[192,6144]{1,0:T(8,128)(2,1)}, u32[]{:S(2)}) %copy-start.2) | copy-done | bytes 2359320
  7.4 3.0 %collective-permute-start.2 = (bf16[784,128]{1,0:T(8,128)(2,1)S(1)}, bf16[784,128]{1,0:T(8,128)(2,1)S(1)}, u32[]{:S(2)}, u32[]{:S(2)}) collective-permute-start(bf16[784,128]{1,0:T(8,128)(2,1)S(1)} %get-tuple-element.49), channel_id=1, source_target_pairs={{0,2},{1,3},{2,0},{3,1},{4,6},{5,7},{6,4},{7,5},{8,10},{9,11},{10,... | collective-permute-start | bytes 602120 | tf_op jit(solution)/shard_map/ppermute | solution.py:17
  10.6 5.0 %collective-permute-done.2.got_ref = bf16[784,128]{1,0:T(8,128)(2,1)S(1)} collective-permute-done((bf16[784,128]{1,0:T(8,128)(2,1)S(1)}, bf16[784,128]{1,0:T(8,128)(2,1)S(1)}, u32[]{:S(2)}, u32[]{:S(2)}) %collective-permute-start.2) | collective-permute-done | bytes 200736 | tf_op jit(solution)/shard_map/ppermute | solution.py:17
  15.7 1.8 %collective-permute-start.11 = (bf16[2,192,768]{2,1,0:T(8,128)(2,1)S(1)}, bf16[2,192,768]{2,1,0:T(8,128)(2,1)S(1)}, u32[]{:S(2)}, u32[]{:S(2)}) collective-permute-start(bf16[2,192,768]{2,1,0:T(8,128)(2,1)S(1)} %get-tuple-element.60.refs_0_), channel_id=1, source_target_pairs={{0,2},{1,3},{2,0},{3,1},{4,6},{5,7},{6,4},{7,5},{8,10},{9,11},{10,... | collective-permute-start | bytes 1769480 | tf_op jit(solution)/shard_map/ppermute | solution.py:17
  17.5 1.5 %collective-permute-start = (bf16[4,64,1536]{2,1,0:T(8,128)(2,1)S(1)}, bf16[4,64,1536]{2,1,0:T(8,128)(2,1)S(1)}, u32[]{:S(2)}, u32[]{:S(2)}) collective-permute-start(bf16[4,64,1536]{2,1,0:T(8,128)(2,1)S(1)} %image_pack.1.refs_1_), channel_id=1, source_target_pairs={{0,4},{4,0},{1,5},{5,1},{2,6},{6,2},{3,7},{7,3},{8,12},{12,8},{9,1... | collective-permute-start | bytes 2359304 | tf_op jit(solution)/shard_map/ppermute | solution.py:17
  19.0 1.6 %collective-permute-start.4 = (bf16[208,128]{1,0:T(8,128)(2,1)S(1)}, bf16[208,128]{1,0:T(8,128)(2,1)S(1)}, u32[]{:S(2)}, u32[]{:S(2)}) collective-permute-start(bf16[208,128]{1,0:T(8,128)(2,1)S(1)} %get-tuple-element.56), channel_id=1, source_target_pairs={{0,8},{8,0},{16,24},{24,16},{1,9},{9,1},{17,25},{25,17},{2,10},{10... | collective-permute-start | bytes 159752 | tf_op jit(solution)/shard_map/ppermute | solution.py:17
  20.6 2.6 %collective-permute-start.5 = (bf16[208,128]{1,0:T(8,128)(2,1)S(1)}, bf16[208,128]{1,0:T(8,128)(2,1)S(1)}, u32[]{:S(2)}, u32[]{:S(2)}) collective-permute-start(bf16[208,128]{1,0:T(8,128)(2,1)S(1)} %get-tuple-element.57), channel_id=1, source_target_pairs={{0,16},{8,24},{16,0},{24,8},{1,17},{9,25},{17,1},{25,9},{2,18},{10... | collective-permute-start | bytes 159752 | tf_op jit(solution)/shard_map/ppermute | solution.py:17
  24.7 2.0 %collective-permute-done.5.refs_1_ = bf16[208,128]{1,0:T(8,128)(2,1)S(1)} collective-permute-done((bf16[208,128]{1,0:T(8,128)(2,1)S(1)}, bf16[208,128]{1,0:T(8,128)(2,1)S(1)}, u32[]{:S(2)}, u32[]{:S(2)}) %collective-permute-start.5) | collective-permute-done | bytes 53280 | tf_op jit(solution)/shard_map/ppermute | solution.py:17
  26.7 2.3 %collective-permute-done.6.refs_2_ = bf16[208,128]{1,0:T(8,128)(2,1)S(1)} collective-permute-done((bf16[208,128]{1,0:T(8,128)(2,1)S(1)}, bf16[208,128]{1,0:T(8,128)(2,1)S(1)}, u32[]{:S(2)}, u32[]{:S(2)}) %collective-permute-start.6) | collective-permute-done | bytes 53280 | tf_op jit(solution)/shard_map/ppermute | solution.py:17
  29.9 7.1 %collective-permute-done.7.got_ref = bf16[208,128]{1,0:T(8,128)(2,1)S(1)} collective-permute-done((bf16[208,128]{1,0:T(8,128)(2,1)S(1)}, bf16[208,128]{1,0:T(8,128)(2,1)S(1)}, u32[]{:S(2)}, u32[]{:S(2)}) %collective-permute-start.7) | collective-permute-done | bytes 53280 | tf_op jit(solution)/shard_map/ppermute | solution.py:17
  38.0 1.4 %collective-permute-start.9 = (bf16[416,128]{1,0:T(8,128)(2,1)S(1)}, bf16[416,128]{1,0:T(8,128)(2,1)S(1)}, u32[]{:S(2)}, u32[]{:S(2)}) collective-permute-start(bf16[416,128]{1,0:T(8,128)(2,1)S(1)} %join.1.dep_ref.refs_0_), channel_id=1, source_target_pairs={{0,2},{1,3},{2,0},{3,1},{4,6},{5,7},{6,4},{7,5},{8,10},{9,11},{10,... | collective-permute-start | bytes 319496 | tf_op jit(solution)/shard_map/ppermute | solution.py:17
  39.4 2.6 %collective-permute-done.10.refs_3_ = bf16[416,128]{1,0:T(8,128)(2,1)S(1)} collective-permute-done((bf16[416,128]{1,0:T(8,128)(2,1)S(1)}, bf16[416,128]{1,0:T(8,128)(2,1)S(1)}, u32[]{:S(2)}, u32[]{:S(2)}) %collective-permute-start.10) | collective-permute-done | bytes 106528 | tf_op jit(solution)/shard_map/ppermute | solution.py:17
  41.9 2.8 %collective-permute-done.9.refs_2_ = bf16[416,128]{1,0:T(8,128)(2,1)S(1)} collective-permute-done((bf16[416,128]{1,0:T(8,128)(2,1)S(1)}, bf16[416,128]{1,0:T(8,128)(2,1)S(1)}, u32[]{:S(2)}, u32[]{:S(2)}) %collective-permute-start.9) | collective-permute-done | bytes 106528 | tf_op jit(solution)/shard_map/ppermute | solution.py:17
  44.8 1.2 %project.1 = (s32[8]{0:T(128)S(1)}, f32[400,128]{1,0:T(8,128)S(1)}, bf16[400,128]{1,0:T(8,128)(2,1)S(1)}, bf16[400,128]{1,0:T(8,128)(2,1)S(1)}, bf16[400,128]{1,0:T(8,128)(2,1)S(1)}) custom-call(bf16[4,64,1536]{2,1,0:T(8,128)(2,1)S(1)} %collective-permute-done.dep_ref.got_ref.refs_0_, bf16[416,128]{1,0:T(8,128)(2,1)S(1)} %join.1.dep_ref.refs_0_, ...), custom_call_target="tpu_custom_call" | custom-call | tf_op jit(solution)/shard_map/project/pallas_call | solution.py:273
  46.8 1.5 %collective-permute-start.14 = (bf16[400,128]{1,0:T(8,128)(2,1)S(1)}, bf16[400,128]{1,0:T(8,128)(2,1)S(1)}, u32[]{:S(2)}, u32[]{:S(2)}) collective-permute-start(bf16[400,128]{1,0:T(8,128)(2,1)S(1)} %get-tuple-element.65), channel_id=1, source_target_pairs={{0,8},{8,0},{16,24},{24,16},{1,9},{9,1},{17,25},{25,17},{2,10},{10... | collective-permute-start | bytes 307208 | tf_op jit(solution)/shard_map/ppermute | solution.py:17
  48.3 2.6 %collective-permute-start.15 = (bf16[400,128]{1,0:T(8,128)(2,1)S(1)}, bf16[400,128]{1,0:T(8,128)(2,1)S(1)}, u32[]{:S(2)}, u32[]{:S(2)}) collective-permute-start(bf16[400,128]{1,0:T(8,128)(2,1)S(1)} %get-tuple-element.66), channel_id=1, source_target_pairs={{0,16},{8,24},{16,0},{24,8},{1,17},{9,25},{17,1},{25,9},{2,18},{10... | collective-permute-start | bytes 307208 | tf_op jit(solution)/shard_map/ppermute | solution.py:17
  51.2 1.3 %collective-permute-done.14.refs_0_ = bf16[400,128]{1,0:T(8,128)(2,1)S(1)} collective-permute-done((bf16[400,128]{1,0:T(8,128)(2,1)S(1)}, bf16[400,128]{1,0:T(8,128)(2,1)S(1)}, u32[]{:S(2)}, u32[]{:S(2)}) %collective-permute-start.14) | collective-permute-done | bytes 102432 | tf_op jit(solution)/shard_map/ppermute | solution.py:17
  52.5 5.9 %collective-permute-done.15.refs_1_ = bf16[400,128]{1,0:T(8,128)(2,1)S(1)} collective-permute-done((bf16[400,128]{1,0:T(8,128)(2,1)S(1)}, bf16[400,128]{1,0:T(8,128)(2,1)S(1)}, u32[]{:S(2)}, u32[]{:S(2)}) %collective-permute-start.15) | collective-permute-done | bytes 102432 | tf_op jit(solution)/shard_map/ppermute | solution.py:17
  59.4 1.7 %collective-permute-start.19 = (bf16[64,768]{1,0:T(8,128)(2,1)S(1)}, bf16[64,768]{1,0:T(8,128)(2,1)S(1)}, u32[]{:S(2)}, u32[]{:S(2)}) collective-permute-start(bf16[64,768]{1,0:T(8,128)(2,1)S(1)} %finish.1.dep_ref.refs_0_), channel_id=1, source_target_pairs={{0,8},{8,0},{16,24},{24,16},{1,9},{9,1},{17,25},{25,17},{2,10},{10... | collective-permute-start | bytes 294920 | tf_op jit(solution)/shard_map/ppermute | solution.py:17
  61.1 1.4 %collective-permute-start.20 = (bf16[64,768]{1,0:T(8,128)(2,1)S(1)}, bf16[64,768]{1,0:T(8,128)(2,1)S(1)}, u32[]{:S(2)}, u32[]{:S(2)}) collective-permute-start(bf16[64,768]{1,0:T(8,128)(2,1)S(1)} %finish.1.dep_ref.refs_0_), channel_id=1, source_target_pairs={{0,16},{8,24},{16,0},{24,8},{1,17},{9,25},{17,1},{25,9},{2,18},{10... | collective-permute-start | bytes 294920 | tf_op jit(solution)/shard_map/ppermute | solution.py:17
  62.5 1.3 %collective-permute-start.21 = (bf16[64,768]{1,0:T(8,128)(2,1)S(1)}, bf16[64,768]{1,0:T(8,128)(2,1)S(1)}, u32[]{:S(2)}, u32[]{:S(2)}) collective-permute-start(bf16[64,768]{1,0:T(8,128)(2,1)S(1)} %finish.1.dep_ref.refs_0_), channel_id=1, source_target_pairs={{0,24},{8,16},{16,8},{24,0},{1,25},{9,17},{17,9},{25,1},{2,26},{10... | collective-permute-start | bytes 294920 | tf_op jit(solution)/shard_map/ppermute | solution.py:17
  64.1 1.5 %collective-permute-start.18 = (f32[2,64,64]{2,1,0:T(8,128)S(1)}, f32[2,64,64]{2,1,0:T(8,128)S(1)}, u32[]{:S(2)}, u32[]{:S(2)}) collective-permute-start(f32[2,64,64]{2,1,0:T(8,128)S(1)} %get-tuple-element.70.low_ref), channel_id=1, source_target_pairs={{0,4},{4,0},{1,5},{5,1},{2,6},{6,2},{3,7},{7,3},{8,12},{12,8},{9,1... | collective-permute-start | bytes 98312 | tf_op jit(solution)/shard_map/ppermute | solution.py:17
  65.6 2.8 %collective-permute-done.18.other_ref = f32[2,64,64]{2,1,0:T(8,128)S(1)} collective-permute-done((f32[2,64,64]{2,1,0:T(8,128)S(1)}, f32[2,64,64]{2,1,0:T(8,128)S(1)}, u32[]{:S(2)}, u32[]{:S(2)}) %collective-permute-start.18) | collective-permute-done | bytes 32800 | tf_op jit(solution)/shard_map/ppermute | solution.py:17
  68.7 3.2 %collective-permute-done.20.refs_2_ = bf16[64,768]{1,0:T(8,128)(2,1)S(1)} collective-permute-done((bf16[64,768]{1,0:T(8,128)(2,1)S(1)}, bf16[64,768]{1,0:T(8,128)(2,1)S(1)}, u32[]{:S(2)}, u32[]{:S(2)}) %collective-permute-start.20) | collective-permute-done | bytes 98336 | tf_op jit(solution)/shard_map/ppermute | solution.py:17
  72.7 1.6 %collective-permute-start.25 = (bf16[128,768]{1,0:T(8,128)(2,1)S(1)}, bf16[128,768]{1,0:T(8,128)(2,1)S(1)}, u32[]{:S(2)}, u32[]{:S(2)}) collective-permute-start(bf16[128,768]{1,0:T(8,128)(2,1)S(1)} %get-tuple-element.81), channel_id=1, source_target_pairs={{0,2},{1,3},{2,0},{3,1},{4,6},{5,7},{6,4},{7,5},{8,10},{9,11},{10,... | collective-permute-start | bytes 589832 | tf_op jit(solution)/shard_map/ppermute | solution.py:17
  75.5 1.6 %collective-permute-start.22 = (bf16[64,384]{1,0:T(8,128)(2,1)S(1)}, bf16[64,384]{1,0:T(8,128)(2,1)S(1)}, u32[]{:S(2)}, u32[]{:S(2)}) collective-permute-start(bf16[64,384]{1,0:T(8,128)(2,1)S(1)} %get-tuple-element.77), channel_id=1, source_target_pairs={{0,4},{4,0},{1,5},{5,1},{2,6},{6,2},{3,7},{7,3},{8,12},{12,8},{9,1... | collective-permute-start | bytes 147464 | tf_op jit(solution)/shard_map/ppermute | solution.py:17
  78.6 1.1 %collective-permute-done.22.refs_1_ = bf16[64,384]{1,0:T(8,128)(2,1)S(1)} collective-permute-done((bf16[64,384]{1,0:T(8,128)(2,1)S(1)}, bf16[64,384]{1,0:T(8,128)(2,1)S(1)}, u32[]{:S(2)}, u32[]{:S(2)}) %collective-permute-start.22) | collective-permute-done | bytes 49184 | tf_op jit(solution)/shard_map/ppermute | solution.py:17
  81.4 1.6 %collective-permute-start.26 = (bf16[64,384]{1,0:T(8,128)(2,1)S(1)}, bf16[64,384]{1,0:T(8,128)(2,1)S(1)}, u32[]{:S(2)}, u32[]{:S(2)}) collective-permute-start(bf16[64,384]{1,0:T(8,128)(2,1)S(1)} %get-tuple-element.83), channel_id=1, source_target_pairs={{0,4},{4,0},{1,5},{5,1},{2,6},{6,2},{3,7},{7,3},{8,12},{12,8},{9,1... | collective-permute-start | bytes 147464 | tf_op jit(solution)/shard_map/ppermute | solution.py:17
  84.7 1.6 %collective-permute-start.28 = (bf16[64,384]{1,0:T(8,128)(2,1)S(1)}, bf16[64,384]{1,0:T(8,128)(2,1)S(1)}, u32[]{:S(2)}, u32[]{:S(2)}) collective-permute-start(bf16[64,384]{1,0:T(8,128)(2,1)S(1)} %get-tuple-element.86), channel_id=1, source_target_pairs={{0,4},{4,0},{1,5},{5,1},{2,6},{6,2},{3,7},{7,3},{8,12},{12,8},{9,1... | collective-permute-start | bytes 147464 | tf_op jit(solution)/shard_map/ppermute | solution.py:17
  86.3 2.6 %collective-permute-done.28.refs_7_ = bf16[64,384]{1,0:T(8,128)(2,1)S(1)} collective-permute-done((bf16[64,384]{1,0:T(8,128)(2,1)S(1)}, bf16[64,384]{1,0:T(8,128)(2,1)S(1)}, u32[]{:S(2)}, u32[]{:S(2)}) %collective-permute-start.28) | collective-permute-done | bytes 49184 | tf_op jit(solution)/shard_map/ppermute | solution.py:17
  (79 shorter events, 15.2 us)
Async XLA Ops:
  0.0 74.6 %copy-start = (s32[2,128]{1,0:T(2,128)S(1)}, s32[2,128]{1,0:T(2,128)}, u32[]{:S(2)}) copy-start(s32[2,128]{1,0:T(2,128)} %param.16) | copy-start | bytes 3076
  4.7 2.6 %collective-permute-start.1 = (bf16[1552,128]{1,0:T(8,128)(2,1)S(1)}, bf16[1552,128]{1,0:T(8,128)(2,1)S(1)}, u32[]{:S(2)}, u32[]{:S(2)}) collective-permute-start(bf16[1552,128]{1,0:T(8,128)(2,1)S(1)} %get-tuple-element.47), channel_id=1, source_target_pairs={{0,1},{1,0},{2,3},{3,2},{4,5},{5,4},{6,7},{7,6},{8,9},{9,8},{10,11... | collective-permute-start | bytes 1191944 | tf_op jit(solution)/shard_map/ppermute | solution.py:17
  7.1 3.5 %collective-permute-start.3 = (bf16[192,768]{1,0:T(8,128)(2,1)S(1)}, bf16[192,768]{1,0:T(8,128)(2,1)S(1)}, u32[]{:S(2)}, u32[]{:S(2)}) collective-permute-start(bf16[192,768]{1,0:T(8,128)(2,1)S(1)} %get-tuple-element.53), channel_id=1, source_target_pairs={{0,1},{1,0},{2,3},{3,2},{4,5},{5,4},{6,7},{7,6},{8,9},{9,8},{10,11... | collective-permute-start | bytes 884744 | tf_op jit(solution)/shard_map/ppermute | solution.py:17
  7.4 8.2 %collective-permute-start.2 = (bf16[784,128]{1,0:T(8,128)(2,1)S(1)}, bf16[784,128]{1,0:T(8,128)(2,1)S(1)}, u32[]{:S(2)}, u32[]{:S(2)}) collective-permute-start(bf16[784,128]{1,0:T(8,128)(2,1)S(1)} %get-tuple-element.49), channel_id=1, source_target_pairs={{0,2},{1,3},{2,0},{3,1},{4,6},{5,7},{6,4},{7,5},{8,10},{9,11},{10,... | collective-permute-start | bytes 602120 | tf_op jit(solution)/shard_map/ppermute | solution.py:17
  15.7 30.3 %copy-start.6 = (bf16[1,3072,64]{1,2,0:T(8,128)(2,1)S(1)}, bf16[1,3072,64]{1,2,0:T(8,128)(2,1)}, u32[]{:S(2)}) copy-start(bf16[1,3072,64]{1,2,0:T(8,128)(2,1)} %param.25) | copy-start | bytes 1179652
  15.7 30.3 %copy-start.7 = (bf16[1,64,3072]{2,1,0:T(8,128)(2,1)S(1)}, bf16[1,64,3072]{2,1,0:T(8,128)(2,1)}, u32[]{:S(2)}) copy-start(bf16[1,64,3072]{2,1,0:T(8,128)(2,1)} %param.26) | copy-start | bytes 1179652
  15.7 21.4 %collective-permute-start.11 = (bf16[2,192,768]{2,1,0:T(8,128)(2,1)S(1)}, bf16[2,192,768]{2,1,0:T(8,128)(2,1)S(1)}, u32[]{:S(2)}, u32[]{:S(2)}) collective-permute-start(bf16[2,192,768]{2,1,0:T(8,128)(2,1)S(1)} %get-tuple-element.60.refs_0_), channel_id=1, source_target_pairs={{0,2},{1,3},{2,0},{3,1},{4,6},{5,7},{6,4},{7,5},{8,10},{9,11},{10,... | collective-permute-start | bytes 1769480 | tf_op jit(solution)/shard_map/ppermute | solution.py:17
  17.5 21.9 %collective-permute-start = (bf16[4,64,1536]{2,1,0:T(8,128)(2,1)S(1)}, bf16[4,64,1536]{2,1,0:T(8,128)(2,1)S(1)}, u32[]{:S(2)}, u32[]{:S(2)}) collective-permute-start(bf16[4,64,1536]{2,1,0:T(8,128)(2,1)S(1)} %image_pack.1.refs_1_), channel_id=1, source_target_pairs={{0,4},{4,0},{1,5},{5,1},{2,6},{6,2},{3,7},{7,3},{8,12},{12,8},{9,1... | collective-permute-start | bytes 2359304 | tf_op jit(solution)/shard_map/ppermute | solution.py:17
  19.0 5.7 %collective-permute-start.4 = (bf16[208,128]{1,0:T(8,128)(2,1)S(1)}, bf16[208,128]{1,0:T(8,128)(2,1)S(1)}, u32[]{:S(2)}, u32[]{:S(2)}) collective-permute-start(bf16[208,128]{1,0:T(8,128)(2,1)S(1)} %get-tuple-element.56), channel_id=1, source_target_pairs={{0,8},{8,0},{16,24},{24,16},{1,9},{9,1},{17,25},{25,17},{2,10},{10... | collective-permute-start | bytes 159752 | tf_op jit(solution)/shard_map/ppermute | solution.py:17
  20.6 6.2 %collective-permute-start.5 = (bf16[208,128]{1,0:T(8,128)(2,1)S(1)}, bf16[208,128]{1,0:T(8,128)(2,1)S(1)}, u32[]{:S(2)}, u32[]{:S(2)}) collective-permute-start(bf16[208,128]{1,0:T(8,128)(2,1)S(1)} %get-tuple-element.57), channel_id=1, source_target_pairs={{0,16},{8,24},{16,0},{24,8},{1,17},{9,25},{17,1},{25,9},{2,18},{10... | collective-permute-start | bytes 159752 | tf_op jit(solution)/shard_map/ppermute | solution.py:17
  23.1 5.9 %collective-permute-start.6 = (bf16[208,128]{1,0:T(8,128)(2,1)S(1)}, bf16[208,128]{1,0:T(8,128)(2,1)S(1)}, u32[]{:S(2)}, u32[]{:S(2)}) collective-permute-start(bf16[208,128]{1,0:T(8,128)(2,1)S(1)} %get-tuple-element.58), channel_id=1, source_target_pairs={{0,24},{8,16},{16,8},{24,0},{1,25},{9,17},{17,9},{25,1},{2,26},{10... | collective-permute-start | bytes 159752 | tf_op jit(solution)/shard_map/ppermute | solution.py:17
  29.3 7.7 %collective-permute-start.7 = (bf16[208,128]{1,0:T(8,128)(2,1)S(1)}, bf16[208,128]{1,0:T(8,128)(2,1)S(1)}, u32[]{:S(2)}, u32[]{:S(2)}) collective-permute-start(bf16[208,128]{1,0:T(8,128)(2,1)S(1)} %centre.1.own_ref), channel_id=1, source_target_pairs={{0,4},{4,0},{1,5},{5,1},{2,6},{6,2},{3,7},{7,3},{8,12},{12,8},{9,1... | collective-permute-start | bytes 159752 | tf_op jit(solution)/shard_map/ppermute | solution.py:17
  37.1 7.7 %collective-permute-start.12 = (bf16[192,768]{1,0:T(8,128)(2,1)S(1)}, bf16[192,768]{1,0:T(8,128)(2,1)S(1)}, u32[]{:S(2)}, u32[]{:S(2)}) collective-permute-start(bf16[192,768]{1,0:T(8,128)(2,1)S(1)} %get-tuple-element.62), channel_id=1, source_target_pairs={{0,1},{1,0},{2,3},{3,2},{4,5},{5,4},{6,7},{7,6},{8,9},{9,8},{10,11... | collective-permute-start | bytes 884744 | tf_op jit(solution)/shard_map/ppermute | solution.py:17
  37.2 4.8 %collective-permute-start.10 = (bf16[416,128]{1,0:T(8,128)(2,1)S(1)}, bf16[416,128]{1,0:T(8,128)(2,1)S(1)}, u32[]{:S(2)}, u32[]{:S(2)}) collective-permute-start(bf16[416,128]{1,0:T(8,128)(2,1)S(1)} %join.1.dep_ref.refs_0_), channel_id=1, source_target_pairs={{0,3},{1,2},{2,1},{3,0},{4,7},{5,6},{6,5},{7,4},{8,11},{9,10},{10,... | collective-permute-start | bytes 319496 | tf_op jit(solution)/shard_map/ppermute | solution.py:17
  37.9 4.0 %collective-permute-start.8 = (bf16[416,128]{1,0:T(8,128)(2,1)S(1)}, bf16[416,128]{1,0:T(8,128)(2,1)S(1)}, u32[]{:S(2)}, u32[]{:S(2)}) collective-permute-start(bf16[416,128]{1,0:T(8,128)(2,1)S(1)} %join.1.dep_ref.refs_0_), channel_id=1, source_target_pairs={{0,1},{1,0},{2,3},{3,2},{4,5},{5,4},{6,7},{7,6},{8,9},{9,8},{10,11... | collective-permute-start | bytes 319496 | tf_op jit(solution)/shard_map/ppermute | solution.py:17
  38.0 6.8 %collective-permute-start.9 = (bf16[416,128]{1,0:T(8,128)(2,1)S(1)}, bf16[416,128]{1,0:T(8,128)(2,1)S(1)}, u32[]{:S(2)}, u32[]{:S(2)}) collective-permute-start(bf16[416,128]{1,0:T(8,128)(2,1)S(1)} %join.1.dep_ref.refs_0_), channel_id=1, source_target_pairs={{0,2},{1,3},{2,0},{3,1},{4,6},{5,7},{6,4},{7,5},{8,10},{9,11},{10,... | collective-permute-start | bytes 319496 | tf_op jit(solution)/shard_map/ppermute | solution.py:17
  46.1 12.3 %collective-permute-start.13 = (bf16[128,1536]{1,0:T(8,128)(2,1)S(1)}, bf16[128,1536]{1,0:T(8,128)(2,1)S(1)}, u32[]{:S(2)}, u32[]{:S(2)}) collective-permute-start(bf16[128,1536]{1,0:T(8,128)(2,1)S(1)} %maps_pack.1.own_ref), channel_id=1, source_target_pairs={{0,2},{1,3},{2,0},{3,1},{4,6},{5,7},{6,4},{7,5},{8,10},{9,11},{10,... | collective-permute-start | bytes 1179656 | tf_op jit(solution)/shard_map/ppermute | solution.py:17
  46.8 5.7 %collective-permute-start.14 = (bf16[400,128]{1,0:T(8,128)(2,1)S(1)}, bf16[400,128]{1,0:T(8,128)(2,1)S(1)}, u32[]{:S(2)}, u32[]{:S(2)}) collective-permute-start(bf16[400,128]{1,0:T(8,128)(2,1)S(1)} %get-tuple-element.65), channel_id=1, source_target_pairs={{0,8},{8,0},{16,24},{24,16},{1,9},{9,1},{17,25},{25,17},{2,10},{10... | collective-permute-start | bytes 307208 | tf_op jit(solution)/shard_map/ppermute | solution.py:17
  48.3 10.2 %collective-permute-start.15 = (bf16[400,128]{1,0:T(8,128)(2,1)S(1)}, bf16[400,128]{1,0:T(8,128)(2,1)S(1)}, u32[]{:S(2)}, u32[]{:S(2)}) collective-permute-start(bf16[400,128]{1,0:T(8,128)(2,1)S(1)} %get-tuple-element.66), channel_id=1, source_target_pairs={{0,16},{8,24},{16,0},{24,8},{1,17},{9,25},{17,1},{25,9},{2,18},{10... | collective-permute-start | bytes 307208 | tf_op jit(solution)/shard_map/ppermute | solution.py:17
  50.9 7.6 %collective-permute-start.16 = (bf16[400,128]{1,0:T(8,128)(2,1)S(1)}, bf16[400,128]{1,0:T(8,128)(2,1)S(1)}, u32[]{:S(2)}, u32[]{:S(2)}) collective-permute-start(bf16[400,128]{1,0:T(8,128)(2,1)S(1)} %get-tuple-element.67), channel_id=1, source_target_pairs={{0,24},{8,16},{16,8},{24,0},{1,25},{9,17},{17,9},{25,1},{2,26},{10... | collective-permute-start | bytes 307208 | tf_op jit(solution)/shard_map/ppermute | solution.py:17
  59.3 4.5 %collective-permute-start.17 = (bf16[128,1536]{1,0:T(8,128)(2,1)S(1)}, bf16[128,1536]{1,0:T(8,128)(2,1)S(1)}, u32[]{:S(2)}, u32[]{:S(2)}) collective-permute-start(bf16[128,1536]{1,0:T(8,128)(2,1)S(1)} %get-tuple-element.69), channel_id=1, source_target_pairs={{0,1},{1,0},{2,3},{3,2},{4,5},{5,4},{6,7},{7,6},{8,9},{9,8},{10,11... | collective-permute-start | bytes 1179656 | tf_op jit(solution)/shard_map/ppermute | solution.py:17
  59.4 9.3 %collective-permute-start.19 = (bf16[64,768]{1,0:T(8,128)(2,1)S(1)}, bf16[64,768]{1,0:T(8,128)(2,1)S(1)}, u32[]{:S(2)}, u32[]{:S(2)}) collective-permute-start(bf16[64,768]{1,0:T(8,128)(2,1)S(1)} %finish.1.dep_ref.refs_0_), channel_id=1, source_target_pairs={{0,8},{8,0},{16,24},{24,16},{1,9},{9,1},{17,25},{25,17},{2,10},{10... | collective-permute-start | bytes 294920 | tf_op jit(solution)/shard_map/ppermute | solution.py:17
  61.1 10.8 %collective-permute-start.20 = (bf16[64,768]{1,0:T(8,128)(2,1)S(1)}, bf16[64,768]{1,0:T(8,128)(2,1)S(1)}, u32[]{:S(2)}, u32[]{:S(2)}) collective-permute-start(bf16[64,768]{1,0:T(8,128)(2,1)S(1)} %finish.1.dep_ref.refs_0_), channel_id=1, source_target_pairs={{0,16},{8,24},{16,0},{24,8},{1,17},{9,25},{17,1},{25,9},{2,18},{10... | collective-permute-start | bytes 294920 | tf_op jit(solution)/shard_map/ppermute | solution.py:17
  62.5 9.4 %collective-permute-start.21 = (bf16[64,768]{1,0:T(8,128)(2,1)S(1)}, bf16[64,768]{1,0:T(8,128)(2,1)S(1)}, u32[]{:S(2)}, u32[]{:S(2)}) collective-permute-start(bf16[64,768]{1,0:T(8,128)(2,1)S(1)} %finish.1.dep_ref.refs_0_), channel_id=1, source_target_pairs={{0,24},{8,16},{16,8},{24,0},{1,25},{9,17},{17,9},{25,1},{2,26},{10... | collective-permute-start | bytes 294920 | tf_op jit(solution)/shard_map/ppermute | solution.py:17
  64.1 4.3 %collective-permute-start.18 = (f32[2,64,64]{2,1,0:T(8,128)S(1)}, f32[2,64,64]{2,1,0:T(8,128)S(1)}, u32[]{:S(2)}, u32[]{:S(2)}) collective-permute-start(f32[2,64,64]{2,1,0:T(8,128)S(1)} %get-tuple-element.70.low_ref), channel_id=1, source_target_pairs={{0,4},{4,0},{1,5},{5,1},{2,6},{6,2},{3,7},{7,3},{8,12},{12,8},{9,1... | collective-permute-start | bytes 98312 | tf_op jit(solution)/shard_map/ppermute | solution.py:17
  72.6 4.4 %collective-permute-start.23 = (bf16[128,768]{1,0:T(8,128)(2,1)S(1)}, bf16[128,768]{1,0:T(8,128)(2,1)S(1)}, u32[]{:S(2)}, u32[]{:S(2)}) collective-permute-start(bf16[128,768]{1,0:T(8,128)(2,1)S(1)} %get-tuple-element.78), channel_id=1, source_target_pairs={{0,1},{1,0},{2,3},{3,2},{4,5},{5,4},{6,7},{7,6},{8,9},{9,8},{10,11... | collective-permute-start | bytes 589832 | tf_op jit(solution)/shard_map/ppermute | solution.py:17
  72.7 7.8 %collective-permute-start.25 = (bf16[128,768]{1,0:T(8,128)(2,1)S(1)}, bf16[128,768]{1,0:T(8,128)(2,1)S(1)}, u32[]{:S(2)}, u32[]{:S(2)}) collective-permute-start(bf16[128,768]{1,0:T(8,128)(2,1)S(1)} %get-tuple-element.81), channel_id=1, source_target_pairs={{0,2},{1,3},{2,0},{3,1},{4,6},{5,7},{6,4},{7,5},{8,10},{9,11},{10,... | collective-permute-start | bytes 589832 | tf_op jit(solution)/shard_map/ppermute | solution.py:17
  74.3 9.5 %collective-permute-start.27 = (bf16[128,768]{1,0:T(8,128)(2,1)S(1)}, bf16[128,768]{1,0:T(8,128)(2,1)S(1)}, u32[]{:S(2)}, u32[]{:S(2)}) collective-permute-start(bf16[128,768]{1,0:T(8,128)(2,1)S(1)} %get-tuple-element.84), channel_id=1, source_target_pairs={{0,3},{1,2},{2,1},{3,0},{4,7},{5,6},{6,5},{7,4},{8,11},{9,10},{10,... | collective-permute-start | bytes 589832 | tf_op jit(solution)/shard_map/ppermute | solution.py:17
  75.5 4.2 %collective-permute-start.22 = (bf16[64,384]{1,0:T(8,128)(2,1)S(1)}, bf16[64,384]{1,0:T(8,128)(2,1)S(1)}, u32[]{:S(2)}, u32[]{:S(2)}) collective-permute-start(bf16[64,384]{1,0:T(8,128)(2,1)S(1)} %get-tuple-element.77), channel_id=1, source_target_pairs={{0,4},{4,0},{1,5},{5,1},{2,6},{6,2},{3,7},{7,3},{8,12},{12,8},{9,1... | collective-permute-start | bytes 147464 | tf_op jit(solution)/shard_map/ppermute | solution.py:17
  78.0 5.8 %collective-permute-start.24 = (bf16[64,384]{1,0:T(8,128)(2,1)S(1)}, bf16[64,384]{1,0:T(8,128)(2,1)S(1)}, u32[]{:S(2)}, u32[]{:S(2)}) collective-permute-start(bf16[64,384]{1,0:T(8,128)(2,1)S(1)} %get-tuple-element.80), channel_id=1, source_target_pairs={{0,4},{4,0},{1,5},{5,1},{2,6},{6,2},{3,7},{7,3},{8,12},{12,8},{9,1... | collective-permute-start | bytes 147464 | tf_op jit(solution)/shard_map/ppermute | solution.py:17
  81.4 4.9 %collective-permute-start.26 = (bf16[64,384]{1,0:T(8,128)(2,1)S(1)}, bf16[64,384]{1,0:T(8,128)(2,1)S(1)}, u32[]{:S(2)}, u32[]{:S(2)}) collective-permute-start(bf16[64,384]{1,0:T(8,128)(2,1)S(1)} %get-tuple-element.83), channel_id=1, source_target_pairs={{0,4},{4,0},{1,5},{5,1},{2,6},{6,2},{3,7},{7,3},{8,12},{12,8},{9,1... | collective-permute-start | bytes 147464 | tf_op jit(solution)/shard_map/ppermute | solution.py:17
  84.7 4.2 %collective-permute-start.28 = (bf16[64,384]{1,0:T(8,128)(2,1)S(1)}, bf16[64,384]{1,0:T(8,128)(2,1)S(1)}, u32[]{:S(2)}, u32[]{:S(2)}) collective-permute-start(bf16[64,384]{1,0:T(8,128)(2,1)S(1)} %get-tuple-element.86), channel_id=1, source_target_pairs={{0,4},{4,0},{1,5},{5,1},{2,6},{6,2},{3,7},{7,3},{8,12},{12,8},{9,1... | collective-permute-start | bytes 147464 | tf_op jit(solution)/shard_map/ppermute | solution.py:17
  (11 other events, 97.7 us)

commit v5 on v4

--- a/solution.py
+++ b/solution.py
@@ -269,14 +269,14 @@
 TN = (((0,), (0,)), ((), ()))
 
 
-def call(kernel, outs, ins, specs=None, scratch=(), name=None, out_specs=None):
+def call(kernel, outs, ins, specs=None, scratch=(), name=None, out_specs=None, vmem=16):
     return pl.pallas_call(
         kernel,
         out_shape=outs,
         in_specs=specs if specs is not None else [VMEM] * len(ins),
         out_specs=out_specs if out_specs is not None else jax.tree.map(lambda _: VMEM, outs),
         scratch_shapes=list(scratch),
-        compiler_params=pltpu.CompilerParams(vmem_limit_bytes=16 * 1024 * 1024),
+        compiler_params=pltpu.CompilerParams(vmem_limit_bytes=int(vmem * 1024 * 1024)),
         name=name,
     )(*ins)
 
@@ -353,27 +353,33 @@
 
 
 def scatter_kernel(features, deps, got_ref, keep_ref, stat_ref, *refs):
-    kept_ref, out_stat_ref, *send_refs = refs[deps:]
+    kept_ref, out_stat_ref, send_ref = refs[deps:]
     e = lax.axis_index("enc")
     count = keep_ref.shape[0] // features
     stat = stat_ref[0:1] + stat_of(got_ref[count * features :])
+    for i in range(count):
+        rows = slice(i * features, (i + 1) * features)
+        total = keep_ref[rows] + got_ref[rows].astype(F32)
+        send_ref[i, :features] = total.astype(BF16)
+        send_ref[i, features:] = stat_rows(stat)
     own = at(e, features)
-    for k, send_ref in enumerate(send_refs):
-        other = at(e ^ (k + 1), features)
-        send_ref[:features] = (keep_ref[other] + got_ref[other].astype(F32)).astype(BF16)
-        send_ref[features:] = stat_rows(stat)
     kept_ref[...] = keep_ref[own] + got_ref[own].astype(F32)
     out_stat_ref[...] = jnp.broadcast_to(stat, out_stat_ref.shape)
 
 
+def add_others(total, got_ref):
+    e = lax.axis_index("enc")
+    for i in range(got_ref.shape[0]):
+        total = total + jnp.where(e == i, 0.0, got_ref[i].astype(F32))
+    return total
+
+
 def centre_kernel(width, prompt_ref, adapter_ref, keep_ref, stat_ref, bias_ref, scale_ref, shift_ref, *refs):
-    got_refs, out_ref = refs[:-1], refs[-1]
+    got_ref, out_ref = refs
     features, tokens = keep_ref.shape
-    total = keep_ref[...] + bias_ref[...]
-    stat = stat_ref[0:1]
-    for got_ref in got_refs:
-        total = total + got_ref[:features].astype(F32)
-        stat = stat + stat_of(got_ref[features:])
+    others = add_others(0.0, got_ref)
+    total = keep_ref[...] + bias_ref[...] + others[:features]
+    stat = stat_ref[0:1] + stat_of(others[features:])
     centred = total - stat * (1.0 / width)
     out_ref[:features] = (scale_ref[...] * centred).astype(BF16)
     squares = jnp.sum(centred * centred, axis=0, keepdims=True)
@@ -402,12 +408,11 @@
     out_ref[size:] = got_ref[...]
 
 
-def project_kernel(n_seq, n_req, n_enc, dep_ref, *refs):
+def project_kernel(n_seq, n_req, n_enc, *refs):
     payload_refs = refs[:n_req]
     weight_refs = refs[n_req : 2 * n_req]
     prompts_ref, keep_ref = refs[2 * n_req : 2 * n_req + 2]
-    send_refs = refs[2 * n_req + 2 : -1]
-    rows_ref = refs[-1]
+    send_ref, rows_ref = refs[-2:]
     features, width = weight_refs[0].shape
     tokens = payload_refs[0].shape[1]
     stride = features + ROWS
@@ -457,20 +462,18 @@
         rows_ref[z * step + heads * size : (z + 1) * step] = extra
     e = lax.axis_index("enc")
     keep_ref[...] = rows_ref[at(e, step)]
-    for k, send_ref in enumerate(send_refs):
-        send_ref[...] = rows_ref[at(e ^ (k + 1), step)].astype(BF16)
+    for z in range(n_enc):
+        send_ref[z] = rows_ref[z * step : (z + 1) * step].astype(BF16)
 
 
 def finish_kernel(n_req, model_width, dep_ref, keep_ref, bias_ref, *refs):
-    got_refs, out_ref = refs[:-1], refs[-1]
+    got_ref, out_ref = refs
     r, s = lax.axis_index("req"), lax.axis_index("seq")
     size, width = out_ref.shape
     heads = width // HDIM
     half = width // 2
     inner = bias_ref.shape[1] // 2
-    total = keep_ref[...]
-    for got_ref in got_refs:
-        total = total + got_ref[...].astype(F32)
+    total = add_others(keep_ref[...], got_ref)
     extra = total[heads * size :]
     squares = extra[2 * heads : 2 * heads + 1] + extra[2 * heads + 1 : 2 * heads + 2]
     squares = jnp.broadcast_to(squares, (HDIM, HDIM)).T[:size]
@@ -485,19 +488,14 @@
         out_ref[:, h * HDIM : (h + 1) * HDIM] = head.astype(BF16)
 
 
-def choose_kernel(n_seq, n_enc, chosen_ref, dep_ref, *refs):
-    part_refs, out_refs = refs[:n_enc], refs[n_enc:]
-    e, r, s = lax.axis_index("enc"), lax.axis_index("req"), lax.axis_index("seq")
-    halves = n_enc // n_seq
-    size = part_refs[0].shape[0]
+def choose_kernel(n_seq, chosen_ref, dep_ref, part_ref, *out_refs):
+    s = lax.axis_index("seq")
+    halves = part_ref.shape[0] // n_seq
+    size = part_ref.shape[1]
     for k, out_ref in enumerate(out_refs):
         prompt = s ^ chosen_ref[k]
         for h in range(halves):
-            place = e ^ (prompt * halves + h)
-            for j in range(n_enc):
-                @pl.when(place == j)
-                def _():
-                    out_ref[h * size : (h + 1) * size] = part_refs[j][...]
+            out_ref[h * size : (h + 1) * size] = part_ref[prompt * halves + h]
 
 
 def weight_kernel(n_req, part, inner, w_ref, dep_ref, own_ref, core_ref, pair_ref, sems):
@@ -688,31 +686,9 @@
             dma((2 + n_enc,)),
         ],
         name="context",
+        vmem=52.25,
     )
     got = swap(send, "req", n_req, 1)
-
-    packed = [
-        call(
-            functools.partial(image_kernel, part, inner, k),
-            struct((4, image_rows, part)),
-            (qk, base, stream, keep),
-            [ANY] * 4,
-            [dma((4,))],
-            name="image_pack",
-        )
-        for k in range(1, n_seq)
-    ]
-    image_got = [swap(packed[k - 1], "seq", n_seq, k) for k in range(1, n_seq)]
-    weight = struct((features, 2 * half))
-    weight_own, weight_core, weight_pair = call(
-        functools.partial(weight_kernel, n_req, part, inner),
-        (weight, weight, struct((2, features, 2 * half))),
-        (key_value_weight, keep),
-        [ANY] * 2,
-        [dma((2 * n_req,))],
-        name="weight_pack",
-    )
-    weight_core_got = swap(weight_core, "req", n_req, 1)
 
     send, keep, sums = call(
         functools.partial(halve_kernel, features),
@@ -725,15 +701,28 @@
         name="halve",
     )
     got = swap(send, "req", n_req, 2)
-    keep, sums, *sends = call(
-        functools.partial(scatter_kernel, features, 3),
-        (struct((features, tokens), F32), stat)
-        + tuple(struct((features + ROWS, tokens)) for _ in range(1, n_enc)),
-        (got, keep, sums, weight_pair, packed[0], weight_core_got),
-        [VMEM] * 3 + [ANY] * 3,
+    weight = struct((features, 2 * half))
+    weight_own, weight_core, weight_pair = call(
+        functools.partial(weight_kernel, n_req, part, inner),
+        (weight, weight, struct((2, features, 2 * half))),
+        (key_value_weight, keep),
+        [ANY] * 2,
+        [dma((2 * n_req,))],
+        name="weight_pack",
+    )
+    weight_core_got = swap(weight_core, "req", n_req, 1)
+    keep, sums, send = call(
+        functools.partial(scatter_kernel, features, 2),
+        (
+            struct((features, tokens), F32),
+            stat,
+            struct((n_enc, features + ROWS, tokens)),
+        ),
+        (got, keep, sums, weight_pair, weight_core_got),
+        [VMEM] * 3 + [ANY] * 2,
         name="scatter",
     )
-    arrived = [swap(sends[k - 1], "enc", n_enc, k) for k in range(1, n_enc)]
+    arrived = lax.all_to_all(send, "enc", 0, 0, tiled=True)
     weight_pair = lax.optimization_barrier((weight_pair, keep))[0]
     weight_pair_got = swap(weight_pair, "req", n_req, 2)
 
@@ -752,9 +741,9 @@
             bias_columns,
             scale_columns,
             modulation_shift,
-            *arrived,
+            arrived,
         ),
-        [SMEM] * 2 + [VMEM] * (5 + len(arrived)),
+        [SMEM] * 2 + [VMEM] * 6,
         name="centre",
     )
     joined = call(
@@ -764,6 +753,18 @@
         name="join",
     )
     payloads = [joined] + [swap(joined, "req", n_req, k) for k in range(1, n_req)]
+    packed = [
+        call(
+            functools.partial(image_kernel, part, inner, k),
+            struct((4, image_rows, part)),
+            (qk, base, stream, joined),
+            [ANY] * 4,
+            [dma((4,))],
+            name="image_pack",
+        )
+        for k in range(1, n_seq)
+    ]
+    image_got = [swap(packed[k - 1], "seq", n_seq, k) for k in range(1, n_seq)]
     weight_own_pair, weight_next = call(
         pass_on_kernel,
         (weight, weight),
@@ -775,17 +776,19 @@
 
     size = n_seq * tokens // n_enc
     step = 2 * half // HDIM * size + ROWS
-    ids, keep, *sends = call(
+    ids, keep, send = call(
         functools.partial(project_kernel, n_seq, n_req, n_enc),
-        (struct((2 * n_req,), jnp.int32), struct((step, HDIM), F32))
-        + tuple(struct((step, HDIM)) for _ in range(1, n_enc)),
-        (image_got[0], *payloads, *weights),
-        [ANY] + [VMEM] * (2 * n_req),
+        (
+            struct((2 * n_req,), jnp.int32),
+            struct((step, HDIM), F32),
+            struct((n_enc, step, HDIM)),
+        ),
+        (*payloads, *weights),
         scratch=[pltpu.VMEM((n_enc * step, HDIM), F32)],
-        out_specs=(SMEM,) + (VMEM,) * n_enc,
+        out_specs=(SMEM, VMEM, VMEM),
         name="project",
     )
-    arrived = [swap(sends[k - 1], "enc", n_enc, k) for k in range(1, n_enc)]
+    arrived = lax.all_to_all(send, "enc", 0, 0, tiled=True)
 
     maps = call(
         functools.partial(maps_kernel, part),
@@ -800,8 +803,8 @@
     text = call(
         functools.partial(finish_kernel, n_req, model_width),
         struct((size, 2 * half)),
-        (maps_pair, keep, key_value_bias[None], *arrived),
-        [ANY] + [VMEM] * (2 + len(arrived)),
+        (maps_pair, keep, key_value_bias[None], arrived),
+        [ANY] + [VMEM] * 3,
         name="finish",
     )
     maps_mine, maps_core = call(
@@ -825,12 +828,12 @@
         (low, swap(low, "seq", n_seq, 1), chosen_maps, qk, base, *image_got),
         name="arrange",
     )
-    parts = [text] + [swap(text, "enc", n_enc, k) for k in range(1, n_enc)]
+    parts = lax.all_gather(text, "enc", axis=0, tiled=False)
     rows = call(
-        functools.partial(choose_kernel, n_seq, n_enc),
+        functools.partial(choose_kernel, n_seq),
         tuple(struct((tokens, 2 * half)) for _ in range(n_req)),
-        (ids, image_values, *parts),
-        [SMEM, ANY] + [VMEM] * n_enc,
+        (ids, image_values, parts),
+        [SMEM, ANY, VMEM],
         name="choose",
     )
     rows = [rows[0]] + [swap(rows[k], "req", n_req, k) for k in range(1, n_req)]

time: 89.9 us -> 105 us (1.17)
  blocking collectives: 0 us -> 14.7 us
  starting transfers between devices: 32.5 us -> 26.7 us
  waiting for transfers between devices: 40.4 us -> 44.1 us
  Pallas kernels: 10.3 us -> 13.7 us
    all_gather x0 -> x1, blocking collectives: none -> 14.7 us  [per_device_heads(): parts = lax.all_gather(text, 'enc', axis=0, tiled=False)]
    ppermute x29 -> x20, starting transfers between devices: 32.5 us -> 18.4 us  [swap(): return lax.ppermute(block, axis, [(i, i ^ step) for i in range(size)])]
    all_to_all x0 -> x2, starting transfers between devices: none -> 8.34 us  [per_device_heads(): arrived = lax.all_to_all(send, 'enc', 0, 0, tiled=True)]
    all_to_all x0 -> x2, waiting for transfers between devices: none -> 7.42 us  [per_device_heads(): arrived = lax.all_to_all(send, 'enc', 0, 0, tiled=True)]
    ppermute x29 -> x20, waiting for transfers between devices: 40.4 us -> 36.6 us  [swap(): return lax.ppermute(block, axis, [(i, i ^ step) for i in range(size)])]
    pallas_call x16, Pallas kernels: 6.61 us -> 10 us  [call(): pl.pallas_call(kernel, out_shape=outs, in_specs=specs if specs is not Non...]
    unnamed x28 -> x34, local copies, waits for them, and re-layouts: 4.63 us -> 3.67 us
  transfers between devices with their start and end apart: 29 -> 22, of which waited for: 14 -> 14; matrix products, arithmetic and copies ran while one was open for 0% -> 0% of each run, Pallas kernels for 5% -> 6%
where the time goes in v5:
time: 105 us
  waiting for transfers between devices  44.1 us (42%)
  starting transfers between devices  26.7 us (25%)
  blocking collectives  14.7 us (14%)
  Pallas kernels  13.7 us (13%)
  local copies, waits for them, and re-layouts  3.85 us (4%)
  between operations  1.64 us (2%)
    ppermute x20, waiting for transfers between devices, swap(): return lax.ppermute(block, axis, [(i, i ^ step) for i in range(size)])  36.6 us
    ppermute x20, starting transfers between devices, swap(): return lax.ppermute(block, axis, [(i, i ^ step) for i in range(size)])  18.4 us
    all_gather x1, blocking collectives, per_device_heads(): parts = lax.all_gather(text, 'enc', axis=0, tiled=False)  14.7 us
    pallas_call x16, Pallas kernels, call(): pl.pallas_call(kernel, out_shape=outs, in_specs=specs if specs is not Non...  10 us
    all_to_all x2, starting transfers between devices, per_device_heads(): arrived = lax.all_to_all(send, 'enc', 0, 0, tiled=True)  8.34 us
    all_to_all x2, waiting for transfers between devices, per_device_heads(): arrived = lax.all_to_all(send, 'enc', 0, 0, tiled=True)  7.42 us
    unnamed x34, local copies, waits for them, and re-layouts  3.67 us
    pallas_call x4, Pallas kernels, per_device_heads(): pl.pallas_call(functools.partial(heads_kernel, HDIM ** (-0.5)), grid=(1,)...  3.66 us
  transfers between devices with their start and end apart: 22, of which 14 were waited for; matrix products, arithmetic and copies ran while one was open for 0% of the time, Pallas kernels for 6%

profile of v5, /device:TPU:0, one launch (start us, length us, event | category | flops | bytes accessed | tf_op | source)
XLA Modules:
  0.0 104.7 jit_solution(10162184044999576515)
XLA Ops:
  0.0 1.0 copy-done.11
  1.7 2.6 %context.1 = (bf16[1552,128]{1,0:T(8,128)(2,1)S(1)}, f32[1536,128]{1,0:T(8,128)S(1)}, f32[8,128]{1,0:T(8,128)S(1)}) custom-call(bf16[128,256]{1,0:T(8,128)(2,1)S(1)} %bitcast.24, bf16[256,3072]{1,0:T(8,128)(2,1)} %w_hbm.1, bf16[192]{0:T(256)(128)(2,1)S(1)} %copy-done.12), custom_call_target="tpu_custom_call" | custom-call | tf_op jit(solution)/shard_map/context/pallas_call | solution.py:273
  4.7 1.4 %collective-permute-done.got_ref = bf16[1552,128]{1,0:T(8,128)(2,1)S(1)} collective-permute-done((bf16[1552,128]{1,0:T(8,128)(2,1)S(1)}, bf16[1552,128]{1,0:T(8,128)(2,1)S(1)}, u32[]{:S(2)}, u32[]{:S(2)}) %collective-permute-start) | collective-permute-done | bytes 397344 | tf_op jit(solution)/shard_map/ppermute | solution.py:17
  6.3 1.1 %weight_pack.1 = (bf16[192,768]{1,0:T(8,128)(2,1)S(1)}, bf16[192,768]{1,0:T(8,128)(2,1)S(1)}, bf16[2,192,768]{2,1,0:T(8,128)(2,1)}) custom-call(bf16[192,6144]{1,0:T(8,128)(2,1)S(1)} %copy-done.2, f32[768,128]{1,0:T(8,128)S(1)} %get-tuple-element.46.dep_ref.keep_ref), custom_call_target="tpu_custom_call" | custom-call | tf_op jit(solution)/shard_map/weight_pack/pallas_call | solution.py:273
  7.8 2.7 %collective-permute-start.1 = (bf16[784,128]{1,0:T(8,128)(2,1)S(1)}, bf16[784,128]{1,0:T(8,128)(2,1)S(1)}, u32[]{:S(2)}, u32[]{:S(2)}) collective-permute-start(bf16[784,128]{1,0:T(8,128)(2,1)S(1)} %get-tuple-element.45), channel_id=1, source_target_pairs={{0,2},{1,3},{2,0},{3,1},{4,6},{5,7},{6,4},{7,5},{8,10},{9,11},{10,... | collective-permute-start | bytes 602120 | tf_op jit(solution)/shard_map/ppermute | solution.py:17
  10.5 5.5 %collective-permute-done.1.got_ref = bf16[784,128]{1,0:T(8,128)(2,1)S(1)} collective-permute-done((bf16[784,128]{1,0:T(8,128)(2,1)S(1)}, bf16[784,128]{1,0:T(8,128)(2,1)S(1)}, u32[]{:S(2)}, u32[]{:S(2)}) %collective-permute-start.1) | collective-permute-done | bytes 200736 | tf_op jit(solution)/shard_map/ppermute | solution.py:17
  16.7 1.7 %collective-permute-start.7 = (bf16[2,192,768]{2,1,0:T(8,128)(2,1)}, bf16[2,192,768]{2,1,0:T(8,128)(2,1)S(1)}, u32[]{:S(2)}, u32[]{:S(2)}) collective-permute-start(bf16[2,192,768]{2,1,0:T(8,128)(2,1)} %get-tuple-element.54.refs_0_), channel_id=1, source_target_pairs={{0,2},{1,3},{2,0},{3,1},{4,6},{5,7},{6,4},{7,5},{8,10},{9,11},{10,... | collective-permute-start | bytes 1769480 | tf_op jit(solution)/shard_map/ppermute | solution.py:17
  18.5 4.9 %all-to-all-start = ((bf16[4,208,128]{2,1,0:T(8,128)(2,1)}), bf16[4,208,128]{2,1,0:T(8,128)(2,1)S(1)}, u32[]{:S(2)}, u32[]{:S(2)}) async-start(bf16[4,208,128]{2,1,0:T(8,128)(2,1)} %get-tuple-element.52), calls=%async_computation | async-start | bytes 425984 | tf_op jit(solution)/shard_map/all_to_all | solution.py:725
  24.6 6.2 %all-to-all-done.refs_0_ = bf16[4,208,128]{2,1,0:T(8,128)(2,1)S(1)} async-done(((bf16[4,208,128]{2,1,0:T(8,128)(2,1)}), bf16[4,208,128]{2,1,0:T(8,128)(2,1)S(1)}, u32[]{:S(2)}, u32[]{:S(2)}) %all-to-all-start) | async-done | bytes 213024 | tf_op jit(solution)/shard_map/all_to_all | solution.py:725
  31.2 1.6 %collective-permute-start.3 = (bf16[208,128]{1,0:T(8,128)(2,1)S(1)}, bf16[208,128]{1,0:T(8,128)(2,1)S(1)}, u32[]{:S(2)}, u32[]{:S(2)}) collective-permute-start(bf16[208,128]{1,0:T(8,128)(2,1)S(1)} %centre.1.own_ref), channel_id=1, source_target_pairs={{0,4},{4,0},{1,5},{5,1},{2,6},{6,2},{3,7},{7,3},{8,12},{12,8},{9,1... | collective-permute-start | bytes 159752 | tf_op jit(solution)/shard_map/ppermute | solution.py:17
  32.7 2.6 %collective-permute-done.3.got_ref = bf16[208,128]{1,0:T(8,128)(2,1)S(1)} collective-permute-done((bf16[208,128]{1,0:T(8,128)(2,1)S(1)}, bf16[208,128]{1,0:T(8,128)(2,1)S(1)}, u32[]{:S(2)}, u32[]{:S(2)}) %collective-permute-start.3) | collective-permute-done | bytes 53280 | tf_op jit(solution)/shard_map/ppermute | solution.py:17
  36.5 0.9 collective-permute-start.6
  37.5 4.4 %collective-permute-done.5.refs_2_ = bf16[416,128]{1,0:T(8,128)(2,1)S(1)} collective-permute-done((bf16[416,128]{1,0:T(8,128)(2,1)S(1)}, bf16[416,128]{1,0:T(8,128)(2,1)S(1)}, u32[]{:S(2)}, u32[]{:S(2)}) %collective-permute-start.5) | collective-permute-done | bytes 106528 | tf_op jit(solution)/shard_map/ppermute | solution.py:17
  42.4 1.0 copy-done.10
  43.3 1.5 %project.1 = (s32[8]{0:T(128)S(1)}, f32[400,128]{1,0:T(8,128)S(1)}, bf16[4,400,128]{2,1,0:T(8,128)(2,1)}) custom-call(bf16[416,128]{1,0:T(8,128)(2,1)S(1)} %join.1.dep_ref.refs_0_, bf16[416,128]{1,0:T(8,128)(2,1)S(1)} %collective-permute-done.4.refs_1_, bf16[416,128]{1,0:T(8,128)(2,1)S(1)} %collective-permute-done.5.refs_2_, ...), custom_call_target="tpu_custom_call" | custom-call | tf_op jit(solution)/shard_map/project/pallas_call | solution.py:273
  44.8 3.5 %all-to-all-start.1 = ((bf16[4,400,128]{2,1,0:T(8,128)(2,1)}), bf16[4,400,128]{2,1,0:T(8,128)(2,1)S(1)}, u32[]{:S(2)}, u32[]{:S(2)}) async-start(bf16[4,400,128]{2,1,0:T(8,128)(2,1)} %get-tuple-element.59), calls=%async_computation.1 | async-start | bytes 819200 | tf_op jit(solution)/shard_map/all_to_all | solution.py:791
  48.5 1.0 collective-permute-start.9
  49.5 1.1 %image_pack.1 = bf16[4,64,1536]{2,1,0:T(8,128)(2,1)} custom-call(bf16[64,6144]{1,0:T(8,128)(2,1)S(1)} %bitcast.15, bf16[64,3072]{1,0:T(8,128)(2,1)S(1)} %bitcast.17, bf16[64,3072]{1,0:T(8,128)(2,1)S(1)} %bitcast.19, bf16[416,128]{1,0:T(8,128)(2,1)S(1)} %join.1.dep_ref.refs_0_), custom_call_target="tpu_custom_call" | custom-call | tf_op jit(solution)/shard_map/image_pack/pallas_call | solution.py:273
  50.5 1.6 %collective-permute-start.11 = (bf16[4,64,1536]{2,1,0:T(8,128)(2,1)}, bf16[4,64,1536]{2,1,0:T(8,128)(2,1)S(1)}, u32[]{:S(2)}, u32[]{:S(2)}) collective-permute-start(bf16[4,64,1536]{2,1,0:T(8,128)(2,1)} %image_pack.1), channel_id=1, source_target_pairs={{0,4},{4,0},{1,5},{5,1},{2,6},{6,2},{3,7},{7,3},{8,12},{12,8},{9,1... | collective-permute-start | bytes 2359304 | tf_op jit(solution)/shard_map/ppermute | solution.py:17
  52.1 8.1 %collective-permute-done.9.dep_ref.pair_ref = bf16[128,1536]{1,0:T(8,128)(2,1)S(1)} collective-permute-done((bf16[128,1536]{1,0:T(8,128)(2,1)S(1)}, bf16[128,1536]{1,0:T(8,128)(2,1)S(1)}, u32[]{:S(2)}, u32[]{:S(2)}) %collective-permute-start.9) | collective-permute-done | bytes 393248 | tf_op jit(solution)/shard_map/ppermute | solution.py:17
  60.3 1.2 %all-to-all-done.1.refs_0_ = bf16[4,400,128]{2,1,0:T(8,128)(2,1)S(1)} async-done(((bf16[4,400,128]{2,1,0:T(8,128)(2,1)}), bf16[4,400,128]{2,1,0:T(8,128)(2,1)S(1)}, u32[]{:S(2)}, u32[]{:S(2)}) %all-to-all-start.1) | async-done | bytes 409632 | tf_op jit(solution)/shard_map/all_to_all | solution.py:791
  61.7 1.0 copy-done.6
  63.4 6.9 %collective-permute-done.11.got_ref.refs_0_ = bf16[4,64,1536]{2,1,0:T(8,128)(2,1)S(1)} collective-permute-done((bf16[4,64,1536]{2,1,0:T(8,128)(2,1)}, bf16[4,64,1536]{2,1,0:T(8,128)(2,1)S(1)}, u32[]{:S(2)}, u32[]{:S(2)}) %collective-permute-start.11) | collective-permute-done | bytes 786464 | tf_op jit(solution)/shard_map/ppermute | solution.py:17
  70.5 1.5 %collective-permute-start.12 = (f32[2,64,64]{2,1,0:T(8,128)S(1)}, f32[2,64,64]{2,1,0:T(8,128)S(1)}, u32[]{:S(2)}, u32[]{:S(2)}) collective-permute-start(f32[2,64,64]{2,1,0:T(8,128)S(1)} %get-tuple-element.62.low_ref), channel_id=1, source_target_pairs={{0,4},{4,0},{1,5},{5,1},{2,6},{6,2},{3,7},{7,3},{8,12},{12,8},{9,1... | collective-permute-start | bytes 98312 | tf_op jit(solution)/shard_map/ppermute | solution.py:17
  72.0 14.7 %all-gather = bf16[256,768]{1,0:T(8,128)(2,1)S(1)} all-gather(bf16[64,768]{1,0:T(8,128)(2,1)S(1)} %finish.1.dep_ref), channel_id=2, replica_groups=mesh['enc'=4,'seq'=2,'req'=4] {'enc'}, dimensions={0}, use_global_device_ids=true | all-gather | bytes 491520 | tf_op jit(solution)/shard_map/all_gather | solution.py:831
  87.7 1.4 %collective-permute-start.16 = (bf16[128,768]{1,0:T(8,128)(2,1)S(1)}, bf16[128,768]{1,0:T(8,128)(2,1)S(1)}, u32[]{:S(2)}, u32[]{:S(2)}) collective-permute-start(bf16[128,768]{1,0:T(8,128)(2,1)S(1)} %get-tuple-element.73), channel_id=1, source_target_pairs={{0,2},{1,3},{2,0},{3,1},{4,6},{5,7},{6,4},{7,5},{8,10},{9,11},{10,... | collective-permute-start | bytes 589832 | tf_op jit(solution)/shard_map/ppermute | solution.py:17
  91.1 0.9 heads.5
  92.0 1.6 %collective-permute-start.15 = (bf16[64,384]{1,0:T(8,128)(2,1)S(1)}, bf16[64,384]{1,0:T(8,128)(2,1)S(1)}, u32[]{:S(2)}, u32[]{:S(2)}) collective-permute-start(bf16[64,384]{1,0:T(8,128)(2,1)S(1)} %get-tuple-element.72), channel_id=1, source_target_pairs={{0,4},{4,0},{1,5},{5,1},{2,6},{6,2},{3,7},{7,3},{8,12},{12,8},{9,1... | collective-permute-start | bytes 147464 | tf_op jit(solution)/shard_map/ppermute | solution.py:17
  93.6 1.1 %collective-permute-done.13.refs_1_ = bf16[64,384]{1,0:T(8,128)(2,1)S(1)} collective-permute-done((bf16[64,384]{1,0:T(8,128)(2,1)S(1)}, bf16[64,384]{1,0:T(8,128)(2,1)S(1)}, u32[]{:S(2)}, u32[]{:S(2)}) %collective-permute-start.13) | collective-permute-done | bytes 49184 | tf_op jit(solution)/shard_map/ppermute | solution.py:17
  97.0 1.8 %collective-permute-done.18.text_ref = bf16[128,768]{1,0:T(8,128)(2,1)S(1)} collective-permute-done((bf16[128,768]{1,0:T(8,128)(2,1)S(1)}, bf16[128,768]{1,0:T(8,128)(2,1)S(1)}, u32[]{:S(2)}, u32[]{:S(2)}) %collective-permute-start.18) | collective-permute-done | bytes 196640 | tf_op jit(solution)/shard_map/ppermute | solution.py:17
  98.8 0.9 heads.7
  100.6 3.3 %collective-permute-done.19.refs_7_ = bf16[64,384]{1,0:T(8,128)(2,1)S(1)} collective-permute-done((bf16[64,384]{1,0:T(8,128)(2,1)S(1)}, bf16[64,384]{1,0:T(8,128)(2,1)S(1)}, u32[]{:S(2)}, u32[]{:S(2)}) %collective-permute-start.19) | collective-permute-done | bytes 49184 | tf_op jit(solution)/shard_map/ppermute | solution.py:17
  (72 shorter events, 12.6 us)
Async XLA Ops:
  0.0 89.6 %copy-start = (s32[2,128]{1,0:T(2,128)S(1)}, s32[2,128]{1,0:T(2,128)}, u32[]{:S(2)}) copy-start(s32[2,128]{1,0:T(2,128)} %param.16) | copy-start | bytes 3076
  4.2 1.9 %collective-permute-start = (bf16[1552,128]{1,0:T(8,128)(2,1)S(1)}, bf16[1552,128]{1,0:T(8,128)(2,1)S(1)}, u32[]{:S(2)}, u32[]{:S(2)}) collective-permute-start(bf16[1552,128]{1,0:T(8,128)(2,1)S(1)} %get-tuple-element.42), channel_id=1, source_target_pairs={{0,1},{1,0},{2,3},{3,2},{4,5},{5,4},{6,7},{7,6},{8,9},{9,8},{10,11... | collective-permute-start | bytes 1191944 | tf_op jit(solution)/shard_map/ppermute | solution.py:17
  6.2 18.4 %copy-start.16 = (bf16[1,192]{1,0:T(2,128)(2,1)S(1)}, bf16[1,192]{1,0:T(2,128)(2,1)}, u32[]{:S(2)}) copy-start(bf16[1,192]{1,0:T(2,128)(2,1)} %param.20) | copy-start | bytes 1156
  6.2 24.7 %copy-start.13 = (bf16[192]{0:T(256)(128)(2,1)S(1)}, bf16[192]{0:T(256)(128)(2,1)}, u32[]{:S(2)}) copy-start(bf16[192]{0:T(256)(128)(2,1)} %b_hbm.1) | copy-start | bytes 1156
  6.2 24.8 %copy-start.14 = (bf16[1,192]{1,0:T(2,128)(2,1)S(1)}, bf16[1,192]{1,0:T(2,128)(2,1)}, u32[]{:S(2)}) copy-start(bf16[1,192]{1,0:T(2,128)(2,1)} %shift_ref.1) | copy-start | bytes 1156
  7.4 9.4 %copy-start.9 = (bf16[192,768]{1,0:T(8,128)(2,1)}, bf16[192,768]{1,0:T(8,128)(2,1)S(1)}, u32[]{:S(2)}) copy-start(bf16[192,768]{1,0:T(8,128)(2,1)S(1)} %get-tuple-element.53.refs_4_) | copy-start | bytes 884740
  7.4 8.6 %collective-permute-start.2 = (bf16[192,768]{1,0:T(8,128)(2,1)S(1)}, bf16[192,768]{1,0:T(8,128)(2,1)S(1)}, u32[]{:S(2)}, u32[]{:S(2)}) collective-permute-start(bf16[192,768]{1,0:T(8,128)(2,1)S(1)} %get-tuple-element.49), channel_id=1, source_target_pairs={{0,1},{1,0},{2,3},{3,2},{4,5},{5,4},{6,7},{7,6},{8,9},{9,8},{10,11... | collective-permute-start | bytes 884744 | tf_op jit(solution)/shard_map/ppermute | solution.py:17
  7.8 8.2 %collective-permute-start.1 = (bf16[784,128]{1,0:T(8,128)(2,1)S(1)}, bf16[784,128]{1,0:T(8,128)(2,1)S(1)}, u32[]{:S(2)}, u32[]{:S(2)}) collective-permute-start(bf16[784,128]{1,0:T(8,128)(2,1)S(1)} %get-tuple-element.45), channel_id=1, source_target_pairs={{0,2},{1,3},{2,0},{3,1},{4,6},{5,7},{6,4},{7,5},{8,10},{9,11},{10,... | collective-permute-start | bytes 602120 | tf_op jit(solution)/shard_map/ppermute | solution.py:17
  16.7 31.6 %copy-start.7 = (bf16[1,3072,64]{1,2,0:T(8,128)(2,1)S(1)}, bf16[1,3072,64]{1,2,0:T(8,128)(2,1)}, u32[]{:S(2)}) copy-start(bf16[1,3072,64]{1,2,0:T(8,128)(2,1)} %param.25) | copy-start | bytes 1179652
  16.7 31.6 %copy-start.8 = (bf16[1,64,3072]{2,1,0:T(8,128)(2,1)S(1)}, bf16[1,64,3072]{2,1,0:T(8,128)(2,1)}, u32[]{:S(2)}) copy-start(bf16[1,64,3072]{2,1,0:T(8,128)(2,1)} %param.26) | copy-start | bytes 1179652
  16.7 18.7 %collective-permute-start.7 = (bf16[2,192,768]{2,1,0:T(8,128)(2,1)}, bf16[2,192,768]{2,1,0:T(8,128)(2,1)S(1)}, u32[]{:S(2)}, u32[]{:S(2)}) collective-permute-start(bf16[2,192,768]{2,1,0:T(8,128)(2,1)} %get-tuple-element.54.refs_0_), channel_id=1, source_target_pairs={{0,2},{1,3},{2,0},{3,1},{4,6},{5,7},{6,4},{7,5},{8,10},{9,11},{10,... | collective-permute-start | bytes 1769480 | tf_op jit(solution)/shard_map/ppermute | solution.py:17
  18.5 12.4 %all-to-all-start = ((bf16[4,208,128]{2,1,0:T(8,128)(2,1)}), bf16[4,208,128]{2,1,0:T(8,128)(2,1)S(1)}, u32[]{:S(2)}, u32[]{:S(2)}) async-start(bf16[4,208,128]{2,1,0:T(8,128)(2,1)} %get-tuple-element.52), calls=%async_computation | async-start | bytes 425984 | tf_op jit(solution)/shard_map/all_to_all | solution.py:725
  31.1 18.3 %copy-start.1 = (bf16[1,1,64,6144]{3,2,1,0:T(8,128)(2,1)S(1)}, bf16[1,1,64,6144]{3,2,1,0:T(8,128)(2,1)}, u32[]{:S(2)}) copy-start(bf16[1,1,64,6144]{3,2,1,0:T(8,128)(2,1)} %param.28) | copy-start | bytes 2359300
  31.2 18.3 %copy-start.3 = (bf16[1,1,64,3072]{3,2,1,0:T(8,128)(2,1)S(1)}, bf16[1,1,64,3072]{3,2,1,0:T(8,128)(2,1)}, u32[]{:S(2)}) copy-start(bf16[1,1,64,3072]{3,2,1,0:T(8,128)(2,1)} %param.29) | copy-start | bytes 1179652
  31.2 18.3 %copy-start.4 = (bf16[1,1,64,3072]{3,2,1,0:T(8,128)(2,1)S(1)}, bf16[1,1,64,3072]{3,2,1,0:T(8,128)(2,1)}, u32[]{:S(2)}) copy-start(bf16[1,1,64,3072]{3,2,1,0:T(8,128)(2,1)} %param.27) | copy-start | bytes 1179652
  31.2 4.2 %collective-permute-start.3 = (bf16[208,128]{1,0:T(8,128)(2,1)S(1)}, bf16[208,128]{1,0:T(8,128)(2,1)S(1)}, u32[]{:S(2)}, u32[]{:S(2)}) collective-permute-start(bf16[208,128]{1,0:T(8,128)(2,1)S(1)} %centre.1.own_ref), channel_id=1, source_target_pairs={{0,4},{4,0},{1,5},{5,1},{2,6},{6,2},{3,7},{7,3},{8,12},{12,8},{9,1... | collective-permute-start | bytes 159752 | tf_op jit(solution)/shard_map/ppermute | solution.py:17
  35.4 6.9 %collective-permute-start.8 = (bf16[192,768]{1,0:T(8,128)(2,1)S(1)}, bf16[192,768]{1,0:T(8,128)(2,1)S(1)}, u32[]{:S(2)}, u32[]{:S(2)}) collective-permute-start(bf16[192,768]{1,0:T(8,128)(2,1)S(1)} %get-tuple-element.56), channel_id=1, source_target_pairs={{0,1},{1,0},{2,3},{3,2},{4,5},{5,4},{6,7},{7,6},{8,9},{9,8},{10,11... | collective-permute-start | bytes 884744 | tf_op jit(solution)/shard_map/ppermute | solution.py:17
  35.5 1.9 %collective-permute-start.4 = (bf16[416,128]{1,0:T(8,128)(2,1)S(1)}, bf16[416,128]{1,0:T(8,128)(2,1)S(1)}, u32[]{:S(2)}, u32[]{:S(2)}) collective-permute-start(bf16[416,128]{1,0:T(8,128)(2,1)S(1)} %join.1.dep_ref.refs_0_), channel_id=1, source_target_pairs={{0,1},{1,0},{2,3},{3,2},{4,5},{5,4},{6,7},{7,6},{8,9},{9,8},{10,11... | collective-permute-start | bytes 319496 | tf_op jit(solution)/shard_map/ppermute | solution.py:17
  36.0 5.8 %collective-permute-start.5 = (bf16[416,128]{1,0:T(8,128)(2,1)S(1)}, bf16[416,128]{1,0:T(8,128)(2,1)S(1)}, u32[]{:S(2)}, u32[]{:S(2)}) collective-permute-start(bf16[416,128]{1,0:T(8,128)(2,1)S(1)} %join.1.dep_ref.refs_0_), channel_id=1, source_target_pairs={{0,2},{1,3},{2,0},{3,1},{4,6},{5,7},{6,4},{7,5},{8,10},{9,11},{10,... | collective-permute-start | bytes 319496 | tf_op jit(solution)/shard_map/ppermute | solution.py:17
  36.5 5.9 %collective-permute-start.6 = (bf16[416,128]{1,0:T(8,128)(2,1)S(1)}, bf16[416,128]{1,0:T(8,128)(2,1)S(1)}, u32[]{:S(2)}, u32[]{:S(2)}) collective-permute-start(bf16[416,128]{1,0:T(8,128)(2,1)S(1)} %join.1.dep_ref.refs_0_), channel_id=1, source_target_pairs={{0,3},{1,2},{2,1},{3,0},{4,7},{5,6},{6,5},{7,4},{8,11},{9,10},{10,... | collective-permute-start | bytes 319496 | tf_op jit(solution)/shard_map/ppermute | solution.py:17
  44.8 16.6 %all-to-all-start.1 = ((bf16[4,400,128]{2,1,0:T(8,128)(2,1)}), bf16[4,400,128]{2,1,0:T(8,128)(2,1)S(1)}, u32[]{:S(2)}, u32[]{:S(2)}) async-start(bf16[4,400,128]{2,1,0:T(8,128)(2,1)} %get-tuple-element.59), calls=%async_computation.1 | async-start | bytes 819200 | tf_op jit(solution)/shard_map/all_to_all | solution.py:791
  48.5 11.8 %collective-permute-start.9 = (bf16[128,1536]{1,0:T(8,128)(2,1)S(1)}, bf16[128,1536]{1,0:T(8,128)(2,1)S(1)}, u32[]{:S(2)}, u32[]{:S(2)}) collective-permute-start(bf16[128,1536]{1,0:T(8,128)(2,1)S(1)} %maps_pack.1.own_ref), channel_id=1, source_target_pairs={{0,2},{1,3},{2,0},{3,1},{4,6},{5,7},{6,4},{7,5},{8,10},{9,11},{10,... | collective-permute-start | bytes 1179656 | tf_op jit(solution)/shard_map/ppermute | solution.py:17
  50.5 19.7 %collective-permute-start.11 = (bf16[4,64,1536]{2,1,0:T(8,128)(2,1)}, bf16[4,64,1536]{2,1,0:T(8,128)(2,1)S(1)}, u32[]{:S(2)}, u32[]{:S(2)}) collective-permute-start(bf16[4,64,1536]{2,1,0:T(8,128)(2,1)} %image_pack.1), channel_id=1, source_target_pairs={{0,4},{4,0},{1,5},{5,1},{2,6},{6,2},{3,7},{7,3},{8,12},{12,8},{9,1... | collective-permute-start | bytes 2359304 | tf_op jit(solution)/shard_map/ppermute | solution.py:17
  63.3 6.9 %collective-permute-start.10 = (bf16[128,1536]{1,0:T(8,128)(2,1)S(1)}, bf16[128,1536]{1,0:T(8,128)(2,1)S(1)}, u32[]{:S(2)}, u32[]{:S(2)}) collective-permute-start(bf16[128,1536]{1,0:T(8,128)(2,1)S(1)} %get-tuple-element.61), channel_id=1, source_target_pairs={{0,1},{1,0},{2,3},{3,2},{4,5},{5,4},{6,7},{7,6},{8,9},{9,8},{10,11... | collective-permute-start | bytes 1179656 | tf_op jit(solution)/shard_map/ppermute | solution.py:17
  70.5 16.2 %collective-permute-start.12 = (f32[2,64,64]{2,1,0:T(8,128)S(1)}, f32[2,64,64]{2,1,0:T(8,128)S(1)}, u32[]{:S(2)}, u32[]{:S(2)}) collective-permute-start(f32[2,64,64]{2,1,0:T(8,128)S(1)} %get-tuple-element.62.low_ref), channel_id=1, source_target_pairs={{0,4},{4,0},{1,5},{5,1},{2,6},{6,2},{3,7},{7,3},{8,12},{12,8},{9,1... | collective-permute-start | bytes 98312 | tf_op jit(solution)/shard_map/ppermute | solution.py:17
  87.6 3.5 %collective-permute-start.14 = (bf16[128,768]{1,0:T(8,128)(2,1)S(1)}, bf16[128,768]{1,0:T(8,128)(2,1)S(1)}, u32[]{:S(2)}, u32[]{:S(2)}) collective-permute-start(bf16[128,768]{1,0:T(8,128)(2,1)S(1)} %get-tuple-element.70), channel_id=1, source_target_pairs={{0,1},{1,0},{2,3},{3,2},{4,5},{5,4},{6,7},{7,6},{8,9},{9,8},{10,11... | collective-permute-start | bytes 589832 | tf_op jit(solution)/shard_map/ppermute | solution.py:17
  87.7 7.8 %collective-permute-start.16 = (bf16[128,768]{1,0:T(8,128)(2,1)S(1)}, bf16[128,768]{1,0:T(8,128)(2,1)S(1)}, u32[]{:S(2)}, u32[]{:S(2)}) collective-permute-start(bf16[128,768]{1,0:T(8,128)(2,1)S(1)} %get-tuple-element.73), channel_id=1, source_target_pairs={{0,2},{1,3},{2,0},{3,1},{4,6},{5,7},{6,4},{7,5},{8,10},{9,11},{10,... | collective-permute-start | bytes 589832 | tf_op jit(solution)/shard_map/ppermute | solution.py:17
  89.1 9.7 %collective-permute-start.18 = (bf16[128,768]{1,0:T(8,128)(2,1)S(1)}, bf16[128,768]{1,0:T(8,128)(2,1)S(1)}, u32[]{:S(2)}, u32[]{:S(2)}) collective-permute-start(bf16[128,768]{1,0:T(8,128)(2,1)S(1)} %get-tuple-element.76), channel_id=1, source_target_pairs={{0,3},{1,2},{2,1},{3,0},{4,7},{5,6},{6,5},{7,4},{8,11},{9,10},{10,... | collective-permute-start | bytes 589832 | tf_op jit(solution)/shard_map/ppermute | solution.py:17
  90.5 4.2 %collective-permute-start.13 = (bf16[64,384]{1,0:T(8,128)(2,1)S(1)}, bf16[64,384]{1,0:T(8,128)(2,1)S(1)}, u32[]{:S(2)}, u32[]{:S(2)}) collective-permute-start(bf16[64,384]{1,0:T(8,128)(2,1)S(1)} %get-tuple-element.69), channel_id=1, source_target_pairs={{0,4},{4,0},{1,5},{5,1},{2,6},{6,2},{3,7},{7,3},{8,12},{12,8},{9,1... | collective-permute-start | bytes 147464 | tf_op jit(solution)/shard_map/ppermute | solution.py:17
  92.0 6.8 %collective-permute-start.15 = (bf16[64,384]{1,0:T(8,128)(2,1)S(1)}, bf16[64,384]{1,0:T(8,128)(2,1)S(1)}, u32[]{:S(2)}, u32[]{:S(2)}) collective-permute-start(bf16[64,384]{1,0:T(8,128)(2,1)S(1)} %get-tuple-element.72), channel_id=1, source_target_pairs={{0,4},{4,0},{1,5},{5,1},{2,6},{6,2},{3,7},{7,3},{8,12},{12,8},{9,1... | collective-permute-start | bytes 147464 | tf_op jit(solution)/shard_map/ppermute | solution.py:17
  96.4 4.2 %collective-permute-start.17 = (bf16[64,384]{1,0:T(8,128)(2,1)S(1)}, bf16[64,384]{1,0:T(8,128)(2,1)S(1)}, u32[]{:S(2)}, u32[]{:S(2)}) collective-permute-start(bf16[64,384]{1,0:T(8,128)(2,1)S(1)} %get-tuple-element.75), channel_id=1, source_target_pairs={{0,4},{4,0},{1,5},{5,1},{2,6},{6,2},{3,7},{7,3},{8,12},{12,8},{9,1... | collective-permute-start | bytes 147464 | tf_op jit(solution)/shard_map/ppermute | solution.py:17
  99.7 4.2 %collective-permute-start.19 = (bf16[64,384]{1,0:T(8,128)(2,1)S(1)}, bf16[64,384]{1,0:T(8,128)(2,1)S(1)}, u32[]{:S(2)}, u32[]{:S(2)}) collective-permute-start(bf16[64,384]{1,0:T(8,128)(2,1)S(1)} %get-tuple-element.78), channel_id=1, source_target_pairs={{0,4},{4,0},{1,5},{5,1},{2,6},{6,2},{3,7},{7,3},{8,12},{12,8},{9,1... | collective-permute-start | bytes 147464 | tf_op jit(solution)/shard_map/ppermute | solution.py:17
  (7 other events, 20.8 us)

commit v6 on v4

--- a/solution.py
+++ b/solution.py
@@ -269,14 +269,22 @@
 TN = (((0,), (0,)), ((), ()))
 
 
-def call(kernel, outs, ins, specs=None, scratch=(), name=None, out_specs=None):
+def partners(send, axis, size):
+    return {k: swap(send(k), axis, size, k) for k in far_first(size)}
+
+
+def far_first(size):
+    return [k for k in range(2, size)] + [1]
+
+
+def call(kernel, outs, ins, specs=None, scratch=(), name=None, out_specs=None, vmem=16):
     return pl.pallas_call(
         kernel,
         out_shape=outs,
         in_specs=specs if specs is not None else [VMEM] * len(ins),
         out_specs=out_specs if out_specs is not None else jax.tree.map(lambda _: VMEM, outs),
         scratch_shapes=list(scratch),
-        compiler_params=pltpu.CompilerParams(vmem_limit_bytes=16 * 1024 * 1024),
+        compiler_params=pltpu.CompilerParams(vmem_limit_bytes=int(vmem * 1024 * 1024)),
         name=name,
     )(*ins)
 
@@ -391,22 +399,23 @@
     out_ref[features:] = extra.astype(BF16)
 
 
-def pass_on_kernel(got_ref, dep_ref, own_ref, next_ref):
+def pass_on_kernel(core_ref, got_ref, dep_ref, own_ref, next_ref):
     own_ref[...] = got_ref[0]
-    next_ref[...] = got_ref[1]
-
-
-def join_kernel(own_ref, got_ref, out_ref):
+    next_ref[0] = core_ref[...]
+    next_ref[1] = got_ref[1]
+
+
+def join_kernel(own_ref, got_ref, dep_ref, out_ref):
     size = own_ref.shape[0]
     out_ref[:size] = own_ref[...]
     out_ref[size:] = got_ref[...]
 
 
-def project_kernel(n_seq, n_req, n_enc, dep_ref, *refs):
-    payload_refs = refs[:n_req]
-    weight_refs = refs[n_req : 2 * n_req]
-    prompts_ref, keep_ref = refs[2 * n_req : 2 * n_req + 2]
-    send_refs = refs[2 * n_req + 2 : -1]
+def project_kernel(n_seq, n_req, n_enc, own_ref, pair_ref, next_ref, *refs):
+    payload_refs = dict(zip([0] + far_first(n_req), refs))
+    weight_refs = (own_ref, next_ref.at[0], pair_ref, next_ref.at[1])
+    prompts_ref, keep_ref = refs[n_req : n_req + 2]
+    send_refs = refs[n_req + 2 : -1]
     rows_ref = refs[-1]
     features, width = weight_refs[0].shape
     tokens = payload_refs[0].shape[1]
@@ -461,7 +470,7 @@
         send_ref[...] = rows_ref[at(e ^ (k + 1), step)].astype(BF16)
 
 
-def finish_kernel(n_req, model_width, dep_ref, keep_ref, bias_ref, *refs):
+def finish_kernel(n_req, model_width, dep_ref, image_ref, keep_ref, bias_ref, *refs):
     got_refs, out_ref = refs[:-1], refs[-1]
     r, s = lax.axis_index("req"), lax.axis_index("seq")
     size, width = out_ref.shape
@@ -486,7 +495,7 @@
 
 
 def choose_kernel(n_seq, n_enc, chosen_ref, dep_ref, *refs):
-    part_refs, out_refs = refs[:n_enc], refs[n_enc:]
+    part_refs, out_refs = dict(zip([0] + far_first(n_enc), refs)), refs[n_enc:]
     e, r, s = lax.axis_index("enc"), lax.axis_index("req"), lax.axis_index("seq")
     halves = n_enc // n_seq
     size = part_refs[0].shape[0]
@@ -547,25 +556,21 @@
         copy.wait()
 
 
-def select_kernel(ids_ref, own_ref, pair_ref, dep_ref, mine_ref, core_ref):
-    r = lax.axis_index("req")
-    for out_ref, adapter in ((mine_ref, ids_ref[4]), (core_ref, ids_ref[5])):
-        other = lax.rem((adapter ^ r) // 2, 2)
-
-        @pl.when(other == 0)
+def select_kernel(ids_ref, own_ref, pair_ref, dep_ref, core_ref):
+    other = lax.rem((ids_ref[5] ^ lax.axis_index("req")) // 2, 2)
+    for k, ref in enumerate((own_ref, pair_ref)):
+        @pl.when(other == k)
         def _():
-            out_ref[...] = own_ref[...]
-
-        @pl.when(other == 1)
-        def _():
-            out_ref[...] = pair_ref[...]
-
-
-def lowrank_kernel(part, adapter_ref, x_ref, mine_ref, core_ref, got_ref, out_ref, chosen_ref):
-    other = lax.rem(adapter_ref[0, 0] ^ lax.axis_index("req"), 2)
+            core_ref[...] = ref[...]
+
+
+def lowrank_kernel(part, adapter_ref, x_ref, got_ref, *refs):
+    map_refs, (out_ref, chosen_ref) = refs[:3], refs[3:]
+    other = adapter_ref[0, 0] ^ lax.axis_index("req")
+    place = jnp.where(lax.rem(other, 2) == 1, 2, other // 2)
     rank = out_ref.shape[-1]
-    for k, ref in enumerate((mine_ref, core_ref)):
-        @pl.when(other == k)
+    for k, ref in enumerate(map_refs):
+        @pl.when(place == k)
         def _():
             chosen_ref[...] = ref[rank:]
             own = x_ref[:, pl.ds(pl.multiple_of(lax.axis_index("seq") * part, HDIM), part)]
@@ -685,12 +690,34 @@
             pltpu.VMEM(encoder_hidden.shape[1:], BF16),
             pltpu.VMEM(context_weight.shape, BF16),
             pltpu.VMEM(context_bias.shape, BF16),
-            dma((2 + n_enc,)),
+            dma((2 + 2 * n_enc,)),
         ],
         name="context",
+        vmem=52.65,
     )
     got = swap(send, "req", n_req, 1)
 
+    weight = struct((features, 2 * half))
+    weight_own, weight_core, weight_pair = call(
+        functools.partial(weight_kernel, n_req, part, inner),
+        (weight, weight, struct((2, features, 2 * half))),
+        (key_value_weight, send),
+        [ANY] * 2,
+        [dma((2 * n_req,))],
+        name="weight_pack",
+    )
+
+    send, keep, sums = call(
+        functools.partial(halve_kernel, features),
+        (
+            struct((n_enc * features + ROWS, tokens)),
+            struct((n_enc * features, tokens), F32),
+            stat,
+        ),
+        (got, keep, sums),
+        name="halve",
+    )
+    got = swap(send, "req", n_req, 2)
     packed = [
         call(
             functools.partial(image_kernel, part, inner, k),
@@ -703,37 +730,15 @@
         for k in range(1, n_seq)
     ]
     image_got = [swap(packed[k - 1], "seq", n_seq, k) for k in range(1, n_seq)]
-    weight = struct((features, 2 * half))
-    weight_own, weight_core, weight_pair = call(
-        functools.partial(weight_kernel, n_req, part, inner),
-        (weight, weight, struct((2, features, 2 * half))),
-        (key_value_weight, keep),
-        [ANY] * 2,
-        [dma((2 * n_req,))],
-        name="weight_pack",
-    )
-    weight_core_got = swap(weight_core, "req", n_req, 1)
-
-    send, keep, sums = call(
-        functools.partial(halve_kernel, features),
-        (
-            struct((n_enc * features + ROWS, tokens)),
-            struct((n_enc * features, tokens), F32),
-            stat,
-        ),
-        (got, keep, sums),
-        name="halve",
-    )
-    got = swap(send, "req", n_req, 2)
     keep, sums, *sends = call(
-        functools.partial(scatter_kernel, features, 3),
+        functools.partial(scatter_kernel, features, 1),
         (struct((features, tokens), F32), stat)
         + tuple(struct((features + ROWS, tokens)) for _ in range(1, n_enc)),
-        (got, keep, sums, weight_pair, packed[0], weight_core_got),
-        [VMEM] * 3 + [ANY] * 3,
+        (got, keep, sums, weight_pair),
+        [VMEM] * 3 + [ANY],
         name="scatter",
     )
-    arrived = [swap(sends[k - 1], "enc", n_enc, k) for k in range(1, n_enc)]
+    arrived = partners(lambda k: sends[k - 1], "enc", n_enc).values()
     weight_pair = lax.optimization_barrier((weight_pair, keep))[0]
     weight_pair_got = swap(weight_pair, "req", n_req, 2)
 
@@ -760,18 +765,19 @@
     joined = call(
         join_kernel,
         struct((n_seq * (features + ROWS), tokens)),
-        (own, swap(own, "seq", n_seq, 1)),
+        (own, swap(own, "seq", n_seq, 1), image_got[0]),
+        [VMEM, VMEM, ANY],
         name="join",
     )
-    payloads = [joined] + [swap(joined, "req", n_req, k) for k in range(1, n_req)]
+    payloads = partners(lambda k: joined, "req", n_req)
     weight_own_pair, weight_next = call(
         pass_on_kernel,
-        (weight, weight),
-        (weight_pair_got, joined),
-        [VMEM, ANY],
+        (weight, struct((2, features, 2 * half))),
+        (weight_core, weight_pair_got, joined),
+        [VMEM, VMEM, ANY],
         name="pass_on",
     )
-    weights = (weight_own, weight_core_got, weight_own_pair, swap(weight_next, "req", n_req, 1))
+    weight_next = swap(weight_next, "req", n_req, 1)
 
     size = n_seq * tokens // n_enc
     step = 2 * half // HDIM * size + ROWS
@@ -779,13 +785,12 @@
         functools.partial(project_kernel, n_seq, n_req, n_enc),
         (struct((2 * n_req,), jnp.int32), struct((step, HDIM), F32))
         + tuple(struct((step, HDIM)) for _ in range(1, n_enc)),
-        (image_got[0], *payloads, *weights),
-        [ANY] + [VMEM] * (2 * n_req),
+        (weight_own, weight_own_pair, weight_next, joined, *payloads.values()),
         scratch=[pltpu.VMEM((n_enc * step, HDIM), F32)],
         out_specs=(SMEM,) + (VMEM,) * n_enc,
         name="project",
     )
-    arrived = [swap(sends[k - 1], "enc", n_enc, k) for k in range(1, n_enc)]
+    arrived = partners(lambda k: sends[k - 1], "enc", n_enc).values()
 
     maps = call(
         functools.partial(maps_kernel, part),
@@ -800,13 +805,13 @@
     text = call(
         functools.partial(finish_kernel, n_req, model_width),
         struct((size, 2 * half)),
-        (maps_pair, keep, key_value_bias[None], *arrived),
-        [ANY] + [VMEM] * (2 + len(arrived)),
+        (maps_pair, image_got[0], keep, key_value_bias[None], *arrived),
+        [ANY] * 2 + [VMEM] * (2 + len(arrived)),
         name="finish",
     )
-    maps_mine, maps_core = call(
+    maps_core = call(
         select_kernel,
-        (struct((2 * rank, part)), struct((2 * rank, part))),
+        struct((2 * rank, part)),
         (ids, maps, maps_pair, text),
         [SMEM, VMEM, VMEM, ANY],
         name="select",
@@ -814,8 +819,15 @@
     low, chosen_maps = call(
         functools.partial(lowrank_kernel, part),
         (struct((n_seq, image_rows, rank), F32), struct((rank, part))),
-        (adapter_of_request, stream, maps_mine, swap(maps_core, "req", n_req, 1), image_got[0]),
-        [SMEM] + [VMEM] * 4,
+        (
+            adapter_of_request,
+            stream,
+            image_got[0],
+            maps,
+            maps_pair,
+            swap(maps_core, "req", n_req, 1),
+        ),
+        [SMEM] + [VMEM] * 5,
         name="lowrank",
     )
     arranged = struct((n_req, n_seq * image_rows, half))
@@ -825,15 +837,15 @@
         (low, swap(low, "seq", n_seq, 1), chosen_maps, qk, base, *image_got),
         name="arrange",
     )
-    parts = [text] + [swap(text, "enc", n_enc, k) for k in range(1, n_enc)]
+    parts = partners(lambda k: text, "enc", n_enc)
     rows = call(
         functools.partial(choose_kernel, n_seq, n_enc),
         tuple(struct((tokens, 2 * half)) for _ in range(n_req)),
-        (ids, image_values, *parts),
+        (ids, image_values, text, *parts.values()),
         [SMEM, ANY] + [VMEM] * n_enc,
         name="choose",
     )
-    rows = [rows[0]] + [swap(rows[k], "req", n_req, k) for k in range(1, n_req)]
+    rows = {0: rows[0], **partners(lambda k: rows[k], "req", n_req)}
     live = lax.dynamic_slice_in_dim(prompt_token_ids, request_prompt[0, 0], 1, 0)
     pieces = [None] * n_req
     last = (live, live)

time: 89.9 us -> 83.4 us (0.928)
  waiting for transfers between devices: 40.4 us -> 34.7 us
  local copies, waits for them, and re-layouts: 4.81 us -> 1.84 us
  Pallas kernels: 10.3 us -> 12.1 us
    ppermute x29 -> x28, waiting for transfers between devices: 40.4 us -> 34.7 us  [swap(): return lax.ppermute(block, axis, [(i, i ^ step) for i in range(size)])]
    unnamed x28 -> x24, local copies, waits for them, and re-layouts: 4.63 us -> 1.66 us
    pallas_call x16, Pallas kernels: 6.61 us -> 8.43 us  [call(): pl.pallas_call(kernel, out_shape=outs, in_specs=specs if specs is not Non...]
    ppermute x29 -> x28, starting transfers between devices: 32.5 us -> 33 us  [swap(): return lax.ppermute(block, axis, [(i, i ^ step) for i in range(size)])]
  transfers between devices with their start and end apart: 29 -> 28, of which waited for: 14 -> 15; matrix products, arithmetic and copies ran while one was open for 0% -> 0% of each run, Pallas kernels for 5% -> 6%
where the time goes in v6:
time: 83.4 us; the launch traced here: 83.2 us
  waiting for transfers between devices  34.7 us (42%)
  starting transfers between devices  33 us (40%)
  Pallas kernels  12.1 us (15%)
  local copies, waits for them, and re-layouts  1.84 us (2%)
  between operations  1.59 us (2%)
    ppermute x28, waiting for transfers between devices, swap(): return lax.ppermute(block, axis, [(i, i ^ step) for i in range(size)])  34.7 us
    ppermute x28, starting transfers between devices, swap(): return lax.ppermute(block, axis, [(i, i ^ step) for i in range(size)])  33 us
    pallas_call x16, Pallas kernels, call(): pl.pallas_call(kernel, out_shape=outs, in_specs=specs if specs is not Non...  8.43 us
    pallas_call x4, Pallas kernels, per_device_heads(): pl.pallas_call(functools.partial(heads_kernel, HDIM ** (-0.5)), grid=(1,)...  3.66 us
  transfers between devices with their start and end apart: 28, of which 15 were waited for; matrix products, arithmetic and copies ran while one was open for 0% of the time, Pallas kernels for 6%

profile of v6, /device:TPU:0, one launch (start us, length us, event | category | flops | bytes accessed | tf_op | source)
XLA Modules:
  0.0 83.2 jit_solution(14784475746980111602)
XLA Ops:
  0.0 0.9 %copy-done.7 = bf16[1,128,256]{2,1,0:T(8,128)(2,1)S(1)} copy-done((bf16[1,128,256]{2,1,0:T(8,128)(2,1)S(1)}, bf16[1,128,256]{2,1,0:T(8,128)(2,1)}, u32[]{:S(2)}) %copy-start.7) | copy-done | bytes 65560
  1.6 3.6 %context.1 = (bf16[1552,128]{1,0:T(8,128)(2,1)S(1)}, f32[1536,128]{1,0:T(8,128)S(1)}, f32[8,128]{1,0:T(8,128)S(1)}) custom-call(bf16[128,256]{1,0:T(8,128)(2,1)S(1)} %bitcast.22, bf16[256,3072]{1,0:T(8,128)(2,1)} %w_hbm.1, bf16[192]{0:T(256)(128)(2,1)S(1)} %copy-done.8), custom_call_target="tpu_custom_call" | custom-call | tf_op jit(solution)/shard_map/context/pallas_call | solution.py:281
  5.7 1.4 %collective-permute-done.got_ref = bf16[1552,128]{1,0:T(8,128)(2,1)S(1)} collective-permute-done((bf16[1552,128]{1,0:T(8,128)(2,1)S(1)}, bf16[1552,128]{1,0:T(8,128)(2,1)S(1)}, u32[]{:S(2)}, u32[]{:S(2)}) %collective-permute-start) | collective-permute-done | bytes 397344 | tf_op jit(solution)/shard_map/ppermute | solution.py:17
  7.2 2.9 %collective-permute-start.1 = (bf16[784,128]{1,0:T(8,128)(2,1)S(1)}, bf16[784,128]{1,0:T(8,128)(2,1)S(1)}, u32[]{:S(2)}, u32[]{:S(2)}) collective-permute-start(bf16[784,128]{1,0:T(8,128)(2,1)S(1)} %get-tuple-element.50), channel_id=1, source_target_pairs={{0,2},{1,3},{2,0},{3,1},{4,6},{5,7},{6,4},{7,5},{8,10},{9,11},{10,... | collective-permute-start | bytes 602120 | tf_op jit(solution)/shard_map/ppermute | solution.py:17
  10.4 1.6 %collective-permute-start.7 = (bf16[4,64,1536]{2,1,0:T(8,128)(2,1)S(1)}, bf16[4,64,1536]{2,1,0:T(8,128)(2,1)S(1)}, u32[]{:S(2)}, u32[]{:S(2)}) collective-permute-start(bf16[4,64,1536]{2,1,0:T(8,128)(2,1)S(1)} %image_pack.1), channel_id=1, source_target_pairs={{0,4},{4,0},{1,5},{5,1},{2,6},{6,2},{3,7},{7,3},{8,12},{12,8},{9,1... | collective-permute-start | bytes 2359304 | tf_op jit(solution)/shard_map/ppermute | solution.py:17
  12.2 3.2 %collective-permute-done.1.got_ref = bf16[784,128]{1,0:T(8,128)(2,1)S(1)} collective-permute-done((bf16[784,128]{1,0:T(8,128)(2,1)S(1)}, bf16[784,128]{1,0:T(8,128)(2,1)S(1)}, u32[]{:S(2)}, u32[]{:S(2)}) %collective-permute-start.1) | collective-permute-done | bytes 200736 | tf_op jit(solution)/shard_map/ppermute | solution.py:17
  15.5 1.8 %collective-permute-start.2 = (bf16[2,192,768]{2,1,0:T(8,128)(2,1)S(1)}, bf16[2,192,768]{2,1,0:T(8,128)(2,1)S(1)}, u32[]{:S(2)}, u32[]{:S(2)}) collective-permute-start(bf16[2,192,768]{2,1,0:T(8,128)(2,1)S(1)} %get-tuple-element.54.refs_0_), channel_id=1, source_target_pairs={{0,2},{1,3},{2,0},{3,1},{4,6},{5,7},{6,4},{7,5},{8,10},{9,11},{10,... | collective-permute-start | bytes 1769480 | tf_op jit(solution)/shard_map/ppermute | solution.py:17
  17.3 2.6 %collective-permute-start.3 = (bf16[208,128]{1,0:T(8,128)(2,1)S(1)}, bf16[208,128]{1,0:T(8,128)(2,1)S(1)}, u32[]{:S(2)}, u32[]{:S(2)}) collective-permute-start(bf16[208,128]{1,0:T(8,128)(2,1)S(1)} %get-tuple-element.56), channel_id=1, source_target_pairs={{0,16},{8,24},{16,0},{24,8},{1,17},{9,25},{17,1},{25,9},{2,18},{10... | collective-permute-start | bytes 159752 | tf_op jit(solution)/shard_map/ppermute | solution.py:17
  19.9 1.3 %collective-permute-start.4 = (bf16[208,128]{1,0:T(8,128)(2,1)S(1)}, bf16[208,128]{1,0:T(8,128)(2,1)S(1)}, u32[]{:S(2)}, u32[]{:S(2)}) collective-permute-start(bf16[208,128]{1,0:T(8,128)(2,1)S(1)} %get-tuple-element.57), channel_id=1, source_target_pairs={{0,24},{8,16},{16,8},{24,0},{1,25},{9,17},{17,9},{25,1},{2,26},{10... | collective-permute-start | bytes 159752 | tf_op jit(solution)/shard_map/ppermute | solution.py:17
  22.8 3.1 %collective-permute-done.4.refs_1_ = bf16[208,128]{1,0:T(8,128)(2,1)S(1)} collective-permute-done((bf16[208,128]{1,0:T(8,128)(2,1)S(1)}, bf16[208,128]{1,0:T(8,128)(2,1)S(1)}, u32[]{:S(2)}, u32[]{:S(2)}) %collective-permute-start.4) | collective-permute-done | bytes 53280 | tf_op jit(solution)/shard_map/ppermute | solution.py:17
  26.2 1.6 %collective-permute-start.6 = (bf16[208,128]{1,0:T(8,128)(2,1)S(1)}, bf16[208,128]{1,0:T(8,128)(2,1)S(1)}, u32[]{:S(2)}, u32[]{:S(2)}) collective-permute-start(bf16[208,128]{1,0:T(8,128)(2,1)S(1)} %centre.1.own_ref), channel_id=1, source_target_pairs={{0,4},{4,0},{1,5},{5,1},{2,6},{6,2},{3,7},{7,3},{8,12},{12,8},{9,1... | collective-permute-start | bytes 159752 | tf_op jit(solution)/shard_map/ppermute | solution.py:17
  27.8 3.1 %collective-permute-done.6.got_ref = bf16[208,128]{1,0:T(8,128)(2,1)S(1)} collective-permute-done((bf16[208,128]{1,0:T(8,128)(2,1)S(1)}, bf16[208,128]{1,0:T(8,128)(2,1)S(1)}, u32[]{:S(2)}, u32[]{:S(2)}) %collective-permute-start.6) | collective-permute-done | bytes 53280 | tf_op jit(solution)/shard_map/ppermute | solution.py:17
  31.1 1.0 %collective-permute-start.9 = (bf16[416,128]{1,0:T(8,128)(2,1)S(1)}, bf16[416,128]{1,0:T(8,128)(2,1)S(1)}, u32[]{:S(2)}, u32[]{:S(2)}) collective-permute-start(bf16[416,128]{1,0:T(8,128)(2,1)S(1)} %join.1.dep_ref.refs_0_), channel_id=1, source_target_pairs={{0,2},{1,3},{2,0},{3,1},{4,6},{5,7},{6,4},{7,5},{8,10},{9,11},{10,... | collective-permute-start | bytes 319496 | tf_op jit(solution)/shard_map/ppermute | solution.py:17
  33.3 3.6 %collective-permute-done.9.refs_1_ = bf16[416,128]{1,0:T(8,128)(2,1)S(1)} collective-permute-done((bf16[416,128]{1,0:T(8,128)(2,1)S(1)}, bf16[416,128]{1,0:T(8,128)(2,1)S(1)}, u32[]{:S(2)}, u32[]{:S(2)}) %collective-permute-start.9) | collective-permute-done | bytes 106528 | tf_op jit(solution)/shard_map/ppermute | solution.py:17
  36.9 1.4 %collective-permute-done.10.refs_2_ = bf16[416,128]{1,0:T(8,128)(2,1)S(1)} collective-permute-done((bf16[416,128]{1,0:T(8,128)(2,1)S(1)}, bf16[416,128]{1,0:T(8,128)(2,1)S(1)}, u32[]{:S(2)}, u32[]{:S(2)}) %collective-permute-start.10) | collective-permute-done | bytes 106528 | tf_op jit(solution)/shard_map/ppermute | solution.py:17
  38.3 1.2 %project.1 = (s32[8]{0:T(128)S(1)}, f32[400,128]{1,0:T(8,128)S(1)}, bf16[400,128]{1,0:T(8,128)(2,1)S(1)}, bf16[400,128]{1,0:T(8,128)(2,1)S(1)}, bf16[400,128]{1,0:T(8,128)(2,1)S(1)}) custom-call(bf16[192,768]{1,0:T(8,128)(2,1)S(1)} %get-tuple-element.45.own_ref, bf16[192,768]{1,0:T(8,128)(2,1)S(1)} %get-tuple-element.59.pair_ref, ...), custom_call_target="tpu_custom_call" | custom-call | tf_op jit(solution)/shard_map/project/pallas_call | solution.py:281
  39.6 1.0 %collective-permute-start.12 = (bf16[128,1536]{1,0:T(8,128)(2,1)S(1)}, bf16[128,1536]{1,0:T(8,128)(2,1)S(1)}, u32[]{:S(2)}, u32[]{:S(2)}) collective-permute-start(bf16[128,1536]{1,0:T(8,128)(2,1)S(1)} %maps_pack.1.own_ref.refs_0_), channel_id=1, source_target_pairs={{0,2},{1,3},{2,0},{3,1},{4,6},{5,7},{6,4},{7,5},{8,10},{9,11},{10,... | collective-permute-start | bytes 1179656 | tf_op jit(solution)/shard_map/ppermute | solution.py:17
  40.6 2.6 %collective-permute-start.13 = (bf16[400,128]{1,0:T(8,128)(2,1)S(1)}, bf16[400,128]{1,0:T(8,128)(2,1)S(1)}, u32[]{:S(2)}, u32[]{:S(2)}) collective-permute-start(bf16[400,128]{1,0:T(8,128)(2,1)S(1)} %get-tuple-element.63), channel_id=1, source_target_pairs={{0,16},{8,24},{16,0},{24,8},{1,17},{9,25},{17,1},{25,9},{2,18},{10... | collective-permute-start | bytes 307208 | tf_op jit(solution)/shard_map/ppermute | solution.py:17
  43.2 1.3 %collective-permute-start.14 = (bf16[400,128]{1,0:T(8,128)(2,1)S(1)}, bf16[400,128]{1,0:T(8,128)(2,1)S(1)}, u32[]{:S(2)}, u32[]{:S(2)}) collective-permute-start(bf16[400,128]{1,0:T(8,128)(2,1)S(1)} %get-tuple-element.64), channel_id=1, source_target_pairs={{0,24},{8,16},{16,8},{24,0},{1,25},{9,17},{17,9},{25,1},{2,26},{10... | collective-permute-start | bytes 307208 | tf_op jit(solution)/shard_map/ppermute | solution.py:17
  44.8 6.9 %collective-permute-done.13.refs_0_ = bf16[400,128]{1,0:T(8,128)(2,1)S(1)} collective-permute-done((bf16[400,128]{1,0:T(8,128)(2,1)S(1)}, bf16[400,128]{1,0:T(8,128)(2,1)S(1)}, u32[]{:S(2)}, u32[]{:S(2)}) %collective-permute-start.13) | collective-permute-done | bytes 102432 | tf_op jit(solution)/shard_map/ppermute | solution.py:17
  53.0 3.5 %collective-permute-start.18 = (bf16[64,768]{1,0:T(8,128)(2,1)S(1)}, bf16[64,768]{1,0:T(8,128)(2,1)S(1)}, u32[]{:S(2)}, u32[]{:S(2)}) collective-permute-start(bf16[64,768]{1,0:T(8,128)(2,1)S(1)} %finish.1.dep_ref.refs_0_), channel_id=1, source_target_pairs={{0,16},{8,24},{16,0},{24,8},{1,17},{9,25},{17,1},{25,9},{2,18},{10... | collective-permute-start | bytes 294920 | tf_op jit(solution)/shard_map/ppermute | solution.py:17
  57.4 1.5 %collective-permute-start.17 = (f32[2,64,64]{2,1,0:T(8,128)S(1)}, f32[2,64,64]{2,1,0:T(8,128)S(1)}, u32[]{:S(2)}, u32[]{:S(2)}) collective-permute-start(f32[2,64,64]{2,1,0:T(8,128)S(1)} %get-tuple-element.66.low_ref), channel_id=1, source_target_pairs={{0,4},{4,0},{1,5},{5,1},{2,6},{6,2},{3,7},{7,3},{8,12},{12,8},{9,1... | collective-permute-start | bytes 98312 | tf_op jit(solution)/shard_map/ppermute | solution.py:17
  58.9 2.8 %collective-permute-done.17.other_ref = f32[2,64,64]{2,1,0:T(8,128)S(1)} collective-permute-done((f32[2,64,64]{2,1,0:T(8,128)S(1)}, f32[2,64,64]{2,1,0:T(8,128)S(1)}, u32[]{:S(2)}, u32[]{:S(2)}) %collective-permute-start.17) | collective-permute-done | bytes 32800 | tf_op jit(solution)/shard_map/ppermute | solution.py:17
  62.0 2.4 %collective-permute-done.18.refs_1_ = bf16[64,768]{1,0:T(8,128)(2,1)S(1)} collective-permute-done((bf16[64,768]{1,0:T(8,128)(2,1)S(1)}, bf16[64,768]{1,0:T(8,128)(2,1)S(1)}, u32[]{:S(2)}, u32[]{:S(2)}) %collective-permute-start.18) | collective-permute-done | bytes 98336 | tf_op jit(solution)/shard_map/ppermute | solution.py:17
  64.4 1.1 %collective-permute-done.20.refs_3_ = bf16[64,768]{1,0:T(8,128)(2,1)S(1)} collective-permute-done((bf16[64,768]{1,0:T(8,128)(2,1)S(1)}, bf16[64,768]{1,0:T(8,128)(2,1)S(1)}, u32[]{:S(2)}, u32[]{:S(2)}) %collective-permute-start.20) | collective-permute-done | bytes 98336 | tf_op jit(solution)/shard_map/ppermute | solution.py:17
  66.3 1.1 %collective-permute-start.24 = (bf16[128,768]{1,0:T(8,128)(2,1)S(1)}, bf16[128,768]{1,0:T(8,128)(2,1)S(1)}, u32[]{:S(2)}, u32[]{:S(2)}) collective-permute-start(bf16[128,768]{1,0:T(8,128)(2,1)S(1)} %get-tuple-element.77), channel_id=1, source_target_pairs={{0,2},{1,3},{2,0},{3,1},{4,6},{5,7},{6,4},{7,5},{8,10},{9,11},{10,... | collective-permute-start | bytes 589832 | tf_op jit(solution)/shard_map/ppermute | solution.py:17
  69.1 1.6 %collective-permute-start.21 = (bf16[64,384]{1,0:T(8,128)(2,1)S(1)}, bf16[64,384]{1,0:T(8,128)(2,1)S(1)}, u32[]{:S(2)}, u32[]{:S(2)}) collective-permute-start(bf16[64,384]{1,0:T(8,128)(2,1)S(1)} %get-tuple-element.73), channel_id=1, source_target_pairs={{0,4},{4,0},{1,5},{5,1},{2,6},{6,2},{3,7},{7,3},{8,12},{12,8},{9,1... | collective-permute-start | bytes 147464 | tf_op jit(solution)/shard_map/ppermute | solution.py:17
  72.2 1.1 %collective-permute-done.21.refs_1_ = bf16[64,384]{1,0:T(8,128)(2,1)S(1)} collective-permute-done((bf16[64,384]{1,0:T(8,128)(2,1)S(1)}, bf16[64,384]{1,0:T(8,128)(2,1)S(1)}, u32[]{:S(2)}, u32[]{:S(2)}) %collective-permute-start.21) | collective-permute-done | bytes 49184 | tf_op jit(solution)/shard_map/ppermute | solution.py:17
  74.1 0.9 %heads.6 = (bf16[64,384]{1,0:T(8,128)(2,1)S(1)}, bf16[64,384]{1,0:T(8,128)(2,1)S(1)}) custom-call(s32[1,128]{1,0:T(1,128)S(1)} %constant_dynamic-slice_fusion.live_ref.refs_0_.refs_1_, bf16[128,768]{1,0:T(8,128)(2,1)S(1)} %collective-permute-done.24.text_ref, bf16[4,128,384]{2,1,0:T(8,128)(2,1)S(1)} %get-tuple-element.70.q_ref, ...), custom_call_target="tpu_custom_call" | custom-call | tf_op jit(solution)/shard_map/heads/pallas_call | solution.py:855
  75.0 1.6 %collective-permute-start.25 = (bf16[64,384]{1,0:T(8,128)(2,1)S(1)}, bf16[64,384]{1,0:T(8,128)(2,1)S(1)}, u32[]{:S(2)}, u32[]{:S(2)}) collective-permute-start(bf16[64,384]{1,0:T(8,128)(2,1)S(1)} %get-tuple-element.79), channel_id=1, source_target_pairs={{0,4},{4,0},{1,5},{5,1},{2,6},{6,2},{3,7},{7,3},{8,12},{12,8},{9,1... | collective-permute-start | bytes 147464 | tf_op jit(solution)/shard_map/ppermute | solution.py:17
  78.3 1.6 %collective-permute-start.27 = (bf16[64,384]{1,0:T(8,128)(2,1)S(1)}, bf16[64,384]{1,0:T(8,128)(2,1)S(1)}, u32[]{:S(2)}, u32[]{:S(2)}) collective-permute-start(bf16[64,384]{1,0:T(8,128)(2,1)S(1)} %get-tuple-element.82), channel_id=1, source_target_pairs={{0,4},{4,0},{1,5},{5,1},{2,6},{6,2},{3,7},{7,3},{8,12},{12,8},{9,1... | collective-permute-start | bytes 147464 | tf_op jit(solution)/shard_map/ppermute | solution.py:17
  79.9 2.6 %collective-permute-done.27.refs_7_ = bf16[64,384]{1,0:T(8,128)(2,1)S(1)} collective-permute-done((bf16[64,384]{1,0:T(8,128)(2,1)S(1)}, bf16[64,384]{1,0:T(8,128)(2,1)S(1)}, u32[]{:S(2)}, u32[]{:S(2)}) %collective-permute-start.27) | collective-permute-done | bytes 49184 | tf_op jit(solution)/shard_map/ppermute | solution.py:17
  (73 shorter events, 13.7 us)
Async XLA Ops:
  0.0 68.2 %copy-start = (s32[2,128]{1,0:T(2,128)S(1)}, s32[2,128]{1,0:T(2,128)}, u32[]{:S(2)}) copy-start(s32[2,128]{1,0:T(2,128)} %param.16) | copy-start | bytes 3076
  5.2 1.9 %collective-permute-start = (bf16[1552,128]{1,0:T(8,128)(2,1)S(1)}, bf16[1552,128]{1,0:T(8,128)(2,1)S(1)}, u32[]{:S(2)}, u32[]{:S(2)}) collective-permute-start(bf16[1552,128]{1,0:T(8,128)(2,1)S(1)} %get-tuple-element.44.dep_ref), channel_id=1, source_target_pairs={{0,1},{1,0},{2,3},{3,2},{4,5},{5,4},{6,7},{7,6},{8,9},{9,8},{10,11... | collective-permute-start | bytes 1191944 | tf_op jit(solution)/shard_map/ppermute | solution.py:17
  7.2 8.2 %collective-permute-start.1 = (bf16[784,128]{1,0:T(8,128)(2,1)S(1)}, bf16[784,128]{1,0:T(8,128)(2,1)S(1)}, u32[]{:S(2)}, u32[]{:S(2)}) collective-permute-start(bf16[784,128]{1,0:T(8,128)(2,1)S(1)} %get-tuple-element.50), channel_id=1, source_target_pairs={{0,2},{1,3},{2,0},{3,1},{4,6},{5,7},{6,4},{7,5},{8,10},{9,11},{10,... | collective-permute-start | bytes 602120 | tf_op jit(solution)/shard_map/ppermute | solution.py:17
  10.4 20.5 %collective-permute-start.7 = (bf16[4,64,1536]{2,1,0:T(8,128)(2,1)S(1)}, bf16[4,64,1536]{2,1,0:T(8,128)(2,1)S(1)}, u32[]{:S(2)}, u32[]{:S(2)}) collective-permute-start(bf16[4,64,1536]{2,1,0:T(8,128)(2,1)S(1)} %image_pack.1), channel_id=1, source_target_pairs={{0,4},{4,0},{1,5},{5,1},{2,6},{6,2},{3,7},{7,3},{8,12},{12,8},{9,1... | collective-permute-start | bytes 2359304 | tf_op jit(solution)/shard_map/ppermute | solution.py:17
  15.5 24.0 %copy-start.5 = (bf16[1,3072,64]{1,2,0:T(8,128)(2,1)S(1)}, bf16[1,3072,64]{1,2,0:T(8,128)(2,1)}, u32[]{:S(2)}) copy-start(bf16[1,3072,64]{1,2,0:T(8,128)(2,1)} %param.25) | copy-start | bytes 1179652
  15.5 24.0 %copy-start.6 = (bf16[1,64,3072]{2,1,0:T(8,128)(2,1)S(1)}, bf16[1,64,3072]{2,1,0:T(8,128)(2,1)}, u32[]{:S(2)}) copy-start(bf16[1,64,3072]{2,1,0:T(8,128)(2,1)} %param.26) | copy-start | bytes 1179652
  15.5 15.4 %collective-permute-start.2 = (bf16[2,192,768]{2,1,0:T(8,128)(2,1)S(1)}, bf16[2,192,768]{2,1,0:T(8,128)(2,1)S(1)}, u32[]{:S(2)}, u32[]{:S(2)}) collective-permute-start(bf16[2,192,768]{2,1,0:T(8,128)(2,1)S(1)} %get-tuple-element.54.refs_0_), channel_id=1, source_target_pairs={{0,2},{1,3},{2,0},{3,1},{4,6},{5,7},{6,4},{7,5},{8,10},{9,11},{10,... | collective-permute-start | bytes 1769480 | tf_op jit(solution)/shard_map/ppermute | solution.py:17
  17.3 5.5 %collective-permute-start.3 = (bf16[208,128]{1,0:T(8,128)(2,1)S(1)}, bf16[208,128]{1,0:T(8,128)(2,1)S(1)}, u32[]{:S(2)}, u32[]{:S(2)}) collective-permute-start(bf16[208,128]{1,0:T(8,128)(2,1)S(1)} %get-tuple-element.56), channel_id=1, source_target_pairs={{0,16},{8,24},{16,0},{24,8},{1,17},{9,25},{17,1},{25,9},{2,18},{10... | collective-permute-start | bytes 159752 | tf_op jit(solution)/shard_map/ppermute | solution.py:17
  19.9 6.0 %collective-permute-start.4 = (bf16[208,128]{1,0:T(8,128)(2,1)S(1)}, bf16[208,128]{1,0:T(8,128)(2,1)S(1)}, u32[]{:S(2)}, u32[]{:S(2)}) collective-permute-start(bf16[208,128]{1,0:T(8,128)(2,1)S(1)} %get-tuple-element.57), channel_id=1, source_target_pairs={{0,24},{8,16},{16,8},{24,0},{1,25},{9,17},{17,9},{25,1},{2,26},{10... | collective-permute-start | bytes 159752 | tf_op jit(solution)/shard_map/ppermute | solution.py:17
  21.3 4.7 %collective-permute-start.5 = (bf16[208,128]{1,0:T(8,128)(2,1)S(1)}, bf16[208,128]{1,0:T(8,128)(2,1)S(1)}, u32[]{:S(2)}, u32[]{:S(2)}) collective-permute-start(bf16[208,128]{1,0:T(8,128)(2,1)S(1)} %get-tuple-element.58), channel_id=1, source_target_pairs={{0,8},{8,0},{16,24},{24,16},{1,9},{9,1},{17,25},{25,17},{2,10},{10... | collective-permute-start | bytes 159752 | tf_op jit(solution)/shard_map/ppermute | solution.py:17
  26.2 18.6 %copy-start.10 = (bf16[6144]{0:T(1024)(128)(2,1)S(1)}, bf16[6144]{0:T(1024)(128)(2,1)}, u32[]{:S(2)}) copy-start(bf16[6144]{0:T(1024)(128)(2,1)} %param.22) | copy-start | bytes 36868
  26.2 4.6 %collective-permute-start.6 = (bf16[208,128]{1,0:T(8,128)(2,1)S(1)}, bf16[208,128]{1,0:T(8,128)(2,1)S(1)}, u32[]{:S(2)}, u32[]{:S(2)}) collective-permute-start(bf16[208,128]{1,0:T(8,128)(2,1)S(1)} %centre.1.own_ref), channel_id=1, source_target_pairs={{0,4},{4,0},{1,5},{5,1},{2,6},{6,2},{3,7},{7,3},{8,12},{12,8},{9,1... | collective-permute-start | bytes 159752 | tf_op jit(solution)/shard_map/ppermute | solution.py:17
  31.0 7.3 %collective-permute-start.8 = (bf16[2,192,768]{2,1,0:T(8,128)(2,1)S(1)}, bf16[2,192,768]{2,1,0:T(8,128)(2,1)S(1)}, u32[]{:S(2)}, u32[]{:S(2)}) collective-permute-start(bf16[2,192,768]{2,1,0:T(8,128)(2,1)S(1)} %get-tuple-element.60), channel_id=1, source_target_pairs={{0,1},{1,0},{2,3},{3,2},{4,5},{5,4},{6,7},{7,6},{8,9},{9,8},{10,11... | collective-permute-start | bytes 1769480 | tf_op jit(solution)/shard_map/ppermute | solution.py:17
  31.1 5.8 %collective-permute-start.9 = (bf16[416,128]{1,0:T(8,128)(2,1)S(1)}, bf16[416,128]{1,0:T(8,128)(2,1)S(1)}, u32[]{:S(2)}, u32[]{:S(2)}) collective-permute-start(bf16[416,128]{1,0:T(8,128)(2,1)S(1)} %join.1.dep_ref.refs_0_), channel_id=1, source_target_pairs={{0,2},{1,3},{2,0},{3,1},{4,6},{5,7},{6,4},{7,5},{8,10},{9,11},{10,... | collective-permute-start | bytes 319496 | tf_op jit(solution)/shard_map/ppermute | solution.py:17
  32.1 6.2 %collective-permute-start.10 = (bf16[416,128]{1,0:T(8,128)(2,1)S(1)}, bf16[416,128]{1,0:T(8,128)(2,1)S(1)}, u32[]{:S(2)}, u32[]{:S(2)}) collective-permute-start(bf16[416,128]{1,0:T(8,128)(2,1)S(1)} %join.1.dep_ref.refs_0_), channel_id=1, source_target_pairs={{0,3},{1,2},{2,1},{3,0},{4,7},{5,6},{6,5},{7,4},{8,11},{9,10},{10,... | collective-permute-start | bytes 319496 | tf_op jit(solution)/shard_map/ppermute | solution.py:17
  32.9 5.4 %collective-permute-start.11 = (bf16[416,128]{1,0:T(8,128)(2,1)S(1)}, bf16[416,128]{1,0:T(8,128)(2,1)S(1)}, u32[]{:S(2)}, u32[]{:S(2)}) collective-permute-start(bf16[416,128]{1,0:T(8,128)(2,1)S(1)} %join.1.dep_ref.refs_0_), channel_id=1, source_target_pairs={{0,1},{1,0},{2,3},{3,2},{4,5},{5,4},{6,7},{7,6},{8,9},{9,8},{10,11... | collective-permute-start | bytes 319496 | tf_op jit(solution)/shard_map/ppermute | solution.py:17
  39.6 12.5 %collective-permute-start.12 = (bf16[128,1536]{1,0:T(8,128)(2,1)S(1)}, bf16[128,1536]{1,0:T(8,128)(2,1)S(1)}, u32[]{:S(2)}, u32[]{:S(2)}) collective-permute-start(bf16[128,1536]{1,0:T(8,128)(2,1)S(1)} %maps_pack.1.own_ref.refs_0_), channel_id=1, source_target_pairs={{0,2},{1,3},{2,0},{3,1},{4,6},{5,7},{6,4},{7,5},{8,10},{9,11},{10,... | collective-permute-start | bytes 1179656 | tf_op jit(solution)/shard_map/ppermute | solution.py:17
  40.6 11.1 %collective-permute-start.13 = (bf16[400,128]{1,0:T(8,128)(2,1)S(1)}, bf16[400,128]{1,0:T(8,128)(2,1)S(1)}, u32[]{:S(2)}, u32[]{:S(2)}) collective-permute-start(bf16[400,128]{1,0:T(8,128)(2,1)S(1)} %get-tuple-element.63), channel_id=1, source_target_pairs={{0,16},{8,24},{16,0},{24,8},{1,17},{9,25},{17,1},{25,9},{2,18},{10... | collective-permute-start | bytes 307208 | tf_op jit(solution)/shard_map/ppermute | solution.py:17
  43.2 8.5 %collective-permute-start.14 = (bf16[400,128]{1,0:T(8,128)(2,1)S(1)}, bf16[400,128]{1,0:T(8,128)(2,1)S(1)}, u32[]{:S(2)}, u32[]{:S(2)}) collective-permute-start(bf16[400,128]{1,0:T(8,128)(2,1)S(1)} %get-tuple-element.64), channel_id=1, source_target_pairs={{0,24},{8,16},{16,8},{24,0},{1,25},{9,17},{17,9},{25,1},{2,26},{10... | collective-permute-start | bytes 307208 | tf_op jit(solution)/shard_map/ppermute | solution.py:17
  44.6 7.5 %collective-permute-start.15 = (bf16[400,128]{1,0:T(8,128)(2,1)S(1)}, bf16[400,128]{1,0:T(8,128)(2,1)S(1)}, u32[]{:S(2)}, u32[]{:S(2)}) collective-permute-start(bf16[400,128]{1,0:T(8,128)(2,1)S(1)} %get-tuple-element.65), channel_id=1, source_target_pairs={{0,8},{8,0},{16,24},{24,16},{1,9},{9,1},{17,25},{25,17},{2,10},{10... | collective-permute-start | bytes 307208 | tf_op jit(solution)/shard_map/ppermute | solution.py:17
  52.9 4.3 %collective-permute-start.16 = (bf16[128,1536]{1,0:T(8,128)(2,1)S(1)}, bf16[128,1536]{1,0:T(8,128)(2,1)S(1)}, u32[]{:S(2)}, u32[]{:S(2)}) collective-permute-start(bf16[128,1536]{1,0:T(8,128)(2,1)S(1)} %select.1), channel_id=1, source_target_pairs={{0,1},{1,0},{2,3},{3,2},{4,5},{5,4},{6,7},{7,6},{8,9},{9,8},{10,11... | collective-permute-start | bytes 1179656 | tf_op jit(solution)/shard_map/ppermute | solution.py:17
  53.0 11.4 %collective-permute-start.18 = (bf16[64,768]{1,0:T(8,128)(2,1)S(1)}, bf16[64,768]{1,0:T(8,128)(2,1)S(1)}, u32[]{:S(2)}, u32[]{:S(2)}) collective-permute-start(bf16[64,768]{1,0:T(8,128)(2,1)S(1)} %finish.1.dep_ref.refs_0_), channel_id=1, source_target_pairs={{0,16},{8,24},{16,0},{24,8},{1,17},{9,25},{17,1},{25,9},{2,18},{10... | collective-permute-start | bytes 294920 | tf_op jit(solution)/shard_map/ppermute | solution.py:17
  56.5 7.9 %collective-permute-start.19 = (bf16[64,768]{1,0:T(8,128)(2,1)S(1)}, bf16[64,768]{1,0:T(8,128)(2,1)S(1)}, u32[]{:S(2)}, u32[]{:S(2)}) collective-permute-start(bf16[64,768]{1,0:T(8,128)(2,1)S(1)} %finish.1.dep_ref.refs_0_), channel_id=1, source_target_pairs={{0,24},{8,16},{16,8},{24,0},{1,25},{9,17},{17,9},{25,1},{2,26},{10... | collective-permute-start | bytes 294920 | tf_op jit(solution)/shard_map/ppermute | solution.py:17
  56.9 8.5 %collective-permute-start.20 = (bf16[64,768]{1,0:T(8,128)(2,1)S(1)}, bf16[64,768]{1,0:T(8,128)(2,1)S(1)}, u32[]{:S(2)}, u32[]{:S(2)}) collective-permute-start(bf16[64,768]{1,0:T(8,128)(2,1)S(1)} %finish.1.dep_ref.refs_0_), channel_id=1, source_target_pairs={{0,8},{8,0},{16,24},{24,16},{1,9},{9,1},{17,25},{25,17},{2,10},{10... | collective-permute-start | bytes 294920 | tf_op jit(solution)/shard_map/ppermute | solution.py:17
  57.4 4.3 %collective-permute-start.17 = (f32[2,64,64]{2,1,0:T(8,128)S(1)}, f32[2,64,64]{2,1,0:T(8,128)S(1)}, u32[]{:S(2)}, u32[]{:S(2)}) collective-permute-start(f32[2,64,64]{2,1,0:T(8,128)S(1)} %get-tuple-element.66.low_ref), channel_id=1, source_target_pairs={{0,4},{4,0},{1,5},{5,1},{2,6},{6,2},{3,7},{7,3},{8,12},{12,8},{9,1... | collective-permute-start | bytes 98312 | tf_op jit(solution)/shard_map/ppermute | solution.py:17
  66.2 4.4 %collective-permute-start.22 = (bf16[128,768]{1,0:T(8,128)(2,1)S(1)}, bf16[128,768]{1,0:T(8,128)(2,1)S(1)}, u32[]{:S(2)}, u32[]{:S(2)}) collective-permute-start(bf16[128,768]{1,0:T(8,128)(2,1)S(1)} %get-tuple-element.74), channel_id=1, source_target_pairs={{0,1},{1,0},{2,3},{3,2},{4,5},{5,4},{6,7},{7,6},{8,9},{9,8},{10,11... | collective-permute-start | bytes 589832 | tf_op jit(solution)/shard_map/ppermute | solution.py:17
  66.3 7.8 %collective-permute-start.24 = (bf16[128,768]{1,0:T(8,128)(2,1)S(1)}, bf16[128,768]{1,0:T(8,128)(2,1)S(1)}, u32[]{:S(2)}, u32[]{:S(2)}) collective-permute-start(bf16[128,768]{1,0:T(8,128)(2,1)S(1)} %get-tuple-element.77), channel_id=1, source_target_pairs={{0,2},{1,3},{2,0},{3,1},{4,6},{5,7},{6,4},{7,5},{8,10},{9,11},{10,... | collective-permute-start | bytes 589832 | tf_op jit(solution)/shard_map/ppermute | solution.py:17
  67.4 9.9 %collective-permute-start.26 = (bf16[128,768]{1,0:T(8,128)(2,1)S(1)}, bf16[128,768]{1,0:T(8,128)(2,1)S(1)}, u32[]{:S(2)}, u32[]{:S(2)}) collective-permute-start(bf16[128,768]{1,0:T(8,128)(2,1)S(1)} %get-tuple-element.80), channel_id=1, source_target_pairs={{0,3},{1,2},{2,1},{3,0},{4,7},{5,6},{6,5},{7,4},{8,11},{9,10},{10,... | collective-permute-start | bytes 589832 | tf_op jit(solution)/shard_map/ppermute | solution.py:17
  69.1 4.2 %collective-permute-start.21 = (bf16[64,384]{1,0:T(8,128)(2,1)S(1)}, bf16[64,384]{1,0:T(8,128)(2,1)S(1)}, u32[]{:S(2)}, u32[]{:S(2)}) collective-permute-start(bf16[64,384]{1,0:T(8,128)(2,1)S(1)} %get-tuple-element.73), channel_id=1, source_target_pairs={{0,4},{4,0},{1,5},{5,1},{2,6},{6,2},{3,7},{7,3},{8,12},{12,8},{9,1... | collective-permute-start | bytes 147464 | tf_op jit(solution)/shard_map/ppermute | solution.py:17
  71.6 5.8 %collective-permute-start.23 = (bf16[64,384]{1,0:T(8,128)(2,1)S(1)}, bf16[64,384]{1,0:T(8,128)(2,1)S(1)}, u32[]{:S(2)}, u32[]{:S(2)}) collective-permute-start(bf16[64,384]{1,0:T(8,128)(2,1)S(1)} %get-tuple-element.76), channel_id=1, source_target_pairs={{0,4},{4,0},{1,5},{5,1},{2,6},{6,2},{3,7},{7,3},{8,12},{12,8},{9,1... | collective-permute-start | bytes 147464 | tf_op jit(solution)/shard_map/ppermute | solution.py:17
  75.0 4.9 %collective-permute-start.25 = (bf16[64,384]{1,0:T(8,128)(2,1)S(1)}, bf16[64,384]{1,0:T(8,128)(2,1)S(1)}, u32[]{:S(2)}, u32[]{:S(2)}) collective-permute-start(bf16[64,384]{1,0:T(8,128)(2,1)S(1)} %get-tuple-element.79), channel_id=1, source_target_pairs={{0,4},{4,0},{1,5},{5,1},{2,6},{6,2},{3,7},{7,3},{8,12},{12,8},{9,1... | collective-permute-start | bytes 147464 | tf_op jit(solution)/shard_map/ppermute | solution.py:17
  78.3 4.2 %collective-permute-start.27 = (bf16[64,384]{1,0:T(8,128)(2,1)S(1)}, bf16[64,384]{1,0:T(8,128)(2,1)S(1)}, u32[]{:S(2)}, u32[]{:S(2)}) collective-permute-start(bf16[64,384]{1,0:T(8,128)(2,1)S(1)} %get-tuple-element.82), channel_id=1, source_target_pairs={{0,4},{4,0},{1,5},{5,1},{2,6},{6,2},{3,7},{7,3},{8,12},{12,8},{9,1... | collective-permute-start | bytes 147464 | tf_op jit(solution)/shard_map/ppermute | solution.py:17
  (8 other events, 65.7 us)

commit v7 on v6

--- a/solution.py
+++ b/solution.py
@@ -264,7 +264,6 @@
 ANY = pl.BlockSpec(memory_space=pl.ANY)
 VMEM = pl.BlockSpec(memory_space=pltpu.VMEM)
 SMEM = pl.BlockSpec(memory_space=pltpu.SMEM)
-HBM = pl.BlockSpec(memory_space=pltpu.HBM)
 NT = (((1,), (1,)), ((), ()))
 TN = (((0,), (0,)), ((), ()))
 
@@ -308,30 +307,12 @@
     return rows[0:1] + rows[1:2]
 
 
-def context_kernel(
-    h_hbm, w_hbm, b_hbm, send_ref, keep_ref, stat_ref, h_ref, w_ref, b_ref, sems
-):
+def context_kernel(h_ref, w_ref, b_ref, send_ref, keep_ref, stat_ref):
     mine = lax.rem(lax.axis_index("req"), 2)
     features = b_ref.shape[0]
     pairs = w_ref.shape[1] // (2 * features)
-    count = sems.shape[0] - 2
-    chunk = w_ref.shape[1] // count
-    copies = [pltpu.make_async_copy(h_hbm, h_ref, sems.at[0])]
-    for i in range(count):
-        columns = pl.ds(i * chunk, chunk)
-        copies.append(
-            pltpu.make_async_copy(w_hbm.at[:, columns], w_ref.at[:, columns], sems.at[i + 1])
-        )
-    copies.append(pltpu.make_async_copy(b_hbm, b_ref, sems.at[count + 1]))
-    for copy in copies:
-        copy.start()
-    copies[0].wait()
-    arrived = 0
     total = jnp.zeros((1, h_ref.shape[0]), F32)
     for p in range(pairs):
-        while arrived * chunk < (p + 1) * 2 * features:
-            arrived += 1
-            copies[arrived].wait()
         product = jnp.dot(
             h_ref[...], w_ref[:, p * 2 * features : (p + 1) * 2 * features],
             preferred_element_type=F32,
@@ -341,7 +322,6 @@
         rows = slice(p * features, (p + 1) * features)
         keep_ref[rows] = jnp.where(mine == 0, low, high)
         send_ref[rows] = jnp.where(mine == 0, high, low).astype(BF16)
-    copies[-1].wait()
     stat = total + jnp.sum(b_ref[...].astype(F32))
     send_ref[pairs * features :] = stat_rows(stat)
     stat_ref[...] = jnp.broadcast_to(stat, stat_ref.shape)
@@ -374,7 +354,7 @@
     out_stat_ref[...] = jnp.broadcast_to(stat, out_stat_ref.shape)
 
 
-def centre_kernel(width, prompt_ref, adapter_ref, keep_ref, stat_ref, bias_ref, scale_ref, shift_ref, *refs):
+def centre_kernel(width, prompt_ref, dep_ref, keep_ref, stat_ref, bias_ref, scale_ref, shift_ref, *refs):
     got_refs, out_ref = refs[:-1], refs[-1]
     features, tokens = keep_ref.shape
     total = keep_ref[...] + bias_ref[...]
@@ -395,7 +375,6 @@
             piece = jnp.concatenate([piece, jnp.zeros((1, gap), F32)], axis=1)
         extra = jnp.where(row == 2 + j, piece, extra)
     extra = jnp.where(row == ROWS - 1, prompt_ref[0, 0].astype(F32), extra)
-    extra = jnp.where(row == ROWS - 2, adapter_ref[0, 0].astype(F32), extra)
     out_ref[features:] = extra.astype(BF16)
 
 
@@ -434,7 +413,6 @@
             shifts.append(jnp.concatenate(pieces, axis=1)[:, :features])
             if p == 0:
                 prompts_ref[k] = jnp.max(extra[ROWS - 1 : ROWS]).astype(jnp.int32)
-                prompts_ref[n_req + k] = jnp.max(extra[ROWS - 2 : ROWS - 1]).astype(jnp.int32)
         shifts.append(jnp.zeros((ROWS - n_seq, features), F32))
         left.append(jnp.concatenate(shifts, axis=0).astype(BF16))
         term = jnp.dot(
@@ -470,7 +448,7 @@
         send_ref[...] = rows_ref[at(e ^ (k + 1), step)].astype(BF16)
 
 
-def finish_kernel(n_req, model_width, dep_ref, image_ref, keep_ref, bias_ref, *refs):
+def finish_kernel(n_req, model_width, keep_ref, bias_ref, *refs):
     got_refs, out_ref = refs[:-1], refs[-1]
     r, s = lax.axis_index("req"), lax.axis_index("seq")
     size, width = out_ref.shape
@@ -556,18 +534,15 @@
         copy.wait()
 
 
-def select_kernel(ids_ref, own_ref, pair_ref, dep_ref, core_ref):
-    other = lax.rem((ids_ref[5] ^ lax.axis_index("req")) // 2, 2)
-    for k, ref in enumerate((own_ref, pair_ref)):
-        @pl.when(other == k)
-        def _():
-            core_ref[...] = ref[...]
+def join_maps_kernel(own_ref, core_ref, dep_ref, out_ref):
+    out_ref[0] = own_ref[...]
+    out_ref[1] = core_ref[...]
 
 
 def lowrank_kernel(part, adapter_ref, x_ref, got_ref, *refs):
-    map_refs, (out_ref, chosen_ref) = refs[:3], refs[3:]
-    other = adapter_ref[0, 0] ^ lax.axis_index("req")
-    place = jnp.where(lax.rem(other, 2) == 1, 2, other // 2)
+    own_ref, pair_ref, out_ref, chosen_ref = refs
+    map_refs = (own_ref.at[0], own_ref.at[1], pair_ref.at[0], pair_ref.at[1])
+    place = adapter_ref[0, 0] ^ lax.axis_index("req")
     rank = out_ref.shape[-1]
     for k, ref in enumerate(map_refs):
         @pl.when(place == k)
@@ -608,7 +583,7 @@
             ).astype(BF16)
 
 
-def heads_kernel(scale, live_ref, text_ref, q_ref, k_ref, v_ref, *refs):
+def heads_kernel(place, scale, live_ref, text_ref, q_ref, k_ref, v_ref, *refs):
     out_refs = refs[2:]
     live = live_ref[...] != 0
     half = q_ref.shape[2]
@@ -616,9 +591,9 @@
     for h in range(half // HDIM):
         cols = slice(h * HDIM, (h + 1) * HDIM)
         vals = slice(half + h * HDIM, half + (h + 1) * HDIM)
-        q = q_ref[0, :, cols]
+        q = q_ref[place, :, cols]
         st = lax.dot_general(q, text_ref[:, cols], NT, preferred_element_type=F32) * scale
-        si = lax.dot_general(q, k_ref[0, :, cols], NT, preferred_element_type=F32) * scale
+        si = lax.dot_general(q, k_ref[place, :, cols], NT, preferred_element_type=F32) * scale
         st = jnp.where(live, st, -jnp.inf)
         top = jnp.maximum(
             jnp.max(st, axis=1, keepdims=True), jnp.max(si, axis=1, keepdims=True)
@@ -628,7 +603,7 @@
         total = jnp.sum(wt, axis=1, keepdims=True) + jnp.sum(wi, axis=1, keepdims=True)
         mixed = jnp.dot(
             wt.astype(BF16), text_ref[:, vals], preferred_element_type=F32
-        ) + jnp.dot(wi.astype(BF16), v_ref[0, :, cols], preferred_element_type=F32)
+        ) + jnp.dot(wi.astype(BF16), v_ref[place, :, cols], preferred_element_type=F32)
         mixed = (mixed / total).astype(BF16)
         for i, out_ref in enumerate(out_refs):
             out_ref[:, cols] = mixed[i * size : (i + 1) * size]
@@ -685,18 +660,19 @@
             stat,
         ),
         (encoder_hidden[0], context_weight, context_bias),
-        [HBM] * 3,
-        [
-            pltpu.VMEM(encoder_hidden.shape[1:], BF16),
-            pltpu.VMEM(context_weight.shape, BF16),
-            pltpu.VMEM(context_bias.shape, BF16),
-            dma((2 + 2 * n_enc,)),
-        ],
         name="context",
-        vmem=52.65,
     )
     got = swap(send, "req", n_req, 1)
 
+    maps = call(
+        functools.partial(maps_kernel, part),
+        struct((2 * rank, part)),
+        (adapter_down_maps[0].T, adapter_up_maps[0], send),
+        [ANY] * 3,
+        [dma((2,))],
+        name="maps_pack",
+    )
+    maps_core = swap(maps, "req", n_req, 1)
     weight = struct((features, 2 * half))
     weight_own, weight_core, weight_pair = call(
         functools.partial(weight_kernel, n_req, part, inner),
@@ -751,7 +727,7 @@
         struct((features + ROWS, tokens)),
         (
             request_prompt,
-            adapter_of_request,
+            maps_core,
             keep,
             sums,
             bias_columns,
@@ -759,7 +735,7 @@
             modulation_shift,
             *arrived,
         ),
-        [SMEM] * 2 + [VMEM] * (5 + len(arrived)),
+        [SMEM, ANY] + [VMEM] * (5 + len(arrived)),
         name="centre",
     )
     joined = call(
@@ -783,7 +759,7 @@
     step = 2 * half // HDIM * size + ROWS
     ids, keep, *sends = call(
         functools.partial(project_kernel, n_seq, n_req, n_enc),
-        (struct((2 * n_req,), jnp.int32), struct((step, HDIM), F32))
+        (struct((n_req,), jnp.int32), struct((step, HDIM), F32))
         + tuple(struct((step, HDIM)) for _ in range(1, n_enc)),
         (weight_own, weight_own_pair, weight_next, joined, *payloads.values()),
         scratch=[pltpu.VMEM((n_enc * step, HDIM), F32)],
@@ -793,28 +769,21 @@
     arrived = partners(lambda k: sends[k - 1], "enc", n_enc).values()
 
     maps = call(
-        functools.partial(maps_kernel, part),
-        struct((2 * rank, part)),
-        (adapter_down_maps[0].T, adapter_up_maps[0], keep),
-        [ANY] * 3,
-        [dma((2,))],
-        name="maps_pack",
-    )
+        join_maps_kernel,
+        struct((2, 2 * rank, part)),
+        (maps, maps_core, joined),
+        [VMEM, VMEM, ANY],
+        name="maps_join",
+    )
+    maps = lax.optimization_barrier((maps, keep))[0]
     maps_pair = swap(maps, "req", n_req, 2)
 
     text = call(
         functools.partial(finish_kernel, n_req, model_width),
         struct((size, 2 * half)),
-        (maps_pair, image_got[0], keep, key_value_bias[None], *arrived),
-        [ANY] * 2 + [VMEM] * (2 + len(arrived)),
+        (keep, key_value_bias[None], *arrived),
+        [VMEM] * (2 + len(arrived)),
         name="finish",
-    )
-    maps_core = call(
-        select_kernel,
-        struct((2 * rank, part)),
-        (ids, maps, maps_pair, text),
-        [SMEM, VMEM, VMEM, ANY],
-        name="select",
     )
     low, chosen_maps = call(
         functools.partial(lowrank_kernel, part),
@@ -825,9 +794,8 @@
             image_got[0],
             maps,
             maps_pair,
-            swap(maps_core, "req", n_req, 1),
         ),
-        [SMEM] + [VMEM] * 5,
+        [SMEM] + [VMEM] * 4,
         name="lowrank",
     )
     arranged = struct((n_req, n_seq * image_rows, half))
@@ -840,7 +808,7 @@
     parts = partners(lambda k: text, "enc", n_enc)
     rows = call(
         functools.partial(choose_kernel, n_seq, n_enc),
-        tuple(struct((tokens, 2 * half)) for _ in range(n_req)),
+        [struct((tokens, 2 * half)) for _ in range(n_req)],
         (ids, image_values, text, *parts.values()),
         [SMEM, ANY] + [VMEM] * n_enc,
         name="choose",
@@ -850,17 +818,13 @@
     pieces = [None] * n_req
     last = (live, live)
     for k in range(n_req):
-        block = pl.BlockSpec((1, n_seq * image_rows, half), lambda i, k=k: (k, 0, 0))
-        whole = lambda shape: pl.BlockSpec(shape, lambda i: (0, 0))
-        mixed = pl.pallas_call(
-            functools.partial(heads_kernel, HDIM ** (-0.5)),
-            grid=(1,),
-            out_shape=[struct((image_rows, half)) for _ in range(n_seq)],
-            in_specs=[whole((1, tokens)), whole((tokens, 2 * half)), block, block, block, ANY, ANY],
-            out_specs=[whole((image_rows, half)) for _ in range(n_seq)],
-            compiler_params=pltpu.CompilerParams(vmem_limit_bytes=16 * 1024 * 1024),
+        mixed = call(
+            functools.partial(heads_kernel, k, HDIM ** (-0.5)),
+            [struct((image_rows, half))] * n_seq,
+            (live, rows[k], queries, image_keys, image_values, *last),
+            [VMEM] * 5 + [ANY] * 2,
             name="heads",
-        )(live, rows[k], queries, image_keys, image_values, *last)
+        )
         pieces[k] = [mixed[0], swap(mixed[1], "seq", n_seq, 1)]
         last = (mixed[0], pieces[k - 1][1] if k else live)
     result = call(

time: 83.4 us -> 80.7 us (0.968)
  Pallas kernels: 12.1 us -> 8.64 us
  local copies, waits for them, and re-layouts: 1.84 us -> 3.22 us
    pallas_call x4 -> x0, Pallas kernels: 3.66 us -> none  [per_device_heads(): pl.pallas_call(functools.partial(heads_kernel, HDIM ** (-0.5)), grid=(1,)...]
    unnamed x24 -> x28, local copies, waits for them, and re-layouts: 1.66 us -> 3.03 us
    pallas_call x16 -> x20, Pallas kernels: 8.43 us -> 8.64 us  [call(): pl.pallas_call(kernel, out_shape=outs, in_specs=specs if specs is not Non...]
  transfers between devices with their start and end apart: 28 -> 28, of which waited for: 15 -> 16; matrix products, arithmetic and copies ran while one was open for 0% -> 0% of each run, Pallas kernels for 6% -> 6%
where the time goes in v7:
time: 80.7 us; the launch traced here: 80.5 us
  waiting for transfers between devices  34 us (42%)
  starting transfers between devices  33 us (41%)
  Pallas kernels  8.64 us (11%)
  local copies, waits for them, and re-layouts  3.22 us (4%)
  between operations  1.59 us (2%)
    ppermute x28, waiting for transfers between devices, swap(): return lax.ppermute(block, axis, [(i, i ^ step) for i in range(size)])  34 us
    ppermute x28, starting transfers between devices, swap(): return lax.ppermute(block, axis, [(i, i ^ step) for i in range(size)])  33 us
    pallas_call x20, Pallas kernels, call(): pl.pallas_call(kernel, out_shape=outs, in_specs=specs if specs is not Non...  8.64 us
    unnamed x28, local copies, waits for them, and re-layouts  3.03 us
  transfers between devices with their start and end apart: 28, of which 16 were waited for; matrix products, arithmetic and copies ran while one was open for 0% of the time, Pallas kernels for 6%

profile of v7, /device:TPU:0, one launch (start us, length us, event | category | flops | bytes accessed | tf_op | source)
XLA Modules:
  0.0 80.5 jit_solution(13271533199253073683)
XLA Ops:
  0.0 1.5 %copy-done.3 = bf16[256,3072]{1,0:T(8,128)(2,1)S(1)} copy-done((bf16[256,3072]{1,0:T(8,128)(2,1)S(1)}, bf16[256,3072]{1,0:T(8,128)(2,1)}, u32[]{:S(2)}) %copy-start.3) | copy-done | bytes 1572888
  4.2 1.4 %collective-permute-done.got_ref = bf16[1552,128]{1,0:T(8,128)(2,1)S(1)} collective-permute-done((bf16[1552,128]{1,0:T(8,128)(2,1)S(1)}, bf16[1552,128]{1,0:T(8,128)(2,1)S(1)}, u32[]{:S(2)}, u32[]{:S(2)}) %collective-permute-start) | collective-permute-done | bytes 397344 | tf_op jit(solution)/shard_map/ppermute | solution.py:17
  5.7 3.0 %collective-permute-start.1 = (bf16[784,128]{1,0:T(8,128)(2,1)S(1)}, bf16[784,128]{1,0:T(8,128)(2,1)S(1)}, u32[]{:S(2)}, u32[]{:S(2)}) collective-permute-start(bf16[784,128]{1,0:T(8,128)(2,1)S(1)} %get-tuple-element.51), channel_id=1, source_target_pairs={{0,2},{1,3},{2,0},{3,1},{4,6},{5,7},{6,4},{7,5},{8,10},{9,11},{10,... | collective-permute-start | bytes 602120 | tf_op jit(solution)/shard_map/ppermute | solution.py:17
  8.8 1.6 %collective-permute-start.8 = (bf16[4,64,1536]{2,1,0:T(8,128)(2,1)S(1)}, bf16[4,64,1536]{2,1,0:T(8,128)(2,1)S(1)}, u32[]{:S(2)}, u32[]{:S(2)}) collective-permute-start(bf16[4,64,1536]{2,1,0:T(8,128)(2,1)S(1)} %image_pack.1), channel_id=1, source_target_pairs={{0,4},{4,0},{1,5},{5,1},{2,6},{6,2},{3,7},{7,3},{8,12},{12,8},{9,1... | collective-permute-start | bytes 2359304 | tf_op jit(solution)/shard_map/ppermute | solution.py:17
  10.9 3.0 %collective-permute-done.1.got_ref = bf16[784,128]{1,0:T(8,128)(2,1)S(1)} collective-permute-done((bf16[784,128]{1,0:T(8,128)(2,1)S(1)}, bf16[784,128]{1,0:T(8,128)(2,1)S(1)}, u32[]{:S(2)}, u32[]{:S(2)}) %collective-permute-start.1) | collective-permute-done | bytes 200736 | tf_op jit(solution)/shard_map/ppermute | solution.py:17
  14.0 1.8 %collective-permute-start.2 = (bf16[2,192,768]{2,1,0:T(8,128)(2,1)S(1)}, bf16[2,192,768]{2,1,0:T(8,128)(2,1)S(1)}, u32[]{:S(2)}, u32[]{:S(2)}) collective-permute-start(bf16[2,192,768]{2,1,0:T(8,128)(2,1)S(1)} %get-tuple-element.55.refs_0_), channel_id=1, source_target_pairs={{0,2},{1,3},{2,0},{3,1},{4,6},{5,7},{6,4},{7,5},{8,10},{9,11},{10,... | collective-permute-start | bytes 1769480 | tf_op jit(solution)/shard_map/ppermute | solution.py:17
  15.8 2.6 %collective-permute-start.4 = (bf16[208,128]{1,0:T(8,128)(2,1)S(1)}, bf16[208,128]{1,0:T(8,128)(2,1)S(1)}, u32[]{:S(2)}, u32[]{:S(2)}) collective-permute-start(bf16[208,128]{1,0:T(8,128)(2,1)S(1)} %get-tuple-element.57), channel_id=1, source_target_pairs={{0,16},{8,24},{16,0},{24,8},{1,17},{9,25},{17,1},{25,9},{2,18},{10... | collective-permute-start | bytes 159752 | tf_op jit(solution)/shard_map/ppermute | solution.py:17
  18.4 1.3 %collective-permute-start.5 = (bf16[208,128]{1,0:T(8,128)(2,1)S(1)}, bf16[208,128]{1,0:T(8,128)(2,1)S(1)}, u32[]{:S(2)}, u32[]{:S(2)}) collective-permute-start(bf16[208,128]{1,0:T(8,128)(2,1)S(1)} %get-tuple-element.58), channel_id=1, source_target_pairs={{0,24},{8,16},{16,8},{24,0},{1,25},{9,17},{17,9},{25,1},{2,26},{10... | collective-permute-start | bytes 159752 | tf_op jit(solution)/shard_map/ppermute | solution.py:17
  21.0 3.4 %collective-permute-done.5.refs_1_ = bf16[208,128]{1,0:T(8,128)(2,1)S(1)} collective-permute-done((bf16[208,128]{1,0:T(8,128)(2,1)S(1)}, bf16[208,128]{1,0:T(8,128)(2,1)S(1)}, u32[]{:S(2)}, u32[]{:S(2)}) %collective-permute-start.5) | collective-permute-done | bytes 53280 | tf_op jit(solution)/shard_map/ppermute | solution.py:17
  24.7 1.6 %collective-permute-start.7 = (bf16[208,128]{1,0:T(8,128)(2,1)S(1)}, bf16[208,128]{1,0:T(8,128)(2,1)S(1)}, u32[]{:S(2)}, u32[]{:S(2)}) collective-permute-start(bf16[208,128]{1,0:T(8,128)(2,1)S(1)} %centre.1.own_ref), channel_id=1, source_target_pairs={{0,4},{4,0},{1,5},{5,1},{2,6},{6,2},{3,7},{7,3},{8,12},{12,8},{9,1... | collective-permute-start | bytes 159752 | tf_op jit(solution)/shard_map/ppermute | solution.py:17
  26.2 3.1 %collective-permute-done.7.got_ref = bf16[208,128]{1,0:T(8,128)(2,1)S(1)} collective-permute-done((bf16[208,128]{1,0:T(8,128)(2,1)S(1)}, bf16[208,128]{1,0:T(8,128)(2,1)S(1)}, u32[]{:S(2)}, u32[]{:S(2)}) %collective-permute-start.7) | collective-permute-done | bytes 53280 | tf_op jit(solution)/shard_map/ppermute | solution.py:17
  29.5 1.0 %collective-permute-start.10 = (bf16[416,128]{1,0:T(8,128)(2,1)S(1)}, bf16[416,128]{1,0:T(8,128)(2,1)S(1)}, u32[]{:S(2)}, u32[]{:S(2)}) collective-permute-start(bf16[416,128]{1,0:T(8,128)(2,1)S(1)} %join.1.dep_ref.refs_0_), channel_id=1, source_target_pairs={{0,2},{1,3},{2,0},{3,1},{4,6},{5,7},{6,4},{7,5},{8,10},{9,11},{10,... | collective-permute-start | bytes 319496 | tf_op jit(solution)/shard_map/ppermute | solution.py:17
  31.8 3.6 %collective-permute-done.10.refs_1_ = bf16[416,128]{1,0:T(8,128)(2,1)S(1)} collective-permute-done((bf16[416,128]{1,0:T(8,128)(2,1)S(1)}, bf16[416,128]{1,0:T(8,128)(2,1)S(1)}, u32[]{:S(2)}, u32[]{:S(2)}) %collective-permute-start.10) | collective-permute-done | bytes 106528 | tf_op jit(solution)/shard_map/ppermute | solution.py:17
  35.3 1.4 %collective-permute-done.11.refs_2_ = bf16[416,128]{1,0:T(8,128)(2,1)S(1)} collective-permute-done((bf16[416,128]{1,0:T(8,128)(2,1)S(1)}, bf16[416,128]{1,0:T(8,128)(2,1)S(1)}, u32[]{:S(2)}, u32[]{:S(2)}) %collective-permute-start.11) | collective-permute-done | bytes 106528 | tf_op jit(solution)/shard_map/ppermute | solution.py:17
  36.7 1.2 %project.1 = (s32[4]{0:T(128)S(1)}, f32[400,128]{1,0:T(8,128)S(1)}, bf16[400,128]{1,0:T(8,128)(2,1)S(1)}, bf16[400,128]{1,0:T(8,128)(2,1)S(1)}, bf16[400,128]{1,0:T(8,128)(2,1)S(1)}) custom-call(bf16[192,768]{1,0:T(8,128)(2,1)S(1)} %get-tuple-element.46.own_ref, bf16[192,768]{1,0:T(8,128)(2,1)S(1)} %get-tuple-element.60.pair_ref, ...), custom_call_target="tpu_custom_call" | custom-call | tf_op jit(solution)/shard_map/project/pallas_call | solution.py:280
  37.9 1.0 %collective-permute-start.13 = (bf16[2,128,1536]{2,1,0:T(8,128)(2,1)S(1)}, bf16[2,128,1536]{2,1,0:T(8,128)(2,1)S(1)}, u32[]{:S(2)}, u32[]{:S(2)}) collective-permute-start(bf16[2,128,1536]{2,1,0:T(8,128)(2,1)S(1)} %maps_join.1.refs_0_), channel_id=1, source_target_pairs={{0,2},{1,3},{2,0},{3,1},{4,6},{5,7},{6,4},{7,5},{8,10},{9,11},{10,... | collective-permute-start | bytes 2359304 | tf_op jit(solution)/shard_map/ppermute | solution.py:17
  38.9 2.6 %collective-permute-start.15 = (bf16[400,128]{1,0:T(8,128)(2,1)S(1)}, bf16[400,128]{1,0:T(8,128)(2,1)S(1)}, u32[]{:S(2)}, u32[]{:S(2)}) collective-permute-start(bf16[400,128]{1,0:T(8,128)(2,1)S(1)} %get-tuple-element.68), channel_id=1, source_target_pairs={{0,16},{8,24},{16,0},{24,8},{1,17},{9,25},{17,1},{25,9},{2,18},{10... | collective-permute-start | bytes 307208 | tf_op jit(solution)/shard_map/ppermute | solution.py:17
  41.5 1.4 %collective-permute-start.16 = (bf16[400,128]{1,0:T(8,128)(2,1)S(1)}, bf16[400,128]{1,0:T(8,128)(2,1)S(1)}, u32[]{:S(2)}, u32[]{:S(2)}) collective-permute-start(bf16[400,128]{1,0:T(8,128)(2,1)S(1)} %get-tuple-element.69), channel_id=1, source_target_pairs={{0,24},{8,16},{16,8},{24,0},{1,25},{9,17},{17,9},{25,1},{2,26},{10... | collective-permute-start | bytes 307208 | tf_op jit(solution)/shard_map/ppermute | solution.py:17
  43.1 6.9 %collective-permute-done.15.refs_0_ = bf16[400,128]{1,0:T(8,128)(2,1)S(1)} collective-permute-done((bf16[400,128]{1,0:T(8,128)(2,1)S(1)}, bf16[400,128]{1,0:T(8,128)(2,1)S(1)}, u32[]{:S(2)}, u32[]{:S(2)}) %collective-permute-start.15) | collective-permute-done | bytes 102432 | tf_op jit(solution)/shard_map/ppermute | solution.py:17
  50.6 3.5 %collective-permute-start.18 = (bf16[64,768]{1,0:T(8,128)(2,1)S(1)}, bf16[64,768]{1,0:T(8,128)(2,1)S(1)}, u32[]{:S(2)}, u32[]{:S(2)}) collective-permute-start(bf16[64,768]{1,0:T(8,128)(2,1)S(1)} %finish.1.refs_0_), channel_id=1, source_target_pairs={{0,16},{8,24},{16,0},{24,8},{1,17},{9,25},{17,1},{25,9},{2,18},{10... | collective-permute-start | bytes 294920 | tf_op jit(solution)/shard_map/ppermute | solution.py:17
  55.4 2.3 %collective-permute-done.13.refs_1_ = bf16[2,128,1536]{2,1,0:T(8,128)(2,1)S(1)} collective-permute-done((bf16[2,128,1536]{2,1,0:T(8,128)(2,1)S(1)}, bf16[2,128,1536]{2,1,0:T(8,128)(2,1)S(1)}, u32[]{:S(2)}, u32[]{:S(2)}) %collective-permute-start.13) | collective-permute-done | bytes 786464 | tf_op jit(solution)/shard_map/ppermute | solution.py:17
  58.0 1.5 %collective-permute-start.14 = (f32[2,64,64]{2,1,0:T(8,128)S(1)}, f32[2,64,64]{2,1,0:T(8,128)S(1)}, u32[]{:S(2)}, u32[]{:S(2)}) collective-permute-start(f32[2,64,64]{2,1,0:T(8,128)S(1)} %get-tuple-element.65.low_ref), channel_id=1, source_target_pairs={{0,4},{4,0},{1,5},{5,1},{2,6},{6,2},{3,7},{7,3},{8,12},{12,8},{9,1... | collective-permute-start | bytes 98312 | tf_op jit(solution)/shard_map/ppermute | solution.py:17
  59.5 2.8 %collective-permute-done.14.other_ref = f32[2,64,64]{2,1,0:T(8,128)S(1)} collective-permute-done((f32[2,64,64]{2,1,0:T(8,128)S(1)}, f32[2,64,64]{2,1,0:T(8,128)S(1)}, u32[]{:S(2)}, u32[]{:S(2)}) %collective-permute-start.14) | collective-permute-done | bytes 32800 | tf_op jit(solution)/shard_map/ppermute | solution.py:17
  63.5 1.2 %collective-permute-start.24 = (bf16[128,768]{1,0:T(8,128)(2,1)S(1)}, bf16[128,768]{1,0:T(8,128)(2,1)S(1)}, u32[]{:S(2)}, u32[]{:S(2)}) collective-permute-start(bf16[128,768]{1,0:T(8,128)(2,1)S(1)} %get-tuple-element.79), channel_id=1, source_target_pairs={{0,2},{1,3},{2,0},{3,1},{4,6},{5,7},{6,4},{7,5},{8,10},{9,11},{10,... | collective-permute-start | bytes 589832 | tf_op jit(solution)/shard_map/ppermute | solution.py:17
  65.4 0.9 %heads.4 = (bf16[64,384]{1,0:T(8,128)(2,1)S(1)}, bf16[64,384]{1,0:T(8,128)(2,1)S(1)}) custom-call(s32[1,128]{1,0:T(1,128)S(1)} %constant_dynamic-slice_fusion.live_ref.refs_0_.refs_1_, bf16[128,768]{1,0:T(8,128)(2,1)S(1)} %get-tuple-element.71.text_ref, bf16[4,128,384]{2,1,0:T(8,128)(2,1)S(1)} %get-tuple-element.72.q_ref, ...), custom_call_target="tpu_custom_call" | custom-call | tf_op jit(solution)/shard_map/heads/pallas_call | solution.py:280
  66.3 1.6 %collective-permute-start.21 = (bf16[64,384]{1,0:T(8,128)(2,1)S(1)}, bf16[64,384]{1,0:T(8,128)(2,1)S(1)}, u32[]{:S(2)}, u32[]{:S(2)}) collective-permute-start(bf16[64,384]{1,0:T(8,128)(2,1)S(1)} %get-tuple-element.75), channel_id=1, source_target_pairs={{0,4},{4,0},{1,5},{5,1},{2,6},{6,2},{3,7},{7,3},{8,12},{12,8},{9,1... | collective-permute-start | bytes 147464 | tf_op jit(solution)/shard_map/ppermute | solution.py:17
  67.9 0.9 %heads.5 = (bf16[64,384]{1,0:T(8,128)(2,1)S(1)}, bf16[64,384]{1,0:T(8,128)(2,1)S(1)}) custom-call(s32[1,128]{1,0:T(1,128)S(1)} %constant_dynamic-slice_fusion.live_ref.refs_0_.refs_1_, bf16[128,768]{1,0:T(8,128)(2,1)S(1)} %collective-permute-done.22.text_ref, bf16[4,128,384]{2,1,0:T(8,128)(2,1)S(1)} %get-tuple-element.72.q_ref, ...), custom_call_target="tpu_custom_call" | custom-call | tf_op jit(solution)/shard_map/heads/pallas_call | solution.py:280
  69.4 1.1 %collective-permute-done.21.refs_1_ = bf16[64,384]{1,0:T(8,128)(2,1)S(1)} collective-permute-done((bf16[64,384]{1,0:T(8,128)(2,1)S(1)}, bf16[64,384]{1,0:T(8,128)(2,1)S(1)}, u32[]{:S(2)}, u32[]{:S(2)}) %collective-permute-start.21) | collective-permute-done | bytes 49184 | tf_op jit(solution)/shard_map/ppermute | solution.py:17
  72.2 1.6 %collective-permute-start.25 = (bf16[64,384]{1,0:T(8,128)(2,1)S(1)}, bf16[64,384]{1,0:T(8,128)(2,1)S(1)}, u32[]{:S(2)}, u32[]{:S(2)}) collective-permute-start(bf16[64,384]{1,0:T(8,128)(2,1)S(1)} %get-tuple-element.81), channel_id=1, source_target_pairs={{0,4},{4,0},{1,5},{5,1},{2,6},{6,2},{3,7},{7,3},{8,12},{12,8},{9,1... | collective-permute-start | bytes 147464 | tf_op jit(solution)/shard_map/ppermute | solution.py:17
  74.6 0.9 %heads.7 = (bf16[64,384]{1,0:T(8,128)(2,1)S(1)}, bf16[64,384]{1,0:T(8,128)(2,1)S(1)}) custom-call(s32[1,128]{1,0:T(1,128)S(1)} %constant_dynamic-slice_fusion.live_ref.refs_0_.refs_1_, bf16[128,768]{1,0:T(8,128)(2,1)S(1)} %collective-permute-done.26.text_ref, bf16[4,128,384]{2,1,0:T(8,128)(2,1)S(1)} %get-tuple-element.72.q_ref, ...), custom_call_target="tpu_custom_call" | custom-call | tf_op jit(solution)/shard_map/heads/pallas_call | solution.py:280
  75.5 1.6 %collective-permute-start.27 = (bf16[64,384]{1,0:T(8,128)(2,1)S(1)}, bf16[64,384]{1,0:T(8,128)(2,1)S(1)}, u32[]{:S(2)}, u32[]{:S(2)}) collective-permute-start(bf16[64,384]{1,0:T(8,128)(2,1)S(1)} %get-tuple-element.84), channel_id=1, source_target_pairs={{0,4},{4,0},{1,5},{5,1},{2,6},{6,2},{3,7},{7,3},{8,12},{12,8},{9,1... | collective-permute-start | bytes 147464 | tf_op jit(solution)/shard_map/ppermute | solution.py:17
  77.1 2.6 %collective-permute-done.27.refs_7_ = bf16[64,384]{1,0:T(8,128)(2,1)S(1)} collective-permute-done((bf16[64,384]{1,0:T(8,128)(2,1)S(1)}, bf16[64,384]{1,0:T(8,128)(2,1)S(1)}, u32[]{:S(2)}, u32[]{:S(2)}) %collective-permute-start.27) | collective-permute-done | bytes 49184 | tf_op jit(solution)/shard_map/ppermute | solution.py:17
  (77 shorter events, 13.3 us)
Async XLA Ops:
  0.0 65.4 %copy-start = (s32[2,128]{1,0:T(2,128)S(1)}, s32[2,128]{1,0:T(2,128)}, u32[]{:S(2)}) copy-start(s32[2,128]{1,0:T(2,128)} %param.16) | copy-start | bytes 3076
  3.7 1.9 %collective-permute-start = (bf16[1552,128]{1,0:T(8,128)(2,1)S(1)}, bf16[1552,128]{1,0:T(8,128)(2,1)S(1)}, u32[]{:S(2)}, u32[]{:S(2)}) collective-permute-start(bf16[1552,128]{1,0:T(8,128)(2,1)S(1)} %get-tuple-element.45.dep_ref), channel_id=1, source_target_pairs={{0,1},{1,0},{2,3},{3,2},{4,5},{5,4},{6,7},{7,6},{8,9},{9,8},{10,11... | collective-permute-start | bytes 1191944 | tf_op jit(solution)/shard_map/ppermute | solution.py:17
  5.7 8.2 %collective-permute-start.1 = (bf16[784,128]{1,0:T(8,128)(2,1)S(1)}, bf16[784,128]{1,0:T(8,128)(2,1)S(1)}, u32[]{:S(2)}, u32[]{:S(2)}) collective-permute-start(bf16[784,128]{1,0:T(8,128)(2,1)S(1)} %get-tuple-element.51), channel_id=1, source_target_pairs={{0,2},{1,3},{2,0},{3,1},{4,6},{5,7},{6,4},{7,5},{8,10},{9,11},{10,... | collective-permute-start | bytes 602120 | tf_op jit(solution)/shard_map/ppermute | solution.py:17
  8.8 20.5 %collective-permute-start.8 = (bf16[4,64,1536]{2,1,0:T(8,128)(2,1)S(1)}, bf16[4,64,1536]{2,1,0:T(8,128)(2,1)S(1)}, u32[]{:S(2)}, u32[]{:S(2)}) collective-permute-start(bf16[4,64,1536]{2,1,0:T(8,128)(2,1)S(1)} %image_pack.1), channel_id=1, source_target_pairs={{0,4},{4,0},{1,5},{5,1},{2,6},{6,2},{3,7},{7,3},{8,12},{12,8},{9,1... | collective-permute-start | bytes 2359304 | tf_op jit(solution)/shard_map/ppermute | solution.py:17
  10.5 13.9 %copy-start.10 = (bf16[192]{0:T(256)(128)(2,1)S(1)}, bf16[192]{0:T(256)(128)(2,1)}, u32[]{:S(2)}) copy-start(bf16[192]{0:T(256)(128)(2,1)} %b_ref.1) | copy-start | bytes 1156
  10.5 14.1 %copy-start.11 = (bf16[1,192]{1,0:T(2,128)(2,1)S(1)}, bf16[1,192]{1,0:T(2,128)(2,1)}, u32[]{:S(2)}) copy-start(bf16[1,192]{1,0:T(2,128)(2,1)} %shift_ref.1) | copy-start | bytes 1156
  10.5 9.2 %collective-permute-start.3 = (bf16[128,1536]{1,0:T(8,128)(2,1)S(1)}, bf16[128,1536]{1,0:T(8,128)(2,1)S(1)}, u32[]{:S(2)}, u32[]{:S(2)}) collective-permute-start(bf16[128,1536]{1,0:T(8,128)(2,1)S(1)} %maps_pack.1.own_ref), channel_id=1, source_target_pairs={{0,1},{1,0},{2,3},{3,2},{4,5},{5,4},{6,7},{7,6},{8,9},{9,8},{10,11... | collective-permute-start | bytes 1179656 | tf_op jit(solution)/shard_map/ppermute | solution.py:17
  14.0 15.4 %collective-permute-start.2 = (bf16[2,192,768]{2,1,0:T(8,128)(2,1)S(1)}, bf16[2,192,768]{2,1,0:T(8,128)(2,1)S(1)}, u32[]{:S(2)}, u32[]{:S(2)}) collective-permute-start(bf16[2,192,768]{2,1,0:T(8,128)(2,1)S(1)} %get-tuple-element.55.refs_0_), channel_id=1, source_target_pairs={{0,2},{1,3},{2,0},{3,1},{4,6},{5,7},{6,4},{7,5},{8,10},{9,11},{10,... | collective-permute-start | bytes 1769480 | tf_op jit(solution)/shard_map/ppermute | solution.py:17
  15.8 5.2 %collective-permute-start.4 = (bf16[208,128]{1,0:T(8,128)(2,1)S(1)}, bf16[208,128]{1,0:T(8,128)(2,1)S(1)}, u32[]{:S(2)}, u32[]{:S(2)}) collective-permute-start(bf16[208,128]{1,0:T(8,128)(2,1)S(1)} %get-tuple-element.57), channel_id=1, source_target_pairs={{0,16},{8,24},{16,0},{24,8},{1,17},{9,25},{17,1},{25,9},{2,18},{10... | collective-permute-start | bytes 159752 | tf_op jit(solution)/shard_map/ppermute | solution.py:17
  18.4 6.0 %collective-permute-start.5 = (bf16[208,128]{1,0:T(8,128)(2,1)S(1)}, bf16[208,128]{1,0:T(8,128)(2,1)S(1)}, u32[]{:S(2)}, u32[]{:S(2)}) collective-permute-start(bf16[208,128]{1,0:T(8,128)(2,1)S(1)} %get-tuple-element.58), channel_id=1, source_target_pairs={{0,24},{8,16},{16,8},{24,0},{1,25},{9,17},{17,9},{25,1},{2,26},{10... | collective-permute-start | bytes 159752 | tf_op jit(solution)/shard_map/ppermute | solution.py:17
  19.7 4.7 %collective-permute-start.6 = (bf16[208,128]{1,0:T(8,128)(2,1)S(1)}, bf16[208,128]{1,0:T(8,128)(2,1)S(1)}, u32[]{:S(2)}, u32[]{:S(2)}) collective-permute-start(bf16[208,128]{1,0:T(8,128)(2,1)S(1)} %get-tuple-element.59), channel_id=1, source_target_pairs={{0,8},{8,0},{16,24},{24,16},{1,9},{9,1},{17,25},{25,17},{2,10},{10... | collective-permute-start | bytes 159752 | tf_op jit(solution)/shard_map/ppermute | solution.py:17
  24.7 4.7 %collective-permute-start.7 = (bf16[208,128]{1,0:T(8,128)(2,1)S(1)}, bf16[208,128]{1,0:T(8,128)(2,1)S(1)}, u32[]{:S(2)}, u32[]{:S(2)}) collective-permute-start(bf16[208,128]{1,0:T(8,128)(2,1)S(1)} %centre.1.own_ref), channel_id=1, source_target_pairs={{0,4},{4,0},{1,5},{5,1},{2,6},{6,2},{3,7},{7,3},{8,12},{12,8},{9,1... | collective-permute-start | bytes 159752 | tf_op jit(solution)/shard_map/ppermute | solution.py:17
  29.3 13.8 %copy-start.12 = (bf16[6144]{0:T(1024)(128)(2,1)S(1)}, bf16[6144]{0:T(1024)(128)(2,1)}, u32[]{:S(2)}) copy-start(bf16[6144]{0:T(1024)(128)(2,1)} %param.22) | copy-start | bytes 36868
  29.4 7.3 %collective-permute-start.9 = (bf16[2,192,768]{2,1,0:T(8,128)(2,1)S(1)}, bf16[2,192,768]{2,1,0:T(8,128)(2,1)S(1)}, u32[]{:S(2)}, u32[]{:S(2)}) collective-permute-start(bf16[2,192,768]{2,1,0:T(8,128)(2,1)S(1)} %get-tuple-element.61), channel_id=1, source_target_pairs={{0,1},{1,0},{2,3},{3,2},{4,5},{5,4},{6,7},{7,6},{8,9},{9,8},{10,11... | collective-permute-start | bytes 1769480 | tf_op jit(solution)/shard_map/ppermute | solution.py:17
  29.5 5.8 %collective-permute-start.10 = (bf16[416,128]{1,0:T(8,128)(2,1)S(1)}, bf16[416,128]{1,0:T(8,128)(2,1)S(1)}, u32[]{:S(2)}, u32[]{:S(2)}) collective-permute-start(bf16[416,128]{1,0:T(8,128)(2,1)S(1)} %join.1.dep_ref.refs_0_), channel_id=1, source_target_pairs={{0,2},{1,3},{2,0},{3,1},{4,6},{5,7},{6,4},{7,5},{8,10},{9,11},{10,... | collective-permute-start | bytes 319496 | tf_op jit(solution)/shard_map/ppermute | solution.py:17
  30.5 6.2 %collective-permute-start.11 = (bf16[416,128]{1,0:T(8,128)(2,1)S(1)}, bf16[416,128]{1,0:T(8,128)(2,1)S(1)}, u32[]{:S(2)}, u32[]{:S(2)}) collective-permute-start(bf16[416,128]{1,0:T(8,128)(2,1)S(1)} %join.1.dep_ref.refs_0_), channel_id=1, source_target_pairs={{0,3},{1,2},{2,1},{3,0},{4,7},{5,6},{6,5},{7,4},{8,11},{9,10},{10,... | collective-permute-start | bytes 319496 | tf_op jit(solution)/shard_map/ppermute | solution.py:17
  31.4 5.4 %collective-permute-start.12 = (bf16[416,128]{1,0:T(8,128)(2,1)S(1)}, bf16[416,128]{1,0:T(8,128)(2,1)S(1)}, u32[]{:S(2)}, u32[]{:S(2)}) collective-permute-start(bf16[416,128]{1,0:T(8,128)(2,1)S(1)} %join.1.dep_ref.refs_0_), channel_id=1, source_target_pairs={{0,1},{1,0},{2,3},{3,2},{4,5},{5,4},{6,7},{7,6},{8,9},{9,8},{10,11... | collective-permute-start | bytes 319496 | tf_op jit(solution)/shard_map/ppermute | solution.py:17
  37.9 19.8 %collective-permute-start.13 = (bf16[2,128,1536]{2,1,0:T(8,128)(2,1)S(1)}, bf16[2,128,1536]{2,1,0:T(8,128)(2,1)S(1)}, u32[]{:S(2)}, u32[]{:S(2)}) collective-permute-start(bf16[2,128,1536]{2,1,0:T(8,128)(2,1)S(1)} %maps_join.1.refs_0_), channel_id=1, source_target_pairs={{0,2},{1,3},{2,0},{3,1},{4,6},{5,7},{6,4},{7,5},{8,10},{9,11},{10,... | collective-permute-start | bytes 2359304 | tf_op jit(solution)/shard_map/ppermute | solution.py:17
  38.9 11.1 %collective-permute-start.15 = (bf16[400,128]{1,0:T(8,128)(2,1)S(1)}, bf16[400,128]{1,0:T(8,128)(2,1)S(1)}, u32[]{:S(2)}, u32[]{:S(2)}) collective-permute-start(bf16[400,128]{1,0:T(8,128)(2,1)S(1)} %get-tuple-element.68), channel_id=1, source_target_pairs={{0,16},{8,24},{16,0},{24,8},{1,17},{9,25},{17,1},{25,9},{2,18},{10... | collective-permute-start | bytes 307208 | tf_op jit(solution)/shard_map/ppermute | solution.py:17
  41.5 8.5 %collective-permute-start.16 = (bf16[400,128]{1,0:T(8,128)(2,1)S(1)}, bf16[400,128]{1,0:T(8,128)(2,1)S(1)}, u32[]{:S(2)}, u32[]{:S(2)}) collective-permute-start(bf16[400,128]{1,0:T(8,128)(2,1)S(1)} %get-tuple-element.69), channel_id=1, source_target_pairs={{0,24},{8,16},{16,8},{24,0},{1,25},{9,17},{17,9},{25,1},{2,26},{10... | collective-permute-start | bytes 307208 | tf_op jit(solution)/shard_map/ppermute | solution.py:17
  42.9 7.5 %collective-permute-start.17 = (bf16[400,128]{1,0:T(8,128)(2,1)S(1)}, bf16[400,128]{1,0:T(8,128)(2,1)S(1)}, u32[]{:S(2)}, u32[]{:S(2)}) collective-permute-start(bf16[400,128]{1,0:T(8,128)(2,1)S(1)} %get-tuple-element.70), channel_id=1, source_target_pairs={{0,8},{8,0},{16,24},{24,16},{1,9},{9,1},{17,25},{25,17},{2,10},{10... | collective-permute-start | bytes 307208 | tf_op jit(solution)/shard_map/ppermute | solution.py:17
  50.6 11.9 %collective-permute-start.18 = (bf16[64,768]{1,0:T(8,128)(2,1)S(1)}, bf16[64,768]{1,0:T(8,128)(2,1)S(1)}, u32[]{:S(2)}, u32[]{:S(2)}) collective-permute-start(bf16[64,768]{1,0:T(8,128)(2,1)S(1)} %finish.1.refs_0_), channel_id=1, source_target_pairs={{0,16},{8,24},{16,0},{24,8},{1,17},{9,25},{17,1},{25,9},{2,18},{10... | collective-permute-start | bytes 294920 | tf_op jit(solution)/shard_map/ppermute | solution.py:17
  54.1 8.4 %collective-permute-start.19 = (bf16[64,768]{1,0:T(8,128)(2,1)S(1)}, bf16[64,768]{1,0:T(8,128)(2,1)S(1)}, u32[]{:S(2)}, u32[]{:S(2)}) collective-permute-start(bf16[64,768]{1,0:T(8,128)(2,1)S(1)} %finish.1.refs_0_), channel_id=1, source_target_pairs={{0,24},{8,16},{16,8},{24,0},{1,25},{9,17},{17,9},{25,1},{2,26},{10... | collective-permute-start | bytes 294920 | tf_op jit(solution)/shard_map/ppermute | solution.py:17
  54.6 8.1 %collective-permute-start.20 = (bf16[64,768]{1,0:T(8,128)(2,1)S(1)}, bf16[64,768]{1,0:T(8,128)(2,1)S(1)}, u32[]{:S(2)}, u32[]{:S(2)}) collective-permute-start(bf16[64,768]{1,0:T(8,128)(2,1)S(1)} %finish.1.refs_0_), channel_id=1, source_target_pairs={{0,8},{8,0},{16,24},{24,16},{1,9},{9,1},{17,25},{25,17},{2,10},{10... | collective-permute-start | bytes 294920 | tf_op jit(solution)/shard_map/ppermute | solution.py:17
  58.0 4.3 %collective-permute-start.14 = (f32[2,64,64]{2,1,0:T(8,128)S(1)}, f32[2,64,64]{2,1,0:T(8,128)S(1)}, u32[]{:S(2)}, u32[]{:S(2)}) collective-permute-start(f32[2,64,64]{2,1,0:T(8,128)S(1)} %get-tuple-element.65.low_ref), channel_id=1, source_target_pairs={{0,4},{4,0},{1,5},{5,1},{2,6},{6,2},{3,7},{7,3},{8,12},{12,8},{9,1... | collective-permute-start | bytes 98312 | tf_op jit(solution)/shard_map/ppermute | solution.py:17
  63.4 4.4 %collective-permute-start.22 = (bf16[128,768]{1,0:T(8,128)(2,1)S(1)}, bf16[128,768]{1,0:T(8,128)(2,1)S(1)}, u32[]{:S(2)}, u32[]{:S(2)}) collective-permute-start(bf16[128,768]{1,0:T(8,128)(2,1)S(1)} %get-tuple-element.76), channel_id=1, source_target_pairs={{0,1},{1,0},{2,3},{3,2},{4,5},{5,4},{6,7},{7,6},{8,9},{9,8},{10,11... | collective-permute-start | bytes 589832 | tf_op jit(solution)/shard_map/ppermute | solution.py:17
  63.5 7.8 %collective-permute-start.24 = (bf16[128,768]{1,0:T(8,128)(2,1)S(1)}, bf16[128,768]{1,0:T(8,128)(2,1)S(1)}, u32[]{:S(2)}, u32[]{:S(2)}) collective-permute-start(bf16[128,768]{1,0:T(8,128)(2,1)S(1)} %get-tuple-element.79), channel_id=1, source_target_pairs={{0,2},{1,3},{2,0},{3,1},{4,6},{5,7},{6,4},{7,5},{8,10},{9,11},{10,... | collective-permute-start | bytes 589832 | tf_op jit(solution)/shard_map/ppermute | solution.py:17
  64.7 9.9 %collective-permute-start.26 = (bf16[128,768]{1,0:T(8,128)(2,1)S(1)}, bf16[128,768]{1,0:T(8,128)(2,1)S(1)}, u32[]{:S(2)}, u32[]{:S(2)}) collective-permute-start(bf16[128,768]{1,0:T(8,128)(2,1)S(1)} %get-tuple-element.82), channel_id=1, source_target_pairs={{0,3},{1,2},{2,1},{3,0},{4,7},{5,6},{6,5},{7,4},{8,11},{9,10},{10,... | collective-permute-start | bytes 589832 | tf_op jit(solution)/shard_map/ppermute | solution.py:17
  66.3 4.2 %collective-permute-start.21 = (bf16[64,384]{1,0:T(8,128)(2,1)S(1)}, bf16[64,384]{1,0:T(8,128)(2,1)S(1)}, u32[]{:S(2)}, u32[]{:S(2)}) collective-permute-start(bf16[64,384]{1,0:T(8,128)(2,1)S(1)} %get-tuple-element.75), channel_id=1, source_target_pairs={{0,4},{4,0},{1,5},{5,1},{2,6},{6,2},{3,7},{7,3},{8,12},{12,8},{9,1... | collective-permute-start | bytes 147464 | tf_op jit(solution)/shard_map/ppermute | solution.py:17
  68.8 5.8 %collective-permute-start.23 = (bf16[64,384]{1,0:T(8,128)(2,1)S(1)}, bf16[64,384]{1,0:T(8,128)(2,1)S(1)}, u32[]{:S(2)}, u32[]{:S(2)}) collective-permute-start(bf16[64,384]{1,0:T(8,128)(2,1)S(1)} %get-tuple-element.78), channel_id=1, source_target_pairs={{0,4},{4,0},{1,5},{5,1},{2,6},{6,2},{3,7},{7,3},{8,12},{12,8},{9,1... | collective-permute-start | bytes 147464 | tf_op jit(solution)/shard_map/ppermute | solution.py:17
  72.2 4.9 %collective-permute-start.25 = (bf16[64,384]{1,0:T(8,128)(2,1)S(1)}, bf16[64,384]{1,0:T(8,128)(2,1)S(1)}, u32[]{:S(2)}, u32[]{:S(2)}) collective-permute-start(bf16[64,384]{1,0:T(8,128)(2,1)S(1)} %get-tuple-element.81), channel_id=1, source_target_pairs={{0,4},{4,0},{1,5},{5,1},{2,6},{6,2},{3,7},{7,3},{8,12},{12,8},{9,1... | collective-permute-start | bytes 147464 | tf_op jit(solution)/shard_map/ppermute | solution.py:17
  75.5 4.2 %collective-permute-start.27 = (bf16[64,384]{1,0:T(8,128)(2,1)S(1)}, bf16[64,384]{1,0:T(8,128)(2,1)S(1)}, u32[]{:S(2)}, u32[]{:S(2)}) collective-permute-start(bf16[64,384]{1,0:T(8,128)(2,1)S(1)} %get-tuple-element.84), channel_id=1, source_target_pairs={{0,4},{4,0},{1,5},{5,1},{2,6},{6,2},{3,7},{7,3},{8,12},{12,8},{9,1... | collective-permute-start | bytes 147464 | tf_op jit(solution)/shard_map/ppermute | solution.py:17
  (10 other events, 50.7 us)

commit v8 on v7

--- a/solution.py
+++ b/solution.py
@@ -354,7 +354,7 @@
     out_stat_ref[...] = jnp.broadcast_to(stat, out_stat_ref.shape)
 
 
-def centre_kernel(width, prompt_ref, dep_ref, keep_ref, stat_ref, bias_ref, scale_ref, shift_ref, *refs):
+def centre_kernel(width, prompt_ref, maps_ref, image_ref, keep_ref, stat_ref, bias_ref, scale_ref, shift_ref, *refs):
     got_refs, out_ref = refs[:-1], refs[-1]
     features, tokens = keep_ref.shape
     total = keep_ref[...] + bias_ref[...]
@@ -384,7 +384,7 @@
     next_ref[1] = got_ref[1]
 
 
-def join_kernel(own_ref, got_ref, dep_ref, out_ref):
+def join_kernel(own_ref, got_ref, out_ref):
     size = own_ref.shape[0]
     out_ref[:size] = own_ref[...]
     out_ref[size:] = got_ref[...]
@@ -664,6 +664,18 @@
     )
     got = swap(send, "req", n_req, 1)
 
+    packed = [
+        call(
+            functools.partial(image_kernel, part, inner, k),
+            struct((4, image_rows, part)),
+            (qk, base, stream, send),
+            [ANY] * 4,
+            [dma((4,))],
+            name="image_pack",
+        )
+        for k in range(1, n_seq)
+    ]
+    image_got = [swap(packed[k - 1], "seq", n_seq, k) for k in range(1, n_seq)]
     maps = call(
         functools.partial(maps_kernel, part),
         struct((2 * rank, part)),
@@ -694,18 +706,6 @@
         name="halve",
     )
     got = swap(send, "req", n_req, 2)
-    packed = [
-        call(
-            functools.partial(image_kernel, part, inner, k),
-            struct((4, image_rows, part)),
-            (qk, base, stream, keep),
-            [ANY] * 4,
-            [dma((4,))],
-            name="image_pack",
-        )
-        for k in range(1, n_seq)
-    ]
-    image_got = [swap(packed[k - 1], "seq", n_seq, k) for k in range(1, n_seq)]
     keep, sums, *sends = call(
         functools.partial(scatter_kernel, features, 1),
         (struct((features, tokens), F32), stat)
@@ -728,6 +728,7 @@
         (
             request_prompt,
             maps_core,
+            image_got[0],
             keep,
             sums,
             bias_columns,
@@ -735,14 +736,13 @@
             modulation_shift,
             *arrived,
         ),
-        [SMEM, ANY] + [VMEM] * (5 + len(arrived)),
+        [SMEM] + [ANY] * 2 + [VMEM] * (5 + len(arrived)),
         name="centre",
     )
     joined = call(
         join_kernel,
         struct((n_seq * (features + ROWS), tokens)),
-        (own, swap(own, "seq", n_seq, 1), image_got[0]),
-        [VMEM, VMEM, ANY],
+        (own, swap(own, "seq", n_seq, 1)),
         name="join",
     )
     payloads = partners(lambda k: joined, "req", n_req)
@@ -809,7 +809,7 @@
     rows = call(
         functools.partial(choose_kernel, n_seq, n_enc),
         [struct((tokens, 2 * half)) for _ in range(n_req)],
-        (ids, image_values, text, *parts.values()),
+        (ids, low, text, *parts.values()),
         [SMEM, ANY] + [VMEM] * n_enc,
         name="choose",
     )

time: 80.7 us -> 88.8 us (1.10)
  waiting for transfers between devices: 34 us -> 38.9 us
  local copies, waits for them, and re-layouts: 3.22 us -> 6.27 us
    ppermute x28, waiting for transfers between devices: 34 us -> 38.9 us  [swap(): return lax.ppermute(block, axis, [(i, i ^ step) for i in range(size)])]
    unnamed x28 -> x32, local copies, waits for them, and re-layouts: 3.03 us -> 6.09 us
where the time goes in v8:
time: 88.8 us; the launch traced here: 88.5 us
  waiting for transfers between devices  38.9 us (44%)
  starting transfers between devices  32.4 us (36%)
  Pallas kernels  9.33 us (11%)
  local copies, waits for them, and re-layouts  6.27 us (7%)
  between operations  1.55 us (2%)
    ppermute x28, waiting for transfers between devices, swap(): return lax.ppermute(block, axis, [(i, i ^ step) for i in range(size)])  38.9 us
    ppermute x28, starting transfers between devices, swap(): return lax.ppermute(block, axis, [(i, i ^ step) for i in range(size)])  32.4 us
    pallas_call x20, Pallas kernels, call(): pl.pallas_call(kernel, out_shape=outs, in_specs=specs if specs is not Non...  9.33 us
    unnamed x32, local copies, waits for them, and re-layouts  6.09 us
  transfers between devices with their start and end apart: 28, of which 16 were waited for; matrix products, arithmetic and copies ran while one was open for 0% of the time, Pallas kernels for 6%

profile of v8, /device:TPU:0, one launch (start us, length us, event | category | flops | bytes accessed | tf_op | source)
XLA Modules:
  0.0 88.5 jit_solution(15948892111756319876)
XLA Ops:
  0.0 1.4 %copy-done.4 = bf16[256,3072]{1,0:T(8,128)(2,1)S(1)} copy-done((bf16[256,3072]{1,0:T(8,128)(2,1)S(1)}, bf16[256,3072]{1,0:T(8,128)(2,1)}, u32[]{:S(2)}) %copy-start.4) | copy-done | bytes 1572888
  4.1 1.1 %copy-done.1 = bf16[1,1,64,6144]{3,2,1,0:T(8,128)(2,1)S(1)} copy-done((bf16[1,1,64,6144]{3,2,1,0:T(8,128)(2,1)S(1)}, bf16[1,1,64,6144]{3,2,1,0:T(8,128)(2,1)}, u32[]{:S(2)}) %copy-start.1) | copy-done | bytes 786456
  7.4 2.6 %collective-permute-start.4 = (bf16[4,64,1536]{2,1,0:T(8,128)(2,1)S(1)}, bf16[4,64,1536]{2,1,0:T(8,128)(2,1)S(1)}, u32[]{:S(2)}, u32[]{:S(2)}) collective-permute-start(bf16[4,64,1536]{2,1,0:T(8,128)(2,1)S(1)} %image_pack.1), channel_id=1, source_target_pairs={{0,4},{4,0},{1,5},{5,1},{2,6},{6,2},{3,7},{7,3},{8,12},{12,8},{9,1... | collective-permute-start | bytes 2359304 | tf_op jit(solution)/shard_map/ppermute | solution.py:17
  10.1 1.6 %collective-permute-start.1 = (bf16[784,128]{1,0:T(8,128)(2,1)S(1)}, bf16[784,128]{1,0:T(8,128)(2,1)S(1)}, u32[]{:S(2)}, u32[]{:S(2)}) collective-permute-start(bf16[784,128]{1,0:T(8,128)(2,1)S(1)} %get-tuple-element.51), channel_id=1, source_target_pairs={{0,2},{1,3},{2,0},{3,1},{4,6},{5,7},{6,4},{7,5},{8,10},{9,11},{10,... | collective-permute-start | bytes 602120 | tf_op jit(solution)/shard_map/ppermute | solution.py:17
  12.2 5.1 %collective-permute-done.1.got_ref = bf16[784,128]{1,0:T(8,128)(2,1)S(1)} collective-permute-done((bf16[784,128]{1,0:T(8,128)(2,1)S(1)}, bf16[784,128]{1,0:T(8,128)(2,1)S(1)}, u32[]{:S(2)}, u32[]{:S(2)}) %collective-permute-start.1) | collective-permute-done | bytes 200736 | tf_op jit(solution)/shard_map/ppermute | solution.py:17
  17.3 1.6 %collective-permute-start.2 = (bf16[2,192,768]{2,1,0:T(8,128)(2,1)S(1)}, bf16[2,192,768]{2,1,0:T(8,128)(2,1)S(1)}, u32[]{:S(2)}, u32[]{:S(2)}) collective-permute-start(bf16[2,192,768]{2,1,0:T(8,128)(2,1)S(1)} %get-tuple-element.55.refs_0_), channel_id=1, source_target_pairs={{0,2},{1,3},{2,0},{3,1},{4,6},{5,7},{6,4},{7,5},{8,10},{9,11},{10,... | collective-permute-start | bytes 1769480 | tf_op jit(solution)/shard_map/ppermute | solution.py:17
  18.9 2.6 %collective-permute-start.5 = (bf16[208,128]{1,0:T(8,128)(2,1)S(1)}, bf16[208,128]{1,0:T(8,128)(2,1)S(1)}, u32[]{:S(2)}, u32[]{:S(2)}) collective-permute-start(bf16[208,128]{1,0:T(8,128)(2,1)S(1)} %get-tuple-element.57), channel_id=1, source_target_pairs={{0,16},{8,24},{16,0},{24,8},{1,17},{9,25},{17,1},{25,9},{2,18},{10... | collective-permute-start | bytes 159752 | tf_op jit(solution)/shard_map/ppermute | solution.py:17
  21.5 1.3 %collective-permute-start.6 = (bf16[208,128]{1,0:T(8,128)(2,1)S(1)}, bf16[208,128]{1,0:T(8,128)(2,1)S(1)}, u32[]{:S(2)}, u32[]{:S(2)}) collective-permute-start(bf16[208,128]{1,0:T(8,128)(2,1)S(1)} %get-tuple-element.58), channel_id=1, source_target_pairs={{0,24},{8,16},{16,8},{24,0},{1,25},{9,17},{17,9},{25,1},{2,26},{10... | collective-permute-start | bytes 159752 | tf_op jit(solution)/shard_map/ppermute | solution.py:17
  24.0 3.6 %collective-permute-done.6.refs_1_ = bf16[208,128]{1,0:T(8,128)(2,1)S(1)} collective-permute-done((bf16[208,128]{1,0:T(8,128)(2,1)S(1)}, bf16[208,128]{1,0:T(8,128)(2,1)S(1)}, u32[]{:S(2)}, u32[]{:S(2)}) %collective-permute-start.6) | collective-permute-done | bytes 53280 | tf_op jit(solution)/shard_map/ppermute | solution.py:17
  28.5 1.8 %collective-permute-start.8 = (bf16[208,128]{1,0:T(8,128)(2,1)S(1)}, bf16[208,128]{1,0:T(8,128)(2,1)S(1)}, u32[]{:S(2)}, u32[]{:S(2)}) collective-permute-start(bf16[208,128]{1,0:T(8,128)(2,1)S(1)} %centre.1.own_ref), channel_id=1, source_target_pairs={{0,4},{4,0},{1,5},{5,1},{2,6},{6,2},{3,7},{7,3},{8,12},{12,8},{9,1... | collective-permute-start | bytes 159752 | tf_op jit(solution)/shard_map/ppermute | solution.py:17
  30.3 2.4 %collective-permute-done.8.got_ref = bf16[208,128]{1,0:T(8,128)(2,1)S(1)} collective-permute-done((bf16[208,128]{1,0:T(8,128)(2,1)S(1)}, bf16[208,128]{1,0:T(8,128)(2,1)S(1)}, u32[]{:S(2)}, u32[]{:S(2)}) %collective-permute-start.8) | collective-permute-done | bytes 53280 | tf_op jit(solution)/shard_map/ppermute | solution.py:17
  32.9 1.8 %collective-permute-start.10 = (bf16[416,128]{1,0:T(8,128)(2,1)S(1)}, bf16[416,128]{1,0:T(8,128)(2,1)S(1)}, u32[]{:S(2)}, u32[]{:S(2)}) collective-permute-start(bf16[416,128]{1,0:T(8,128)(2,1)S(1)} %join.1.dep_ref.refs_0_), channel_id=1, source_target_pairs={{0,2},{1,3},{2,0},{3,1},{4,6},{5,7},{6,4},{7,5},{8,10},{9,11},{10,... | collective-permute-start | bytes 319496 | tf_op jit(solution)/shard_map/ppermute | solution.py:17
  35.1 3.6 %collective-permute-done.10.refs_1_ = bf16[416,128]{1,0:T(8,128)(2,1)S(1)} collective-permute-done((bf16[416,128]{1,0:T(8,128)(2,1)S(1)}, bf16[416,128]{1,0:T(8,128)(2,1)S(1)}, u32[]{:S(2)}, u32[]{:S(2)}) %collective-permute-start.10) | collective-permute-done | bytes 106528 | tf_op jit(solution)/shard_map/ppermute | solution.py:17
  38.7 1.4 %collective-permute-done.11.refs_2_ = bf16[416,128]{1,0:T(8,128)(2,1)S(1)} collective-permute-done((bf16[416,128]{1,0:T(8,128)(2,1)S(1)}, bf16[416,128]{1,0:T(8,128)(2,1)S(1)}, u32[]{:S(2)}, u32[]{:S(2)}) %collective-permute-start.11) | collective-permute-done | bytes 106528 | tf_op jit(solution)/shard_map/ppermute | solution.py:17
  40.1 1.2 %project.1 = (s32[4]{0:T(128)S(1)}, f32[400,128]{1,0:T(8,128)S(1)}, bf16[400,128]{1,0:T(8,128)(2,1)S(1)}, bf16[400,128]{1,0:T(8,128)(2,1)S(1)}, bf16[400,128]{1,0:T(8,128)(2,1)S(1)}) custom-call(bf16[192,768]{1,0:T(8,128)(2,1)S(1)} %get-tuple-element.46.own_ref, bf16[192,768]{1,0:T(8,128)(2,1)S(1)} %get-tuple-element.60.pair_ref, ...), custom_call_target="tpu_custom_call" | custom-call | tf_op jit(solution)/shard_map/project/pallas_call | solution.py:280
  41.3 1.8 %collective-permute-start.13 = (bf16[2,128,1536]{2,1,0:T(8,128)(2,1)S(1)}, bf16[2,128,1536]{2,1,0:T(8,128)(2,1)S(1)}, u32[]{:S(2)}, u32[]{:S(2)}) collective-permute-start(bf16[2,128,1536]{2,1,0:T(8,128)(2,1)S(1)} %maps_join.1.refs_0_), channel_id=1, source_target_pairs={{0,2},{1,3},{2,0},{3,1},{4,6},{5,7},{6,4},{7,5},{8,10},{9,11},{10,... | collective-permute-start | bytes 2359304 | tf_op jit(solution)/shard_map/ppermute | solution.py:17
  43.1 2.6 %collective-permute-start.14 = (bf16[400,128]{1,0:T(8,128)(2,1)S(1)}, bf16[400,128]{1,0:T(8,128)(2,1)S(1)}, u32[]{:S(2)}, u32[]{:S(2)}) collective-permute-start(bf16[400,128]{1,0:T(8,128)(2,1)S(1)} %get-tuple-element.66), channel_id=1, source_target_pairs={{0,16},{8,24},{16,0},{24,8},{1,17},{9,25},{17,1},{25,9},{2,18},{10... | collective-permute-start | bytes 307208 | tf_op jit(solution)/shard_map/ppermute | solution.py:17
  45.7 1.3 %collective-permute-start.15 = (bf16[400,128]{1,0:T(8,128)(2,1)S(1)}, bf16[400,128]{1,0:T(8,128)(2,1)S(1)}, u32[]{:S(2)}, u32[]{:S(2)}) collective-permute-start(bf16[400,128]{1,0:T(8,128)(2,1)S(1)} %get-tuple-element.67), channel_id=1, source_target_pairs={{0,24},{8,16},{16,8},{24,0},{1,25},{9,17},{17,9},{25,1},{2,26},{10... | collective-permute-start | bytes 307208 | tf_op jit(solution)/shard_map/ppermute | solution.py:17
  47.3 6.9 %collective-permute-done.14.refs_0_ = bf16[400,128]{1,0:T(8,128)(2,1)S(1)} collective-permute-done((bf16[400,128]{1,0:T(8,128)(2,1)S(1)}, bf16[400,128]{1,0:T(8,128)(2,1)S(1)}, u32[]{:S(2)}, u32[]{:S(2)}) %collective-permute-start.14) | collective-permute-done | bytes 102432 | tf_op jit(solution)/shard_map/ppermute | solution.py:17
  54.8 3.5 %collective-permute-start.17 = (bf16[64,768]{1,0:T(8,128)(2,1)S(1)}, bf16[64,768]{1,0:T(8,128)(2,1)S(1)}, u32[]{:S(2)}, u32[]{:S(2)}) collective-permute-start(bf16[64,768]{1,0:T(8,128)(2,1)S(1)} %finish.1.refs_0_), channel_id=1, source_target_pairs={{0,16},{8,24},{16,0},{24,8},{1,17},{9,25},{17,1},{25,9},{2,18},{10... | collective-permute-start | bytes 294920 | tf_op jit(solution)/shard_map/ppermute | solution.py:17
  59.6 1.5 %collective-permute-done.13.refs_1_ = bf16[2,128,1536]{2,1,0:T(8,128)(2,1)S(1)} collective-permute-done((bf16[2,128,1536]{2,1,0:T(8,128)(2,1)S(1)}, bf16[2,128,1536]{2,1,0:T(8,128)(2,1)S(1)}, u32[]{:S(2)}, u32[]{:S(2)}) %collective-permute-start.13) | collective-permute-done | bytes 786464 | tf_op jit(solution)/shard_map/ppermute | solution.py:17
  61.3 4.5 %collective-permute-done.17.refs_1_ = bf16[64,768]{1,0:T(8,128)(2,1)S(1)} collective-permute-done((bf16[64,768]{1,0:T(8,128)(2,1)S(1)}, bf16[64,768]{1,0:T(8,128)(2,1)S(1)}, u32[]{:S(2)}, u32[]{:S(2)}) %collective-permute-start.17) | collective-permute-done | bytes 98336 | tf_op jit(solution)/shard_map/ppermute | solution.py:17
  65.8 1.1 %collective-permute-done.19.refs_3_ = bf16[64,768]{1,0:T(8,128)(2,1)S(1)} collective-permute-done((bf16[64,768]{1,0:T(8,128)(2,1)S(1)}, bf16[64,768]{1,0:T(8,128)(2,1)S(1)}, u32[]{:S(2)}, u32[]{:S(2)}) %collective-permute-start.19) | collective-permute-done | bytes 98336 | tf_op jit(solution)/shard_map/ppermute | solution.py:17
  66.9 1.4 %choose.1 = (bf16[128,768]{1,0:T(8,128)(2,1)S(1)}, bf16[128,768]{1,0:T(8,128)(2,1)}, bf16[128,768]{1,0:T(8,128)(2,1)S(1)}, bf16[128,768]{1,0:T(8,128)(2,1)S(1)}) custom-call(s32[4]{0:T(128)S(1)} %get-tuple-element.62.chosen_ref, f32[2,64,64]{2,1,0:T(8,128)S(1)} %get-tuple-element.65.dep_ref.low_ref, bf16[64,768]{1,0:T(8,128)(2,1)S(1)} %finish.1.refs_0_, ...), custom_call_target="tpu_custom_call" | custom-call | tf_op jit(solution)/shard_map/choose/pallas_call | solution.py:280
  68.8 1.4 %collective-permute-start.26 = (bf16[128,768]{1,0:T(8,128)(2,1)S(1)}, bf16[128,768]{1,0:T(8,128)(2,1)S(1)}, u32[]{:S(2)}, u32[]{:S(2)}) collective-permute-start(bf16[128,768]{1,0:T(8,128)(2,1)S(1)} %get-tuple-element.82), channel_id=1, source_target_pairs={{0,3},{1,2},{2,1},{3,0},{4,7},{5,6},{6,5},{7,4},{8,11},{9,10},{10,... | collective-permute-start | bytes 589832 | tf_op jit(solution)/shard_map/ppermute | solution.py:17
  70.2 1.5 %collective-permute-start.20 = (f32[2,64,64]{2,1,0:T(8,128)S(1)}, f32[2,64,64]{2,1,0:T(8,128)S(1)}, u32[]{:S(2)}, u32[]{:S(2)}) collective-permute-start(f32[2,64,64]{2,1,0:T(8,128)S(1)} %get-tuple-element.65.dep_ref.low_ref), channel_id=1, source_target_pairs={{0,4},{4,0},{1,5},{5,1},{2,6},{6,2},{3,7},{7,3},{8,12},{12,8},{9,1... | collective-permute-start | bytes 98312 | tf_op jit(solution)/shard_map/ppermute | solution.py:17
  71.7 2.8 %collective-permute-done.20.other_ref = f32[2,64,64]{2,1,0:T(8,128)S(1)} collective-permute-done((f32[2,64,64]{2,1,0:T(8,128)S(1)}, f32[2,64,64]{2,1,0:T(8,128)S(1)}, u32[]{:S(2)}, u32[]{:S(2)}) %collective-permute-start.20) | collective-permute-done | bytes 32800 | tf_op jit(solution)/shard_map/ppermute | solution.py:17
  75.7 1.6 %collective-permute-start.21 = (bf16[64,384]{1,0:T(8,128)(2,1)S(1)}, bf16[64,384]{1,0:T(8,128)(2,1)S(1)}, u32[]{:S(2)}, u32[]{:S(2)}) collective-permute-start(bf16[64,384]{1,0:T(8,128)(2,1)S(1)} %get-tuple-element.75), channel_id=1, source_target_pairs={{0,4},{4,0},{1,5},{5,1},{2,6},{6,2},{3,7},{7,3},{8,12},{12,8},{9,1... | collective-permute-start | bytes 147464 | tf_op jit(solution)/shard_map/ppermute | solution.py:17
  78.7 1.1 %collective-permute-done.21.refs_1_ = bf16[64,384]{1,0:T(8,128)(2,1)S(1)} collective-permute-done((bf16[64,384]{1,0:T(8,128)(2,1)S(1)}, bf16[64,384]{1,0:T(8,128)(2,1)S(1)}, u32[]{:S(2)}, u32[]{:S(2)}) %collective-permute-start.21) | collective-permute-done | bytes 49184 | tf_op jit(solution)/shard_map/ppermute | solution.py:17
  80.7 1.8 %collective-permute-start.25 = (bf16[64,384]{1,0:T(8,128)(2,1)S(1)}, bf16[64,384]{1,0:T(8,128)(2,1)S(1)}, u32[]{:S(2)}, u32[]{:S(2)}) collective-permute-start(bf16[64,384]{1,0:T(8,128)(2,1)S(1)} %get-tuple-element.81), channel_id=1, source_target_pairs={{0,4},{4,0},{1,5},{5,1},{2,6},{6,2},{3,7},{7,3},{8,12},{12,8},{9,1... | collective-permute-start | bytes 147464 | tf_op jit(solution)/shard_map/ppermute | solution.py:17
  83.8 1.4 %collective-permute-done.25.refs_5_ = bf16[64,384]{1,0:T(8,128)(2,1)S(1)} collective-permute-done((bf16[64,384]{1,0:T(8,128)(2,1)S(1)}, bf16[64,384]{1,0:T(8,128)(2,1)S(1)}, u32[]{:S(2)}, u32[]{:S(2)}) %collective-permute-start.25) | collective-permute-done | bytes 49184 | tf_op jit(solution)/shard_map/ppermute | solution.py:17
  85.3 2.4 %collective-permute-done.27.refs_7_ = bf16[64,384]{1,0:T(8,128)(2,1)S(1)} collective-permute-done((bf16[64,384]{1,0:T(8,128)(2,1)S(1)}, bf16[64,384]{1,0:T(8,128)(2,1)S(1)}, u32[]{:S(2)}, u32[]{:S(2)}) %collective-permute-start.27) | collective-permute-done | bytes 49184 | tf_op jit(solution)/shard_map/ppermute | solution.py:17
  (81 shorter events, 15.3 us)
Async XLA Ops:
  0.0 71.7 %copy-start = (s32[2,128]{1,0:T(2,128)S(1)}, s32[2,128]{1,0:T(2,128)}, u32[]{:S(2)}) copy-start(s32[2,128]{1,0:T(2,128)} %param.16) | copy-start | bytes 3076
  3.6 6.4 %collective-permute-start = (bf16[1552,128]{1,0:T(8,128)(2,1)S(1)}, bf16[1552,128]{1,0:T(8,128)(2,1)S(1)}, u32[]{:S(2)}, u32[]{:S(2)}) collective-permute-start(bf16[1552,128]{1,0:T(8,128)(2,1)S(1)} %get-tuple-element.45.dep_ref), channel_id=1, source_target_pairs={{0,1},{1,0},{2,3},{3,2},{4,5},{5,4},{6,7},{7,6},{8,9},{9,8},{10,11... | collective-permute-start | bytes 1191944 | tf_op jit(solution)/shard_map/ppermute | solution.py:17
  7.4 20.8 %collective-permute-start.4 = (bf16[4,64,1536]{2,1,0:T(8,128)(2,1)S(1)}, bf16[4,64,1536]{2,1,0:T(8,128)(2,1)S(1)}, u32[]{:S(2)}, u32[]{:S(2)}) collective-permute-start(bf16[4,64,1536]{2,1,0:T(8,128)(2,1)S(1)} %image_pack.1), channel_id=1, source_target_pairs={{0,4},{4,0},{1,5},{5,1},{2,6},{6,2},{3,7},{7,3},{8,12},{12,8},{9,1... | collective-permute-start | bytes 2359304 | tf_op jit(solution)/shard_map/ppermute | solution.py:17
  10.1 7.2 %collective-permute-start.1 = (bf16[784,128]{1,0:T(8,128)(2,1)S(1)}, bf16[784,128]{1,0:T(8,128)(2,1)S(1)}, u32[]{:S(2)}, u32[]{:S(2)}) collective-permute-start(bf16[784,128]{1,0:T(8,128)(2,1)S(1)} %get-tuple-element.51), channel_id=1, source_target_pairs={{0,2},{1,3},{2,0},{3,1},{4,6},{5,7},{6,4},{7,5},{8,10},{9,11},{10,... | collective-permute-start | bytes 602120 | tf_op jit(solution)/shard_map/ppermute | solution.py:17
  11.8 11.0 %collective-permute-start.3 = (bf16[128,1536]{1,0:T(8,128)(2,1)S(1)}, bf16[128,1536]{1,0:T(8,128)(2,1)S(1)}, u32[]{:S(2)}, u32[]{:S(2)}) collective-permute-start(bf16[128,1536]{1,0:T(8,128)(2,1)S(1)} %maps_pack.1.own_ref), channel_id=1, source_target_pairs={{0,1},{1,0},{2,3},{3,2},{4,5},{5,4},{6,7},{7,6},{8,9},{9,8},{10,11... | collective-permute-start | bytes 1179656 | tf_op jit(solution)/shard_map/ppermute | solution.py:17
  17.3 15.4 %collective-permute-start.2 = (bf16[2,192,768]{2,1,0:T(8,128)(2,1)S(1)}, bf16[2,192,768]{2,1,0:T(8,128)(2,1)S(1)}, u32[]{:S(2)}, u32[]{:S(2)}) collective-permute-start(bf16[2,192,768]{2,1,0:T(8,128)(2,1)S(1)} %get-tuple-element.55.refs_0_), channel_id=1, source_target_pairs={{0,2},{1,3},{2,0},{3,1},{4,6},{5,7},{6,4},{7,5},{8,10},{9,11},{10,... | collective-permute-start | bytes 1769480 | tf_op jit(solution)/shard_map/ppermute | solution.py:17
  18.9 5.0 %collective-permute-start.5 = (bf16[208,128]{1,0:T(8,128)(2,1)S(1)}, bf16[208,128]{1,0:T(8,128)(2,1)S(1)}, u32[]{:S(2)}, u32[]{:S(2)}) collective-permute-start(bf16[208,128]{1,0:T(8,128)(2,1)S(1)} %get-tuple-element.57), channel_id=1, source_target_pairs={{0,16},{8,24},{16,0},{24,8},{1,17},{9,25},{17,1},{25,9},{2,18},{10... | collective-permute-start | bytes 159752 | tf_op jit(solution)/shard_map/ppermute | solution.py:17
  21.5 6.0 %collective-permute-start.6 = (bf16[208,128]{1,0:T(8,128)(2,1)S(1)}, bf16[208,128]{1,0:T(8,128)(2,1)S(1)}, u32[]{:S(2)}, u32[]{:S(2)}) collective-permute-start(bf16[208,128]{1,0:T(8,128)(2,1)S(1)} %get-tuple-element.58), channel_id=1, source_target_pairs={{0,24},{8,16},{16,8},{24,0},{1,25},{9,17},{17,9},{25,1},{2,26},{10... | collective-permute-start | bytes 159752 | tf_op jit(solution)/shard_map/ppermute | solution.py:17
  22.9 4.7 %collective-permute-start.7 = (bf16[208,128]{1,0:T(8,128)(2,1)S(1)}, bf16[208,128]{1,0:T(8,128)(2,1)S(1)}, u32[]{:S(2)}, u32[]{:S(2)}) collective-permute-start(bf16[208,128]{1,0:T(8,128)(2,1)S(1)} %get-tuple-element.59), channel_id=1, source_target_pairs={{0,8},{8,0},{16,24},{24,16},{1,9},{9,1},{17,25},{25,17},{2,10},{10... | collective-permute-start | bytes 159752 | tf_op jit(solution)/shard_map/ppermute | solution.py:17
  28.5 4.2 %collective-permute-start.8 = (bf16[208,128]{1,0:T(8,128)(2,1)S(1)}, bf16[208,128]{1,0:T(8,128)(2,1)S(1)}, u32[]{:S(2)}, u32[]{:S(2)}) collective-permute-start(bf16[208,128]{1,0:T(8,128)(2,1)S(1)} %centre.1.own_ref), channel_id=1, source_target_pairs={{0,4},{4,0},{1,5},{5,1},{2,6},{6,2},{3,7},{7,3},{8,12},{12,8},{9,1... | collective-permute-start | bytes 159752 | tf_op jit(solution)/shard_map/ppermute | solution.py:17
  32.7 28.4 %copy-start.8 = (bf16[1,1,64,3072]{3,2,1,0:T(8,128)(2,1)S(1)}, bf16[1,1,64,3072]{3,2,1,0:T(8,128)(2,1)}, u32[]{:S(2)}) copy-start(bf16[1,1,64,3072]{3,2,1,0:T(8,128)(2,1)} %param.27) | copy-start | bytes 1179652
  32.8 7.3 %collective-permute-start.9 = (bf16[2,192,768]{2,1,0:T(8,128)(2,1)S(1)}, bf16[2,192,768]{2,1,0:T(8,128)(2,1)S(1)}, u32[]{:S(2)}, u32[]{:S(2)}) collective-permute-start(bf16[2,192,768]{2,1,0:T(8,128)(2,1)S(1)} %get-tuple-element.61), channel_id=1, source_target_pairs={{0,1},{1,0},{2,3},{3,2},{4,5},{5,4},{6,7},{7,6},{8,9},{9,8},{10,11... | collective-permute-start | bytes 1769480 | tf_op jit(solution)/shard_map/ppermute | solution.py:17
  32.9 5.8 %collective-permute-start.10 = (bf16[416,128]{1,0:T(8,128)(2,1)S(1)}, bf16[416,128]{1,0:T(8,128)(2,1)S(1)}, u32[]{:S(2)}, u32[]{:S(2)}) collective-permute-start(bf16[416,128]{1,0:T(8,128)(2,1)S(1)} %join.1.dep_ref.refs_0_), channel_id=1, source_target_pairs={{0,2},{1,3},{2,0},{3,1},{4,6},{5,7},{6,4},{7,5},{8,10},{9,11},{10,... | collective-permute-start | bytes 319496 | tf_op jit(solution)/shard_map/ppermute | solution.py:17
  34.7 5.4 %collective-permute-start.11 = (bf16[416,128]{1,0:T(8,128)(2,1)S(1)}, bf16[416,128]{1,0:T(8,128)(2,1)S(1)}, u32[]{:S(2)}, u32[]{:S(2)}) collective-permute-start(bf16[416,128]{1,0:T(8,128)(2,1)S(1)} %join.1.dep_ref.refs_0_), channel_id=1, source_target_pairs={{0,3},{1,2},{2,1},{3,0},{4,7},{5,6},{6,5},{7,4},{8,11},{9,10},{10,... | collective-permute-start | bytes 319496 | tf_op jit(solution)/shard_map/ppermute | solution.py:17
  34.8 5.3 %collective-permute-start.12 = (bf16[416,128]{1,0:T(8,128)(2,1)S(1)}, bf16[416,128]{1,0:T(8,128)(2,1)S(1)}, u32[]{:S(2)}, u32[]{:S(2)}) collective-permute-start(bf16[416,128]{1,0:T(8,128)(2,1)S(1)} %join.1.dep_ref.refs_0_), channel_id=1, source_target_pairs={{0,1},{1,0},{2,3},{3,2},{4,5},{5,4},{6,7},{7,6},{8,9},{9,8},{10,11... | collective-permute-start | bytes 319496 | tf_op jit(solution)/shard_map/ppermute | solution.py:17
  41.3 33.2 %copy-start.2 = (bf16[1,1,64,6144]{3,2,1,0:T(8,128)(2,1)S(1)}, bf16[1,1,64,6144]{3,2,1,0:T(8,128)(2,1)}, u32[]{:S(2)}) copy-start(bf16[1,1,64,6144]{3,2,1,0:T(8,128)(2,1)} %param.28) | copy-start | bytes 2359300
  41.3 33.2 %copy-start.6 = (bf16[1,1,64,3072]{3,2,1,0:T(8,128)(2,1)S(1)}, bf16[1,1,64,3072]{3,2,1,0:T(8,128)(2,1)}, u32[]{:S(2)}) copy-start(bf16[1,1,64,3072]{3,2,1,0:T(8,128)(2,1)} %param.29) | copy-start | bytes 1179652
  41.3 19.8 %collective-permute-start.13 = (bf16[2,128,1536]{2,1,0:T(8,128)(2,1)S(1)}, bf16[2,128,1536]{2,1,0:T(8,128)(2,1)S(1)}, u32[]{:S(2)}, u32[]{:S(2)}) collective-permute-start(bf16[2,128,1536]{2,1,0:T(8,128)(2,1)S(1)} %maps_join.1.refs_0_), channel_id=1, source_target_pairs={{0,2},{1,3},{2,0},{3,1},{4,6},{5,7},{6,4},{7,5},{8,10},{9,11},{10,... | collective-permute-start | bytes 2359304 | tf_op jit(solution)/shard_map/ppermute | solution.py:17
  43.1 11.1 %collective-permute-start.14 = (bf16[400,128]{1,0:T(8,128)(2,1)S(1)}, bf16[400,128]{1,0:T(8,128)(2,1)S(1)}, u32[]{:S(2)}, u32[]{:S(2)}) collective-permute-start(bf16[400,128]{1,0:T(8,128)(2,1)S(1)} %get-tuple-element.66), channel_id=1, source_target_pairs={{0,16},{8,24},{16,0},{24,8},{1,17},{9,25},{17,1},{25,9},{2,18},{10... | collective-permute-start | bytes 307208 | tf_op jit(solution)/shard_map/ppermute | solution.py:17
  45.7 8.5 %collective-permute-start.15 = (bf16[400,128]{1,0:T(8,128)(2,1)S(1)}, bf16[400,128]{1,0:T(8,128)(2,1)S(1)}, u32[]{:S(2)}, u32[]{:S(2)}) collective-permute-start(bf16[400,128]{1,0:T(8,128)(2,1)S(1)} %get-tuple-element.67), channel_id=1, source_target_pairs={{0,24},{8,16},{16,8},{24,0},{1,25},{9,17},{17,9},{25,1},{2,26},{10... | collective-permute-start | bytes 307208 | tf_op jit(solution)/shard_map/ppermute | solution.py:17
  47.1 7.5 %collective-permute-start.16 = (bf16[400,128]{1,0:T(8,128)(2,1)S(1)}, bf16[400,128]{1,0:T(8,128)(2,1)S(1)}, u32[]{:S(2)}, u32[]{:S(2)}) collective-permute-start(bf16[400,128]{1,0:T(8,128)(2,1)S(1)} %get-tuple-element.68), channel_id=1, source_target_pairs={{0,8},{8,0},{16,24},{24,16},{1,9},{9,1},{17,25},{25,17},{2,10},{10... | collective-permute-start | bytes 307208 | tf_op jit(solution)/shard_map/ppermute | solution.py:17
  54.8 11.0 %collective-permute-start.17 = (bf16[64,768]{1,0:T(8,128)(2,1)S(1)}, bf16[64,768]{1,0:T(8,128)(2,1)S(1)}, u32[]{:S(2)}, u32[]{:S(2)}) collective-permute-start(bf16[64,768]{1,0:T(8,128)(2,1)S(1)} %finish.1.refs_0_), channel_id=1, source_target_pairs={{0,16},{8,24},{16,0},{24,8},{1,17},{9,25},{17,1},{25,9},{2,18},{10... | collective-permute-start | bytes 294920 | tf_op jit(solution)/shard_map/ppermute | solution.py:17
  58.3 7.5 %collective-permute-start.18 = (bf16[64,768]{1,0:T(8,128)(2,1)S(1)}, bf16[64,768]{1,0:T(8,128)(2,1)S(1)}, u32[]{:S(2)}, u32[]{:S(2)}) collective-permute-start(bf16[64,768]{1,0:T(8,128)(2,1)S(1)} %finish.1.refs_0_), channel_id=1, source_target_pairs={{0,24},{8,16},{16,8},{24,0},{1,25},{9,17},{17,9},{25,1},{2,26},{10... | collective-permute-start | bytes 294920 | tf_op jit(solution)/shard_map/ppermute | solution.py:17
  58.8 8.1 %collective-permute-start.19 = (bf16[64,768]{1,0:T(8,128)(2,1)S(1)}, bf16[64,768]{1,0:T(8,128)(2,1)S(1)}, u32[]{:S(2)}, u32[]{:S(2)}) collective-permute-start(bf16[64,768]{1,0:T(8,128)(2,1)S(1)} %finish.1.refs_0_), channel_id=1, source_target_pairs={{0,8},{8,0},{16,24},{24,16},{1,9},{9,1},{17,25},{25,17},{2,10},{10... | collective-permute-start | bytes 294920 | tf_op jit(solution)/shard_map/ppermute | solution.py:17
  68.3 8.9 %collective-permute-start.22 = (bf16[128,768]{1,0:T(8,128)(2,1)}, bf16[128,768]{1,0:T(8,128)(2,1)S(1)}, u32[]{:S(2)}, u32[]{:S(2)}) collective-permute-start(bf16[128,768]{1,0:T(8,128)(2,1)} %get-tuple-element.76), channel_id=1, source_target_pairs={{0,1},{1,0},{2,3},{3,2},{4,5},{5,4},{6,7},{7,6},{8,9},{9,8},{10,11... | collective-permute-start | bytes 589832 | tf_op jit(solution)/shard_map/ppermute | solution.py:17
  68.3 11.5 %collective-permute-start.24 = (bf16[128,768]{1,0:T(8,128)(2,1)S(1)}, bf16[128,768]{1,0:T(8,128)(2,1)S(1)}, u32[]{:S(2)}, u32[]{:S(2)}) collective-permute-start(bf16[128,768]{1,0:T(8,128)(2,1)S(1)} %get-tuple-element.79), channel_id=1, source_target_pairs={{0,2},{1,3},{2,0},{3,1},{4,6},{5,7},{6,4},{7,5},{8,10},{9,11},{10,... | collective-permute-start | bytes 589832 | tf_op jit(solution)/shard_map/ppermute | solution.py:17
  68.8 13.8 %collective-permute-start.26 = (bf16[128,768]{1,0:T(8,128)(2,1)S(1)}, bf16[128,768]{1,0:T(8,128)(2,1)S(1)}, u32[]{:S(2)}, u32[]{:S(2)}) collective-permute-start(bf16[128,768]{1,0:T(8,128)(2,1)S(1)} %get-tuple-element.82), channel_id=1, source_target_pairs={{0,3},{1,2},{2,1},{3,0},{4,7},{5,6},{6,5},{7,4},{8,11},{9,10},{10,... | collective-permute-start | bytes 589832 | tf_op jit(solution)/shard_map/ppermute | solution.py:17
  70.2 4.3 %collective-permute-start.20 = (f32[2,64,64]{2,1,0:T(8,128)S(1)}, f32[2,64,64]{2,1,0:T(8,128)S(1)}, u32[]{:S(2)}, u32[]{:S(2)}) collective-permute-start(f32[2,64,64]{2,1,0:T(8,128)S(1)} %get-tuple-element.65.dep_ref.low_ref), channel_id=1, source_target_pairs={{0,4},{4,0},{1,5},{5,1},{2,6},{6,2},{3,7},{7,3},{8,12},{12,8},{9,1... | collective-permute-start | bytes 98312 | tf_op jit(solution)/shard_map/ppermute | solution.py:17
  75.7 4.2 %collective-permute-start.21 = (bf16[64,384]{1,0:T(8,128)(2,1)S(1)}, bf16[64,384]{1,0:T(8,128)(2,1)S(1)}, u32[]{:S(2)}, u32[]{:S(2)}) collective-permute-start(bf16[64,384]{1,0:T(8,128)(2,1)S(1)} %get-tuple-element.75), channel_id=1, source_target_pairs={{0,4},{4,0},{1,5},{5,1},{2,6},{6,2},{3,7},{7,3},{8,12},{12,8},{9,1... | collective-permute-start | bytes 147464 | tf_op jit(solution)/shard_map/ppermute | solution.py:17
  78.1 4.4 %collective-permute-start.23 = (bf16[64,384]{1,0:T(8,128)(2,1)S(1)}, bf16[64,384]{1,0:T(8,128)(2,1)S(1)}, u32[]{:S(2)}, u32[]{:S(2)}) collective-permute-start(bf16[64,384]{1,0:T(8,128)(2,1)S(1)} %get-tuple-element.78), channel_id=1, source_target_pairs={{0,4},{4,0},{1,5},{5,1},{2,6},{6,2},{3,7},{7,3},{8,12},{12,8},{9,1... | collective-permute-start | bytes 147464 | tf_op jit(solution)/shard_map/ppermute | solution.py:17
  80.7 4.5 %collective-permute-start.25 = (bf16[64,384]{1,0:T(8,128)(2,1)S(1)}, bf16[64,384]{1,0:T(8,128)(2,1)S(1)}, u32[]{:S(2)}, u32[]{:S(2)}) collective-permute-start(bf16[64,384]{1,0:T(8,128)(2,1)S(1)} %get-tuple-element.81), channel_id=1, source_target_pairs={{0,4},{4,0},{1,5},{5,1},{2,6},{6,2},{3,7},{7,3},{8,12},{12,8},{9,1... | collective-permute-start | bytes 147464 | tf_op jit(solution)/shard_map/ppermute | solution.py:17
  83.5 4.2 %collective-permute-start.27 = (bf16[64,384]{1,0:T(8,128)(2,1)S(1)}, bf16[64,384]{1,0:T(8,128)(2,1)S(1)}, u32[]{:S(2)}, u32[]{:S(2)}) collective-permute-start(bf16[64,384]{1,0:T(8,128)(2,1)S(1)} %get-tuple-element.84), channel_id=1, source_target_pairs={{0,4},{4,0},{1,5},{5,1},{2,6},{6,2},{3,7},{7,3},{8,12},{12,8},{9,1... | collective-permute-start | bytes 147464 | tf_op jit(solution)/shard_map/ppermute | solution.py:17
  (12 other events, 75.0 us)

commit v9 on v7

--- a/solution.py
+++ b/solution.py
@@ -378,36 +378,29 @@
     out_ref[features:] = extra.astype(BF16)
 
 
-def pass_on_kernel(core_ref, got_ref, dep_ref, own_ref, next_ref):
+def pass_on_kernel(core_ref, got_ref, *refs):
+    own_ref, next_ref = refs[-2:]
     own_ref[...] = got_ref[0]
     next_ref[0] = core_ref[...]
     next_ref[1] = got_ref[1]
 
 
-def join_kernel(own_ref, got_ref, dep_ref, out_ref):
-    size = own_ref.shape[0]
-    out_ref[:size] = own_ref[...]
-    out_ref[size:] = got_ref[...]
-
-
-def project_kernel(n_seq, n_req, n_enc, own_ref, pair_ref, next_ref, *refs):
-    payload_refs = dict(zip([0] + far_first(n_req), refs))
+def project_kernel(n_seq, n_req, n_enc, order, own_ref, pair_ref, next_ref, *refs):
+    payload_refs = dict(zip([(0, 0)] + order, refs))
     weight_refs = (own_ref, next_ref.at[0], pair_ref, next_ref.at[1])
-    prompts_ref, keep_ref = refs[n_req : n_req + 2]
-    send_refs = refs[n_req + 2 : -1]
+    prompts_ref, keep_ref, *send_refs = refs[n_seq * n_req : -1]
     rows_ref = refs[-1]
     features, width = weight_refs[0].shape
-    tokens = payload_refs[0].shape[1]
-    stride = features + ROWS
+    tokens = payload_refs[0, 0].shape[1]
     total = None
     squares = [jnp.zeros((1, tokens), F32) for _ in range(n_seq)]
     for k in range(n_req):
         left = []
         shifts = []
         for p in range(n_seq):
-            payload = payload_refs[k]
-            left.append(payload[p * stride : p * stride + features].T)
-            extra = payload[p * stride + features : (p + 1) * stride].astype(F32)
+            payload = payload_refs[p, k]
+            left.append(payload[:features].T)
+            extra = payload[features:].astype(F32)
             squares[p] = squares[p] + extra[0:1] + extra[1:2]
             pieces = [extra[2 + j : 3 + j] for j in range(pl.cdiv(features, tokens))]
             shifts.append(jnp.concatenate(pieces, axis=1)[:, :features])
@@ -738,19 +731,25 @@
         [SMEM, ANY] + [VMEM] * (5 + len(arrived)),
         name="centre",
     )
-    joined = call(
-        join_kernel,
-        struct((n_seq * (features + ROWS), tokens)),
-        (own, swap(own, "seq", n_seq, 1), image_got[0]),
-        [VMEM, VMEM, ANY],
-        name="join",
-    )
-    payloads = partners(lambda k: joined, "req", n_req)
+    order = [(i, k) for k in far_first(n_req) + [0] for i in (1, 0) if i or k]
+    payloads = {
+        (i, k): lax.ppermute(
+            own,
+            ("seq", "req"),
+            [
+                (a * n_req + b, (a ^ i) * n_req + (b ^ k))
+                for a in range(n_seq)
+                for b in range(n_req)
+            ],
+        )
+        for i, k in order
+    }
+    early = [payloads[place] for place in order[:5]]
     weight_own_pair, weight_next = call(
         pass_on_kernel,
         (weight, struct((2, features, 2 * half))),
-        (weight_core, weight_pair_got, joined),
-        [VMEM, VMEM, ANY],
+        (weight_core, weight_pair_got, image_got[0], *early),
+        [VMEM, VMEM] + [ANY] * (1 + len(early)),
         name="pass_on",
     )
     weight_next = swap(weight_next, "req", n_req, 1)
@@ -758,10 +757,10 @@
     size = n_seq * tokens // n_enc
     step = 2 * half // HDIM * size + ROWS
     ids, keep, *sends = call(
-        functools.partial(project_kernel, n_seq, n_req, n_enc),
+        functools.partial(project_kernel, n_seq, n_req, n_enc, order),
         (struct((n_req,), jnp.int32), struct((step, HDIM), F32))
         + tuple(struct((step, HDIM)) for _ in range(1, n_enc)),
-        (weight_own, weight_own_pair, weight_next, joined, *payloads.values()),
+        (weight_own, weight_own_pair, weight_next, own, *payloads.values()),
         scratch=[pltpu.VMEM((n_enc * step, HDIM), F32)],
         out_specs=(SMEM,) + (VMEM,) * n_enc,
         name="project",
@@ -771,7 +770,7 @@
     maps = call(
         join_maps_kernel,
         struct((2, 2 * rank, part)),
-        (maps, maps_core, joined),
+        (maps, maps_core, own),
         [VMEM, VMEM, ANY],
         name="maps_join",
     )

time: 80.7 us -> 84.2 us (1.043)
  waiting for transfers between devices: 34 us -> 38.4 us
  starting transfers between devices: 33 us -> 32.1 us
    ppermute x0 -> x7, waiting for transfers between devices: none -> 11.9 us  [per_device_heads(): lax.ppermute(own, ('seq', 'req'), [(a * n_req + b, (a ^ i) * n_req + (b ^...]
    ppermute x28 -> x24, waiting for transfers between devices: 34 us -> 26.5 us  [swap(): return lax.ppermute(block, axis, [(i, i ^ step) for i in range(size)])]
    ppermute x28 -> x24, starting transfers between devices: 33 us -> 27.8 us  [swap(): return lax.ppermute(block, axis, [(i, i ^ step) for i in range(size)])]
    ppermute x0 -> x7, starting transfers between devices: none -> 4.36 us  [per_device_heads(): lax.ppermute(own, ('seq', 'req'), [(a * n_req + b, (a ^ i) * n_req + (b ^...]
    pallas_call x20 -> x19, Pallas kernels: 8.64 us -> 8.65 us  [call(): pl.pallas_call(kernel, out_shape=outs, in_specs=specs if specs is not Non...]
  transfers between devices with their start and end apart: 28 -> 31, of which waited for: 16 -> 20; matrix products, arithmetic and copies ran while one was open for 0% -> 0% of each run, Pallas kernels for 6% -> 6%
where the time goes in v9:
time: 84.2 us; the launch traced here: 84 us
  waiting for transfers between devices  38.4 us (46%)
  starting transfers between devices  32.1 us (38%)
  Pallas kernels  8.65 us (10%)
  local copies, waits for them, and re-layouts  3.22 us (4%)
  between operations  1.57 us (2%)
    ppermute x24, starting transfers between devices, swap(): return lax.ppermute(block, axis, [(i, i ^ step) for i in range(size)])  27.8 us
    ppermute x24, waiting for transfers between devices, swap(): return lax.ppermute(block, axis, [(i, i ^ step) for i in range(size)])  26.5 us
    ppermute x7, waiting for transfers between devices, per_device_heads(): lax.ppermute(own, ('seq', 'req'), [(a * n_req + b, (a ^ i) * n_req + (b ^...  11.9 us
    pallas_call x19, Pallas kernels, call(): pl.pallas_call(kernel, out_shape=outs, in_specs=specs if specs is not Non...  8.65 us
    ppermute x7, starting transfers between devices, per_device_heads(): lax.ppermute(own, ('seq', 'req'), [(a * n_req + b, (a ^ i) * n_req + (b ^...  4.36 us
    unnamed x28, local copies, waits for them, and re-layouts  3.03 us
  transfers between devices with their start and end apart: 31, of which 20 were waited for; matrix products, arithmetic and copies ran while one was open for 0% of the time, Pallas kernels for 6%

profile of v9, /device:TPU:0, one launch (start us, length us, event | category | flops | bytes accessed | tf_op | source)
XLA Modules:
  0.0 84.0 jit_solution(12143628583225147233)
XLA Ops:
  0.0 1.5 %copy-done.3 = bf16[256,3072]{1,0:T(8,128)(2,1)S(1)} copy-done((bf16[256,3072]{1,0:T(8,128)(2,1)S(1)}, bf16[256,3072]{1,0:T(8,128)(2,1)}, u32[]{:S(2)}) %copy-start.3) | copy-done | bytes 1572888
  4.2 1.4 %collective-permute-done.got_ref = bf16[1552,128]{1,0:T(8,128)(2,1)S(1)} collective-permute-done((bf16[1552,128]{1,0:T(8,128)(2,1)S(1)}, bf16[1552,128]{1,0:T(8,128)(2,1)S(1)}, u32[]{:S(2)}, u32[]{:S(2)}) %collective-permute-start) | collective-permute-done | bytes 397344 | tf_op jit(solution)/shard_map/ppermute | solution.py:17
  5.7 3.0 %collective-permute-start.1 = (bf16[784,128]{1,0:T(8,128)(2,1)S(1)}, bf16[784,128]{1,0:T(8,128)(2,1)S(1)}, u32[]{:S(2)}, u32[]{:S(2)}) collective-permute-start(bf16[784,128]{1,0:T(8,128)(2,1)S(1)} %get-tuple-element.51), channel_id=1, source_target_pairs={{0,2},{1,3},{2,0},{3,1},{4,6},{5,7},{6,4},{7,5},{8,10},{9,11},{10,... | collective-permute-start | bytes 602120 | tf_op jit(solution)/shard_map/ppermute | solution.py:17
  8.8 1.6 %collective-permute-start.3 = (bf16[4,64,1536]{2,1,0:T(8,128)(2,1)S(1)}, bf16[4,64,1536]{2,1,0:T(8,128)(2,1)S(1)}, u32[]{:S(2)}, u32[]{:S(2)}) collective-permute-start(bf16[4,64,1536]{2,1,0:T(8,128)(2,1)S(1)} %image_pack.1), channel_id=1, source_target_pairs={{0,4},{4,0},{1,5},{5,1},{2,6},{6,2},{3,7},{7,3},{8,12},{12,8},{9,1... | collective-permute-start | bytes 2359304 | tf_op jit(solution)/shard_map/ppermute | solution.py:17
  10.9 3.0 %collective-permute-done.1.got_ref = bf16[784,128]{1,0:T(8,128)(2,1)S(1)} collective-permute-done((bf16[784,128]{1,0:T(8,128)(2,1)S(1)}, bf16[784,128]{1,0:T(8,128)(2,1)S(1)}, u32[]{:S(2)}, u32[]{:S(2)}) %collective-permute-start.1) | collective-permute-done | bytes 200736 | tf_op jit(solution)/shard_map/ppermute | solution.py:17
  14.0 1.8 %collective-permute-start.2 = (bf16[2,192,768]{2,1,0:T(8,128)(2,1)S(1)}, bf16[2,192,768]{2,1,0:T(8,128)(2,1)S(1)}, u32[]{:S(2)}, u32[]{:S(2)}) collective-permute-start(bf16[2,192,768]{2,1,0:T(8,128)(2,1)S(1)} %get-tuple-element.55.refs_0_), channel_id=1, source_target_pairs={{0,2},{1,3},{2,0},{3,1},{4,6},{5,7},{6,4},{7,5},{8,10},{9,11},{10,... | collective-permute-start | bytes 1769480 | tf_op jit(solution)/shard_map/ppermute | solution.py:17
  15.8 2.6 %collective-permute-start.5 = (bf16[208,128]{1,0:T(8,128)(2,1)S(1)}, bf16[208,128]{1,0:T(8,128)(2,1)S(1)}, u32[]{:S(2)}, u32[]{:S(2)}) collective-permute-start(bf16[208,128]{1,0:T(8,128)(2,1)S(1)} %get-tuple-element.57), channel_id=1, source_target_pairs={{0,16},{8,24},{16,0},{24,8},{1,17},{9,25},{17,1},{25,9},{2,18},{10... | collective-permute-start | bytes 159752 | tf_op jit(solution)/shard_map/ppermute | solution.py:17
  18.4 1.3 %collective-permute-start.6 = (bf16[208,128]{1,0:T(8,128)(2,1)S(1)}, bf16[208,128]{1,0:T(8,128)(2,1)S(1)}, u32[]{:S(2)}, u32[]{:S(2)}) collective-permute-start(bf16[208,128]{1,0:T(8,128)(2,1)S(1)} %get-tuple-element.58), channel_id=1, source_target_pairs={{0,24},{8,16},{16,8},{24,0},{1,25},{9,17},{17,9},{25,1},{2,26},{10... | collective-permute-start | bytes 159752 | tf_op jit(solution)/shard_map/ppermute | solution.py:17
  21.0 3.4 %collective-permute-done.6.refs_1_ = bf16[208,128]{1,0:T(8,128)(2,1)S(1)} collective-permute-done((bf16[208,128]{1,0:T(8,128)(2,1)S(1)}, bf16[208,128]{1,0:T(8,128)(2,1)S(1)}, u32[]{:S(2)}, u32[]{:S(2)}) %collective-permute-start.6) | collective-permute-done | bytes 53280 | tf_op jit(solution)/shard_map/ppermute | solution.py:17
  24.7 1.5 %collective-permute-start.8 = (bf16[208,128]{1,0:T(8,128)(2,1)S(1)}, bf16[208,128]{1,0:T(8,128)(2,1)S(1)}, u32[]{:S(2)}, u32[]{:S(2)}) collective-permute-start(bf16[208,128]{1,0:T(8,128)(2,1)S(1)} %centre.1.refs_0_.dep_ref), channel_id=1, source_target_pairs={{0,6},{1,7},{2,4},{3,5},{4,2},{5,3},{6,0},{7,1},{8,14},{9,15},{10,... | collective-permute-start | bytes 159752 | tf_op jit(solution)/shard_map/ppermute | solution.py:736
  26.2 1.5 %collective-permute-start.9 = (bf16[208,128]{1,0:T(8,128)(2,1)S(1)}, bf16[208,128]{1,0:T(8,128)(2,1)S(1)}, u32[]{:S(2)}, u32[]{:S(2)}) collective-permute-start(bf16[208,128]{1,0:T(8,128)(2,1)S(1)} %centre.1.refs_0_.dep_ref), channel_id=1, source_target_pairs={{0,2},{1,3},{2,0},{3,1},{4,6},{5,7},{6,4},{7,5},{8,10},{9,11},{10,... | collective-permute-start | bytes 159752 | tf_op jit(solution)/shard_map/ppermute | solution.py:736
  27.7 2.2 %collective-permute-done.8.refs_1_ = bf16[208,128]{1,0:T(8,128)(2,1)S(1)} collective-permute-done((bf16[208,128]{1,0:T(8,128)(2,1)S(1)}, bf16[208,128]{1,0:T(8,128)(2,1)S(1)}, u32[]{:S(2)}, u32[]{:S(2)}) %collective-permute-start.8) | collective-permute-done | bytes 53280 | tf_op jit(solution)/shard_map/ppermute | solution.py:736
  29.9 2.4 %collective-permute-done.9.refs_2_ = bf16[208,128]{1,0:T(8,128)(2,1)S(1)} collective-permute-done((bf16[208,128]{1,0:T(8,128)(2,1)S(1)}, bf16[208,128]{1,0:T(8,128)(2,1)S(1)}, u32[]{:S(2)}, u32[]{:S(2)}) %collective-permute-start.9) | collective-permute-done | bytes 53280 | tf_op jit(solution)/shard_map/ppermute | solution.py:736
  32.3 1.3 %collective-permute-done.11.refs_4_ = bf16[208,128]{1,0:T(8,128)(2,1)S(1)} collective-permute-done((bf16[208,128]{1,0:T(8,128)(2,1)S(1)}, bf16[208,128]{1,0:T(8,128)(2,1)S(1)}, u32[]{:S(2)}, u32[]{:S(2)}) %collective-permute-start.11) | collective-permute-done | bytes 53280 | tf_op jit(solution)/shard_map/ppermute | solution.py:736
  33.6 2.8 %collective-permute-done.12.refs_5_ = bf16[208,128]{1,0:T(8,128)(2,1)S(1)} collective-permute-done((bf16[208,128]{1,0:T(8,128)(2,1)S(1)}, bf16[208,128]{1,0:T(8,128)(2,1)S(1)}, u32[]{:S(2)}, u32[]{:S(2)}) %collective-permute-start.12) | collective-permute-done | bytes 53280 | tf_op jit(solution)/shard_map/ppermute | solution.py:736
  38.6 2.6 %collective-permute-done.15.refs_7_ = bf16[208,128]{1,0:T(8,128)(2,1)S(1)} collective-permute-done((bf16[208,128]{1,0:T(8,128)(2,1)S(1)}, bf16[208,128]{1,0:T(8,128)(2,1)S(1)}, u32[]{:S(2)}, u32[]{:S(2)}) %collective-permute-start.15) | collective-permute-done | bytes 53280 | tf_op jit(solution)/shard_map/ppermute | solution.py:736
  41.2 1.2 %project.1 = (s32[4]{0:T(128)S(1)}, f32[400,128]{1,0:T(8,128)S(1)}, bf16[400,128]{1,0:T(8,128)(2,1)S(1)}, bf16[400,128]{1,0:T(8,128)(2,1)S(1)}, bf16[400,128]{1,0:T(8,128)(2,1)S(1)}) custom-call(bf16[192,768]{1,0:T(8,128)(2,1)S(1)} %get-tuple-element.46.own_ref, bf16[192,768]{1,0:T(8,128)(2,1)S(1)} %get-tuple-element.60.pair_ref, ...), custom_call_target="tpu_custom_call" | custom-call | tf_op jit(solution)/shard_map/project/pallas_call | solution.py:280
  42.4 1.5 %collective-permute-start.16 = (bf16[2,128,1536]{2,1,0:T(8,128)(2,1)S(1)}, bf16[2,128,1536]{2,1,0:T(8,128)(2,1)S(1)}, u32[]{:S(2)}, u32[]{:S(2)}) collective-permute-start(bf16[2,128,1536]{2,1,0:T(8,128)(2,1)S(1)} %maps_join.1.refs_0_), channel_id=1, source_target_pairs={{0,2},{1,3},{2,0},{3,1},{4,6},{5,7},{6,4},{7,5},{8,10},{9,11},{10,... | collective-permute-start | bytes 2359304 | tf_op jit(solution)/shard_map/ppermute | solution.py:17
  43.9 2.6 %collective-permute-start.18 = (bf16[400,128]{1,0:T(8,128)(2,1)S(1)}, bf16[400,128]{1,0:T(8,128)(2,1)S(1)}, u32[]{:S(2)}, u32[]{:S(2)}) collective-permute-start(bf16[400,128]{1,0:T(8,128)(2,1)S(1)} %get-tuple-element.68), channel_id=1, source_target_pairs={{0,16},{8,24},{16,0},{24,8},{1,17},{9,25},{17,1},{25,9},{2,18},{10... | collective-permute-start | bytes 307208 | tf_op jit(solution)/shard_map/ppermute | solution.py:17
  46.5 1.3 %collective-permute-start.19 = (bf16[400,128]{1,0:T(8,128)(2,1)S(1)}, bf16[400,128]{1,0:T(8,128)(2,1)S(1)}, u32[]{:S(2)}, u32[]{:S(2)}) collective-permute-start(bf16[400,128]{1,0:T(8,128)(2,1)S(1)} %get-tuple-element.69), channel_id=1, source_target_pairs={{0,24},{8,16},{16,8},{24,0},{1,25},{9,17},{17,9},{25,1},{2,26},{10... | collective-permute-start | bytes 307208 | tf_op jit(solution)/shard_map/ppermute | solution.py:17
  48.1 5.2 %collective-permute-done.18.refs_0_ = bf16[400,128]{1,0:T(8,128)(2,1)S(1)} collective-permute-done((bf16[400,128]{1,0:T(8,128)(2,1)S(1)}, bf16[400,128]{1,0:T(8,128)(2,1)S(1)}, u32[]{:S(2)}, u32[]{:S(2)}) %collective-permute-start.18) | collective-permute-done | bytes 102432 | tf_op jit(solution)/shard_map/ppermute | solution.py:17
  54.4 3.4 %collective-permute-start.21 = (bf16[64,768]{1,0:T(8,128)(2,1)S(1)}, bf16[64,768]{1,0:T(8,128)(2,1)S(1)}, u32[]{:S(2)}, u32[]{:S(2)}) collective-permute-start(bf16[64,768]{1,0:T(8,128)(2,1)S(1)} %finish.1.refs_0_), channel_id=1, source_target_pairs={{0,16},{8,24},{16,0},{24,8},{1,17},{9,25},{17,1},{25,9},{2,18},{10... | collective-permute-start | bytes 294920 | tf_op jit(solution)/shard_map/ppermute | solution.py:17
  59.0 1.8 %collective-permute-done.16.refs_1_ = bf16[2,128,1536]{2,1,0:T(8,128)(2,1)S(1)} collective-permute-done((bf16[2,128,1536]{2,1,0:T(8,128)(2,1)S(1)}, bf16[2,128,1536]{2,1,0:T(8,128)(2,1)S(1)}, u32[]{:S(2)}, u32[]{:S(2)}) %collective-permute-start.16) | collective-permute-done | bytes 786464 | tf_op jit(solution)/shard_map/ppermute | solution.py:17
  62.0 3.4 %collective-permute-done.17.other_ref = f32[2,64,64]{2,1,0:T(8,128)S(1)} collective-permute-done((f32[2,64,64]{2,1,0:T(8,128)S(1)}, f32[2,64,64]{2,1,0:T(8,128)S(1)}, u32[]{:S(2)}, u32[]{:S(2)}) %collective-permute-start.17) | collective-permute-done | bytes 32800 | tf_op jit(solution)/shard_map/ppermute | solution.py:17
  67.0 1.0 %collective-permute-start.27 = (bf16[128,768]{1,0:T(8,128)(2,1)S(1)}, bf16[128,768]{1,0:T(8,128)(2,1)S(1)}, u32[]{:S(2)}, u32[]{:S(2)}) collective-permute-start(bf16[128,768]{1,0:T(8,128)(2,1)S(1)} %get-tuple-element.79), channel_id=1, source_target_pairs={{0,2},{1,3},{2,0},{3,1},{4,6},{5,7},{6,4},{7,5},{8,10},{9,11},{10,... | collective-permute-start | bytes 589832 | tf_op jit(solution)/shard_map/ppermute | solution.py:17
  69.8 1.0 %collective-permute-start.24 = (bf16[64,384]{1,0:T(8,128)(2,1)S(1)}, bf16[64,384]{1,0:T(8,128)(2,1)S(1)}, u32[]{:S(2)}, u32[]{:S(2)}) collective-permute-start(bf16[64,384]{1,0:T(8,128)(2,1)S(1)} %get-tuple-element.75), channel_id=1, source_target_pairs={{0,4},{4,0},{1,5},{5,1},{2,6},{6,2},{3,7},{7,3},{8,12},{12,8},{9,1... | collective-permute-start | bytes 147464 | tf_op jit(solution)/shard_map/ppermute | solution.py:17
  71.7 1.2 %collective-permute-start.26 = (bf16[64,384]{1,0:T(8,128)(2,1)S(1)}, bf16[64,384]{1,0:T(8,128)(2,1)S(1)}, u32[]{:S(2)}, u32[]{:S(2)}) collective-permute-start(bf16[64,384]{1,0:T(8,128)(2,1)S(1)} %get-tuple-element.78), channel_id=1, source_target_pairs={{0,4},{4,0},{1,5},{5,1},{2,6},{6,2},{3,7},{7,3},{8,12},{12,8},{9,1... | collective-permute-start | bytes 147464 | tf_op jit(solution)/shard_map/ppermute | solution.py:17
  72.9 1.1 %collective-permute-done.24.refs_1_ = bf16[64,384]{1,0:T(8,128)(2,1)S(1)} collective-permute-done((bf16[64,384]{1,0:T(8,128)(2,1)S(1)}, bf16[64,384]{1,0:T(8,128)(2,1)S(1)}, u32[]{:S(2)}, u32[]{:S(2)}) %collective-permute-start.24) | collective-permute-done | bytes 49184 | tf_op jit(solution)/shard_map/ppermute | solution.py:17
  75.7 1.0 %collective-permute-start.28 = (bf16[64,384]{1,0:T(8,128)(2,1)S(1)}, bf16[64,384]{1,0:T(8,128)(2,1)S(1)}, u32[]{:S(2)}, u32[]{:S(2)}) collective-permute-start(bf16[64,384]{1,0:T(8,128)(2,1)S(1)} %get-tuple-element.81), channel_id=1, source_target_pairs={{0,4},{4,0},{1,5},{5,1},{2,6},{6,2},{3,7},{7,3},{8,12},{12,8},{9,1... | collective-permute-start | bytes 147464 | tf_op jit(solution)/shard_map/ppermute | solution.py:17
  76.7 1.4 %collective-permute-done.29.text_ref = bf16[128,768]{1,0:T(8,128)(2,1)S(1)} collective-permute-done((bf16[128,768]{1,0:T(8,128)(2,1)S(1)}, bf16[128,768]{1,0:T(8,128)(2,1)S(1)}, u32[]{:S(2)}, u32[]{:S(2)}) %collective-permute-start.29) | collective-permute-done | bytes 196640 | tf_op jit(solution)/shard_map/ppermute | solution.py:17
  79.0 1.0 %collective-permute-start.30 = (bf16[64,384]{1,0:T(8,128)(2,1)S(1)}, bf16[64,384]{1,0:T(8,128)(2,1)S(1)}, u32[]{:S(2)}, u32[]{:S(2)}) collective-permute-start(bf16[64,384]{1,0:T(8,128)(2,1)S(1)} %get-tuple-element.84), channel_id=1, source_target_pairs={{0,4},{4,0},{1,5},{5,1},{2,6},{6,2},{3,7},{7,3},{8,12},{12,8},{9,1... | collective-permute-start | bytes 147464 | tf_op jit(solution)/shard_map/ppermute | solution.py:17
  80.0 3.2 %collective-permute-done.30.refs_7_ = bf16[64,384]{1,0:T(8,128)(2,1)S(1)} collective-permute-done((bf16[64,384]{1,0:T(8,128)(2,1)S(1)}, bf16[64,384]{1,0:T(8,128)(2,1)S(1)}, u32[]{:S(2)}, u32[]{:S(2)}) %collective-permute-start.30) | collective-permute-done | bytes 49184 | tf_op jit(solution)/shard_map/ppermute | solution.py:17
  (82 shorter events, 17.5 us)
Async XLA Ops:
  0.0 68.9 %copy-start = (s32[2,128]{1,0:T(2,128)S(1)}, s32[2,128]{1,0:T(2,128)}, u32[]{:S(2)}) copy-start(s32[2,128]{1,0:T(2,128)} %param.16) | copy-start | bytes 3076
  3.7 1.9 %collective-permute-start = (bf16[1552,128]{1,0:T(8,128)(2,1)S(1)}, bf16[1552,128]{1,0:T(8,128)(2,1)S(1)}, u32[]{:S(2)}, u32[]{:S(2)}) collective-permute-start(bf16[1552,128]{1,0:T(8,128)(2,1)S(1)} %get-tuple-element.45.dep_ref), channel_id=1, source_target_pairs={{0,1},{1,0},{2,3},{3,2},{4,5},{5,4},{6,7},{7,6},{8,9},{9,8},{10,11... | collective-permute-start | bytes 1191944 | tf_op jit(solution)/shard_map/ppermute | solution.py:17
  5.7 8.2 %collective-permute-start.1 = (bf16[784,128]{1,0:T(8,128)(2,1)S(1)}, bf16[784,128]{1,0:T(8,128)(2,1)S(1)}, u32[]{:S(2)}, u32[]{:S(2)}) collective-permute-start(bf16[784,128]{1,0:T(8,128)(2,1)S(1)} %get-tuple-element.51), channel_id=1, source_target_pairs={{0,2},{1,3},{2,0},{3,1},{4,6},{5,7},{6,4},{7,5},{8,10},{9,11},{10,... | collective-permute-start | bytes 602120 | tf_op jit(solution)/shard_map/ppermute | solution.py:17
  8.8 27.6 %collective-permute-start.3 = (bf16[4,64,1536]{2,1,0:T(8,128)(2,1)S(1)}, bf16[4,64,1536]{2,1,0:T(8,128)(2,1)S(1)}, u32[]{:S(2)}, u32[]{:S(2)}) collective-permute-start(bf16[4,64,1536]{2,1,0:T(8,128)(2,1)S(1)} %image_pack.1), channel_id=1, source_target_pairs={{0,4},{4,0},{1,5},{5,1},{2,6},{6,2},{3,7},{7,3},{8,12},{12,8},{9,1... | collective-permute-start | bytes 2359304 | tf_op jit(solution)/shard_map/ppermute | solution.py:17
  10.5 9.2 %collective-permute-start.4 = (bf16[128,1536]{1,0:T(8,128)(2,1)S(1)}, bf16[128,1536]{1,0:T(8,128)(2,1)S(1)}, u32[]{:S(2)}, u32[]{:S(2)}) collective-permute-start(bf16[128,1536]{1,0:T(8,128)(2,1)S(1)} %maps_pack.1.own_ref), channel_id=1, source_target_pairs={{0,1},{1,0},{2,3},{3,2},{4,5},{5,4},{6,7},{7,6},{8,9},{9,8},{10,11... | collective-permute-start | bytes 1179656 | tf_op jit(solution)/shard_map/ppermute | solution.py:17
  14.0 22.4 %collective-permute-start.2 = (bf16[2,192,768]{2,1,0:T(8,128)(2,1)S(1)}, bf16[2,192,768]{2,1,0:T(8,128)(2,1)S(1)}, u32[]{:S(2)}, u32[]{:S(2)}) collective-permute-start(bf16[2,192,768]{2,1,0:T(8,128)(2,1)S(1)} %get-tuple-element.55.refs_0_), channel_id=1, source_target_pairs={{0,2},{1,3},{2,0},{3,1},{4,6},{5,7},{6,4},{7,5},{8,10},{9,11},{10,... | collective-permute-start | bytes 1769480 | tf_op jit(solution)/shard_map/ppermute | solution.py:17
  15.8 5.2 %collective-permute-start.5 = (bf16[208,128]{1,0:T(8,128)(2,1)S(1)}, bf16[208,128]{1,0:T(8,128)(2,1)S(1)}, u32[]{:S(2)}, u32[]{:S(2)}) collective-permute-start(bf16[208,128]{1,0:T(8,128)(2,1)S(1)} %get-tuple-element.57), channel_id=1, source_target_pairs={{0,16},{8,24},{16,0},{24,8},{1,17},{9,25},{17,1},{25,9},{2,18},{10... | collective-permute-start | bytes 159752 | tf_op jit(solution)/shard_map/ppermute | solution.py:17
  18.4 6.0 %collective-permute-start.6 = (bf16[208,128]{1,0:T(8,128)(2,1)S(1)}, bf16[208,128]{1,0:T(8,128)(2,1)S(1)}, u32[]{:S(2)}, u32[]{:S(2)}) collective-permute-start(bf16[208,128]{1,0:T(8,128)(2,1)S(1)} %get-tuple-element.58), channel_id=1, source_target_pairs={{0,24},{8,16},{16,8},{24,0},{1,25},{9,17},{17,9},{25,1},{2,26},{10... | collective-permute-start | bytes 159752 | tf_op jit(solution)/shard_map/ppermute | solution.py:17
  19.7 4.7 %collective-permute-start.7 = (bf16[208,128]{1,0:T(8,128)(2,1)S(1)}, bf16[208,128]{1,0:T(8,128)(2,1)S(1)}, u32[]{:S(2)}, u32[]{:S(2)}) collective-permute-start(bf16[208,128]{1,0:T(8,128)(2,1)S(1)} %get-tuple-element.59), channel_id=1, source_target_pairs={{0,8},{8,0},{16,24},{24,16},{1,9},{9,1},{17,25},{25,17},{2,10},{10... | collective-permute-start | bytes 159752 | tf_op jit(solution)/shard_map/ppermute | solution.py:17
  24.7 5.2 %collective-permute-start.8 = (bf16[208,128]{1,0:T(8,128)(2,1)S(1)}, bf16[208,128]{1,0:T(8,128)(2,1)S(1)}, u32[]{:S(2)}, u32[]{:S(2)}) collective-permute-start(bf16[208,128]{1,0:T(8,128)(2,1)S(1)} %centre.1.refs_0_.dep_ref), channel_id=1, source_target_pairs={{0,6},{1,7},{2,4},{3,5},{4,2},{5,3},{6,0},{7,1},{8,14},{9,15},{10,... | collective-permute-start | bytes 159752 | tf_op jit(solution)/shard_map/ppermute | solution.py:736
  26.2 6.1 %collective-permute-start.9 = (bf16[208,128]{1,0:T(8,128)(2,1)S(1)}, bf16[208,128]{1,0:T(8,128)(2,1)S(1)}, u32[]{:S(2)}, u32[]{:S(2)}) collective-permute-start(bf16[208,128]{1,0:T(8,128)(2,1)S(1)} %centre.1.refs_0_.dep_ref), channel_id=1, source_target_pairs={{0,2},{1,3},{2,0},{3,1},{4,6},{5,7},{6,4},{7,5},{8,10},{9,11},{10,... | collective-permute-start | bytes 159752 | tf_op jit(solution)/shard_map/ppermute | solution.py:736
  27.7 4.6 %collective-permute-start.10 = (bf16[208,128]{1,0:T(8,128)(2,1)S(1)}, bf16[208,128]{1,0:T(8,128)(2,1)S(1)}, u32[]{:S(2)}, u32[]{:S(2)}) collective-permute-start(bf16[208,128]{1,0:T(8,128)(2,1)S(1)} %centre.1.refs_0_.dep_ref), channel_id=1, source_target_pairs={{0,7},{1,6},{2,5},{3,4},{4,3},{5,2},{6,1},{7,0},{8,15},{9,14},{10,... | collective-permute-start | bytes 159752 | tf_op jit(solution)/shard_map/ppermute | solution.py:736
  29.9 3.7 %collective-permute-start.11 = (bf16[208,128]{1,0:T(8,128)(2,1)S(1)}, bf16[208,128]{1,0:T(8,128)(2,1)S(1)}, u32[]{:S(2)}, u32[]{:S(2)}) collective-permute-start(bf16[208,128]{1,0:T(8,128)(2,1)S(1)} %centre.1.refs_0_.dep_ref), channel_id=1, source_target_pairs={{0,3},{1,2},{2,1},{3,0},{4,7},{5,6},{6,5},{7,4},{8,11},{9,10},{10,... | collective-permute-start | bytes 159752 | tf_op jit(solution)/shard_map/ppermute | solution.py:736
  32.3 4.1 %collective-permute-start.12 = (bf16[208,128]{1,0:T(8,128)(2,1)S(1)}, bf16[208,128]{1,0:T(8,128)(2,1)S(1)}, u32[]{:S(2)}, u32[]{:S(2)}) collective-permute-start(bf16[208,128]{1,0:T(8,128)(2,1)S(1)} %centre.1.refs_0_.dep_ref), channel_id=1, source_target_pairs={{0,5},{1,4},{2,7},{3,6},{4,1},{5,0},{6,3},{7,2},{8,13},{9,12},{10,... | collective-permute-start | bytes 159752 | tf_op jit(solution)/shard_map/ppermute | solution.py:736
  36.5 4.7 %collective-permute-start.13 = (bf16[2,192,768]{2,1,0:T(8,128)(2,1)S(1)}, bf16[2,192,768]{2,1,0:T(8,128)(2,1)S(1)}, u32[]{:S(2)}, u32[]{:S(2)}) collective-permute-start(bf16[2,192,768]{2,1,0:T(8,128)(2,1)S(1)} %get-tuple-element.61), channel_id=1, source_target_pairs={{0,1},{1,0},{2,3},{3,2},{4,5},{5,4},{6,7},{7,6},{8,9},{9,8},{10,11... | collective-permute-start | bytes 1769480 | tf_op jit(solution)/shard_map/ppermute | solution.py:17
  36.6 2.0 %collective-permute-start.14 = (bf16[208,128]{1,0:T(8,128)(2,1)S(1)}, bf16[208,128]{1,0:T(8,128)(2,1)S(1)}, u32[]{:S(2)}, u32[]{:S(2)}) collective-permute-start(bf16[208,128]{1,0:T(8,128)(2,1)S(1)} %centre.1.refs_0_.dep_ref), channel_id=1, source_target_pairs={{0,1},{1,0},{2,3},{3,2},{4,5},{5,4},{6,7},{7,6},{8,9},{9,8},{10,11... | collective-permute-start | bytes 159752 | tf_op jit(solution)/shard_map/ppermute | solution.py:736
  37.1 4.1 %collective-permute-start.15 = (bf16[208,128]{1,0:T(8,128)(2,1)S(1)}, bf16[208,128]{1,0:T(8,128)(2,1)S(1)}, u32[]{:S(2)}, u32[]{:S(2)}) collective-permute-start(bf16[208,128]{1,0:T(8,128)(2,1)S(1)} %centre.1.refs_0_.dep_ref), channel_id=1, source_target_pairs={{0,4},{1,5},{2,6},{3,7},{4,0},{5,1},{6,2},{7,3},{8,12},{9,13},{10,... | collective-permute-start | bytes 159752 | tf_op jit(solution)/shard_map/ppermute | solution.py:736
  42.4 18.4 %collective-permute-start.16 = (bf16[2,128,1536]{2,1,0:T(8,128)(2,1)S(1)}, bf16[2,128,1536]{2,1,0:T(8,128)(2,1)S(1)}, u32[]{:S(2)}, u32[]{:S(2)}) collective-permute-start(bf16[2,128,1536]{2,1,0:T(8,128)(2,1)S(1)} %maps_join.1.refs_0_), channel_id=1, source_target_pairs={{0,2},{1,3},{2,0},{3,1},{4,6},{5,7},{6,4},{7,5},{8,10},{9,11},{10,... | collective-permute-start | bytes 2359304 | tf_op jit(solution)/shard_map/ppermute | solution.py:17
  43.9 9.4 %collective-permute-start.18 = (bf16[400,128]{1,0:T(8,128)(2,1)S(1)}, bf16[400,128]{1,0:T(8,128)(2,1)S(1)}, u32[]{:S(2)}, u32[]{:S(2)}) collective-permute-start(bf16[400,128]{1,0:T(8,128)(2,1)S(1)} %get-tuple-element.68), channel_id=1, source_target_pairs={{0,16},{8,24},{16,0},{24,8},{1,17},{9,25},{17,1},{25,9},{2,18},{10... | collective-permute-start | bytes 307208 | tf_op jit(solution)/shard_map/ppermute | solution.py:17
  46.5 7.3 %collective-permute-start.19 = (bf16[400,128]{1,0:T(8,128)(2,1)S(1)}, bf16[400,128]{1,0:T(8,128)(2,1)S(1)}, u32[]{:S(2)}, u32[]{:S(2)}) collective-permute-start(bf16[400,128]{1,0:T(8,128)(2,1)S(1)} %get-tuple-element.69), channel_id=1, source_target_pairs={{0,24},{8,16},{16,8},{24,0},{1,25},{9,17},{17,9},{25,1},{2,26},{10... | collective-permute-start | bytes 307208 | tf_op jit(solution)/shard_map/ppermute | solution.py:17
  47.8 6.3 %collective-permute-start.20 = (bf16[400,128]{1,0:T(8,128)(2,1)S(1)}, bf16[400,128]{1,0:T(8,128)(2,1)S(1)}, u32[]{:S(2)}, u32[]{:S(2)}) collective-permute-start(bf16[400,128]{1,0:T(8,128)(2,1)S(1)} %get-tuple-element.70), channel_id=1, source_target_pairs={{0,8},{8,0},{16,24},{24,16},{1,9},{9,1},{17,25},{25,17},{2,10},{10... | collective-permute-start | bytes 307208 | tf_op jit(solution)/shard_map/ppermute | solution.py:17
  54.4 11.3 %collective-permute-start.21 = (bf16[64,768]{1,0:T(8,128)(2,1)S(1)}, bf16[64,768]{1,0:T(8,128)(2,1)S(1)}, u32[]{:S(2)}, u32[]{:S(2)}) collective-permute-start(bf16[64,768]{1,0:T(8,128)(2,1)S(1)} %finish.1.refs_0_), channel_id=1, source_target_pairs={{0,16},{8,24},{16,0},{24,8},{1,17},{9,25},{17,1},{25,9},{2,18},{10... | collective-permute-start | bytes 294920 | tf_op jit(solution)/shard_map/ppermute | solution.py:17
  57.7 7.9 %collective-permute-start.22 = (bf16[64,768]{1,0:T(8,128)(2,1)S(1)}, bf16[64,768]{1,0:T(8,128)(2,1)S(1)}, u32[]{:S(2)}, u32[]{:S(2)}) collective-permute-start(bf16[64,768]{1,0:T(8,128)(2,1)S(1)} %finish.1.refs_0_), channel_id=1, source_target_pairs={{0,24},{8,16},{16,8},{24,0},{1,25},{9,17},{17,9},{25,1},{2,26},{10... | collective-permute-start | bytes 294920 | tf_op jit(solution)/shard_map/ppermute | solution.py:17
  58.2 8.0 %collective-permute-start.23 = (bf16[64,768]{1,0:T(8,128)(2,1)S(1)}, bf16[64,768]{1,0:T(8,128)(2,1)S(1)}, u32[]{:S(2)}, u32[]{:S(2)}) collective-permute-start(bf16[64,768]{1,0:T(8,128)(2,1)S(1)} %finish.1.refs_0_), channel_id=1, source_target_pairs={{0,8},{8,0},{16,24},{24,16},{1,9},{9,1},{17,25},{25,17},{2,10},{10... | collective-permute-start | bytes 294920 | tf_op jit(solution)/shard_map/ppermute | solution.py:17
  61.1 4.3 %collective-permute-start.17 = (f32[2,64,64]{2,1,0:T(8,128)S(1)}, f32[2,64,64]{2,1,0:T(8,128)S(1)}, u32[]{:S(2)}, u32[]{:S(2)}) collective-permute-start(f32[2,64,64]{2,1,0:T(8,128)S(1)} %get-tuple-element.65.low_ref), channel_id=1, source_target_pairs={{0,4},{4,0},{1,5},{5,1},{2,6},{6,2},{3,7},{7,3},{8,12},{12,8},{9,1... | collective-permute-start | bytes 98312 | tf_op jit(solution)/shard_map/ppermute | solution.py:17
  67.0 3.8 %collective-permute-start.25 = (bf16[128,768]{1,0:T(8,128)(2,1)S(1)}, bf16[128,768]{1,0:T(8,128)(2,1)S(1)}, u32[]{:S(2)}, u32[]{:S(2)}) collective-permute-start(bf16[128,768]{1,0:T(8,128)(2,1)S(1)} %get-tuple-element.76), channel_id=1, source_target_pairs={{0,1},{1,0},{2,3},{3,2},{4,5},{5,4},{6,7},{7,6},{8,9},{9,8},{10,11... | collective-permute-start | bytes 589832 | tf_op jit(solution)/shard_map/ppermute | solution.py:17
  67.0 7.8 %collective-permute-start.27 = (bf16[128,768]{1,0:T(8,128)(2,1)S(1)}, bf16[128,768]{1,0:T(8,128)(2,1)S(1)}, u32[]{:S(2)}, u32[]{:S(2)}) collective-permute-start(bf16[128,768]{1,0:T(8,128)(2,1)S(1)} %get-tuple-element.79), channel_id=1, source_target_pairs={{0,2},{1,3},{2,0},{3,1},{4,6},{5,7},{6,4},{7,5},{8,10},{9,11},{10,... | collective-permute-start | bytes 589832 | tf_op jit(solution)/shard_map/ppermute | solution.py:17
  68.1 10.1 %collective-permute-start.29 = (bf16[128,768]{1,0:T(8,128)(2,1)S(1)}, bf16[128,768]{1,0:T(8,128)(2,1)S(1)}, u32[]{:S(2)}, u32[]{:S(2)}) collective-permute-start(bf16[128,768]{1,0:T(8,128)(2,1)S(1)} %get-tuple-element.82), channel_id=1, source_target_pairs={{0,3},{1,2},{2,1},{3,0},{4,7},{5,6},{6,5},{7,4},{8,11},{9,10},{10,... | collective-permute-start | bytes 589832 | tf_op jit(solution)/shard_map/ppermute | solution.py:17
  69.8 4.2 %collective-permute-start.24 = (bf16[64,384]{1,0:T(8,128)(2,1)S(1)}, bf16[64,384]{1,0:T(8,128)(2,1)S(1)}, u32[]{:S(2)}, u32[]{:S(2)}) collective-permute-start(bf16[64,384]{1,0:T(8,128)(2,1)S(1)} %get-tuple-element.75), channel_id=1, source_target_pairs={{0,4},{4,0},{1,5},{5,1},{2,6},{6,2},{3,7},{7,3},{8,12},{12,8},{9,1... | collective-permute-start | bytes 147464 | tf_op jit(solution)/shard_map/ppermute | solution.py:17
  71.7 6.4 %collective-permute-start.26 = (bf16[64,384]{1,0:T(8,128)(2,1)S(1)}, bf16[64,384]{1,0:T(8,128)(2,1)S(1)}, u32[]{:S(2)}, u32[]{:S(2)}) collective-permute-start(bf16[64,384]{1,0:T(8,128)(2,1)S(1)} %get-tuple-element.78), channel_id=1, source_target_pairs={{0,4},{4,0},{1,5},{5,1},{2,6},{6,2},{3,7},{7,3},{8,12},{12,8},{9,1... | collective-permute-start | bytes 147464 | tf_op jit(solution)/shard_map/ppermute | solution.py:17
  75.7 4.3 %collective-permute-start.28 = (bf16[64,384]{1,0:T(8,128)(2,1)S(1)}, bf16[64,384]{1,0:T(8,128)(2,1)S(1)}, u32[]{:S(2)}, u32[]{:S(2)}) collective-permute-start(bf16[64,384]{1,0:T(8,128)(2,1)S(1)} %get-tuple-element.81), channel_id=1, source_target_pairs={{0,4},{4,0},{1,5},{5,1},{2,6},{6,2},{3,7},{7,3},{8,12},{12,8},{9,1... | collective-permute-start | bytes 147464 | tf_op jit(solution)/shard_map/ppermute | solution.py:17
  79.0 4.2 %collective-permute-start.30 = (bf16[64,384]{1,0:T(8,128)(2,1)S(1)}, bf16[64,384]{1,0:T(8,128)(2,1)S(1)}, u32[]{:S(2)}, u32[]{:S(2)}) collective-permute-start(bf16[64,384]{1,0:T(8,128)(2,1)S(1)} %get-tuple-element.84), channel_id=1, source_target_pairs={{0,4},{4,0},{1,5},{5,1},{2,6},{6,2},{3,7},{7,3},{8,12},{12,8},{9,1... | collective-permute-start | bytes 147464 | tf_op jit(solution)/shard_map/ppermute | solution.py:17
  (13 other events, 90.5 us)

commit v10 on v7

--- a/solution.py
+++ b/solution.py
@@ -327,19 +327,6 @@
     stat_ref[...] = jnp.broadcast_to(stat, stat_ref.shape)
 
 
-def halve_kernel(features, got_ref, keep_ref, stat_ref, send_ref, kept_ref, out_stat_ref):
-    mine = lax.rem(lax.axis_index("req") // 2, 2)
-    count = keep_ref.shape[0] // (2 * features)
-    for i in range(count):
-        rows = slice(i * features, (i + 1) * features)
-        own, other = at(2 * i + mine, features), at(2 * i + 1 - mine, features)
-        kept_ref[rows] = keep_ref[own] + got_ref[own].astype(F32)
-        send_ref[rows] = (keep_ref[other] + got_ref[other].astype(F32)).astype(BF16)
-    stat = stat_ref[0:1] + stat_of(got_ref[2 * count * features :])
-    send_ref[count * features :] = stat_rows(stat)
-    out_stat_ref[...] = jnp.broadcast_to(stat, out_stat_ref.shape)
-
-
 def scatter_kernel(features, deps, got_ref, keep_ref, stat_ref, *refs):
     kept_ref, out_stat_ref, *send_refs = refs[deps:]
     e = lax.axis_index("enc")
@@ -354,69 +341,117 @@
     out_stat_ref[...] = jnp.broadcast_to(stat, out_stat_ref.shape)
 
 
-def centre_kernel(width, prompt_ref, dep_ref, keep_ref, stat_ref, bias_ref, scale_ref, shift_ref, *refs):
-    got_refs, out_ref = refs[:-1], refs[-1]
-    features, tokens = keep_ref.shape
-    total = keep_ref[...] + bias_ref[...]
-    stat = stat_ref[0:1]
-    for got_ref in got_refs:
-        total = total + got_ref[:features].astype(F32)
-        stat = stat + stat_of(got_ref[features:])
-    centred = total - stat * (1.0 / width)
-    out_ref[:features] = (scale_ref[...] * centred).astype(BF16)
-    squares = jnp.sum(centred * centred, axis=0, keepdims=True)
-    high = squares.astype(BF16).astype(F32)
-    row = lax.broadcasted_iota(jnp.int32, (ROWS, tokens), 0)
-    extra = jnp.where(row == 0, high, jnp.where(row == 1, squares - high, 0.0))
-    for j in range(pl.cdiv(features, tokens)):
-        piece = shift_ref[:, j * tokens : min((j + 1) * tokens, features)].astype(F32)
+def lane_rows(rows, first, values, extra):
+    tokens = extra.shape[1]
+    for j in range(pl.cdiv(values.shape[1], tokens)):
+        piece = values[:, j * tokens : min((j + 1) * tokens, values.shape[1])]
         gap = tokens - piece.shape[1]
         if gap:
             piece = jnp.concatenate([piece, jnp.zeros((1, gap), F32)], axis=1)
-        extra = jnp.where(row == 2 + j, piece, extra)
-    extra = jnp.where(row == ROWS - 1, prompt_ref[0, 0].astype(F32), extra)
-    out_ref[features:] = extra.astype(BF16)
-
-
-def pass_on_kernel(core_ref, got_ref, dep_ref, own_ref, next_ref):
-    own_ref[...] = got_ref[0]
-    next_ref[0] = core_ref[...]
-    next_ref[1] = got_ref[1]
-
-
-def join_kernel(own_ref, got_ref, dep_ref, out_ref):
+        extra = jnp.where(rows == first + j, piece, extra)
+    return extra
+
+
+def from_rows(extra, first, count):
+    tokens = extra.shape[1]
+    pieces = [extra[first + j : first + j + 1] for j in range(pl.cdiv(count, tokens))]
+    return jnp.concatenate(pieces, axis=1)[:, :count]
+
+
+def merge_kernel(deps, prompt_ref, keep_ref, stat_ref, bias_ref, scale_ref, shift_ref, *refs):
+    got_refs, (send_ref, kept_ref, out_stat_ref) = refs[deps:-3], refs[-3:]
+    features, tokens = bias_ref.shape
+    mine = lax.rem(lax.axis_index("req") // 2, 2)
+    total = keep_ref[...]
+    stat = stat_ref[0:1]
+    for got_ref in got_refs:
+        total = total + got_ref[: 2 * features].astype(F32)
+        stat = stat + stat_of(got_ref[2 * features :])
+    kept_ref[...] = total
+    own = at(mine, features)
+    kept_ref[own] = kept_ref[own] + bias_ref[...]
+    send_ref[: 2 * features] = kept_ref[...].astype(BF16)
+    rows = lax.broadcasted_iota(jnp.int32, (ROWS, tokens), 0)
+    extra = stat_rows(stat).astype(F32)
+    extra = lane_rows(rows, 2, scale_ref[...].astype(F32), extra)
+    extra = lane_rows(rows, 6, shift_ref[...].astype(F32), extra)
+    extra = jnp.where(rows == ROWS - 1, prompt_ref[0, 0].astype(F32), extra)
+    send_ref[2 * features :] = extra.astype(BF16)
+    out_stat_ref[...] = jnp.broadcast_to(stat, out_stat_ref.shape)
+
+
+def centre_kernel(
+    width, prompt_ref, dep_ref, keep_ref, stat_ref, got_ref, scale_ref, shift_ref, out_ref
+):
+    features, tokens = scale_ref.shape
+    mine = lax.rem(lax.axis_index("req") // 2, 2)
+    extra = got_ref[2 * features :].astype(F32)
+    stat = stat_ref[0:1] + extra[0:1] + extra[1:2]
+    average = stat * (1.0 / width)
+    scale = from_rows(extra, 2, features)
+    columns = []
+    for first in range(0, features, tokens):
+        piece = scale[:, first : min(first + tokens, features)]
+        piece = jnp.broadcast_to(piece, (tokens, piece.shape[1]))
+        gap = tokens - piece.shape[1]
+        if gap:
+            piece = jnp.concatenate([piece, jnp.zeros((tokens, gap), F32)], axis=1)
+        columns.append(piece.T[: min(tokens, features - first)])
+    scales = (scale_ref[...], 1.0 + jnp.concatenate(columns, axis=0))
+    squares = jnp.zeros((1, tokens), F32)
+    for i in range(2):
+        block = at(mine ^ i, features)
+        centred = keep_ref[block] + got_ref[block].astype(F32) - average
+        squares = squares + jnp.sum(centred * centred, axis=0, keepdims=True)
+        out_ref[i * features : (i + 1) * features] = (scales[i] * centred).astype(BF16)
+    shift = jnp.concatenate([shift_ref[...].astype(F32), from_rows(extra, 6, features)], axis=1)
+    other_prompt = extra[ROWS - 1 : ROWS]
+    rows = lax.broadcasted_iota(jnp.int32, (ROWS, tokens), 0)
+    extra = stat_rows(squares).astype(F32)
+    extra = lane_rows(rows, 2, shift, extra)
+    extra = jnp.where(rows == ROWS - 1, prompt_ref[0, 0].astype(F32), extra)
+    extra = jnp.where(rows == ROWS - 2, other_prompt, extra)
+    out_ref[2 * features :] = extra.astype(BF16)
+
+
+def pass_on_kernel(own_ref, core_ref, got_ref, dep_ref, mine_ref, next_ref):
+    features = own_ref.shape[0]
+    mine_ref[:features] = own_ref[...]
+    mine_ref[features:] = got_ref[0]
+    next_ref[:features] = core_ref[...]
+    next_ref[features:] = got_ref[1]
+
+
+def join_kernel(own_ref, got_ref, out_ref):
     size = own_ref.shape[0]
     out_ref[:size] = own_ref[...]
     out_ref[size:] = got_ref[...]
 
 
-def project_kernel(n_seq, n_req, n_enc, own_ref, pair_ref, next_ref, *refs):
-    payload_refs = dict(zip([0] + far_first(n_req), refs))
-    weight_refs = (own_ref, next_ref.at[0], pair_ref, next_ref.at[1])
-    prompts_ref, keep_ref = refs[n_req : n_req + 2]
-    send_refs = refs[n_req + 2 : -1]
+def project_kernel(n_seq, n_enc, *refs):
+    payload_refs, weight_refs, refs = refs[:2], refs[2:4], refs[4:]
+    prompts_ref, keep_ref, *send_refs = refs[:-1]
     rows_ref = refs[-1]
     features, width = weight_refs[0].shape
     tokens = payload_refs[0].shape[1]
     stride = features + ROWS
     total = None
     squares = [jnp.zeros((1, tokens), F32) for _ in range(n_seq)]
-    for k in range(n_req):
+    for k, (payload, weight_ref) in enumerate(zip(payload_refs, weight_refs)):
         left = []
         shifts = []
         for p in range(n_seq):
-            payload = payload_refs[k]
             left.append(payload[p * stride : p * stride + features].T)
             extra = payload[p * stride + features : (p + 1) * stride].astype(F32)
             squares[p] = squares[p] + extra[0:1] + extra[1:2]
-            pieces = [extra[2 + j : 3 + j] for j in range(pl.cdiv(features, tokens))]
-            shifts.append(jnp.concatenate(pieces, axis=1)[:, :features])
+            shifts.append(from_rows(extra, 2, features))
             if p == 0:
                 prompts_ref[k] = jnp.max(extra[ROWS - 1 : ROWS]).astype(jnp.int32)
+                prompts_ref[2 + k] = jnp.max(extra[ROWS - 2 : ROWS - 1]).astype(jnp.int32)
         shifts.append(jnp.zeros((ROWS - n_seq, features), F32))
         left.append(jnp.concatenate(shifts, axis=0).astype(BF16))
         term = jnp.dot(
-            jnp.concatenate(left, axis=0), weight_refs[k][...], preferred_element_type=F32
+            jnp.concatenate(left, axis=0), weight_ref[...], preferred_element_type=F32
         )
         total = term if total is None else total + term
     size = n_seq * tokens // n_enc
@@ -664,41 +699,79 @@
     )
     got = swap(send, "req", n_req, 1)
 
-    maps = call(
-        functools.partial(maps_kernel, part),
-        struct((2 * rank, part)),
-        (adapter_down_maps[0].T, adapter_up_maps[0], send),
-        [ANY] * 3,
-        [dma((2,))],
-        name="maps_pack",
-    )
-    maps_core = swap(maps, "req", n_req, 1)
+    keep, sums, *sends = call(
+        functools.partial(scatter_kernel, 2 * features, 0),
+        (struct((2 * features, tokens), F32), stat)
+        + tuple(struct((2 * features + ROWS, tokens)) for _ in range(1, n_enc)),
+        (got, keep, sums),
+        name="scatter",
+    )
+    arrived = partners(lambda k: sends[k - 1], "enc", n_enc).values()
     weight = struct((features, 2 * half))
     weight_own, weight_core, weight_pair = call(
         functools.partial(weight_kernel, n_req, part, inner),
         (weight, weight, struct((2, features, 2 * half))),
-        (key_value_weight, send),
+        (key_value_weight, keep),
         [ANY] * 2,
         [dma((2 * n_req,))],
         name="weight_pack",
-    )
-
+        vmem=16,
+    )
+
+    weight_pair_got = swap(weight_pair, "req", n_req, 2)
+    bias_columns = jnp.broadcast_to(context_bias.astype(F32)[:, None], (features, tokens))
+    scale_columns = jnp.broadcast_to(
+        1.0 + modulation_scale[0].astype(F32)[:, None], (features, tokens)
+    )
+    deps = ()
     send, keep, sums = call(
-        functools.partial(halve_kernel, features),
+        functools.partial(merge_kernel, len(deps)),
         (
-            struct((n_enc * features + ROWS, tokens)),
-            struct((n_enc * features, tokens), F32),
+            struct((2 * features + ROWS, tokens)),
+            struct((2 * features, tokens), F32),
             stat,
         ),
-        (got, keep, sums),
-        name="halve",
+        (
+            request_prompt,
+            keep,
+            sums,
+            bias_columns,
+            modulation_scale,
+            modulation_shift,
+            *deps,
+            *arrived,
+        ),
+        [SMEM] + [VMEM] * 5 + [ANY] * len(deps) + [VMEM] * len(arrived),
+        name="merge",
     )
     got = swap(send, "req", n_req, 2)
+    weights = struct((2 * features, 2 * half))
+    weight_mine, weight_next = call(
+        pass_on_kernel,
+        (weights, weights),
+        (weight_own, weight_core, weight_pair_got, keep),
+        [VMEM] * 3 + [ANY],
+        name="pass_on",
+    )
+    weight_next = swap(weight_next, "req", n_req, 1)
+    own = call(
+        functools.partial(centre_kernel, model_width),
+        struct((2 * features + ROWS, tokens)),
+        (request_prompt, weight_mine, keep, sums, got, scale_columns, modulation_shift),
+        [SMEM, ANY] + [VMEM] * 5,
+        name="centre",
+    )
+    joined = call(
+        join_kernel,
+        struct((n_seq * (2 * features + ROWS), tokens)),
+        (own, swap(own, "seq", n_seq, 1)),
+        name="join",
+    )
     packed = [
         call(
             functools.partial(image_kernel, part, inner, k),
             struct((4, image_rows, part)),
-            (qk, base, stream, keep),
+            (qk, base, stream, joined),
             [ANY] * 4,
             [dma((4,))],
             name="image_pack",
@@ -706,68 +779,17 @@
         for k in range(1, n_seq)
     ]
     image_got = [swap(packed[k - 1], "seq", n_seq, k) for k in range(1, n_seq)]
-    keep, sums, *sends = call(
-        functools.partial(scatter_kernel, features, 1),
-        (struct((features, tokens), F32), stat)
-        + tuple(struct((features + ROWS, tokens)) for _ in range(1, n_enc)),
-        (got, keep, sums, weight_pair),
-        [VMEM] * 3 + [ANY],
-        name="scatter",
-    )
-    arrived = partners(lambda k: sends[k - 1], "enc", n_enc).values()
     weight_pair = lax.optimization_barrier((weight_pair, keep))[0]
-    weight_pair_got = swap(weight_pair, "req", n_req, 2)
-
-    bias_columns = jnp.broadcast_to(context_bias.astype(F32)[:, None], (features, tokens))
-    scale_columns = jnp.broadcast_to(
-        1.0 + modulation_scale[0].astype(F32)[:, None], (features, tokens)
-    )
-    own = call(
-        functools.partial(centre_kernel, model_width),
-        struct((features + ROWS, tokens)),
-        (
-            request_prompt,
-            maps_core,
-            keep,
-            sums,
-            bias_columns,
-            scale_columns,
-            modulation_shift,
-            *arrived,
-        ),
-        [SMEM, ANY] + [VMEM] * (5 + len(arrived)),
-        name="centre",
-    )
-    joined = call(
-        join_kernel,
-        struct((n_seq * (features + ROWS), tokens)),
-        (own, swap(own, "seq", n_seq, 1), image_got[0]),
-        [VMEM, VMEM, ANY],
-        name="join",
-    )
-    payloads = partners(lambda k: joined, "req", n_req)
-    weight_own_pair, weight_next = call(
-        pass_on_kernel,
-        (weight, struct((2, features, 2 * half))),
-        (weight_core, weight_pair_got, joined),
-        [VMEM, VMEM, ANY],
-        name="pass_on",
-    )
-    weight_next = swap(weight_next, "req", n_req, 1)
-
-    size = n_seq * tokens // n_enc
-    step = 2 * half // HDIM * size + ROWS
-    ids, keep, *sends = call(
-        functools.partial(project_kernel, n_seq, n_req, n_enc),
-        (struct((n_req,), jnp.int32), struct((step, HDIM), F32))
-        + tuple(struct((step, HDIM)) for _ in range(1, n_enc)),
-        (weight_own, weight_own_pair, weight_next, joined, *payloads.values()),
-        scratch=[pltpu.VMEM((n_enc * step, HDIM), F32)],
-        out_specs=(SMEM,) + (VMEM,) * n_enc,
-        name="project",
-    )
-    arrived = partners(lambda k: sends[k - 1], "enc", n_enc).values()
-
+    joined_core = swap(joined, "req", n_req, 1)
+    maps = call(
+        functools.partial(maps_kernel, part),
+        struct((2 * rank, part)),
+        (adapter_down_maps[0].T, adapter_up_maps[0], joined),
+        [ANY] * 3,
+        [dma((2,))],
+        name="maps_pack",
+    )
+    maps_core = swap(maps, "req", n_req, 1)
     maps = call(
         join_maps_kernel,
         struct((2, 2 * rank, part)),
@@ -775,6 +797,20 @@
         [VMEM, VMEM, ANY],
         name="maps_join",
     )
+
+    size = n_seq * tokens // n_enc
+    step = 2 * half // HDIM * size + ROWS
+    ids, keep, *sends = call(
+        functools.partial(project_kernel, n_seq, n_enc),
+        (struct((n_req,), jnp.int32), struct((step, HDIM), F32))
+        + tuple(struct((step, HDIM)) for _ in range(1, n_enc)),
+        (joined, joined_core, weight_mine, weight_next),
+        scratch=[pltpu.VMEM((n_enc * step, HDIM), F32)],
+        out_specs=(SMEM,) + (VMEM,) * n_enc,
+        name="project",
+    )
+    arrived = partners(lambda k: sends[k - 1], "enc", n_enc).values()
+
     maps = lax.optimization_barrier((maps, keep))[0]
     maps_pair = swap(maps, "req", n_req, 2)
 

time: 80.7 us -> 76.5 us (0.948)
  starting transfers between devices: 33 us -> 30.6 us
  waiting for transfers between devices: 34 us -> 32.1 us
    ppermute x28 -> x26, starting transfers between devices: 33 us -> 30.6 us  [swap(): return lax.ppermute(block, axis, [(i, i ^ step) for i in range(size)])]
    ppermute x28 -> x26, waiting for transfers between devices: 34 us -> 32.1 us  [swap(): return lax.ppermute(block, axis, [(i, i ^ step) for i in range(size)])]
  transfers between devices with their start and end apart: 28 -> 26, of which waited for: 16 -> 15; matrix products, arithmetic and copies ran while one was open for 0% -> 0% of each run, Pallas kernels for 6% -> 8%
where the time goes in v10:
time: 76.5 us; the launch traced here: 76.3 us
  waiting for transfers between devices  32.1 us (42%)
  starting transfers between devices  30.6 us (40%)
  Pallas kernels  8.77 us (11%)
  local copies, waits for them, and re-layouts  3.28 us (4%)
  between operations  1.62 us (2%)
    ppermute x26, waiting for transfers between devices, swap(): return lax.ppermute(block, axis, [(i, i ^ step) for i in range(size)])  32.1 us
    ppermute x26, starting transfers between devices, swap(): return lax.ppermute(block, axis, [(i, i ^ step) for i in range(size)])  30.6 us
    pallas_call x20, Pallas kernels, call(): pl.pallas_call(kernel, out_shape=outs, in_specs=specs if specs is not Non...  8.77 us
    unnamed x28, local copies, waits for them, and re-layouts  3.11 us
  transfers between devices with their start and end apart: 26, of which 15 were waited for; matrix products, arithmetic and copies ran while one was open for 0% of the time, Pallas kernels for 8%

profile of v10, /device:TPU:0, one launch (start us, length us, event | category | flops | bytes accessed | tf_op | source)
XLA Modules:
  0.0 76.3 jit_solution(5041465706180269798)
XLA Ops:
  0.0 1.6 %copy-done.4 = bf16[256,3072]{1,0:T(8,128)(2,1)S(1)} copy-done((bf16[256,3072]{1,0:T(8,128)(2,1)S(1)}, bf16[256,3072]{1,0:T(8,128)(2,1)}, u32[]{:S(2)}) %copy-start.4) | copy-done | bytes 1572888
  1.6 0.8 %copy-done.8 = bf16[1,128,256]{2,1,0:T(8,128)(2,1)S(1)} copy-done((bf16[1,128,256]{2,1,0:T(8,128)(2,1)S(1)}, bf16[1,128,256]{2,1,0:T(8,128)(2,1)}, u32[]{:S(2)}) %copy-start.8) | copy-done | bytes 65560
  4.3 1.4 %collective-permute-done.got_ref = bf16[1552,128]{1,0:T(8,128)(2,1)S(1)} collective-permute-done((bf16[1552,128]{1,0:T(8,128)(2,1)S(1)}, bf16[1552,128]{1,0:T(8,128)(2,1)S(1)}, u32[]{:S(2)}, u32[]{:S(2)}) %collective-permute-start) | collective-permute-done | bytes 397344 | tf_op jit(solution)/shard_map/ppermute | solution.py:17
  6.0 2.9 %collective-permute-start.1 = (bf16[2,192,768]{2,1,0:T(8,128)(2,1)S(1)}, bf16[2,192,768]{2,1,0:T(8,128)(2,1)S(1)}, u32[]{:S(2)}, u32[]{:S(2)}) collective-permute-start(bf16[2,192,768]{2,1,0:T(8,128)(2,1)S(1)} %get-tuple-element.50), channel_id=1, source_target_pairs={{0,2},{1,3},{2,0},{3,1},{4,6},{5,7},{6,4},{7,5},{8,10},{9,11},{10,... | collective-permute-start | bytes 1769480 | tf_op jit(solution)/shard_map/ppermute | solution.py:17
  9.0 2.6 %collective-permute-start.2 = (bf16[400,128]{1,0:T(8,128)(2,1)S(1)}, bf16[400,128]{1,0:T(8,128)(2,1)S(1)}, u32[]{:S(2)}, u32[]{:S(2)}) collective-permute-start(bf16[400,128]{1,0:T(8,128)(2,1)S(1)} %get-tuple-element.52), channel_id=1, source_target_pairs={{0,16},{8,24},{16,0},{24,8},{1,17},{9,25},{17,1},{25,9},{2,18},{10... | collective-permute-start | bytes 307208 | tf_op jit(solution)/shard_map/ppermute | solution.py:17
  11.6 1.3 %collective-permute-start.3 = (bf16[400,128]{1,0:T(8,128)(2,1)S(1)}, bf16[400,128]{1,0:T(8,128)(2,1)S(1)}, u32[]{:S(2)}, u32[]{:S(2)}) collective-permute-start(bf16[400,128]{1,0:T(8,128)(2,1)S(1)} %get-tuple-element.53), channel_id=1, source_target_pairs={{0,24},{8,16},{16,8},{24,0},{1,25},{9,17},{17,9},{25,1},{2,26},{10... | collective-permute-start | bytes 307208 | tf_op jit(solution)/shard_map/ppermute | solution.py:17
  13.8 6.2 %collective-permute-done.2.refs_0_ = bf16[400,128]{1,0:T(8,128)(2,1)S(1)} collective-permute-done((bf16[400,128]{1,0:T(8,128)(2,1)S(1)}, bf16[400,128]{1,0:T(8,128)(2,1)S(1)}, u32[]{:S(2)}, u32[]{:S(2)}) %collective-permute-start.2) | collective-permute-done | bytes 102432 | tf_op jit(solution)/shard_map/ppermute | solution.py:17
  21.0 2.1 %collective-permute-done.1.got_ref = bf16[2,192,768]{2,1,0:T(8,128)(2,1)S(1)} collective-permute-done((bf16[2,192,768]{2,1,0:T(8,128)(2,1)S(1)}, bf16[2,192,768]{2,1,0:T(8,128)(2,1)S(1)}, u32[]{:S(2)}, u32[]{:S(2)}) %collective-permute-start.1) | collective-permute-done | bytes 589856 | tf_op jit(solution)/shard_map/ppermute | solution.py:17
  23.3 2.0 %collective-permute-done.5.got_ref = bf16[400,128]{1,0:T(8,128)(2,1)S(1)} collective-permute-done((bf16[400,128]{1,0:T(8,128)(2,1)S(1)}, bf16[400,128]{1,0:T(8,128)(2,1)S(1)}, u32[]{:S(2)}, u32[]{:S(2)}) %collective-permute-start.5) | collective-permute-done | bytes 102432 | tf_op jit(solution)/shard_map/ppermute | solution.py:17
  25.5 1.6 %collective-permute-start.6 = (bf16[400,128]{1,0:T(8,128)(2,1)S(1)}, bf16[400,128]{1,0:T(8,128)(2,1)S(1)}, u32[]{:S(2)}, u32[]{:S(2)}) collective-permute-start(bf16[400,128]{1,0:T(8,128)(2,1)S(1)} %centre.1.own_ref), channel_id=1, source_target_pairs={{0,4},{4,0},{1,5},{5,1},{2,6},{6,2},{3,7},{7,3},{8,12},{12,8},{9,1... | collective-permute-start | bytes 307208 | tf_op jit(solution)/shard_map/ppermute | solution.py:17
  27.0 3.2 %collective-permute-done.6.got_ref = bf16[400,128]{1,0:T(8,128)(2,1)S(1)} collective-permute-done((bf16[400,128]{1,0:T(8,128)(2,1)S(1)}, bf16[400,128]{1,0:T(8,128)(2,1)S(1)}, u32[]{:S(2)}, u32[]{:S(2)}) %collective-permute-start.6) | collective-permute-done | bytes 102432 | tf_op jit(solution)/shard_map/ppermute | solution.py:17
  31.1 1.6 %collective-permute-start.9 = (bf16[4,64,1536]{2,1,0:T(8,128)(2,1)S(1)}, bf16[4,64,1536]{2,1,0:T(8,128)(2,1)S(1)}, u32[]{:S(2)}, u32[]{:S(2)}) collective-permute-start(bf16[4,64,1536]{2,1,0:T(8,128)(2,1)S(1)} %image_pack.1), channel_id=1, source_target_pairs={{0,4},{4,0},{1,5},{5,1},{2,6},{6,2},{3,7},{7,3},{8,12},{12,8},{9,1... | collective-permute-start | bytes 2359304 | tf_op jit(solution)/shard_map/ppermute | solution.py:17
  32.8 1.2 %project.1 = (s32[4]{0:T(128)S(1)}, f32[400,128]{1,0:T(8,128)S(1)}, bf16[400,128]{1,0:T(8,128)(2,1)S(1)}, bf16[400,128]{1,0:T(8,128)(2,1)S(1)}, bf16[400,128]{1,0:T(8,128)(2,1)S(1)}) custom-call(bf16[800,128]{1,0:T(8,128)(2,1)S(1)} %join.1.refs_0_.dep_ref, bf16[800,128]{1,0:T(8,128)(2,1)S(1)} %collective-permute-done.7.refs_1_, ...), custom_call_target="tpu_custom_call" | custom-call | tf_op jit(solution)/shard_map/project/pallas_call | solution.py:280
  33.9 1.4 %collective-permute-start.11 = (bf16[2,128,1536]{2,1,0:T(8,128)(2,1)S(1)}, bf16[2,128,1536]{2,1,0:T(8,128)(2,1)S(1)}, u32[]{:S(2)}, u32[]{:S(2)}) collective-permute-start(bf16[2,128,1536]{2,1,0:T(8,128)(2,1)S(1)} %maps_join.1.refs_0_), channel_id=1, source_target_pairs={{0,2},{1,3},{2,0},{3,1},{4,6},{5,7},{6,4},{7,5},{8,10},{9,11},{10,... | collective-permute-start | bytes 2359304 | tf_op jit(solution)/shard_map/ppermute | solution.py:17
  35.3 2.8 %collective-permute-start.13 = (bf16[400,128]{1,0:T(8,128)(2,1)S(1)}, bf16[400,128]{1,0:T(8,128)(2,1)S(1)}, u32[]{:S(2)}, u32[]{:S(2)}) collective-permute-start(bf16[400,128]{1,0:T(8,128)(2,1)S(1)} %get-tuple-element.66), channel_id=1, source_target_pairs={{0,16},{8,24},{16,0},{24,8},{1,17},{9,25},{17,1},{25,9},{2,18},{10... | collective-permute-start | bytes 307208 | tf_op jit(solution)/shard_map/ppermute | solution.py:17
  38.1 1.1 %collective-permute-start.14 = (bf16[400,128]{1,0:T(8,128)(2,1)S(1)}, bf16[400,128]{1,0:T(8,128)(2,1)S(1)}, u32[]{:S(2)}, u32[]{:S(2)}) collective-permute-start(bf16[400,128]{1,0:T(8,128)(2,1)S(1)} %get-tuple-element.67), channel_id=1, source_target_pairs={{0,24},{8,16},{16,8},{24,0},{1,25},{9,17},{17,9},{25,1},{2,26},{10... | collective-permute-start | bytes 307208 | tf_op jit(solution)/shard_map/ppermute | solution.py:17
  39.5 6.6 %collective-permute-done.13.refs_0_ = bf16[400,128]{1,0:T(8,128)(2,1)S(1)} collective-permute-done((bf16[400,128]{1,0:T(8,128)(2,1)S(1)}, bf16[400,128]{1,0:T(8,128)(2,1)S(1)}, u32[]{:S(2)}, u32[]{:S(2)}) %collective-permute-start.13) | collective-permute-done | bytes 102432 | tf_op jit(solution)/shard_map/ppermute | solution.py:17
  46.4 3.7 %collective-permute-start.16 = (bf16[64,768]{1,0:T(8,128)(2,1)S(1)}, bf16[64,768]{1,0:T(8,128)(2,1)S(1)}, u32[]{:S(2)}, u32[]{:S(2)}) collective-permute-start(bf16[64,768]{1,0:T(8,128)(2,1)S(1)} %finish.1.refs_0_), channel_id=1, source_target_pairs={{0,16},{8,24},{16,0},{24,8},{1,17},{9,25},{17,1},{25,9},{2,18},{10... | collective-permute-start | bytes 294920 | tf_op jit(solution)/shard_map/ppermute | solution.py:17
  51.4 1.8 %collective-permute-done.11.refs_1_ = bf16[2,128,1536]{2,1,0:T(8,128)(2,1)S(1)} collective-permute-done((bf16[2,128,1536]{2,1,0:T(8,128)(2,1)S(1)}, bf16[2,128,1536]{2,1,0:T(8,128)(2,1)S(1)}, u32[]{:S(2)}, u32[]{:S(2)}) %collective-permute-start.11) | collective-permute-done | bytes 786464 | tf_op jit(solution)/shard_map/ppermute | solution.py:17
  53.5 1.5 %collective-permute-start.12 = (f32[2,64,64]{2,1,0:T(8,128)S(1)}, f32[2,64,64]{2,1,0:T(8,128)S(1)}, u32[]{:S(2)}, u32[]{:S(2)}) collective-permute-start(f32[2,64,64]{2,1,0:T(8,128)S(1)} %get-tuple-element.63.low_ref), channel_id=1, source_target_pairs={{0,4},{4,0},{1,5},{5,1},{2,6},{6,2},{3,7},{7,3},{8,12},{12,8},{9,1... | collective-permute-start | bytes 98312 | tf_op jit(solution)/shard_map/ppermute | solution.py:17
  55.0 2.8 %collective-permute-done.12.other_ref = f32[2,64,64]{2,1,0:T(8,128)S(1)} collective-permute-done((f32[2,64,64]{2,1,0:T(8,128)S(1)}, f32[2,64,64]{2,1,0:T(8,128)S(1)}, u32[]{:S(2)}, u32[]{:S(2)}) %collective-permute-start.12) | collective-permute-done | bytes 32800 | tf_op jit(solution)/shard_map/ppermute | solution.py:17
  59.4 0.9 %collective-permute-start.22 = (bf16[128,768]{1,0:T(8,128)(2,1)S(1)}, bf16[128,768]{1,0:T(8,128)(2,1)S(1)}, u32[]{:S(2)}, u32[]{:S(2)}) collective-permute-start(bf16[128,768]{1,0:T(8,128)(2,1)S(1)} %get-tuple-element.77), channel_id=1, source_target_pairs={{0,2},{1,3},{2,0},{3,1},{4,6},{5,7},{6,4},{7,5},{8,10},{9,11},{10,... | collective-permute-start | bytes 589832 | tf_op jit(solution)/shard_map/ppermute | solution.py:17
  60.3 0.9 %collective-permute-start.24 = (bf16[128,768]{1,0:T(8,128)(2,1)S(1)}, bf16[128,768]{1,0:T(8,128)(2,1)S(1)}, u32[]{:S(2)}, u32[]{:S(2)}) collective-permute-start(bf16[128,768]{1,0:T(8,128)(2,1)S(1)} %get-tuple-element.80), channel_id=1, source_target_pairs={{0,3},{1,2},{2,1},{3,0},{4,7},{5,6},{6,5},{7,4},{8,11},{9,10},{10,... | collective-permute-start | bytes 589832 | tf_op jit(solution)/shard_map/ppermute | solution.py:17
  61.2 0.9 %heads.4 = (bf16[64,384]{1,0:T(8,128)(2,1)S(1)}, bf16[64,384]{1,0:T(8,128)(2,1)S(1)}) custom-call(s32[1,128]{1,0:T(1,128)S(1)} %constant_dynamic-slice_fusion.live_ref.refs_0_.refs_1_, bf16[128,768]{1,0:T(8,128)(2,1)S(1)} %get-tuple-element.69.text_ref, bf16[4,128,384]{2,1,0:T(8,128)(2,1)S(1)} %get-tuple-element.70.q_ref, ...), custom_call_target="tpu_custom_call" | custom-call | tf_op jit(solution)/shard_map/heads/pallas_call | solution.py:280
  62.2 1.6 %collective-permute-start.19 = (bf16[64,384]{1,0:T(8,128)(2,1)S(1)}, bf16[64,384]{1,0:T(8,128)(2,1)S(1)}, u32[]{:S(2)}, u32[]{:S(2)}) collective-permute-start(bf16[64,384]{1,0:T(8,128)(2,1)S(1)} %get-tuple-element.73), channel_id=1, source_target_pairs={{0,4},{4,0},{1,5},{5,1},{2,6},{6,2},{3,7},{7,3},{8,12},{12,8},{9,1... | collective-permute-start | bytes 147464 | tf_op jit(solution)/shard_map/ppermute | solution.py:17
  63.8 0.9 %heads.5 = (bf16[64,384]{1,0:T(8,128)(2,1)S(1)}, bf16[64,384]{1,0:T(8,128)(2,1)S(1)}) custom-call(s32[1,128]{1,0:T(1,128)S(1)} %constant_dynamic-slice_fusion.live_ref.refs_0_.refs_1_, bf16[128,768]{1,0:T(8,128)(2,1)S(1)} %collective-permute-done.20.text_ref, bf16[4,128,384]{2,1,0:T(8,128)(2,1)S(1)} %get-tuple-element.70.q_ref, ...), custom_call_target="tpu_custom_call" | custom-call | tf_op jit(solution)/shard_map/heads/pallas_call | solution.py:280
  65.2 1.1 %collective-permute-done.19.refs_1_ = bf16[64,384]{1,0:T(8,128)(2,1)S(1)} collective-permute-done((bf16[64,384]{1,0:T(8,128)(2,1)S(1)}, bf16[64,384]{1,0:T(8,128)(2,1)S(1)}, u32[]{:S(2)}, u32[]{:S(2)}) %collective-permute-start.19) | collective-permute-done | bytes 49184 | tf_op jit(solution)/shard_map/ppermute | solution.py:17
  67.1 0.9 %heads.6 = (bf16[64,384]{1,0:T(8,128)(2,1)S(1)}, bf16[64,384]{1,0:T(8,128)(2,1)S(1)}) custom-call(s32[1,128]{1,0:T(1,128)S(1)} %constant_dynamic-slice_fusion.live_ref.refs_0_.refs_1_, bf16[128,768]{1,0:T(8,128)(2,1)S(1)} %collective-permute-done.22.text_ref, bf16[4,128,384]{2,1,0:T(8,128)(2,1)S(1)} %get-tuple-element.70.q_ref, ...), custom_call_target="tpu_custom_call" | custom-call | tf_op jit(solution)/shard_map/heads/pallas_call | solution.py:280
  68.1 1.6 %collective-permute-start.23 = (bf16[64,384]{1,0:T(8,128)(2,1)S(1)}, bf16[64,384]{1,0:T(8,128)(2,1)S(1)}, u32[]{:S(2)}, u32[]{:S(2)}) collective-permute-start(bf16[64,384]{1,0:T(8,128)(2,1)S(1)} %get-tuple-element.79), channel_id=1, source_target_pairs={{0,4},{4,0},{1,5},{5,1},{2,6},{6,2},{3,7},{7,3},{8,12},{12,8},{9,1... | collective-permute-start | bytes 147464 | tf_op jit(solution)/shard_map/ppermute | solution.py:17
  70.5 0.9 %heads.7 = (bf16[64,384]{1,0:T(8,128)(2,1)S(1)}, bf16[64,384]{1,0:T(8,128)(2,1)S(1)}) custom-call(s32[1,128]{1,0:T(1,128)S(1)} %constant_dynamic-slice_fusion.live_ref.refs_0_.refs_1_, bf16[128,768]{1,0:T(8,128)(2,1)S(1)} %collective-permute-done.24.text_ref, bf16[4,128,384]{2,1,0:T(8,128)(2,1)S(1)} %get-tuple-element.70.q_ref, ...), custom_call_target="tpu_custom_call" | custom-call | tf_op jit(solution)/shard_map/heads/pallas_call | solution.py:280
  71.4 1.6 %collective-permute-start.25 = (bf16[64,384]{1,0:T(8,128)(2,1)S(1)}, bf16[64,384]{1,0:T(8,128)(2,1)S(1)}, u32[]{:S(2)}, u32[]{:S(2)}) collective-permute-start(bf16[64,384]{1,0:T(8,128)(2,1)S(1)} %get-tuple-element.82), channel_id=1, source_target_pairs={{0,4},{4,0},{1,5},{5,1},{2,6},{6,2},{3,7},{7,3},{8,12},{12,8},{9,1... | collective-permute-start | bytes 147464 | tf_op jit(solution)/shard_map/ppermute | solution.py:17
  73.0 2.6 %collective-permute-done.25.refs_7_ = bf16[64,384]{1,0:T(8,128)(2,1)S(1)} collective-permute-done((bf16[64,384]{1,0:T(8,128)(2,1)S(1)}, bf16[64,384]{1,0:T(8,128)(2,1)S(1)}, u32[]{:S(2)}, u32[]{:S(2)}) %collective-permute-start.25) | collective-permute-done | bytes 49184 | tf_op jit(solution)/shard_map/ppermute | solution.py:17
  (73 shorter events, 10.7 us)
Async XLA Ops:
  0.0 61.2 %copy-start = (s32[2,128]{1,0:T(2,128)S(1)}, s32[2,128]{1,0:T(2,128)}, u32[]{:S(2)}) copy-start(s32[2,128]{1,0:T(2,128)} %param.16) | copy-start | bytes 3076
  3.1 17.2 %copy-start.12 = (bf16[192]{0:T(256)(128)(2,1)S(1)}, bf16[192]{0:T(256)(128)(2,1)}, u32[]{:S(2)}) copy-start(bf16[192]{0:T(256)(128)(2,1)} %b_ref.1) | copy-start | bytes 1156
  3.1 17.3 %copy-start.9 = (bf16[1,192]{1,0:T(2,128)(2,1)S(1)}, bf16[1,192]{1,0:T(2,128)(2,1)}, u32[]{:S(2)}) copy-start(bf16[1,192]{1,0:T(2,128)(2,1)} %shift_ref.3) | copy-start | bytes 1156
  3.1 17.3 %copy-start.10 = (bf16[1,192]{1,0:T(2,128)(2,1)S(1)}, bf16[1,192]{1,0:T(2,128)(2,1)}, u32[]{:S(2)}) copy-start(bf16[1,192]{1,0:T(2,128)(2,1)} %scale_ref.1) | copy-start | bytes 1156
  3.8 1.9 %collective-permute-start = (bf16[1552,128]{1,0:T(8,128)(2,1)S(1)}, bf16[1552,128]{1,0:T(8,128)(2,1)S(1)}, u32[]{:S(2)}, u32[]{:S(2)}) collective-permute-start(bf16[1552,128]{1,0:T(8,128)(2,1)S(1)} %get-tuple-element.44), channel_id=1, source_target_pairs={{0,1},{1,0},{2,3},{3,2},{4,5},{5,4},{6,7},{7,6},{8,9},{9,8},{10,11... | collective-permute-start | bytes 1191944 | tf_op jit(solution)/shard_map/ppermute | solution.py:17
  6.0 24.2 %copy-start.6 = (bf16[1,3072,64]{1,2,0:T(8,128)(2,1)S(1)}, bf16[1,3072,64]{1,2,0:T(8,128)(2,1)}, u32[]{:S(2)}) copy-start(bf16[1,3072,64]{1,2,0:T(8,128)(2,1)} %param.25) | copy-start | bytes 1179652
  6.0 24.2 %copy-start.7 = (bf16[1,64,3072]{2,1,0:T(8,128)(2,1)S(1)}, bf16[1,64,3072]{2,1,0:T(8,128)(2,1)}, u32[]{:S(2)}) copy-start(bf16[1,64,3072]{2,1,0:T(8,128)(2,1)} %param.26) | copy-start | bytes 1179652
  6.0 17.1 %collective-permute-start.1 = (bf16[2,192,768]{2,1,0:T(8,128)(2,1)S(1)}, bf16[2,192,768]{2,1,0:T(8,128)(2,1)S(1)}, u32[]{:S(2)}, u32[]{:S(2)}) collective-permute-start(bf16[2,192,768]{2,1,0:T(8,128)(2,1)S(1)} %get-tuple-element.50), channel_id=1, source_target_pairs={{0,2},{1,3},{2,0},{3,1},{4,6},{5,7},{6,4},{7,5},{8,10},{9,11},{10,... | collective-permute-start | bytes 1769480 | tf_op jit(solution)/shard_map/ppermute | solution.py:17
  9.0 11.1 %collective-permute-start.2 = (bf16[400,128]{1,0:T(8,128)(2,1)S(1)}, bf16[400,128]{1,0:T(8,128)(2,1)S(1)}, u32[]{:S(2)}, u32[]{:S(2)}) collective-permute-start(bf16[400,128]{1,0:T(8,128)(2,1)S(1)} %get-tuple-element.52), channel_id=1, source_target_pairs={{0,16},{8,24},{16,0},{24,8},{1,17},{9,25},{17,1},{25,9},{2,18},{10... | collective-permute-start | bytes 307208 | tf_op jit(solution)/shard_map/ppermute | solution.py:17
  11.6 8.5 %collective-permute-start.3 = (bf16[400,128]{1,0:T(8,128)(2,1)S(1)}, bf16[400,128]{1,0:T(8,128)(2,1)S(1)}, u32[]{:S(2)}, u32[]{:S(2)}) collective-permute-start(bf16[400,128]{1,0:T(8,128)(2,1)S(1)} %get-tuple-element.53), channel_id=1, source_target_pairs={{0,24},{8,16},{16,8},{24,0},{1,25},{9,17},{17,9},{25,1},{2,26},{10... | collective-permute-start | bytes 307208 | tf_op jit(solution)/shard_map/ppermute | solution.py:17
  12.9 7.4 %collective-permute-start.4 = (bf16[400,128]{1,0:T(8,128)(2,1)S(1)}, bf16[400,128]{1,0:T(8,128)(2,1)S(1)}, u32[]{:S(2)}, u32[]{:S(2)}) collective-permute-start(bf16[400,128]{1,0:T(8,128)(2,1)S(1)} %get-tuple-element.54), channel_id=1, source_target_pairs={{0,8},{8,0},{16,24},{24,16},{1,9},{9,1},{17,25},{25,17},{2,10},{10... | collective-permute-start | bytes 307208 | tf_op jit(solution)/shard_map/ppermute | solution.py:17
  20.5 4.7 %collective-permute-start.5 = (bf16[400,128]{1,0:T(8,128)(2,1)S(1)}, bf16[400,128]{1,0:T(8,128)(2,1)S(1)}, u32[]{:S(2)}, u32[]{:S(2)}) collective-permute-start(bf16[400,128]{1,0:T(8,128)(2,1)S(1)} %get-tuple-element.58), channel_id=1, source_target_pairs={{0,2},{1,3},{2,0},{3,1},{4,6},{5,7},{6,4},{7,5},{8,10},{9,11},{10,... | collective-permute-start | bytes 307208 | tf_op jit(solution)/shard_map/ppermute | solution.py:17
  23.2 9.6 %collective-permute-start.8 = (bf16[384,768]{1,0:T(8,128)(2,1)S(1)}, bf16[384,768]{1,0:T(8,128)(2,1)S(1)}, u32[]{:S(2)}, u32[]{:S(2)}) collective-permute-start(bf16[384,768]{1,0:T(8,128)(2,1)S(1)} %get-tuple-element.59), channel_id=1, source_target_pairs={{0,1},{1,0},{2,3},{3,2},{4,5},{5,4},{6,7},{7,6},{8,9},{9,8},{10,11... | collective-permute-start | bytes 1769480 | tf_op jit(solution)/shard_map/ppermute | solution.py:17
  25.5 4.7 %collective-permute-start.6 = (bf16[400,128]{1,0:T(8,128)(2,1)S(1)}, bf16[400,128]{1,0:T(8,128)(2,1)S(1)}, u32[]{:S(2)}, u32[]{:S(2)}) collective-permute-start(bf16[400,128]{1,0:T(8,128)(2,1)S(1)} %centre.1.own_ref), channel_id=1, source_target_pairs={{0,4},{4,0},{1,5},{5,1},{2,6},{6,2},{3,7},{7,3},{8,12},{12,8},{9,1... | collective-permute-start | bytes 307208 | tf_op jit(solution)/shard_map/ppermute | solution.py:17
  30.3 2.4 %collective-permute-start.10 = (bf16[128,1536]{1,0:T(8,128)(2,1)S(1)}, bf16[128,1536]{1,0:T(8,128)(2,1)S(1)}, u32[]{:S(2)}, u32[]{:S(2)}) collective-permute-start(bf16[128,1536]{1,0:T(8,128)(2,1)S(1)} %maps_pack.1.own_ref), channel_id=1, source_target_pairs={{0,1},{1,0},{2,3},{3,2},{4,5},{5,4},{6,7},{7,6},{8,9},{9,8},{10,11... | collective-permute-start | bytes 1179656 | tf_op jit(solution)/shard_map/ppermute | solution.py:17
  30.4 2.3 %collective-permute-start.7 = (bf16[800,128]{1,0:T(8,128)(2,1)S(1)}, bf16[800,128]{1,0:T(8,128)(2,1)S(1)}, u32[]{:S(2)}, u32[]{:S(2)}) collective-permute-start(bf16[800,128]{1,0:T(8,128)(2,1)S(1)} %join.1.refs_0_.dep_ref), channel_id=1, source_target_pairs={{0,1},{1,0},{2,3},{3,2},{4,5},{5,4},{6,7},{7,6},{8,9},{9,8},{10,11... | collective-permute-start | bytes 614408 | tf_op jit(solution)/shard_map/ppermute | solution.py:17
  31.1 20.3 %collective-permute-start.9 = (bf16[4,64,1536]{2,1,0:T(8,128)(2,1)S(1)}, bf16[4,64,1536]{2,1,0:T(8,128)(2,1)S(1)}, u32[]{:S(2)}, u32[]{:S(2)}) collective-permute-start(bf16[4,64,1536]{2,1,0:T(8,128)(2,1)S(1)} %image_pack.1), channel_id=1, source_target_pairs={{0,4},{4,0},{1,5},{5,1},{2,6},{6,2},{3,7},{7,3},{8,12},{12,8},{9,1... | collective-permute-start | bytes 2359304 | tf_op jit(solution)/shard_map/ppermute | solution.py:17
  33.9 19.3 %collective-permute-start.11 = (bf16[2,128,1536]{2,1,0:T(8,128)(2,1)S(1)}, bf16[2,128,1536]{2,1,0:T(8,128)(2,1)S(1)}, u32[]{:S(2)}, u32[]{:S(2)}) collective-permute-start(bf16[2,128,1536]{2,1,0:T(8,128)(2,1)S(1)} %maps_join.1.refs_0_), channel_id=1, source_target_pairs={{0,2},{1,3},{2,0},{3,1},{4,6},{5,7},{6,4},{7,5},{8,10},{9,11},{10,... | collective-permute-start | bytes 2359304 | tf_op jit(solution)/shard_map/ppermute | solution.py:17
  35.3 10.7 %collective-permute-start.13 = (bf16[400,128]{1,0:T(8,128)(2,1)S(1)}, bf16[400,128]{1,0:T(8,128)(2,1)S(1)}, u32[]{:S(2)}, u32[]{:S(2)}) collective-permute-start(bf16[400,128]{1,0:T(8,128)(2,1)S(1)} %get-tuple-element.66), channel_id=1, source_target_pairs={{0,16},{8,24},{16,0},{24,8},{1,17},{9,25},{17,1},{25,9},{2,18},{10... | collective-permute-start | bytes 307208 | tf_op jit(solution)/shard_map/ppermute | solution.py:17
  38.1 7.9 %collective-permute-start.14 = (bf16[400,128]{1,0:T(8,128)(2,1)S(1)}, bf16[400,128]{1,0:T(8,128)(2,1)S(1)}, u32[]{:S(2)}, u32[]{:S(2)}) collective-permute-start(bf16[400,128]{1,0:T(8,128)(2,1)S(1)} %get-tuple-element.67), channel_id=1, source_target_pairs={{0,24},{8,16},{16,8},{24,0},{1,25},{9,17},{17,9},{25,1},{2,26},{10... | collective-permute-start | bytes 307208 | tf_op jit(solution)/shard_map/ppermute | solution.py:17
  39.2 6.9 %collective-permute-start.15 = (bf16[400,128]{1,0:T(8,128)(2,1)S(1)}, bf16[400,128]{1,0:T(8,128)(2,1)S(1)}, u32[]{:S(2)}, u32[]{:S(2)}) collective-permute-start(bf16[400,128]{1,0:T(8,128)(2,1)S(1)} %get-tuple-element.68), channel_id=1, source_target_pairs={{0,8},{8,0},{16,24},{24,16},{1,9},{9,1},{17,25},{25,17},{2,10},{10... | collective-permute-start | bytes 307208 | tf_op jit(solution)/shard_map/ppermute | solution.py:17
  46.4 11.7 %collective-permute-start.16 = (bf16[64,768]{1,0:T(8,128)(2,1)S(1)}, bf16[64,768]{1,0:T(8,128)(2,1)S(1)}, u32[]{:S(2)}, u32[]{:S(2)}) collective-permute-start(bf16[64,768]{1,0:T(8,128)(2,1)S(1)} %finish.1.refs_0_), channel_id=1, source_target_pairs={{0,16},{8,24},{16,0},{24,8},{1,17},{9,25},{17,1},{25,9},{2,18},{10... | collective-permute-start | bytes 294920 | tf_op jit(solution)/shard_map/ppermute | solution.py:17
  50.1 8.0 %collective-permute-start.17 = (bf16[64,768]{1,0:T(8,128)(2,1)S(1)}, bf16[64,768]{1,0:T(8,128)(2,1)S(1)}, u32[]{:S(2)}, u32[]{:S(2)}) collective-permute-start(bf16[64,768]{1,0:T(8,128)(2,1)S(1)} %finish.1.refs_0_), channel_id=1, source_target_pairs={{0,24},{8,16},{16,8},{24,0},{1,25},{9,17},{17,9},{25,1},{2,26},{10... | collective-permute-start | bytes 294920 | tf_op jit(solution)/shard_map/ppermute | solution.py:17
  50.5 8.0 %collective-permute-start.18 = (bf16[64,768]{1,0:T(8,128)(2,1)S(1)}, bf16[64,768]{1,0:T(8,128)(2,1)S(1)}, u32[]{:S(2)}, u32[]{:S(2)}) collective-permute-start(bf16[64,768]{1,0:T(8,128)(2,1)S(1)} %finish.1.refs_0_), channel_id=1, source_target_pairs={{0,8},{8,0},{16,24},{24,16},{1,9},{9,1},{17,25},{25,17},{2,10},{10... | collective-permute-start | bytes 294920 | tf_op jit(solution)/shard_map/ppermute | solution.py:17
  53.5 4.3 %collective-permute-start.12 = (f32[2,64,64]{2,1,0:T(8,128)S(1)}, f32[2,64,64]{2,1,0:T(8,128)S(1)}, u32[]{:S(2)}, u32[]{:S(2)}) collective-permute-start(f32[2,64,64]{2,1,0:T(8,128)S(1)} %get-tuple-element.63.low_ref), channel_id=1, source_target_pairs={{0,4},{4,0},{1,5},{5,1},{2,6},{6,2},{3,7},{7,3},{8,12},{12,8},{9,1... | collective-permute-start | bytes 98312 | tf_op jit(solution)/shard_map/ppermute | solution.py:17
  59.3 4.5 %collective-permute-start.20 = (bf16[128,768]{1,0:T(8,128)(2,1)S(1)}, bf16[128,768]{1,0:T(8,128)(2,1)S(1)}, u32[]{:S(2)}, u32[]{:S(2)}) collective-permute-start(bf16[128,768]{1,0:T(8,128)(2,1)S(1)} %get-tuple-element.74), channel_id=1, source_target_pairs={{0,1},{1,0},{2,3},{3,2},{4,5},{5,4},{6,7},{7,6},{8,9},{9,8},{10,11... | collective-permute-start | bytes 589832 | tf_op jit(solution)/shard_map/ppermute | solution.py:17
  59.4 7.8 %collective-permute-start.22 = (bf16[128,768]{1,0:T(8,128)(2,1)S(1)}, bf16[128,768]{1,0:T(8,128)(2,1)S(1)}, u32[]{:S(2)}, u32[]{:S(2)}) collective-permute-start(bf16[128,768]{1,0:T(8,128)(2,1)S(1)} %get-tuple-element.77), channel_id=1, source_target_pairs={{0,2},{1,3},{2,0},{3,1},{4,6},{5,7},{6,4},{7,5},{8,10},{9,11},{10,... | collective-permute-start | bytes 589832 | tf_op jit(solution)/shard_map/ppermute | solution.py:17
  60.3 10.2 %collective-permute-start.24 = (bf16[128,768]{1,0:T(8,128)(2,1)S(1)}, bf16[128,768]{1,0:T(8,128)(2,1)S(1)}, u32[]{:S(2)}, u32[]{:S(2)}) collective-permute-start(bf16[128,768]{1,0:T(8,128)(2,1)S(1)} %get-tuple-element.80), channel_id=1, source_target_pairs={{0,3},{1,2},{2,1},{3,0},{4,7},{5,6},{6,5},{7,4},{8,11},{9,10},{10,... | collective-permute-start | bytes 589832 | tf_op jit(solution)/shard_map/ppermute | solution.py:17
  62.2 4.2 %collective-permute-start.19 = (bf16[64,384]{1,0:T(8,128)(2,1)S(1)}, bf16[64,384]{1,0:T(8,128)(2,1)S(1)}, u32[]{:S(2)}, u32[]{:S(2)}) collective-permute-start(bf16[64,384]{1,0:T(8,128)(2,1)S(1)} %get-tuple-element.73), channel_id=1, source_target_pairs={{0,4},{4,0},{1,5},{5,1},{2,6},{6,2},{3,7},{7,3},{8,12},{12,8},{9,1... | collective-permute-start | bytes 147464 | tf_op jit(solution)/shard_map/ppermute | solution.py:17
  64.7 5.8 %collective-permute-start.21 = (bf16[64,384]{1,0:T(8,128)(2,1)S(1)}, bf16[64,384]{1,0:T(8,128)(2,1)S(1)}, u32[]{:S(2)}, u32[]{:S(2)}) collective-permute-start(bf16[64,384]{1,0:T(8,128)(2,1)S(1)} %get-tuple-element.76), channel_id=1, source_target_pairs={{0,4},{4,0},{1,5},{5,1},{2,6},{6,2},{3,7},{7,3},{8,12},{12,8},{9,1... | collective-permute-start | bytes 147464 | tf_op jit(solution)/shard_map/ppermute | solution.py:17
  68.1 4.9 %collective-permute-start.23 = (bf16[64,384]{1,0:T(8,128)(2,1)S(1)}, bf16[64,384]{1,0:T(8,128)(2,1)S(1)}, u32[]{:S(2)}, u32[]{:S(2)}) collective-permute-start(bf16[64,384]{1,0:T(8,128)(2,1)S(1)} %get-tuple-element.79), channel_id=1, source_target_pairs={{0,4},{4,0},{1,5},{5,1},{2,6},{6,2},{3,7},{7,3},{8,12},{12,8},{9,1... | collective-permute-start | bytes 147464 | tf_op jit(solution)/shard_map/ppermute | solution.py:17
  71.4 4.2 %collective-permute-start.25 = (bf16[64,384]{1,0:T(8,128)(2,1)S(1)}, bf16[64,384]{1,0:T(8,128)(2,1)S(1)}, u32[]{:S(2)}, u32[]{:S(2)}) collective-permute-start(bf16[64,384]{1,0:T(8,128)(2,1)S(1)} %get-tuple-element.82), channel_id=1, source_target_pairs={{0,4},{4,0},{1,5},{5,1},{2,6},{6,2},{3,7},{7,3},{8,12},{12,8},{9,1... | collective-permute-start | bytes 147464 | tf_op jit(solution)/shard_map/ppermute | solution.py:17
  (8 other events, 48.8 us)

commit v11 on v10

--- a/solution.py
+++ b/solution.py
@@ -645,13 +645,23 @@
 
 
 def assemble_kernel(n_req, n_seq, *refs):
-    out_ref = refs[-1]
+    piece_refs, out_ref, sems = refs[:-2], refs[-2], refs[-1]
     r, s = lax.axis_index("req"), lax.axis_index("seq")
-    half = refs[0].shape[1]
+    half = piece_refs[0].shape[1]
+    copies = []
     for k in range(n_req):
         for i in range(n_seq):
             start = ((s ^ i) * n_req + (r ^ k)) * half
-            out_ref[:, pl.ds(pl.multiple_of(start, HDIM), half)] = refs[k * n_seq + i][...]
+            columns = pl.ds(pl.multiple_of(start, HDIM), half)
+            copies.append(
+                pltpu.make_async_copy(
+                    piece_refs[k * n_seq + i], out_ref.at[:, columns], sems.at[k * n_seq + i]
+                )
+            )
+    for copy in copies:
+        copy.start()
+    for copy in copies:
+        copy.wait()
 
 
 def per_device_heads(
@@ -853,7 +863,8 @@
     live = lax.dynamic_slice_in_dim(prompt_token_ids, request_prompt[0, 0], 1, 0)
     pieces = [None] * n_req
     last = (live, live)
-    for k in range(n_req):
+    sent = live
+    for k in (0,2,1,3):
         mixed = call(
             functools.partial(heads_kernel, k, HDIM ** (-0.5)),
             [struct((image_rows, half))] * n_seq,
@@ -862,11 +873,13 @@
             name="heads",
         )
         pieces[k] = [mixed[0], swap(mixed[1], "seq", n_seq, 1)]
-        last = (mixed[0], pieces[k - 1][1] if k else live)
+        last, sent = (mixed[0], sent), pieces[k][1]
     result = call(
         functools.partial(assemble_kernel, n_req, n_seq),
         struct((image_rows, inner)),
         tuple(p for group in pieces for p in group),
+        scratch=[dma((n_req * n_seq,))],
+        out_specs=ANY,
         name="assemble",
     )
     return result[None, None]

time: 76.5 us -> 78.3 us (1.024)
  waiting for transfers between devices: 32.1 us -> 33.6 us
    ppermute x26, waiting for transfers between devices: 32.1 us -> 33.6 us  [swap(): return lax.ppermute(block, axis, [(i, i ^ step) for i in range(size)])]
  transfers between devices with their start and end apart: 26 -> 26, of which waited for: 15 -> 14; matrix products, arithmetic and copies ran while one was open for 0% -> 0% of each run, Pallas kernels for 8% -> 8%
where the time goes in v11:
time: 78.3 us; the launch traced here: 78.2 us
  waiting for transfers between devices  33.6 us (43%)
  starting transfers between devices  30.9 us (39%)
  Pallas kernels  8.77 us (11%)
  local copies, waits for them, and re-layouts  3.28 us (4%)
  between operations  1.62 us (2%)
    ppermute x26, waiting for transfers between devices, swap(): return lax.ppermute(block, axis, [(i, i ^ step) for i in range(size)])  33.6 us
    ppermute x26, starting transfers between devices, swap(): return lax.ppermute(block, axis, [(i, i ^ step) for i in range(size)])  30.9 us
    pallas_call x20, Pallas kernels, call(): pl.pallas_call(kernel, out_shape=outs, in_specs=specs if specs is not Non...  8.77 us
    unnamed x28, local copies, waits for them, and re-layouts  3.11 us
  transfers between devices with their start and end apart: 26, of which 14 were waited for; matrix products, arithmetic and copies ran while one was open for 0% of the time, Pallas kernels for 8%

profile of v11, /device:TPU:0, one launch (start us, length us, event | category | flops | bytes accessed | tf_op | source)
XLA Modules:
  0.0 78.2 jit_solution(9728290304691105980)
XLA Ops:
  0.0 1.6 %copy-done.4 = bf16[256,3072]{1,0:T(8,128)(2,1)S(1)} copy-done((bf16[256,3072]{1,0:T(8,128)(2,1)S(1)}, bf16[256,3072]{1,0:T(8,128)(2,1)}, u32[]{:S(2)}) %copy-start.4) | copy-done | bytes 1572888
  4.3 1.4 %collective-permute-done.got_ref = bf16[1552,128]{1,0:T(8,128)(2,1)S(1)} collective-permute-done((bf16[1552,128]{1,0:T(8,128)(2,1)S(1)}, bf16[1552,128]{1,0:T(8,128)(2,1)S(1)}, u32[]{:S(2)}, u32[]{:S(2)}) %collective-permute-start) | collective-permute-done | bytes 397344 | tf_op jit(solution)/shard_map/ppermute | solution.py:17
  6.0 2.9 %collective-permute-start.1 = (bf16[2,192,768]{2,1,0:T(8,128)(2,1)S(1)}, bf16[2,192,768]{2,1,0:T(8,128)(2,1)S(1)}, u32[]{:S(2)}, u32[]{:S(2)}) collective-permute-start(bf16[2,192,768]{2,1,0:T(8,128)(2,1)S(1)} %get-tuple-element.50), channel_id=1, source_target_pairs={{0,2},{1,3},{2,0},{3,1},{4,6},{5,7},{6,4},{7,5},{8,10},{9,11},{10,... | collective-permute-start | bytes 1769480 | tf_op jit(solution)/shard_map/ppermute | solution.py:17
  9.0 2.6 %collective-permute-start.2 = (bf16[400,128]{1,0:T(8,128)(2,1)S(1)}, bf16[400,128]{1,0:T(8,128)(2,1)S(1)}, u32[]{:S(2)}, u32[]{:S(2)}) collective-permute-start(bf16[400,128]{1,0:T(8,128)(2,1)S(1)} %get-tuple-element.52), channel_id=1, source_target_pairs={{0,16},{8,24},{16,0},{24,8},{1,17},{9,25},{17,1},{25,9},{2,18},{10... | collective-permute-start | bytes 307208 | tf_op jit(solution)/shard_map/ppermute | solution.py:17
  11.6 1.3 %collective-permute-start.3 = (bf16[400,128]{1,0:T(8,128)(2,1)S(1)}, bf16[400,128]{1,0:T(8,128)(2,1)S(1)}, u32[]{:S(2)}, u32[]{:S(2)}) collective-permute-start(bf16[400,128]{1,0:T(8,128)(2,1)S(1)} %get-tuple-element.53), channel_id=1, source_target_pairs={{0,24},{8,16},{16,8},{24,0},{1,25},{9,17},{17,9},{25,1},{2,26},{10... | collective-permute-start | bytes 307208 | tf_op jit(solution)/shard_map/ppermute | solution.py:17
  13.8 6.2 %collective-permute-done.2.refs_0_ = bf16[400,128]{1,0:T(8,128)(2,1)S(1)} collective-permute-done((bf16[400,128]{1,0:T(8,128)(2,1)S(1)}, bf16[400,128]{1,0:T(8,128)(2,1)S(1)}, u32[]{:S(2)}, u32[]{:S(2)}) %collective-permute-start.2) | collective-permute-done | bytes 102432 | tf_op jit(solution)/shard_map/ppermute | solution.py:17
  21.0 2.1 %collective-permute-done.1.got_ref = bf16[2,192,768]{2,1,0:T(8,128)(2,1)S(1)} collective-permute-done((bf16[2,192,768]{2,1,0:T(8,128)(2,1)S(1)}, bf16[2,192,768]{2,1,0:T(8,128)(2,1)S(1)}, u32[]{:S(2)}, u32[]{:S(2)}) %collective-permute-start.1) | collective-permute-done | bytes 589856 | tf_op jit(solution)/shard_map/ppermute | solution.py:17
  23.3 2.0 %collective-permute-done.5.got_ref = bf16[400,128]{1,0:T(8,128)(2,1)S(1)} collective-permute-done((bf16[400,128]{1,0:T(8,128)(2,1)S(1)}, bf16[400,128]{1,0:T(8,128)(2,1)S(1)}, u32[]{:S(2)}, u32[]{:S(2)}) %collective-permute-start.5) | collective-permute-done | bytes 102432 | tf_op jit(solution)/shard_map/ppermute | solution.py:17
  25.5 1.6 %collective-permute-start.6 = (bf16[400,128]{1,0:T(8,128)(2,1)S(1)}, bf16[400,128]{1,0:T(8,128)(2,1)S(1)}, u32[]{:S(2)}, u32[]{:S(2)}) collective-permute-start(bf16[400,128]{1,0:T(8,128)(2,1)S(1)} %centre.1.own_ref), channel_id=1, source_target_pairs={{0,4},{4,0},{1,5},{5,1},{2,6},{6,2},{3,7},{7,3},{8,12},{12,8},{9,1... | collective-permute-start | bytes 307208 | tf_op jit(solution)/shard_map/ppermute | solution.py:17
  27.0 3.2 %collective-permute-done.6.got_ref = bf16[400,128]{1,0:T(8,128)(2,1)S(1)} collective-permute-done((bf16[400,128]{1,0:T(8,128)(2,1)S(1)}, bf16[400,128]{1,0:T(8,128)(2,1)S(1)}, u32[]{:S(2)}, u32[]{:S(2)}) %collective-permute-start.6) | collective-permute-done | bytes 102432 | tf_op jit(solution)/shard_map/ppermute | solution.py:17
  31.1 1.6 %collective-permute-start.9 = (bf16[4,64,1536]{2,1,0:T(8,128)(2,1)S(1)}, bf16[4,64,1536]{2,1,0:T(8,128)(2,1)S(1)}, u32[]{:S(2)}, u32[]{:S(2)}) collective-permute-start(bf16[4,64,1536]{2,1,0:T(8,128)(2,1)S(1)} %image_pack.1), channel_id=1, source_target_pairs={{0,4},{4,0},{1,5},{5,1},{2,6},{6,2},{3,7},{7,3},{8,12},{12,8},{9,1... | collective-permute-start | bytes 2359304 | tf_op jit(solution)/shard_map/ppermute | solution.py:17
  32.8 1.2 %project.1 = (s32[4]{0:T(128)S(1)}, f32[400,128]{1,0:T(8,128)S(1)}, bf16[400,128]{1,0:T(8,128)(2,1)S(1)}, bf16[400,128]{1,0:T(8,128)(2,1)S(1)}, bf16[400,128]{1,0:T(8,128)(2,1)S(1)}) custom-call(bf16[800,128]{1,0:T(8,128)(2,1)S(1)} %join.1.refs_0_.dep_ref, bf16[800,128]{1,0:T(8,128)(2,1)S(1)} %collective-permute-done.7.refs_1_, ...), custom_call_target="tpu_custom_call" | custom-call | tf_op jit(solution)/shard_map/project/pallas_call | solution.py:280
  33.9 1.4 %collective-permute-start.11 = (bf16[2,128,1536]{2,1,0:T(8,128)(2,1)S(1)}, bf16[2,128,1536]{2,1,0:T(8,128)(2,1)S(1)}, u32[]{:S(2)}, u32[]{:S(2)}) collective-permute-start(bf16[2,128,1536]{2,1,0:T(8,128)(2,1)S(1)} %maps_join.1.refs_0_), channel_id=1, source_target_pairs={{0,2},{1,3},{2,0},{3,1},{4,6},{5,7},{6,4},{7,5},{8,10},{9,11},{10,... | collective-permute-start | bytes 2359304 | tf_op jit(solution)/shard_map/ppermute | solution.py:17
  35.3 2.8 %collective-permute-start.13 = (bf16[400,128]{1,0:T(8,128)(2,1)S(1)}, bf16[400,128]{1,0:T(8,128)(2,1)S(1)}, u32[]{:S(2)}, u32[]{:S(2)}) collective-permute-start(bf16[400,128]{1,0:T(8,128)(2,1)S(1)} %get-tuple-element.66), channel_id=1, source_target_pairs={{0,16},{8,24},{16,0},{24,8},{1,17},{9,25},{17,1},{25,9},{2,18},{10... | collective-permute-start | bytes 307208 | tf_op jit(solution)/shard_map/ppermute | solution.py:17
  38.1 1.1 %collective-permute-start.14 = (bf16[400,128]{1,0:T(8,128)(2,1)S(1)}, bf16[400,128]{1,0:T(8,128)(2,1)S(1)}, u32[]{:S(2)}, u32[]{:S(2)}) collective-permute-start(bf16[400,128]{1,0:T(8,128)(2,1)S(1)} %get-tuple-element.67), channel_id=1, source_target_pairs={{0,24},{8,16},{16,8},{24,0},{1,25},{9,17},{17,9},{25,1},{2,26},{10... | collective-permute-start | bytes 307208 | tf_op jit(solution)/shard_map/ppermute | solution.py:17
  39.5 6.6 %collective-permute-done.13.refs_0_ = bf16[400,128]{1,0:T(8,128)(2,1)S(1)} collective-permute-done((bf16[400,128]{1,0:T(8,128)(2,1)S(1)}, bf16[400,128]{1,0:T(8,128)(2,1)S(1)}, u32[]{:S(2)}, u32[]{:S(2)}) %collective-permute-start.13) | collective-permute-done | bytes 102432 | tf_op jit(solution)/shard_map/ppermute | solution.py:17
  46.4 3.7 %collective-permute-start.16 = (bf16[64,768]{1,0:T(8,128)(2,1)S(1)}, bf16[64,768]{1,0:T(8,128)(2,1)S(1)}, u32[]{:S(2)}, u32[]{:S(2)}) collective-permute-start(bf16[64,768]{1,0:T(8,128)(2,1)S(1)} %finish.1.refs_0_), channel_id=1, source_target_pairs={{0,16},{8,24},{16,0},{24,8},{1,17},{9,25},{17,1},{25,9},{2,18},{10... | collective-permute-start | bytes 294920 | tf_op jit(solution)/shard_map/ppermute | solution.py:17
  51.4 1.8 %collective-permute-done.11.refs_1_ = bf16[2,128,1536]{2,1,0:T(8,128)(2,1)S(1)} collective-permute-done((bf16[2,128,1536]{2,1,0:T(8,128)(2,1)S(1)}, bf16[2,128,1536]{2,1,0:T(8,128)(2,1)S(1)}, u32[]{:S(2)}, u32[]{:S(2)}) %collective-permute-start.11) | collective-permute-done | bytes 786464 | tf_op jit(solution)/shard_map/ppermute | solution.py:17
  53.5 1.5 %collective-permute-start.12 = (f32[2,64,64]{2,1,0:T(8,128)S(1)}, f32[2,64,64]{2,1,0:T(8,128)S(1)}, u32[]{:S(2)}, u32[]{:S(2)}) collective-permute-start(f32[2,64,64]{2,1,0:T(8,128)S(1)} %get-tuple-element.63.low_ref), channel_id=1, source_target_pairs={{0,4},{4,0},{1,5},{5,1},{2,6},{6,2},{3,7},{7,3},{8,12},{12,8},{9,1... | collective-permute-start | bytes 98312 | tf_op jit(solution)/shard_map/ppermute | solution.py:17
  55.0 2.8 %collective-permute-done.12.other_ref = f32[2,64,64]{2,1,0:T(8,128)S(1)} collective-permute-done((f32[2,64,64]{2,1,0:T(8,128)S(1)}, f32[2,64,64]{2,1,0:T(8,128)S(1)}, u32[]{:S(2)}, u32[]{:S(2)}) %collective-permute-start.12) | collective-permute-done | bytes 32800 | tf_op jit(solution)/shard_map/ppermute | solution.py:17
  59.3 0.9 %collective-permute-start.21 = (bf16[128,768]{1,0:T(8,128)(2,1)S(1)}, bf16[128,768]{1,0:T(8,128)(2,1)S(1)}, u32[]{:S(2)}, u32[]{:S(2)}) collective-permute-start(bf16[128,768]{1,0:T(8,128)(2,1)S(1)} %get-tuple-element.75), channel_id=1, source_target_pairs={{0,2},{1,3},{2,0},{3,1},{4,6},{5,7},{6,4},{7,5},{8,10},{9,11},{10,... | collective-permute-start | bytes 589832 | tf_op jit(solution)/shard_map/ppermute | solution.py:17
  60.2 1.3 %collective-permute-start.24 = (bf16[128,768]{1,0:T(8,128)(2,1)S(1)}, bf16[128,768]{1,0:T(8,128)(2,1)S(1)}, u32[]{:S(2)}, u32[]{:S(2)}) collective-permute-start(bf16[128,768]{1,0:T(8,128)(2,1)S(1)} %get-tuple-element.80), channel_id=1, source_target_pairs={{0,3},{1,2},{2,1},{3,0},{4,7},{5,6},{6,5},{7,4},{8,11},{9,10},{10,... | collective-permute-start | bytes 589832 | tf_op jit(solution)/shard_map/ppermute | solution.py:17
  61.5 0.9 %heads.4 = (bf16[64,384]{1,0:T(8,128)(2,1)S(1)}, bf16[64,384]{1,0:T(8,128)(2,1)S(1)}) custom-call(s32[1,128]{1,0:T(1,128)S(1)} %constant_dynamic-slice_fusion.live_ref.refs_0_.refs_1_, bf16[128,768]{1,0:T(8,128)(2,1)S(1)} %get-tuple-element.69.text_ref, bf16[4,128,384]{2,1,0:T(8,128)(2,1)S(1)} %get-tuple-element.70.q_ref, ...), custom_call_target="tpu_custom_call" | custom-call | tf_op jit(solution)/shard_map/heads/pallas_call | solution.py:280
  62.4 1.6 %collective-permute-start.19 = (bf16[64,384]{1,0:T(8,128)(2,1)S(1)}, bf16[64,384]{1,0:T(8,128)(2,1)S(1)}, u32[]{:S(2)}, u32[]{:S(2)}) collective-permute-start(bf16[64,384]{1,0:T(8,128)(2,1)S(1)} %get-tuple-element.73), channel_id=1, source_target_pairs={{0,4},{4,0},{1,5},{5,1},{2,6},{6,2},{3,7},{7,3},{8,12},{12,8},{9,1... | collective-permute-start | bytes 147464 | tf_op jit(solution)/shard_map/ppermute | solution.py:17
  64.0 3.2 %collective-permute-done.21.text_ref = bf16[128,768]{1,0:T(8,128)(2,1)S(1)} collective-permute-done((bf16[128,768]{1,0:T(8,128)(2,1)S(1)}, bf16[128,768]{1,0:T(8,128)(2,1)S(1)}, u32[]{:S(2)}, u32[]{:S(2)}) %collective-permute-start.21) | collective-permute-done | bytes 196640 | tf_op jit(solution)/shard_map/ppermute | solution.py:17
  67.2 0.9 %heads.5 = (bf16[64,384]{1,0:T(8,128)(2,1)S(1)}, bf16[64,384]{1,0:T(8,128)(2,1)S(1)}) custom-call(s32[1,128]{1,0:T(1,128)S(1)} %constant_dynamic-slice_fusion.live_ref.refs_0_.refs_1_, bf16[128,768]{1,0:T(8,128)(2,1)S(1)} %collective-permute-done.21.text_ref, bf16[4,128,384]{2,1,0:T(8,128)(2,1)S(1)} %get-tuple-element.70.q_ref, ...), custom_call_target="tpu_custom_call" | custom-call | tf_op jit(solution)/shard_map/heads/pallas_call | solution.py:280
  68.1 1.6 %collective-permute-start.23 = (bf16[64,384]{1,0:T(8,128)(2,1)S(1)}, bf16[64,384]{1,0:T(8,128)(2,1)S(1)}, u32[]{:S(2)}, u32[]{:S(2)}) collective-permute-start(bf16[64,384]{1,0:T(8,128)(2,1)S(1)} %get-tuple-element.79), channel_id=1, source_target_pairs={{0,4},{4,0},{1,5},{5,1},{2,6},{6,2},{3,7},{7,3},{8,12},{12,8},{9,1... | collective-permute-start | bytes 147464 | tf_op jit(solution)/shard_map/ppermute | solution.py:17
  69.7 0.9 %heads.6 = (bf16[64,384]{1,0:T(8,128)(2,1)S(1)}, bf16[64,384]{1,0:T(8,128)(2,1)S(1)}) custom-call(s32[1,128]{1,0:T(1,128)S(1)} %constant_dynamic-slice_fusion.live_ref.refs_0_.refs_1_, bf16[128,768]{1,0:T(8,128)(2,1)S(1)} %collective-permute-done.20.text_ref, bf16[4,128,384]{2,1,0:T(8,128)(2,1)S(1)} %get-tuple-element.70.q_ref, ...), custom_call_target="tpu_custom_call" | custom-call | tf_op jit(solution)/shard_map/heads/pallas_call | solution.py:280
  71.2 1.1 %collective-permute-done.23.refs_1_.refs_5_ = bf16[64,384]{1,0:T(8,128)(2,1)S(1)} collective-permute-done((bf16[64,384]{1,0:T(8,128)(2,1)S(1)}, bf16[64,384]{1,0:T(8,128)(2,1)S(1)}, u32[]{:S(2)}, u32[]{:S(2)}) %collective-permute-start.23) | collective-permute-done | bytes 49184 | tf_op jit(solution)/shard_map/ppermute | solution.py:17
  72.3 0.9 %heads.7 = (bf16[64,384]{1,0:T(8,128)(2,1)S(1)}, bf16[64,384]{1,0:T(8,128)(2,1)S(1)}) custom-call(s32[1,128]{1,0:T(1,128)S(1)} %constant_dynamic-slice_fusion.live_ref.refs_0_.refs_1_, bf16[128,768]{1,0:T(8,128)(2,1)S(1)} %collective-permute-done.24.text_ref, bf16[4,128,384]{2,1,0:T(8,128)(2,1)S(1)} %get-tuple-element.70.q_ref, ...), custom_call_target="tpu_custom_call" | custom-call | tf_op jit(solution)/shard_map/heads/pallas_call | solution.py:280
  73.2 1.6 %collective-permute-start.25 = (bf16[64,384]{1,0:T(8,128)(2,1)S(1)}, bf16[64,384]{1,0:T(8,128)(2,1)S(1)}, u32[]{:S(2)}, u32[]{:S(2)}) collective-permute-start(bf16[64,384]{1,0:T(8,128)(2,1)S(1)} %get-tuple-element.82), channel_id=1, source_target_pairs={{0,4},{4,0},{1,5},{5,1},{2,6},{6,2},{3,7},{7,3},{8,12},{12,8},{9,1... | collective-permute-start | bytes 147464 | tf_op jit(solution)/shard_map/ppermute | solution.py:17
  74.8 2.6 %collective-permute-done.25.refs_7_ = bf16[64,384]{1,0:T(8,128)(2,1)S(1)} collective-permute-done((bf16[64,384]{1,0:T(8,128)(2,1)S(1)}, bf16[64,384]{1,0:T(8,128)(2,1)S(1)}, u32[]{:S(2)}, u32[]{:S(2)}) %collective-permute-start.25) | collective-permute-done | bytes 49184 | tf_op jit(solution)/shard_map/ppermute | solution.py:17
  (73 shorter events, 9.9 us)
Async XLA Ops:
  0.0 61.5 %copy-start = (s32[2,128]{1,0:T(2,128)S(1)}, s32[2,128]{1,0:T(2,128)}, u32[]{:S(2)}) copy-start(s32[2,128]{1,0:T(2,128)} %param.16) | copy-start | bytes 3076
  3.1 17.2 %copy-start.12 = (bf16[192]{0:T(256)(128)(2,1)S(1)}, bf16[192]{0:T(256)(128)(2,1)}, u32[]{:S(2)}) copy-start(bf16[192]{0:T(256)(128)(2,1)} %b_ref.1) | copy-start | bytes 1156
  3.1 17.3 %copy-start.9 = (bf16[1,192]{1,0:T(2,128)(2,1)S(1)}, bf16[1,192]{1,0:T(2,128)(2,1)}, u32[]{:S(2)}) copy-start(bf16[1,192]{1,0:T(2,128)(2,1)} %shift_ref.3) | copy-start | bytes 1156
  3.1 17.3 %copy-start.10 = (bf16[1,192]{1,0:T(2,128)(2,1)S(1)}, bf16[1,192]{1,0:T(2,128)(2,1)}, u32[]{:S(2)}) copy-start(bf16[1,192]{1,0:T(2,128)(2,1)} %scale_ref.1) | copy-start | bytes 1156
  3.8 1.9 %collective-permute-start = (bf16[1552,128]{1,0:T(8,128)(2,1)S(1)}, bf16[1552,128]{1,0:T(8,128)(2,1)S(1)}, u32[]{:S(2)}, u32[]{:S(2)}) collective-permute-start(bf16[1552,128]{1,0:T(8,128)(2,1)S(1)} %get-tuple-element.44), channel_id=1, source_target_pairs={{0,1},{1,0},{2,3},{3,2},{4,5},{5,4},{6,7},{7,6},{8,9},{9,8},{10,11... | collective-permute-start | bytes 1191944 | tf_op jit(solution)/shard_map/ppermute | solution.py:17
  6.0 24.2 %copy-start.6 = (bf16[1,3072,64]{1,2,0:T(8,128)(2,1)S(1)}, bf16[1,3072,64]{1,2,0:T(8,128)(2,1)}, u32[]{:S(2)}) copy-start(bf16[1,3072,64]{1,2,0:T(8,128)(2,1)} %param.25) | copy-start | bytes 1179652
  6.0 24.2 %copy-start.7 = (bf16[1,64,3072]{2,1,0:T(8,128)(2,1)S(1)}, bf16[1,64,3072]{2,1,0:T(8,128)(2,1)}, u32[]{:S(2)}) copy-start(bf16[1,64,3072]{2,1,0:T(8,128)(2,1)} %param.26) | copy-start | bytes 1179652
  6.0 17.1 %collective-permute-start.1 = (bf16[2,192,768]{2,1,0:T(8,128)(2,1)S(1)}, bf16[2,192,768]{2,1,0:T(8,128)(2,1)S(1)}, u32[]{:S(2)}, u32[]{:S(2)}) collective-permute-start(bf16[2,192,768]{2,1,0:T(8,128)(2,1)S(1)} %get-tuple-element.50), channel_id=1, source_target_pairs={{0,2},{1,3},{2,0},{3,1},{4,6},{5,7},{6,4},{7,5},{8,10},{9,11},{10,... | collective-permute-start | bytes 1769480 | tf_op jit(solution)/shard_map/ppermute | solution.py:17
  9.0 11.1 %collective-permute-start.2 = (bf16[400,128]{1,0:T(8,128)(2,1)S(1)}, bf16[400,128]{1,0:T(8,128)(2,1)S(1)}, u32[]{:S(2)}, u32[]{:S(2)}) collective-permute-start(bf16[400,128]{1,0:T(8,128)(2,1)S(1)} %get-tuple-element.52), channel_id=1, source_target_pairs={{0,16},{8,24},{16,0},{24,8},{1,17},{9,25},{17,1},{25,9},{2,18},{10... | collective-permute-start | bytes 307208 | tf_op jit(solution)/shard_map/ppermute | solution.py:17
  11.6 8.5 %collective-permute-start.3 = (bf16[400,128]{1,0:T(8,128)(2,1)S(1)}, bf16[400,128]{1,0:T(8,128)(2,1)S(1)}, u32[]{:S(2)}, u32[]{:S(2)}) collective-permute-start(bf16[400,128]{1,0:T(8,128)(2,1)S(1)} %get-tuple-element.53), channel_id=1, source_target_pairs={{0,24},{8,16},{16,8},{24,0},{1,25},{9,17},{17,9},{25,1},{2,26},{10... | collective-permute-start | bytes 307208 | tf_op jit(solution)/shard_map/ppermute | solution.py:17
  12.9 7.4 %collective-permute-start.4 = (bf16[400,128]{1,0:T(8,128)(2,1)S(1)}, bf16[400,128]{1,0:T(8,128)(2,1)S(1)}, u32[]{:S(2)}, u32[]{:S(2)}) collective-permute-start(bf16[400,128]{1,0:T(8,128)(2,1)S(1)} %get-tuple-element.54), channel_id=1, source_target_pairs={{0,8},{8,0},{16,24},{24,16},{1,9},{9,1},{17,25},{25,17},{2,10},{10... | collective-permute-start | bytes 307208 | tf_op jit(solution)/shard_map/ppermute | solution.py:17
  20.5 4.7 %collective-permute-start.5 = (bf16[400,128]{1,0:T(8,128)(2,1)S(1)}, bf16[400,128]{1,0:T(8,128)(2,1)S(1)}, u32[]{:S(2)}, u32[]{:S(2)}) collective-permute-start(bf16[400,128]{1,0:T(8,128)(2,1)S(1)} %get-tuple-element.58), channel_id=1, source_target_pairs={{0,2},{1,3},{2,0},{3,1},{4,6},{5,7},{6,4},{7,5},{8,10},{9,11},{10,... | collective-permute-start | bytes 307208 | tf_op jit(solution)/shard_map/ppermute | solution.py:17
  23.2 9.6 %collective-permute-start.8 = (bf16[384,768]{1,0:T(8,128)(2,1)S(1)}, bf16[384,768]{1,0:T(8,128)(2,1)S(1)}, u32[]{:S(2)}, u32[]{:S(2)}) collective-permute-start(bf16[384,768]{1,0:T(8,128)(2,1)S(1)} %get-tuple-element.59), channel_id=1, source_target_pairs={{0,1},{1,0},{2,3},{3,2},{4,5},{5,4},{6,7},{7,6},{8,9},{9,8},{10,11... | collective-permute-start | bytes 1769480 | tf_op jit(solution)/shard_map/ppermute | solution.py:17
  25.5 4.7 %collective-permute-start.6 = (bf16[400,128]{1,0:T(8,128)(2,1)S(1)}, bf16[400,128]{1,0:T(8,128)(2,1)S(1)}, u32[]{:S(2)}, u32[]{:S(2)}) collective-permute-start(bf16[400,128]{1,0:T(8,128)(2,1)S(1)} %centre.1.own_ref), channel_id=1, source_target_pairs={{0,4},{4,0},{1,5},{5,1},{2,6},{6,2},{3,7},{7,3},{8,12},{12,8},{9,1... | collective-permute-start | bytes 307208 | tf_op jit(solution)/shard_map/ppermute | solution.py:17
  30.3 2.4 %collective-permute-start.10 = (bf16[128,1536]{1,0:T(8,128)(2,1)S(1)}, bf16[128,1536]{1,0:T(8,128)(2,1)S(1)}, u32[]{:S(2)}, u32[]{:S(2)}) collective-permute-start(bf16[128,1536]{1,0:T(8,128)(2,1)S(1)} %maps_pack.1.own_ref), channel_id=1, source_target_pairs={{0,1},{1,0},{2,3},{3,2},{4,5},{5,4},{6,7},{7,6},{8,9},{9,8},{10,11... | collective-permute-start | bytes 1179656 | tf_op jit(solution)/shard_map/ppermute | solution.py:17
  30.4 2.3 %collective-permute-start.7 = (bf16[800,128]{1,0:T(8,128)(2,1)S(1)}, bf16[800,128]{1,0:T(8,128)(2,1)S(1)}, u32[]{:S(2)}, u32[]{:S(2)}) collective-permute-start(bf16[800,128]{1,0:T(8,128)(2,1)S(1)} %join.1.refs_0_.dep_ref), channel_id=1, source_target_pairs={{0,1},{1,0},{2,3},{3,2},{4,5},{5,4},{6,7},{7,6},{8,9},{9,8},{10,11... | collective-permute-start | bytes 614408 | tf_op jit(solution)/shard_map/ppermute | solution.py:17
  31.1 20.3 %collective-permute-start.9 = (bf16[4,64,1536]{2,1,0:T(8,128)(2,1)S(1)}, bf16[4,64,1536]{2,1,0:T(8,128)(2,1)S(1)}, u32[]{:S(2)}, u32[]{:S(2)}) collective-permute-start(bf16[4,64,1536]{2,1,0:T(8,128)(2,1)S(1)} %image_pack.1), channel_id=1, source_target_pairs={{0,4},{4,0},{1,5},{5,1},{2,6},{6,2},{3,7},{7,3},{8,12},{12,8},{9,1... | collective-permute-start | bytes 2359304 | tf_op jit(solution)/shard_map/ppermute | solution.py:17
  33.9 19.3 %collective-permute-start.11 = (bf16[2,128,1536]{2,1,0:T(8,128)(2,1)S(1)}, bf16[2,128,1536]{2,1,0:T(8,128)(2,1)S(1)}, u32[]{:S(2)}, u32[]{:S(2)}) collective-permute-start(bf16[2,128,1536]{2,1,0:T(8,128)(2,1)S(1)} %maps_join.1.refs_0_), channel_id=1, source_target_pairs={{0,2},{1,3},{2,0},{3,1},{4,6},{5,7},{6,4},{7,5},{8,10},{9,11},{10,... | collective-permute-start | bytes 2359304 | tf_op jit(solution)/shard_map/ppermute | solution.py:17
  35.3 10.7 %collective-permute-start.13 = (bf16[400,128]{1,0:T(8,128)(2,1)S(1)}, bf16[400,128]{1,0:T(8,128)(2,1)S(1)}, u32[]{:S(2)}, u32[]{:S(2)}) collective-permute-start(bf16[400,128]{1,0:T(8,128)(2,1)S(1)} %get-tuple-element.66), channel_id=1, source_target_pairs={{0,16},{8,24},{16,0},{24,8},{1,17},{9,25},{17,1},{25,9},{2,18},{10... | collective-permute-start | bytes 307208 | tf_op jit(solution)/shard_map/ppermute | solution.py:17
  38.1 7.9 %collective-permute-start.14 = (bf16[400,128]{1,0:T(8,128)(2,1)S(1)}, bf16[400,128]{1,0:T(8,128)(2,1)S(1)}, u32[]{:S(2)}, u32[]{:S(2)}) collective-permute-start(bf16[400,128]{1,0:T(8,128)(2,1)S(1)} %get-tuple-element.67), channel_id=1, source_target_pairs={{0,24},{8,16},{16,8},{24,0},{1,25},{9,17},{17,9},{25,1},{2,26},{10... | collective-permute-start | bytes 307208 | tf_op jit(solution)/shard_map/ppermute | solution.py:17
  39.2 6.9 %collective-permute-start.15 = (bf16[400,128]{1,0:T(8,128)(2,1)S(1)}, bf16[400,128]{1,0:T(8,128)(2,1)S(1)}, u32[]{:S(2)}, u32[]{:S(2)}) collective-permute-start(bf16[400,128]{1,0:T(8,128)(2,1)S(1)} %get-tuple-element.68), channel_id=1, source_target_pairs={{0,8},{8,0},{16,24},{24,16},{1,9},{9,1},{17,25},{25,17},{2,10},{10... | collective-permute-start | bytes 307208 | tf_op jit(solution)/shard_map/ppermute | solution.py:17
  46.4 11.7 %collective-permute-start.16 = (bf16[64,768]{1,0:T(8,128)(2,1)S(1)}, bf16[64,768]{1,0:T(8,128)(2,1)S(1)}, u32[]{:S(2)}, u32[]{:S(2)}) collective-permute-start(bf16[64,768]{1,0:T(8,128)(2,1)S(1)} %finish.1.refs_0_), channel_id=1, source_target_pairs={{0,16},{8,24},{16,0},{24,8},{1,17},{9,25},{17,1},{25,9},{2,18},{10... | collective-permute-start | bytes 294920 | tf_op jit(solution)/shard_map/ppermute | solution.py:17
  50.1 8.0 %collective-permute-start.17 = (bf16[64,768]{1,0:T(8,128)(2,1)S(1)}, bf16[64,768]{1,0:T(8,128)(2,1)S(1)}, u32[]{:S(2)}, u32[]{:S(2)}) collective-permute-start(bf16[64,768]{1,0:T(8,128)(2,1)S(1)} %finish.1.refs_0_), channel_id=1, source_target_pairs={{0,24},{8,16},{16,8},{24,0},{1,25},{9,17},{17,9},{25,1},{2,26},{10... | collective-permute-start | bytes 294920 | tf_op jit(solution)/shard_map/ppermute | solution.py:17
  50.5 8.0 %collective-permute-start.18 = (bf16[64,768]{1,0:T(8,128)(2,1)S(1)}, bf16[64,768]{1,0:T(8,128)(2,1)S(1)}, u32[]{:S(2)}, u32[]{:S(2)}) collective-permute-start(bf16[64,768]{1,0:T(8,128)(2,1)S(1)} %finish.1.refs_0_), channel_id=1, source_target_pairs={{0,8},{8,0},{16,24},{24,16},{1,9},{9,1},{17,25},{25,17},{2,10},{10... | collective-permute-start | bytes 294920 | tf_op jit(solution)/shard_map/ppermute | solution.py:17
  53.5 4.3 %collective-permute-start.12 = (f32[2,64,64]{2,1,0:T(8,128)S(1)}, f32[2,64,64]{2,1,0:T(8,128)S(1)}, u32[]{:S(2)}, u32[]{:S(2)}) collective-permute-start(f32[2,64,64]{2,1,0:T(8,128)S(1)} %get-tuple-element.63.low_ref), channel_id=1, source_target_pairs={{0,4},{4,0},{1,5},{5,1},{2,6},{6,2},{3,7},{7,3},{8,12},{12,8},{9,1... | collective-permute-start | bytes 98312 | tf_op jit(solution)/shard_map/ppermute | solution.py:17
  59.3 7.9 %collective-permute-start.21 = (bf16[128,768]{1,0:T(8,128)(2,1)S(1)}, bf16[128,768]{1,0:T(8,128)(2,1)S(1)}, u32[]{:S(2)}, u32[]{:S(2)}) collective-permute-start(bf16[128,768]{1,0:T(8,128)(2,1)S(1)} %get-tuple-element.75), channel_id=1, source_target_pairs={{0,2},{1,3},{2,0},{3,1},{4,6},{5,7},{6,4},{7,5},{8,10},{9,11},{10,... | collective-permute-start | bytes 589832 | tf_op jit(solution)/shard_map/ppermute | solution.py:17
  60.2 9.5 %collective-permute-start.20 = (bf16[128,768]{1,0:T(8,128)(2,1)S(1)}, bf16[128,768]{1,0:T(8,128)(2,1)S(1)}, u32[]{:S(2)}, u32[]{:S(2)}) collective-permute-start(bf16[128,768]{1,0:T(8,128)(2,1)S(1)} %get-tuple-element.74), channel_id=1, source_target_pairs={{0,1},{1,0},{2,3},{3,2},{4,5},{5,4},{6,7},{7,6},{8,9},{9,8},{10,11... | collective-permute-start | bytes 589832 | tf_op jit(solution)/shard_map/ppermute | solution.py:17
  60.2 11.0 %collective-permute-start.24 = (bf16[128,768]{1,0:T(8,128)(2,1)S(1)}, bf16[128,768]{1,0:T(8,128)(2,1)S(1)}, u32[]{:S(2)}, u32[]{:S(2)}) collective-permute-start(bf16[128,768]{1,0:T(8,128)(2,1)S(1)} %get-tuple-element.80), channel_id=1, source_target_pairs={{0,3},{1,2},{2,1},{3,0},{4,7},{5,6},{6,5},{7,4},{8,11},{9,10},{10,... | collective-permute-start | bytes 589832 | tf_op jit(solution)/shard_map/ppermute | solution.py:17
  62.4 7.3 %collective-permute-start.19 = (bf16[64,384]{1,0:T(8,128)(2,1)S(1)}, bf16[64,384]{1,0:T(8,128)(2,1)S(1)}, u32[]{:S(2)}, u32[]{:S(2)}) collective-permute-start(bf16[64,384]{1,0:T(8,128)(2,1)S(1)} %get-tuple-element.73), channel_id=1, source_target_pairs={{0,4},{4,0},{1,5},{5,1},{2,6},{6,2},{3,7},{7,3},{8,12},{12,8},{9,1... | collective-permute-start | bytes 147464 | tf_op jit(solution)/shard_map/ppermute | solution.py:17
  68.1 4.2 %collective-permute-start.23 = (bf16[64,384]{1,0:T(8,128)(2,1)S(1)}, bf16[64,384]{1,0:T(8,128)(2,1)S(1)}, u32[]{:S(2)}, u32[]{:S(2)}) collective-permute-start(bf16[64,384]{1,0:T(8,128)(2,1)S(1)} %get-tuple-element.79), channel_id=1, source_target_pairs={{0,4},{4,0},{1,5},{5,1},{2,6},{6,2},{3,7},{7,3},{8,12},{12,8},{9,1... | collective-permute-start | bytes 147464 | tf_op jit(solution)/shard_map/ppermute | solution.py:17
  70.7 4.2 %collective-permute-start.22 = (bf16[64,384]{1,0:T(8,128)(2,1)S(1)}, bf16[64,384]{1,0:T(8,128)(2,1)S(1)}, u32[]{:S(2)}, u32[]{:S(2)}) collective-permute-start(bf16[64,384]{1,0:T(8,128)(2,1)S(1)} %get-tuple-element.78), channel_id=1, source_target_pairs={{0,4},{4,0},{1,5},{5,1},{2,6},{6,2},{3,7},{7,3},{8,12},{12,8},{9,1... | collective-permute-start | bytes 147464 | tf_op jit(solution)/shard_map/ppermute | solution.py:17
  73.2 4.2 %collective-permute-start.25 = (bf16[64,384]{1,0:T(8,128)(2,1)S(1)}, bf16[64,384]{1,0:T(8,128)(2,1)S(1)}, u32[]{:S(2)}, u32[]{:S(2)}) collective-permute-start(bf16[64,384]{1,0:T(8,128)(2,1)S(1)} %get-tuple-element.82), channel_id=1, source_target_pairs={{0,4},{4,0},{1,5},{5,1},{2,6},{6,2},{3,7},{7,3},{8,12},{12,8},{9,1... | collective-permute-start | bytes 147464 | tf_op jit(solution)/shard_map/ppermute | solution.py:17
  (8 other events, 48.8 us)

commit v12 on v10

--- a/solution.py
+++ b/solution.py
@@ -618,7 +618,7 @@
             ).astype(BF16)
 
 
-def heads_kernel(place, scale, live_ref, text_ref, q_ref, k_ref, v_ref, *refs):
+def heads_kernel(place, first, scale, live_ref, text_ref, q_ref, k_ref, v_ref, *refs):
     out_refs = refs[2:]
     live = live_ref[...] != 0
     half = q_ref.shape[2]
@@ -626,7 +626,7 @@
     for h in range(half // HDIM):
         cols = slice(h * HDIM, (h + 1) * HDIM)
         vals = slice(half + h * HDIM, half + (h + 1) * HDIM)
-        q = q_ref[place, :, cols]
+        q = q_ref[place, first * size : (first + len(out_refs)) * size, cols]
         st = lax.dot_general(q, text_ref[:, cols], NT, preferred_element_type=F32) * scale
         si = lax.dot_general(q, k_ref[place, :, cols], NT, preferred_element_type=F32) * scale
         st = jnp.where(live, st, -jnp.inf)
@@ -851,16 +851,24 @@
     )
     rows = {0: rows[0], **partners(lambda k: rows[k], "req", n_req)}
     live = lax.dynamic_slice_in_dim(prompt_token_ids, request_prompt[0, 0], 1, 0)
-    pieces = [None] * n_req
-    last = (live, live)
-    for k in range(n_req):
-        mixed = call(
-            functools.partial(heads_kernel, k, HDIM ** (-0.5)),
-            [struct((image_rows, half))] * n_seq,
+    def heads(k, first, count, last):
+        return call(
+            functools.partial(heads_kernel, k, first, HDIM ** (-0.5)),
+            [struct((image_rows, half))] * count,
             (live, rows[k], queries, image_keys, image_values, *last),
             [VMEM] * 5 + [ANY] * 2,
             name="heads",
         )
+
+    pieces = [None] * n_req
+    last = (live, live)
+    for k in range(n_req):
+        if k < n_req - 1:
+            mixed = heads(k, 0, n_seq, last)
+        else:
+            (back,) = heads(k, 1, 1, last)
+            (mine,) = heads(k, 0, 1, (back, last[1]))
+            mixed = (mine, back)
         pieces[k] = [mixed[0], swap(mixed[1], "seq", n_seq, 1)]
         last = (mixed[0], pieces[k - 1][1] if k else live)
     result = call(

time: 76.5 us -> 76.4 us (level)
  waiting for transfers between devices: 32.1 us -> 31.2 us
  Pallas kernels: 8.77 us -> 9.6 us
    ppermute x26, waiting for transfers between devices: 32.1 us -> 31.2 us  [swap(): return lax.ppermute(block, axis, [(i, i ^ step) for i in range(size)])]
    pallas_call x20 -> x21, Pallas kernels: 8.77 us -> 9.6 us  [call(): pl.pallas_call(kernel, out_shape=outs, in_specs=specs if specs is not Non...]
  transfers between devices with their start and end apart: 26 -> 26, of which waited for: 15 -> 15; matrix products, arithmetic and copies ran while one was open for 0% -> 0% of each run, Pallas kernels for 8% -> 9%
where the time goes in v12:
time: 76.4 us; the launch traced here: 76.3 us
  waiting for transfers between devices  31.2 us (41%)
  starting transfers between devices  30.6 us (40%)
  Pallas kernels  9.6 us (13%)
  local copies, waits for them, and re-layouts  3.28 us (4%)
  between operations  1.62 us (2%)
    ppermute x26, waiting for transfers between devices, swap(): return lax.ppermute(block, axis, [(i, i ^ step) for i in range(size)])  31.2 us
    ppermute x26, starting transfers between devices, swap(): return lax.ppermute(block, axis, [(i, i ^ step) for i in range(size)])  30.6 us
    pallas_call x21, Pallas kernels, call(): pl.pallas_call(kernel, out_shape=outs, in_specs=specs if specs is not Non...  9.6 us
    unnamed x28, local copies, waits for them, and re-layouts  3.11 us
  transfers between devices with their start and end apart: 26, of which 15 were waited for; matrix products, arithmetic and copies ran while one was open for 0% of the time, Pallas kernels for 9%

profile of v12, /device:TPU:0, one launch (start us, length us, event | category | flops | bytes accessed | tf_op | source)
XLA Modules:
  0.0 76.3 jit_solution(2487043737433926126)
XLA Ops:
  0.0 1.6 %copy-done.4 = bf16[256,3072]{1,0:T(8,128)(2,1)S(1)} copy-done((bf16[256,3072]{1,0:T(8,128)(2,1)S(1)}, bf16[256,3072]{1,0:T(8,128)(2,1)}, u32[]{:S(2)}) %copy-start.4) | copy-done | bytes 1572888
  4.3 1.4 %collective-permute-done.got_ref = bf16[1552,128]{1,0:T(8,128)(2,1)S(1)} collective-permute-done((bf16[1552,128]{1,0:T(8,128)(2,1)S(1)}, bf16[1552,128]{1,0:T(8,128)(2,1)S(1)}, u32[]{:S(2)}, u32[]{:S(2)}) %collective-permute-start) | collective-permute-done | bytes 397344 | tf_op jit(solution)/shard_map/ppermute | solution.py:17
  6.0 2.9 %collective-permute-start.1 = (bf16[2,192,768]{2,1,0:T(8,128)(2,1)S(1)}, bf16[2,192,768]{2,1,0:T(8,128)(2,1)S(1)}, u32[]{:S(2)}, u32[]{:S(2)}) collective-permute-start(bf16[2,192,768]{2,1,0:T(8,128)(2,1)S(1)} %get-tuple-element.48), channel_id=1, source_target_pairs={{0,2},{1,3},{2,0},{3,1},{4,6},{5,7},{6,4},{7,5},{8,10},{9,11},{10,... | collective-permute-start | bytes 1769480 | tf_op jit(solution)/shard_map/ppermute | solution.py:17
  9.0 2.6 %collective-permute-start.2 = (bf16[400,128]{1,0:T(8,128)(2,1)S(1)}, bf16[400,128]{1,0:T(8,128)(2,1)S(1)}, u32[]{:S(2)}, u32[]{:S(2)}) collective-permute-start(bf16[400,128]{1,0:T(8,128)(2,1)S(1)} %get-tuple-element.50), channel_id=1, source_target_pairs={{0,16},{8,24},{16,0},{24,8},{1,17},{9,25},{17,1},{25,9},{2,18},{10... | collective-permute-start | bytes 307208 | tf_op jit(solution)/shard_map/ppermute | solution.py:17
  11.6 1.3 %collective-permute-start.3 = (bf16[400,128]{1,0:T(8,128)(2,1)S(1)}, bf16[400,128]{1,0:T(8,128)(2,1)S(1)}, u32[]{:S(2)}, u32[]{:S(2)}) collective-permute-start(bf16[400,128]{1,0:T(8,128)(2,1)S(1)} %get-tuple-element.51), channel_id=1, source_target_pairs={{0,24},{8,16},{16,8},{24,0},{1,25},{9,17},{17,9},{25,1},{2,26},{10... | collective-permute-start | bytes 307208 | tf_op jit(solution)/shard_map/ppermute | solution.py:17
  13.8 6.2 %collective-permute-done.2.refs_0_ = bf16[400,128]{1,0:T(8,128)(2,1)S(1)} collective-permute-done((bf16[400,128]{1,0:T(8,128)(2,1)S(1)}, bf16[400,128]{1,0:T(8,128)(2,1)S(1)}, u32[]{:S(2)}, u32[]{:S(2)}) %collective-permute-start.2) | collective-permute-done | bytes 102432 | tf_op jit(solution)/shard_map/ppermute | solution.py:17
  21.0 2.1 %collective-permute-done.1.got_ref = bf16[2,192,768]{2,1,0:T(8,128)(2,1)S(1)} collective-permute-done((bf16[2,192,768]{2,1,0:T(8,128)(2,1)S(1)}, bf16[2,192,768]{2,1,0:T(8,128)(2,1)S(1)}, u32[]{:S(2)}, u32[]{:S(2)}) %collective-permute-start.1) | collective-permute-done | bytes 589856 | tf_op jit(solution)/shard_map/ppermute | solution.py:17
  23.3 2.0 %collective-permute-done.5.got_ref = bf16[400,128]{1,0:T(8,128)(2,1)S(1)} collective-permute-done((bf16[400,128]{1,0:T(8,128)(2,1)S(1)}, bf16[400,128]{1,0:T(8,128)(2,1)S(1)}, u32[]{:S(2)}, u32[]{:S(2)}) %collective-permute-start.5) | collective-permute-done | bytes 102432 | tf_op jit(solution)/shard_map/ppermute | solution.py:17
  25.5 1.6 %collective-permute-start.6 = (bf16[400,128]{1,0:T(8,128)(2,1)S(1)}, bf16[400,128]{1,0:T(8,128)(2,1)S(1)}, u32[]{:S(2)}, u32[]{:S(2)}) collective-permute-start(bf16[400,128]{1,0:T(8,128)(2,1)S(1)} %centre.1.own_ref), channel_id=1, source_target_pairs={{0,4},{4,0},{1,5},{5,1},{2,6},{6,2},{3,7},{7,3},{8,12},{12,8},{9,1... | collective-permute-start | bytes 307208 | tf_op jit(solution)/shard_map/ppermute | solution.py:17
  27.0 3.2 %collective-permute-done.6.got_ref = bf16[400,128]{1,0:T(8,128)(2,1)S(1)} collective-permute-done((bf16[400,128]{1,0:T(8,128)(2,1)S(1)}, bf16[400,128]{1,0:T(8,128)(2,1)S(1)}, u32[]{:S(2)}, u32[]{:S(2)}) %collective-permute-start.6) | collective-permute-done | bytes 102432 | tf_op jit(solution)/shard_map/ppermute | solution.py:17
  31.1 1.6 %collective-permute-start.9 = (bf16[4,64,1536]{2,1,0:T(8,128)(2,1)S(1)}, bf16[4,64,1536]{2,1,0:T(8,128)(2,1)S(1)}, u32[]{:S(2)}, u32[]{:S(2)}) collective-permute-start(bf16[4,64,1536]{2,1,0:T(8,128)(2,1)S(1)} %image_pack.1), channel_id=1, source_target_pairs={{0,4},{4,0},{1,5},{5,1},{2,6},{6,2},{3,7},{7,3},{8,12},{12,8},{9,1... | collective-permute-start | bytes 2359304 | tf_op jit(solution)/shard_map/ppermute | solution.py:17
  32.8 1.2 %project.1 = (s32[4]{0:T(128)S(1)}, f32[400,128]{1,0:T(8,128)S(1)}, bf16[400,128]{1,0:T(8,128)(2,1)S(1)}, bf16[400,128]{1,0:T(8,128)(2,1)S(1)}, bf16[400,128]{1,0:T(8,128)(2,1)S(1)}) custom-call(bf16[800,128]{1,0:T(8,128)(2,1)S(1)} %join.1.refs_0_.dep_ref, bf16[800,128]{1,0:T(8,128)(2,1)S(1)} %collective-permute-done.7.refs_1_, ...), custom_call_target="tpu_custom_call" | custom-call | tf_op jit(solution)/shard_map/project/pallas_call | solution.py:280
  33.9 1.4 %collective-permute-start.11 = (bf16[2,128,1536]{2,1,0:T(8,128)(2,1)S(1)}, bf16[2,128,1536]{2,1,0:T(8,128)(2,1)S(1)}, u32[]{:S(2)}, u32[]{:S(2)}) collective-permute-start(bf16[2,128,1536]{2,1,0:T(8,128)(2,1)S(1)} %maps_join.1.refs_0_), channel_id=1, source_target_pairs={{0,2},{1,3},{2,0},{3,1},{4,6},{5,7},{6,4},{7,5},{8,10},{9,11},{10,... | collective-permute-start | bytes 2359304 | tf_op jit(solution)/shard_map/ppermute | solution.py:17
  35.3 2.8 %collective-permute-start.13 = (bf16[400,128]{1,0:T(8,128)(2,1)S(1)}, bf16[400,128]{1,0:T(8,128)(2,1)S(1)}, u32[]{:S(2)}, u32[]{:S(2)}) collective-permute-start(bf16[400,128]{1,0:T(8,128)(2,1)S(1)} %get-tuple-element.64), channel_id=1, source_target_pairs={{0,16},{8,24},{16,0},{24,8},{1,17},{9,25},{17,1},{25,9},{2,18},{10... | collective-permute-start | bytes 307208 | tf_op jit(solution)/shard_map/ppermute | solution.py:17
  38.1 1.1 %collective-permute-start.14 = (bf16[400,128]{1,0:T(8,128)(2,1)S(1)}, bf16[400,128]{1,0:T(8,128)(2,1)S(1)}, u32[]{:S(2)}, u32[]{:S(2)}) collective-permute-start(bf16[400,128]{1,0:T(8,128)(2,1)S(1)} %get-tuple-element.65), channel_id=1, source_target_pairs={{0,24},{8,16},{16,8},{24,0},{1,25},{9,17},{17,9},{25,1},{2,26},{10... | collective-permute-start | bytes 307208 | tf_op jit(solution)/shard_map/ppermute | solution.py:17
  39.5 6.6 %collective-permute-done.13.refs_0_ = bf16[400,128]{1,0:T(8,128)(2,1)S(1)} collective-permute-done((bf16[400,128]{1,0:T(8,128)(2,1)S(1)}, bf16[400,128]{1,0:T(8,128)(2,1)S(1)}, u32[]{:S(2)}, u32[]{:S(2)}) %collective-permute-start.13) | collective-permute-done | bytes 102432 | tf_op jit(solution)/shard_map/ppermute | solution.py:17
  46.4 3.7 %collective-permute-start.16 = (bf16[64,768]{1,0:T(8,128)(2,1)S(1)}, bf16[64,768]{1,0:T(8,128)(2,1)S(1)}, u32[]{:S(2)}, u32[]{:S(2)}) collective-permute-start(bf16[64,768]{1,0:T(8,128)(2,1)S(1)} %finish.1.refs_0_), channel_id=1, source_target_pairs={{0,16},{8,24},{16,0},{24,8},{1,17},{9,25},{17,1},{25,9},{2,18},{10... | collective-permute-start | bytes 294920 | tf_op jit(solution)/shard_map/ppermute | solution.py:17
  51.4 1.8 %collective-permute-done.11.refs_1_ = bf16[2,128,1536]{2,1,0:T(8,128)(2,1)S(1)} collective-permute-done((bf16[2,128,1536]{2,1,0:T(8,128)(2,1)S(1)}, bf16[2,128,1536]{2,1,0:T(8,128)(2,1)S(1)}, u32[]{:S(2)}, u32[]{:S(2)}) %collective-permute-start.11) | collective-permute-done | bytes 786464 | tf_op jit(solution)/shard_map/ppermute | solution.py:17
  53.5 1.5 %collective-permute-start.12 = (f32[2,64,64]{2,1,0:T(8,128)S(1)}, f32[2,64,64]{2,1,0:T(8,128)S(1)}, u32[]{:S(2)}, u32[]{:S(2)}) collective-permute-start(f32[2,64,64]{2,1,0:T(8,128)S(1)} %get-tuple-element.61.low_ref), channel_id=1, source_target_pairs={{0,4},{4,0},{1,5},{5,1},{2,6},{6,2},{3,7},{7,3},{8,12},{12,8},{9,1... | collective-permute-start | bytes 98312 | tf_op jit(solution)/shard_map/ppermute | solution.py:17
  55.0 2.8 %collective-permute-done.12.other_ref = f32[2,64,64]{2,1,0:T(8,128)S(1)} collective-permute-done((f32[2,64,64]{2,1,0:T(8,128)S(1)}, f32[2,64,64]{2,1,0:T(8,128)S(1)}, u32[]{:S(2)}, u32[]{:S(2)}) %collective-permute-start.12) | collective-permute-done | bytes 32800 | tf_op jit(solution)/shard_map/ppermute | solution.py:17
  59.4 0.9 %collective-permute-start.22 = (bf16[128,768]{1,0:T(8,128)(2,1)S(1)}, bf16[128,768]{1,0:T(8,128)(2,1)S(1)}, u32[]{:S(2)}, u32[]{:S(2)}) collective-permute-start(bf16[128,768]{1,0:T(8,128)(2,1)S(1)} %get-tuple-element.75), channel_id=1, source_target_pairs={{0,2},{1,3},{2,0},{3,1},{4,6},{5,7},{6,4},{7,5},{8,10},{9,11},{10,... | collective-permute-start | bytes 589832 | tf_op jit(solution)/shard_map/ppermute | solution.py:17
  60.3 0.9 %collective-permute-start.24 = (bf16[128,768]{1,0:T(8,128)(2,1)S(1)}, bf16[128,768]{1,0:T(8,128)(2,1)S(1)}, u32[]{:S(2)}, u32[]{:S(2)}) collective-permute-start(bf16[128,768]{1,0:T(8,128)(2,1)S(1)} %get-tuple-element.78), channel_id=1, source_target_pairs={{0,3},{1,2},{2,1},{3,0},{4,7},{5,6},{6,5},{7,4},{8,11},{9,10},{10,... | collective-permute-start | bytes 589832 | tf_op jit(solution)/shard_map/ppermute | solution.py:17
  61.2 0.9 %heads.5 = (bf16[64,384]{1,0:T(8,128)(2,1)S(1)}, bf16[64,384]{1,0:T(8,128)(2,1)S(1)}) custom-call(s32[1,128]{1,0:T(1,128)S(1)} %constant_dynamic-slice_fusion.live_ref.refs_0_.refs_1_, bf16[128,768]{1,0:T(8,128)(2,1)S(1)} %get-tuple-element.67.text_ref, bf16[4,128,384]{2,1,0:T(8,128)(2,1)S(1)} %get-tuple-element.68.q_ref, ...), custom_call_target="tpu_custom_call" | custom-call | tf_op jit(solution)/shard_map/heads/pallas_call | solution.py:280
  62.2 1.6 %collective-permute-start.19 = (bf16[64,384]{1,0:T(8,128)(2,1)S(1)}, bf16[64,384]{1,0:T(8,128)(2,1)S(1)}, u32[]{:S(2)}, u32[]{:S(2)}) collective-permute-start(bf16[64,384]{1,0:T(8,128)(2,1)S(1)} %get-tuple-element.71), channel_id=1, source_target_pairs={{0,4},{4,0},{1,5},{5,1},{2,6},{6,2},{3,7},{7,3},{8,12},{12,8},{9,1... | collective-permute-start | bytes 147464 | tf_op jit(solution)/shard_map/ppermute | solution.py:17
  63.8 0.9 %heads.6 = (bf16[64,384]{1,0:T(8,128)(2,1)S(1)}, bf16[64,384]{1,0:T(8,128)(2,1)S(1)}) custom-call(s32[1,128]{1,0:T(1,128)S(1)} %constant_dynamic-slice_fusion.live_ref.refs_0_.refs_1_, bf16[128,768]{1,0:T(8,128)(2,1)S(1)} %collective-permute-done.20.text_ref, bf16[4,128,384]{2,1,0:T(8,128)(2,1)S(1)} %get-tuple-element.68.q_ref, ...), custom_call_target="tpu_custom_call" | custom-call | tf_op jit(solution)/shard_map/heads/pallas_call | solution.py:280
  65.2 1.1 %collective-permute-done.19.refs_1_ = bf16[64,384]{1,0:T(8,128)(2,1)S(1)} collective-permute-done((bf16[64,384]{1,0:T(8,128)(2,1)S(1)}, bf16[64,384]{1,0:T(8,128)(2,1)S(1)}, u32[]{:S(2)}, u32[]{:S(2)}) %collective-permute-start.19) | collective-permute-done | bytes 49184 | tf_op jit(solution)/shard_map/ppermute | solution.py:17
  67.1 0.9 %heads.7 = (bf16[64,384]{1,0:T(8,128)(2,1)S(1)}, bf16[64,384]{1,0:T(8,128)(2,1)S(1)}) custom-call(s32[1,128]{1,0:T(1,128)S(1)} %constant_dynamic-slice_fusion.live_ref.refs_0_.refs_1_, bf16[128,768]{1,0:T(8,128)(2,1)S(1)} %collective-permute-done.22.text_ref, bf16[4,128,384]{2,1,0:T(8,128)(2,1)S(1)} %get-tuple-element.68.q_ref, ...), custom_call_target="tpu_custom_call" | custom-call | tf_op jit(solution)/shard_map/heads/pallas_call | solution.py:280
  68.1 1.6 %collective-permute-start.23 = (bf16[64,384]{1,0:T(8,128)(2,1)S(1)}, bf16[64,384]{1,0:T(8,128)(2,1)S(1)}, u32[]{:S(2)}, u32[]{:S(2)}) collective-permute-start(bf16[64,384]{1,0:T(8,128)(2,1)S(1)} %get-tuple-element.77), channel_id=1, source_target_pairs={{0,4},{4,0},{1,5},{5,1},{2,6},{6,2},{3,7},{7,3},{8,12},{12,8},{9,1... | collective-permute-start | bytes 147464 | tf_op jit(solution)/shard_map/ppermute | solution.py:17
  70.5 0.9 %heads.8.refs_0_ = bf16[64,384]{1,0:T(8,128)(2,1)S(1)} custom-call(s32[1,128]{1,0:T(1,128)S(1)} %constant_dynamic-slice_fusion.live_ref.refs_0_.refs_1_, bf16[128,768]{1,0:T(8,128)(2,1)S(1)} %collective-permute-done.24.text_ref, bf16[4,128,384]{2,1,0:T(8,128)(2,1)S(1)} %get-tuple-element.68.q_ref, bf16[4,128,384]{2,1,0:T(8,128)(2,1)S(1)} %get-tuple-element.69.k_ref, ...), custom_call_target="tpu_custom_call" | custom-call | tf_op jit(solution)/shard_map/heads/pallas_call | solution.py:280
  71.3 1.6 %collective-permute-start.25 = (bf16[64,384]{1,0:T(8,128)(2,1)S(1)}, bf16[64,384]{1,0:T(8,128)(2,1)S(1)}, u32[]{:S(2)}, u32[]{:S(2)}) collective-permute-start(bf16[64,384]{1,0:T(8,128)(2,1)S(1)} %heads.8.refs_0_), channel_id=1, source_target_pairs={{0,4},{4,0},{1,5},{5,1},{2,6},{6,2},{3,7},{7,3},{8,12},{12,8},{9,1... | collective-permute-start | bytes 147464 | tf_op jit(solution)/shard_map/ppermute | solution.py:17
  72.9 0.9 %heads.9.refs_6_ = bf16[64,384]{1,0:T(8,128)(2,1)S(1)} custom-call(s32[1,128]{1,0:T(1,128)S(1)} %constant_dynamic-slice_fusion.live_ref.refs_0_.refs_1_, bf16[128,768]{1,0:T(8,128)(2,1)S(1)} %collective-permute-done.24.text_ref, bf16[4,128,384]{2,1,0:T(8,128)(2,1)S(1)} %get-tuple-element.68.q_ref, bf16[4,128,384]{2,1,0:T(8,128)(2,1)S(1)} %get-tuple-element.69.k_ref, ...), custom_call_target="tpu_custom_call" | custom-call | tf_op jit(solution)/shard_map/heads/pallas_call | solution.py:280
  73.8 1.7 %collective-permute-done.25.refs_7_ = bf16[64,384]{1,0:T(8,128)(2,1)S(1)} collective-permute-done((bf16[64,384]{1,0:T(8,128)(2,1)S(1)}, bf16[64,384]{1,0:T(8,128)(2,1)S(1)}, u32[]{:S(2)}, u32[]{:S(2)}) %collective-permute-start.25) | collective-permute-done | bytes 49184 | tf_op jit(solution)/shard_map/ppermute | solution.py:17
  (74 shorter events, 11.5 us)
Async XLA Ops:
  0.0 61.2 %copy-start = (s32[2,128]{1,0:T(2,128)S(1)}, s32[2,128]{1,0:T(2,128)}, u32[]{:S(2)}) copy-start(s32[2,128]{1,0:T(2,128)} %param.16) | copy-start | bytes 3076
  3.1 17.2 %copy-start.12 = (bf16[192]{0:T(256)(128)(2,1)S(1)}, bf16[192]{0:T(256)(128)(2,1)}, u32[]{:S(2)}) copy-start(bf16[192]{0:T(256)(128)(2,1)} %b_ref.1) | copy-start | bytes 1156
  3.1 17.3 %copy-start.9 = (bf16[1,192]{1,0:T(2,128)(2,1)S(1)}, bf16[1,192]{1,0:T(2,128)(2,1)}, u32[]{:S(2)}) copy-start(bf16[1,192]{1,0:T(2,128)(2,1)} %shift_ref.3) | copy-start | bytes 1156
  3.1 17.3 %copy-start.10 = (bf16[1,192]{1,0:T(2,128)(2,1)S(1)}, bf16[1,192]{1,0:T(2,128)(2,1)}, u32[]{:S(2)}) copy-start(bf16[1,192]{1,0:T(2,128)(2,1)} %scale_ref.1) | copy-start | bytes 1156
  3.8 1.9 %collective-permute-start = (bf16[1552,128]{1,0:T(8,128)(2,1)S(1)}, bf16[1552,128]{1,0:T(8,128)(2,1)S(1)}, u32[]{:S(2)}, u32[]{:S(2)}) collective-permute-start(bf16[1552,128]{1,0:T(8,128)(2,1)S(1)} %get-tuple-element.42), channel_id=1, source_target_pairs={{0,1},{1,0},{2,3},{3,2},{4,5},{5,4},{6,7},{7,6},{8,9},{9,8},{10,11... | collective-permute-start | bytes 1191944 | tf_op jit(solution)/shard_map/ppermute | solution.py:17
  6.0 24.2 %copy-start.6 = (bf16[1,3072,64]{1,2,0:T(8,128)(2,1)S(1)}, bf16[1,3072,64]{1,2,0:T(8,128)(2,1)}, u32[]{:S(2)}) copy-start(bf16[1,3072,64]{1,2,0:T(8,128)(2,1)} %param.25) | copy-start | bytes 1179652
  6.0 24.2 %copy-start.7 = (bf16[1,64,3072]{2,1,0:T(8,128)(2,1)S(1)}, bf16[1,64,3072]{2,1,0:T(8,128)(2,1)}, u32[]{:S(2)}) copy-start(bf16[1,64,3072]{2,1,0:T(8,128)(2,1)} %param.26) | copy-start | bytes 1179652
  6.0 17.1 %collective-permute-start.1 = (bf16[2,192,768]{2,1,0:T(8,128)(2,1)S(1)}, bf16[2,192,768]{2,1,0:T(8,128)(2,1)S(1)}, u32[]{:S(2)}, u32[]{:S(2)}) collective-permute-start(bf16[2,192,768]{2,1,0:T(8,128)(2,1)S(1)} %get-tuple-element.48), channel_id=1, source_target_pairs={{0,2},{1,3},{2,0},{3,1},{4,6},{5,7},{6,4},{7,5},{8,10},{9,11},{10,... | collective-permute-start | bytes 1769480 | tf_op jit(solution)/shard_map/ppermute | solution.py:17
  9.0 11.1 %collective-permute-start.2 = (bf16[400,128]{1,0:T(8,128)(2,1)S(1)}, bf16[400,128]{1,0:T(8,128)(2,1)S(1)}, u32[]{:S(2)}, u32[]{:S(2)}) collective-permute-start(bf16[400,128]{1,0:T(8,128)(2,1)S(1)} %get-tuple-element.50), channel_id=1, source_target_pairs={{0,16},{8,24},{16,0},{24,8},{1,17},{9,25},{17,1},{25,9},{2,18},{10... | collective-permute-start | bytes 307208 | tf_op jit(solution)/shard_map/ppermute | solution.py:17
  11.6 8.5 %collective-permute-start.3 = (bf16[400,128]{1,0:T(8,128)(2,1)S(1)}, bf16[400,128]{1,0:T(8,128)(2,1)S(1)}, u32[]{:S(2)}, u32[]{:S(2)}) collective-permute-start(bf16[400,128]{1,0:T(8,128)(2,1)S(1)} %get-tuple-element.51), channel_id=1, source_target_pairs={{0,24},{8,16},{16,8},{24,0},{1,25},{9,17},{17,9},{25,1},{2,26},{10... | collective-permute-start | bytes 307208 | tf_op jit(solution)/shard_map/ppermute | solution.py:17
  12.9 7.4 %collective-permute-start.4 = (bf16[400,128]{1,0:T(8,128)(2,1)S(1)}, bf16[400,128]{1,0:T(8,128)(2,1)S(1)}, u32[]{:S(2)}, u32[]{:S(2)}) collective-permute-start(bf16[400,128]{1,0:T(8,128)(2,1)S(1)} %get-tuple-element.52), channel_id=1, source_target_pairs={{0,8},{8,0},{16,24},{24,16},{1,9},{9,1},{17,25},{25,17},{2,10},{10... | collective-permute-start | bytes 307208 | tf_op jit(solution)/shard_map/ppermute | solution.py:17
  20.5 4.7 %collective-permute-start.5 = (bf16[400,128]{1,0:T(8,128)(2,1)S(1)}, bf16[400,128]{1,0:T(8,128)(2,1)S(1)}, u32[]{:S(2)}, u32[]{:S(2)}) collective-permute-start(bf16[400,128]{1,0:T(8,128)(2,1)S(1)} %get-tuple-element.56), channel_id=1, source_target_pairs={{0,2},{1,3},{2,0},{3,1},{4,6},{5,7},{6,4},{7,5},{8,10},{9,11},{10,... | collective-permute-start | bytes 307208 | tf_op jit(solution)/shard_map/ppermute | solution.py:17
  23.2 9.6 %collective-permute-start.8 = (bf16[384,768]{1,0:T(8,128)(2,1)S(1)}, bf16[384,768]{1,0:T(8,128)(2,1)S(1)}, u32[]{:S(2)}, u32[]{:S(2)}) collective-permute-start(bf16[384,768]{1,0:T(8,128)(2,1)S(1)} %get-tuple-element.57), channel_id=1, source_target_pairs={{0,1},{1,0},{2,3},{3,2},{4,5},{5,4},{6,7},{7,6},{8,9},{9,8},{10,11... | collective-permute-start | bytes 1769480 | tf_op jit(solution)/shard_map/ppermute | solution.py:17
  25.5 4.7 %collective-permute-start.6 = (bf16[400,128]{1,0:T(8,128)(2,1)S(1)}, bf16[400,128]{1,0:T(8,128)(2,1)S(1)}, u32[]{:S(2)}, u32[]{:S(2)}) collective-permute-start(bf16[400,128]{1,0:T(8,128)(2,1)S(1)} %centre.1.own_ref), channel_id=1, source_target_pairs={{0,4},{4,0},{1,5},{5,1},{2,6},{6,2},{3,7},{7,3},{8,12},{12,8},{9,1... | collective-permute-start | bytes 307208 | tf_op jit(solution)/shard_map/ppermute | solution.py:17
  30.3 2.4 %collective-permute-start.10 = (bf16[128,1536]{1,0:T(8,128)(2,1)S(1)}, bf16[128,1536]{1,0:T(8,128)(2,1)S(1)}, u32[]{:S(2)}, u32[]{:S(2)}) collective-permute-start(bf16[128,1536]{1,0:T(8,128)(2,1)S(1)} %maps_pack.1.own_ref), channel_id=1, source_target_pairs={{0,1},{1,0},{2,3},{3,2},{4,5},{5,4},{6,7},{7,6},{8,9},{9,8},{10,11... | collective-permute-start | bytes 1179656 | tf_op jit(solution)/shard_map/ppermute | solution.py:17
  30.4 2.3 %collective-permute-start.7 = (bf16[800,128]{1,0:T(8,128)(2,1)S(1)}, bf16[800,128]{1,0:T(8,128)(2,1)S(1)}, u32[]{:S(2)}, u32[]{:S(2)}) collective-permute-start(bf16[800,128]{1,0:T(8,128)(2,1)S(1)} %join.1.refs_0_.dep_ref), channel_id=1, source_target_pairs={{0,1},{1,0},{2,3},{3,2},{4,5},{5,4},{6,7},{7,6},{8,9},{9,8},{10,11... | collective-permute-start | bytes 614408 | tf_op jit(solution)/shard_map/ppermute | solution.py:17
  31.1 20.3 %collective-permute-start.9 = (bf16[4,64,1536]{2,1,0:T(8,128)(2,1)S(1)}, bf16[4,64,1536]{2,1,0:T(8,128)(2,1)S(1)}, u32[]{:S(2)}, u32[]{:S(2)}) collective-permute-start(bf16[4,64,1536]{2,1,0:T(8,128)(2,1)S(1)} %image_pack.1), channel_id=1, source_target_pairs={{0,4},{4,0},{1,5},{5,1},{2,6},{6,2},{3,7},{7,3},{8,12},{12,8},{9,1... | collective-permute-start | bytes 2359304 | tf_op jit(solution)/shard_map/ppermute | solution.py:17
  33.9 19.3 %collective-permute-start.11 = (bf16[2,128,1536]{2,1,0:T(8,128)(2,1)S(1)}, bf16[2,128,1536]{2,1,0:T(8,128)(2,1)S(1)}, u32[]{:S(2)}, u32[]{:S(2)}) collective-permute-start(bf16[2,128,1536]{2,1,0:T(8,128)(2,1)S(1)} %maps_join.1.refs_0_), channel_id=1, source_target_pairs={{0,2},{1,3},{2,0},{3,1},{4,6},{5,7},{6,4},{7,5},{8,10},{9,11},{10,... | collective-permute-start | bytes 2359304 | tf_op jit(solution)/shard_map/ppermute | solution.py:17
  35.3 10.7 %collective-permute-start.13 = (bf16[400,128]{1,0:T(8,128)(2,1)S(1)}, bf16[400,128]{1,0:T(8,128)(2,1)S(1)}, u32[]{:S(2)}, u32[]{:S(2)}) collective-permute-start(bf16[400,128]{1,0:T(8,128)(2,1)S(1)} %get-tuple-element.64), channel_id=1, source_target_pairs={{0,16},{8,24},{16,0},{24,8},{1,17},{9,25},{17,1},{25,9},{2,18},{10... | collective-permute-start | bytes 307208 | tf_op jit(solution)/shard_map/ppermute | solution.py:17
  38.1 7.9 %collective-permute-start.14 = (bf16[400,128]{1,0:T(8,128)(2,1)S(1)}, bf16[400,128]{1,0:T(8,128)(2,1)S(1)}, u32[]{:S(2)}, u32[]{:S(2)}) collective-permute-start(bf16[400,128]{1,0:T(8,128)(2,1)S(1)} %get-tuple-element.65), channel_id=1, source_target_pairs={{0,24},{8,16},{16,8},{24,0},{1,25},{9,17},{17,9},{25,1},{2,26},{10... | collective-permute-start | bytes 307208 | tf_op jit(solution)/shard_map/ppermute | solution.py:17
  39.2 6.9 %collective-permute-start.15 = (bf16[400,128]{1,0:T(8,128)(2,1)S(1)}, bf16[400,128]{1,0:T(8,128)(2,1)S(1)}, u32[]{:S(2)}, u32[]{:S(2)}) collective-permute-start(bf16[400,128]{1,0:T(8,128)(2,1)S(1)} %get-tuple-element.66), channel_id=1, source_target_pairs={{0,8},{8,0},{16,24},{24,16},{1,9},{9,1},{17,25},{25,17},{2,10},{10... | collective-permute-start | bytes 307208 | tf_op jit(solution)/shard_map/ppermute | solution.py:17
  46.4 11.7 %collective-permute-start.16 = (bf16[64,768]{1,0:T(8,128)(2,1)S(1)}, bf16[64,768]{1,0:T(8,128)(2,1)S(1)}, u32[]{:S(2)}, u32[]{:S(2)}) collective-permute-start(bf16[64,768]{1,0:T(8,128)(2,1)S(1)} %finish.1.refs_0_), channel_id=1, source_target_pairs={{0,16},{8,24},{16,0},{24,8},{1,17},{9,25},{17,1},{25,9},{2,18},{10... | collective-permute-start | bytes 294920 | tf_op jit(solution)/shard_map/ppermute | solution.py:17
  50.1 8.0 %collective-permute-start.17 = (bf16[64,768]{1,0:T(8,128)(2,1)S(1)}, bf16[64,768]{1,0:T(8,128)(2,1)S(1)}, u32[]{:S(2)}, u32[]{:S(2)}) collective-permute-start(bf16[64,768]{1,0:T(8,128)(2,1)S(1)} %finish.1.refs_0_), channel_id=1, source_target_pairs={{0,24},{8,16},{16,8},{24,0},{1,25},{9,17},{17,9},{25,1},{2,26},{10... | collective-permute-start | bytes 294920 | tf_op jit(solution)/shard_map/ppermute | solution.py:17
  50.5 8.0 %collective-permute-start.18 = (bf16[64,768]{1,0:T(8,128)(2,1)S(1)}, bf16[64,768]{1,0:T(8,128)(2,1)S(1)}, u32[]{:S(2)}, u32[]{:S(2)}) collective-permute-start(bf16[64,768]{1,0:T(8,128)(2,1)S(1)} %finish.1.refs_0_), channel_id=1, source_target_pairs={{0,8},{8,0},{16,24},{24,16},{1,9},{9,1},{17,25},{25,17},{2,10},{10... | collective-permute-start | bytes 294920 | tf_op jit(solution)/shard_map/ppermute | solution.py:17
  53.5 4.3 %collective-permute-start.12 = (f32[2,64,64]{2,1,0:T(8,128)S(1)}, f32[2,64,64]{2,1,0:T(8,128)S(1)}, u32[]{:S(2)}, u32[]{:S(2)}) collective-permute-start(f32[2,64,64]{2,1,0:T(8,128)S(1)} %get-tuple-element.61.low_ref), channel_id=1, source_target_pairs={{0,4},{4,0},{1,5},{5,1},{2,6},{6,2},{3,7},{7,3},{8,12},{12,8},{9,1... | collective-permute-start | bytes 98312 | tf_op jit(solution)/shard_map/ppermute | solution.py:17
  59.3 4.5 %collective-permute-start.20 = (bf16[128,768]{1,0:T(8,128)(2,1)S(1)}, bf16[128,768]{1,0:T(8,128)(2,1)S(1)}, u32[]{:S(2)}, u32[]{:S(2)}) collective-permute-start(bf16[128,768]{1,0:T(8,128)(2,1)S(1)} %get-tuple-element.72), channel_id=1, source_target_pairs={{0,1},{1,0},{2,3},{3,2},{4,5},{5,4},{6,7},{7,6},{8,9},{9,8},{10,11... | collective-permute-start | bytes 589832 | tf_op jit(solution)/shard_map/ppermute | solution.py:17
  59.4 7.8 %collective-permute-start.22 = (bf16[128,768]{1,0:T(8,128)(2,1)S(1)}, bf16[128,768]{1,0:T(8,128)(2,1)S(1)}, u32[]{:S(2)}, u32[]{:S(2)}) collective-permute-start(bf16[128,768]{1,0:T(8,128)(2,1)S(1)} %get-tuple-element.75), channel_id=1, source_target_pairs={{0,2},{1,3},{2,0},{3,1},{4,6},{5,7},{6,4},{7,5},{8,10},{9,11},{10,... | collective-permute-start | bytes 589832 | tf_op jit(solution)/shard_map/ppermute | solution.py:17
  60.3 10.2 %collective-permute-start.24 = (bf16[128,768]{1,0:T(8,128)(2,1)S(1)}, bf16[128,768]{1,0:T(8,128)(2,1)S(1)}, u32[]{:S(2)}, u32[]{:S(2)}) collective-permute-start(bf16[128,768]{1,0:T(8,128)(2,1)S(1)} %get-tuple-element.78), channel_id=1, source_target_pairs={{0,3},{1,2},{2,1},{3,0},{4,7},{5,6},{6,5},{7,4},{8,11},{9,10},{10,... | collective-permute-start | bytes 589832 | tf_op jit(solution)/shard_map/ppermute | solution.py:17
  62.2 4.2 %collective-permute-start.19 = (bf16[64,384]{1,0:T(8,128)(2,1)S(1)}, bf16[64,384]{1,0:T(8,128)(2,1)S(1)}, u32[]{:S(2)}, u32[]{:S(2)}) collective-permute-start(bf16[64,384]{1,0:T(8,128)(2,1)S(1)} %get-tuple-element.71), channel_id=1, source_target_pairs={{0,4},{4,0},{1,5},{5,1},{2,6},{6,2},{3,7},{7,3},{8,12},{12,8},{9,1... | collective-permute-start | bytes 147464 | tf_op jit(solution)/shard_map/ppermute | solution.py:17
  64.7 5.8 %collective-permute-start.21 = (bf16[64,384]{1,0:T(8,128)(2,1)S(1)}, bf16[64,384]{1,0:T(8,128)(2,1)S(1)}, u32[]{:S(2)}, u32[]{:S(2)}) collective-permute-start(bf16[64,384]{1,0:T(8,128)(2,1)S(1)} %get-tuple-element.74), channel_id=1, source_target_pairs={{0,4},{4,0},{1,5},{5,1},{2,6},{6,2},{3,7},{7,3},{8,12},{12,8},{9,1... | collective-permute-start | bytes 147464 | tf_op jit(solution)/shard_map/ppermute | solution.py:17
  68.1 5.7 %collective-permute-start.23 = (bf16[64,384]{1,0:T(8,128)(2,1)S(1)}, bf16[64,384]{1,0:T(8,128)(2,1)S(1)}, u32[]{:S(2)}, u32[]{:S(2)}) collective-permute-start(bf16[64,384]{1,0:T(8,128)(2,1)S(1)} %get-tuple-element.77), channel_id=1, source_target_pairs={{0,4},{4,0},{1,5},{5,1},{2,6},{6,2},{3,7},{7,3},{8,12},{12,8},{9,1... | collective-permute-start | bytes 147464 | tf_op jit(solution)/shard_map/ppermute | solution.py:17
  71.3 4.2 %collective-permute-start.25 = (bf16[64,384]{1,0:T(8,128)(2,1)S(1)}, bf16[64,384]{1,0:T(8,128)(2,1)S(1)}, u32[]{:S(2)}, u32[]{:S(2)}) collective-permute-start(bf16[64,384]{1,0:T(8,128)(2,1)S(1)} %heads.8.refs_0_), channel_id=1, source_target_pairs={{0,4},{4,0},{1,5},{5,1},{2,6},{6,2},{3,7},{7,3},{8,12},{12,8},{9,1... | collective-permute-start | bytes 147464 | tf_op jit(solution)/shard_map/ppermute | solution.py:17
  (8 other events, 48.8 us)

commit v13 on v12

--- a/solution.py
+++ b/solution.py
@@ -620,28 +620,28 @@
 
 def heads_kernel(place, first, scale, live_ref, text_ref, q_ref, k_ref, v_ref, *refs):
     out_refs = refs[2:]
-    live = live_ref[...] != 0
     half = q_ref.shape[2]
     size = out_refs[0].shape[0]
-    for h in range(half // HDIM):
-        cols = slice(h * HDIM, (h + 1) * HDIM)
-        vals = slice(half + h * HDIM, half + (h + 1) * HDIM)
+    heads = [slice(h * HDIM, (h + 1) * HDIM) for h in range(half // HDIM)]
+    live = live_ref[...]
+    live = jnp.concatenate([live, jnp.ones((1, k_ref.shape[1]), live.dtype)], axis=1) != 0
+    scores = []
+    for cols in heads:
         q = q_ref[place, first * size : (first + len(out_refs)) * size, cols]
-        st = lax.dot_general(q, text_ref[:, cols], NT, preferred_element_type=F32) * scale
-        si = lax.dot_general(q, k_ref[place, :, cols], NT, preferred_element_type=F32) * scale
-        st = jnp.where(live, st, -jnp.inf)
-        top = jnp.maximum(
-            jnp.max(st, axis=1, keepdims=True), jnp.max(si, axis=1, keepdims=True)
-        )
-        wt = jnp.exp(st - top)
-        wi = jnp.exp(si - top)
-        total = jnp.sum(wt, axis=1, keepdims=True) + jnp.sum(wi, axis=1, keepdims=True)
-        mixed = jnp.dot(
-            wt.astype(BF16), text_ref[:, vals], preferred_element_type=F32
-        ) + jnp.dot(wi.astype(BF16), v_ref[place, :, cols], preferred_element_type=F32)
-        mixed = (mixed / total).astype(BF16)
+        keys = jnp.concatenate([text_ref[:, cols], k_ref[place, :, cols]], axis=0)
+        score = lax.dot_general(q, keys, NT, preferred_element_type=F32) * scale
+        scores.append(jnp.where(live, score, -jnp.inf))
+    weights = [jnp.exp(x - jnp.max(x, axis=1, keepdims=True)) for x in scores]
+    totals = [jnp.sum(w, axis=1, keepdims=True) for w in weights]
+    mixed = []
+    for cols, w in zip(heads, weights):
+        vals = slice(half + cols.start, half + cols.stop)
+        values = jnp.concatenate([text_ref[:, vals], v_ref[place, :, cols]], axis=0)
+        mixed.append(jnp.dot(w.astype(BF16), values, preferred_element_type=F32))
+    for cols, m, total in zip(heads, mixed, totals):
+        rows = (m / total).astype(BF16)
         for i, out_ref in enumerate(out_refs):
-            out_ref[:, cols] = mixed[i * size : (i + 1) * size]
+            out_ref[:, cols] = rows[i * size : (i + 1) * size]
 
 
 def assemble_kernel(n_req, n_seq, *refs):
@@ -834,18 +834,19 @@
         [SMEM] + [VMEM] * 4,
         name="lowrank",
     )
+    low_other = swap(low, "seq", n_seq, 1)
     arranged = struct((n_req, n_seq * image_rows, half))
     queries, image_keys, image_values = call(
         functools.partial(arrange_kernel, n_req, part, inner),
         (arranged, arranged, arranged),
-        (low, swap(low, "seq", n_seq, 1), chosen_maps, qk, base, *image_got),
+        (low, low_other, chosen_maps, qk, base, *image_got),
         name="arrange",
     )
     parts = partners(lambda k: text, "enc", n_enc)
     rows = call(
         functools.partial(choose_kernel, n_seq, n_enc),
         [struct((tokens, 2 * half)) for _ in range(n_req)],
-        (ids, image_values, text, *parts.values()),
+        (ids, low_other, text, *parts.values()),
         [SMEM, ANY] + [VMEM] * n_enc,
         name="choose",
     )

time: 76.4 us -> 76.7 us (level)
  waiting for transfers between devices: 31.2 us -> 33.1 us
  Pallas kernels: 9.6 us -> 7.96 us
    ppermute x26, waiting for transfers between devices: 31.2 us -> 33.1 us  [swap(): return lax.ppermute(block, axis, [(i, i ^ step) for i in range(size)])]
    pallas_call x21, Pallas kernels: 9.6 us -> 7.96 us  [call(): pl.pallas_call(kernel, out_shape=outs, in_specs=specs if specs is not Non...]
  transfers between devices with their start and end apart: 26 -> 26, of which waited for: 15 -> 15; matrix products, arithmetic and copies ran while one was open for 0% -> 0% of each run, Pallas kernels for 9% -> 6%
where the time goes in v13:
time: 76.7 us; the launch traced here: 76.5 us
  waiting for transfers between devices  33.1 us (43%)
  starting transfers between devices  30.5 us (40%)
  Pallas kernels  7.96 us (10%)
  local copies, waits for them, and re-layouts  3.28 us (4%)
  between operations  1.6 us (2%)
    ppermute x26, waiting for transfers between devices, swap(): return lax.ppermute(block, axis, [(i, i ^ step) for i in range(size)])  33.1 us
    ppermute x26, starting transfers between devices, swap(): return lax.ppermute(block, axis, [(i, i ^ step) for i in range(size)])  30.5 us
    pallas_call x21, Pallas kernels, call(): pl.pallas_call(kernel, out_shape=outs, in_specs=specs if specs is not Non...  7.96 us
    unnamed x28, local copies, waits for them, and re-layouts  3.11 us
  transfers between devices with their start and end apart: 26, of which 15 were waited for; matrix products, arithmetic and copies ran while one was open for 0% of the time, Pallas kernels for 6%

profile of v13, /device:TPU:0, one launch (start us, length us, event | category | flops | bytes accessed | tf_op | source)
XLA Modules:
  0.0 76.5 jit_solution(9289537160166294889)
XLA Ops:
  0.0 1.6 %copy-done.4 = bf16[256,3072]{1,0:T(8,128)(2,1)S(1)} copy-done((bf16[256,3072]{1,0:T(8,128)(2,1)S(1)}, bf16[256,3072]{1,0:T(8,128)(2,1)}, u32[]{:S(2)}) %copy-start.4) | copy-done | bytes 1572888
  1.6 0.8 %copy-done.8 = bf16[1,128,256]{2,1,0:T(8,128)(2,1)S(1)} copy-done((bf16[1,128,256]{2,1,0:T(8,128)(2,1)S(1)}, bf16[1,128,256]{2,1,0:T(8,128)(2,1)}, u32[]{:S(2)}) %copy-start.8) | copy-done | bytes 65560
  4.3 1.4 %collective-permute-done.got_ref = bf16[1552,128]{1,0:T(8,128)(2,1)S(1)} collective-permute-done((bf16[1552,128]{1,0:T(8,128)(2,1)S(1)}, bf16[1552,128]{1,0:T(8,128)(2,1)S(1)}, u32[]{:S(2)}, u32[]{:S(2)}) %collective-permute-start) | collective-permute-done | bytes 397344 | tf_op jit(solution)/shard_map/ppermute | solution.py:17
  6.0 2.9 %collective-permute-start.1 = (bf16[2,192,768]{2,1,0:T(8,128)(2,1)S(1)}, bf16[2,192,768]{2,1,0:T(8,128)(2,1)S(1)}, u32[]{:S(2)}, u32[]{:S(2)}) collective-permute-start(bf16[2,192,768]{2,1,0:T(8,128)(2,1)S(1)} %get-tuple-element.48), channel_id=1, source_target_pairs={{0,2},{1,3},{2,0},{3,1},{4,6},{5,7},{6,4},{7,5},{8,10},{9,11},{10,... | collective-permute-start | bytes 1769480 | tf_op jit(solution)/shard_map/ppermute | solution.py:17
  9.0 2.6 %collective-permute-start.2 = (bf16[400,128]{1,0:T(8,128)(2,1)S(1)}, bf16[400,128]{1,0:T(8,128)(2,1)S(1)}, u32[]{:S(2)}, u32[]{:S(2)}) collective-permute-start(bf16[400,128]{1,0:T(8,128)(2,1)S(1)} %get-tuple-element.50), channel_id=1, source_target_pairs={{0,16},{8,24},{16,0},{24,8},{1,17},{9,25},{17,1},{25,9},{2,18},{10... | collective-permute-start | bytes 307208 | tf_op jit(solution)/shard_map/ppermute | solution.py:17
  11.6 1.3 %collective-permute-start.3 = (bf16[400,128]{1,0:T(8,128)(2,1)S(1)}, bf16[400,128]{1,0:T(8,128)(2,1)S(1)}, u32[]{:S(2)}, u32[]{:S(2)}) collective-permute-start(bf16[400,128]{1,0:T(8,128)(2,1)S(1)} %get-tuple-element.51), channel_id=1, source_target_pairs={{0,24},{8,16},{16,8},{24,0},{1,25},{9,17},{17,9},{25,1},{2,26},{10... | collective-permute-start | bytes 307208 | tf_op jit(solution)/shard_map/ppermute | solution.py:17
  13.8 6.2 %collective-permute-done.2.refs_0_ = bf16[400,128]{1,0:T(8,128)(2,1)S(1)} collective-permute-done((bf16[400,128]{1,0:T(8,128)(2,1)S(1)}, bf16[400,128]{1,0:T(8,128)(2,1)S(1)}, u32[]{:S(2)}, u32[]{:S(2)}) %collective-permute-start.2) | collective-permute-done | bytes 102432 | tf_op jit(solution)/shard_map/ppermute | solution.py:17
  21.0 2.1 %collective-permute-done.1.got_ref = bf16[2,192,768]{2,1,0:T(8,128)(2,1)S(1)} collective-permute-done((bf16[2,192,768]{2,1,0:T(8,128)(2,1)S(1)}, bf16[2,192,768]{2,1,0:T(8,128)(2,1)S(1)}, u32[]{:S(2)}, u32[]{:S(2)}) %collective-permute-start.1) | collective-permute-done | bytes 589856 | tf_op jit(solution)/shard_map/ppermute | solution.py:17
  23.3 2.0 %collective-permute-done.5.got_ref = bf16[400,128]{1,0:T(8,128)(2,1)S(1)} collective-permute-done((bf16[400,128]{1,0:T(8,128)(2,1)S(1)}, bf16[400,128]{1,0:T(8,128)(2,1)S(1)}, u32[]{:S(2)}, u32[]{:S(2)}) %collective-permute-start.5) | collective-permute-done | bytes 102432 | tf_op jit(solution)/shard_map/ppermute | solution.py:17
  25.5 1.6 %collective-permute-start.6 = (bf16[400,128]{1,0:T(8,128)(2,1)S(1)}, bf16[400,128]{1,0:T(8,128)(2,1)S(1)}, u32[]{:S(2)}, u32[]{:S(2)}) collective-permute-start(bf16[400,128]{1,0:T(8,128)(2,1)S(1)} %centre.1.own_ref), channel_id=1, source_target_pairs={{0,4},{4,0},{1,5},{5,1},{2,6},{6,2},{3,7},{7,3},{8,12},{12,8},{9,1... | collective-permute-start | bytes 307208 | tf_op jit(solution)/shard_map/ppermute | solution.py:17
  27.0 3.2 %collective-permute-done.6.got_ref = bf16[400,128]{1,0:T(8,128)(2,1)S(1)} collective-permute-done((bf16[400,128]{1,0:T(8,128)(2,1)S(1)}, bf16[400,128]{1,0:T(8,128)(2,1)S(1)}, u32[]{:S(2)}, u32[]{:S(2)}) %collective-permute-start.6) | collective-permute-done | bytes 102432 | tf_op jit(solution)/shard_map/ppermute | solution.py:17
  31.1 1.6 %collective-permute-start.9 = (bf16[4,64,1536]{2,1,0:T(8,128)(2,1)S(1)}, bf16[4,64,1536]{2,1,0:T(8,128)(2,1)S(1)}, u32[]{:S(2)}, u32[]{:S(2)}) collective-permute-start(bf16[4,64,1536]{2,1,0:T(8,128)(2,1)S(1)} %image_pack.1), channel_id=1, source_target_pairs={{0,4},{4,0},{1,5},{5,1},{2,6},{6,2},{3,7},{7,3},{8,12},{12,8},{9,1... | collective-permute-start | bytes 2359304 | tf_op jit(solution)/shard_map/ppermute | solution.py:17
  32.8 1.2 %project.1 = (s32[4]{0:T(128)S(1)}, f32[400,128]{1,0:T(8,128)S(1)}, bf16[400,128]{1,0:T(8,128)(2,1)S(1)}, bf16[400,128]{1,0:T(8,128)(2,1)S(1)}, bf16[400,128]{1,0:T(8,128)(2,1)S(1)}) custom-call(bf16[800,128]{1,0:T(8,128)(2,1)S(1)} %join.1.refs_0_.dep_ref, bf16[800,128]{1,0:T(8,128)(2,1)S(1)} %collective-permute-done.7.refs_1_, ...), custom_call_target="tpu_custom_call" | custom-call | tf_op jit(solution)/shard_map/project/pallas_call | solution.py:280
  33.9 1.4 %collective-permute-start.11 = (bf16[2,128,1536]{2,1,0:T(8,128)(2,1)S(1)}, bf16[2,128,1536]{2,1,0:T(8,128)(2,1)S(1)}, u32[]{:S(2)}, u32[]{:S(2)}) collective-permute-start(bf16[2,128,1536]{2,1,0:T(8,128)(2,1)S(1)} %maps_join.1.refs_0_), channel_id=1, source_target_pairs={{0,2},{1,3},{2,0},{3,1},{4,6},{5,7},{6,4},{7,5},{8,10},{9,11},{10,... | collective-permute-start | bytes 2359304 | tf_op jit(solution)/shard_map/ppermute | solution.py:17
  35.3 2.8 %collective-permute-start.13 = (bf16[400,128]{1,0:T(8,128)(2,1)S(1)}, bf16[400,128]{1,0:T(8,128)(2,1)S(1)}, u32[]{:S(2)}, u32[]{:S(2)}) collective-permute-start(bf16[400,128]{1,0:T(8,128)(2,1)S(1)} %get-tuple-element.62), channel_id=1, source_target_pairs={{0,16},{8,24},{16,0},{24,8},{1,17},{9,25},{17,1},{25,9},{2,18},{10... | collective-permute-start | bytes 307208 | tf_op jit(solution)/shard_map/ppermute | solution.py:17
  38.1 1.1 %collective-permute-start.14 = (bf16[400,128]{1,0:T(8,128)(2,1)S(1)}, bf16[400,128]{1,0:T(8,128)(2,1)S(1)}, u32[]{:S(2)}, u32[]{:S(2)}) collective-permute-start(bf16[400,128]{1,0:T(8,128)(2,1)S(1)} %get-tuple-element.63), channel_id=1, source_target_pairs={{0,24},{8,16},{16,8},{24,0},{1,25},{9,17},{17,9},{25,1},{2,26},{10... | collective-permute-start | bytes 307208 | tf_op jit(solution)/shard_map/ppermute | solution.py:17
  39.5 6.6 %collective-permute-done.13.refs_0_ = bf16[400,128]{1,0:T(8,128)(2,1)S(1)} collective-permute-done((bf16[400,128]{1,0:T(8,128)(2,1)S(1)}, bf16[400,128]{1,0:T(8,128)(2,1)S(1)}, u32[]{:S(2)}, u32[]{:S(2)}) %collective-permute-start.13) | collective-permute-done | bytes 102432 | tf_op jit(solution)/shard_map/ppermute | solution.py:17
  46.4 3.7 %collective-permute-start.16 = (bf16[64,768]{1,0:T(8,128)(2,1)S(1)}, bf16[64,768]{1,0:T(8,128)(2,1)S(1)}, u32[]{:S(2)}, u32[]{:S(2)}) collective-permute-start(bf16[64,768]{1,0:T(8,128)(2,1)S(1)} %finish.1.refs_0_), channel_id=1, source_target_pairs={{0,16},{8,24},{16,0},{24,8},{1,17},{9,25},{17,1},{25,9},{2,18},{10... | collective-permute-start | bytes 294920 | tf_op jit(solution)/shard_map/ppermute | solution.py:17
  51.4 1.8 %collective-permute-done.11.refs_1_ = bf16[2,128,1536]{2,1,0:T(8,128)(2,1)S(1)} collective-permute-done((bf16[2,128,1536]{2,1,0:T(8,128)(2,1)S(1)}, bf16[2,128,1536]{2,1,0:T(8,128)(2,1)S(1)}, u32[]{:S(2)}, u32[]{:S(2)}) %collective-permute-start.11) | collective-permute-done | bytes 786464 | tf_op jit(solution)/shard_map/ppermute | solution.py:17
  53.5 1.5 %collective-permute-start.12 = (f32[2,64,64]{2,1,0:T(8,128)S(1)}, f32[2,64,64]{2,1,0:T(8,128)S(1)}, u32[]{:S(2)}, u32[]{:S(2)}) collective-permute-start(f32[2,64,64]{2,1,0:T(8,128)S(1)} %get-tuple-element.61.low_ref), channel_id=1, source_target_pairs={{0,4},{4,0},{1,5},{5,1},{2,6},{6,2},{3,7},{7,3},{8,12},{12,8},{9,1... | collective-permute-start | bytes 98312 | tf_op jit(solution)/shard_map/ppermute | solution.py:17
  55.0 2.5 %collective-permute-done.16.refs_1_ = bf16[64,768]{1,0:T(8,128)(2,1)S(1)} collective-permute-done((bf16[64,768]{1,0:T(8,128)(2,1)S(1)}, bf16[64,768]{1,0:T(8,128)(2,1)S(1)}, u32[]{:S(2)}, u32[]{:S(2)}) %collective-permute-start.16) | collective-permute-done | bytes 98336 | tf_op jit(solution)/shard_map/ppermute | solution.py:17
  57.5 1.1 %collective-permute-done.18.refs_3_ = bf16[64,768]{1,0:T(8,128)(2,1)S(1)} collective-permute-done((bf16[64,768]{1,0:T(8,128)(2,1)S(1)}, bf16[64,768]{1,0:T(8,128)(2,1)S(1)}, u32[]{:S(2)}, u32[]{:S(2)}) %collective-permute-start.18) | collective-permute-done | bytes 98336 | tf_op jit(solution)/shard_map/ppermute | solution.py:17
  58.5 1.4 %choose.1 = (bf16[128,768]{1,0:T(8,128)(2,1)S(1)}, bf16[128,768]{1,0:T(8,128)(2,1)}, bf16[128,768]{1,0:T(8,128)(2,1)S(1)}, bf16[128,768]{1,0:T(8,128)(2,1)S(1)}) custom-call(s32[4]{0:T(128)S(1)} %get-tuple-element.58.chosen_ref, f32[2,64,64]{2,1,0:T(8,128)S(1)} %collective-permute-done.12.dep_ref.other_ref, bf16[64,768]{1,0:T(8,128)(2,1)S(1)} %finish.1.refs_0_, ...), custom_call_target="tpu_custom_call" | custom-call | tf_op jit(solution)/shard_map/choose/pallas_call | solution.py:280
  60.5 1.3 %collective-permute-start.24 = (bf16[128,768]{1,0:T(8,128)(2,1)S(1)}, bf16[128,768]{1,0:T(8,128)(2,1)S(1)}, u32[]{:S(2)}, u32[]{:S(2)}) collective-permute-start(bf16[128,768]{1,0:T(8,128)(2,1)S(1)} %get-tuple-element.78), channel_id=1, source_target_pairs={{0,3},{1,2},{2,1},{3,0},{4,7},{5,6},{6,5},{7,4},{8,11},{9,10},{10,... | collective-permute-start | bytes 589832 | tf_op jit(solution)/shard_map/ppermute | solution.py:17
  62.6 1.6 %collective-permute-start.19 = (bf16[64,384]{1,0:T(8,128)(2,1)S(1)}, bf16[64,384]{1,0:T(8,128)(2,1)S(1)}, u32[]{:S(2)}, u32[]{:S(2)}) collective-permute-start(bf16[64,384]{1,0:T(8,128)(2,1)S(1)} %get-tuple-element.71), channel_id=1, source_target_pairs={{0,4},{4,0},{1,5},{5,1},{2,6},{6,2},{3,7},{7,3},{8,12},{12,8},{9,1... | collective-permute-start | bytes 147464 | tf_op jit(solution)/shard_map/ppermute | solution.py:17
  65.2 1.5 %collective-permute-done.19.refs_1_ = bf16[64,384]{1,0:T(8,128)(2,1)S(1)} collective-permute-done((bf16[64,384]{1,0:T(8,128)(2,1)S(1)}, bf16[64,384]{1,0:T(8,128)(2,1)S(1)}, u32[]{:S(2)}, u32[]{:S(2)}) %collective-permute-start.19) | collective-permute-done | bytes 49184 | tf_op jit(solution)/shard_map/ppermute | solution.py:17
  66.7 1.0 %collective-permute-done.22.text_ref = bf16[128,768]{1,0:T(8,128)(2,1)S(1)} collective-permute-done((bf16[128,768]{1,0:T(8,128)(2,1)S(1)}, bf16[128,768]{1,0:T(8,128)(2,1)S(1)}, u32[]{:S(2)}, u32[]{:S(2)}) %collective-permute-start.22) | collective-permute-done | bytes 196640 | tf_op jit(solution)/shard_map/ppermute | solution.py:17
  68.1 1.6 %collective-permute-start.23 = (bf16[64,384]{1,0:T(8,128)(2,1)S(1)}, bf16[64,384]{1,0:T(8,128)(2,1)S(1)}, u32[]{:S(2)}, u32[]{:S(2)}) collective-permute-start(bf16[64,384]{1,0:T(8,128)(2,1)S(1)} %get-tuple-element.77), channel_id=1, source_target_pairs={{0,4},{4,0},{1,5},{5,1},{2,6},{6,2},{3,7},{7,3},{8,12},{12,8},{9,1... | collective-permute-start | bytes 147464 | tf_op jit(solution)/shard_map/ppermute | solution.py:17
  69.7 1.4 %collective-permute-done.24.text_ref = bf16[128,768]{1,0:T(8,128)(2,1)S(1)} collective-permute-done((bf16[128,768]{1,0:T(8,128)(2,1)S(1)}, bf16[128,768]{1,0:T(8,128)(2,1)S(1)}, u32[]{:S(2)}, u32[]{:S(2)}) %collective-permute-start.24) | collective-permute-done | bytes 196640 | tf_op jit(solution)/shard_map/ppermute | solution.py:17
  71.5 1.6 %collective-permute-start.25 = (bf16[64,384]{1,0:T(8,128)(2,1)S(1)}, bf16[64,384]{1,0:T(8,128)(2,1)S(1)}, u32[]{:S(2)}, u32[]{:S(2)}) collective-permute-start(bf16[64,384]{1,0:T(8,128)(2,1)S(1)} %heads.8.refs_0_), channel_id=1, source_target_pairs={{0,4},{4,0},{1,5},{5,1},{2,6},{6,2},{3,7},{7,3},{8,12},{12,8},{9,1... | collective-permute-start | bytes 147464 | tf_op jit(solution)/shard_map/ppermute | solution.py:17
  73.6 2.1 %collective-permute-done.25.refs_7_ = bf16[64,384]{1,0:T(8,128)(2,1)S(1)} collective-permute-done((bf16[64,384]{1,0:T(8,128)(2,1)S(1)}, bf16[64,384]{1,0:T(8,128)(2,1)S(1)}, u32[]{:S(2)}, u32[]{:S(2)}) %collective-permute-start.25) | collective-permute-done | bytes 49184 | tf_op jit(solution)/shard_map/ppermute | solution.py:17
  75.7 0.8 %assemble.1 = bf16[64,3072]{1,0:T(8,128)(2,1)} custom-call(bf16[64,384]{1,0:T(8,128)(2,1)S(1)} %get-tuple-element.70.refs_0_, bf16[64,384]{1,0:T(8,128)(2,1)S(1)} %collective-permute-done.19.refs_1_, bf16[64,384]{1,0:T(8,128)(2,1)S(1)} %get-tuple-element.73.refs_0_.refs_2_, bf16[64,384]{1,0:T(8,128)(2,1)S(1)} %collective-permute-done.21.refs_1_.refs_3_, ...), custom_call_target="tpu_custom_call" | custom-call | tf_op jit(solution)/shard_map/assemble/pallas_call | solution.py:280
  (74 shorter events, 9.7 us)
Async XLA Ops:
  0.0 61.8 %copy-start = (s32[2,128]{1,0:T(2,128)S(1)}, s32[2,128]{1,0:T(2,128)}, u32[]{:S(2)}) copy-start(s32[2,128]{1,0:T(2,128)} %param.16) | copy-start | bytes 3076
  3.1 17.2 %copy-start.12 = (bf16[192]{0:T(256)(128)(2,1)S(1)}, bf16[192]{0:T(256)(128)(2,1)}, u32[]{:S(2)}) copy-start(bf16[192]{0:T(256)(128)(2,1)} %b_ref.1) | copy-start | bytes 1156
  3.1 17.3 %copy-start.9 = (bf16[1,192]{1,0:T(2,128)(2,1)S(1)}, bf16[1,192]{1,0:T(2,128)(2,1)}, u32[]{:S(2)}) copy-start(bf16[1,192]{1,0:T(2,128)(2,1)} %shift_ref.3) | copy-start | bytes 1156
  3.1 17.3 %copy-start.10 = (bf16[1,192]{1,0:T(2,128)(2,1)S(1)}, bf16[1,192]{1,0:T(2,128)(2,1)}, u32[]{:S(2)}) copy-start(bf16[1,192]{1,0:T(2,128)(2,1)} %scale_ref.1) | copy-start | bytes 1156
  3.8 1.9 %collective-permute-start = (bf16[1552,128]{1,0:T(8,128)(2,1)S(1)}, bf16[1552,128]{1,0:T(8,128)(2,1)S(1)}, u32[]{:S(2)}, u32[]{:S(2)}) collective-permute-start(bf16[1552,128]{1,0:T(8,128)(2,1)S(1)} %get-tuple-element.42), channel_id=1, source_target_pairs={{0,1},{1,0},{2,3},{3,2},{4,5},{5,4},{6,7},{7,6},{8,9},{9,8},{10,11... | collective-permute-start | bytes 1191944 | tf_op jit(solution)/shard_map/ppermute | solution.py:17
  6.0 24.2 %copy-start.6 = (bf16[1,3072,64]{1,2,0:T(8,128)(2,1)S(1)}, bf16[1,3072,64]{1,2,0:T(8,128)(2,1)}, u32[]{:S(2)}) copy-start(bf16[1,3072,64]{1,2,0:T(8,128)(2,1)} %param.25) | copy-start | bytes 1179652
  6.0 24.2 %copy-start.7 = (bf16[1,64,3072]{2,1,0:T(8,128)(2,1)S(1)}, bf16[1,64,3072]{2,1,0:T(8,128)(2,1)}, u32[]{:S(2)}) copy-start(bf16[1,64,3072]{2,1,0:T(8,128)(2,1)} %param.26) | copy-start | bytes 1179652
  6.0 17.1 %collective-permute-start.1 = (bf16[2,192,768]{2,1,0:T(8,128)(2,1)S(1)}, bf16[2,192,768]{2,1,0:T(8,128)(2,1)S(1)}, u32[]{:S(2)}, u32[]{:S(2)}) collective-permute-start(bf16[2,192,768]{2,1,0:T(8,128)(2,1)S(1)} %get-tuple-element.48), channel_id=1, source_target_pairs={{0,2},{1,3},{2,0},{3,1},{4,6},{5,7},{6,4},{7,5},{8,10},{9,11},{10,... | collective-permute-start | bytes 1769480 | tf_op jit(solution)/shard_map/ppermute | solution.py:17
  9.0 11.1 %collective-permute-start.2 = (bf16[400,128]{1,0:T(8,128)(2,1)S(1)}, bf16[400,128]{1,0:T(8,128)(2,1)S(1)}, u32[]{:S(2)}, u32[]{:S(2)}) collective-permute-start(bf16[400,128]{1,0:T(8,128)(2,1)S(1)} %get-tuple-element.50), channel_id=1, source_target_pairs={{0,16},{8,24},{16,0},{24,8},{1,17},{9,25},{17,1},{25,9},{2,18},{10... | collective-permute-start | bytes 307208 | tf_op jit(solution)/shard_map/ppermute | solution.py:17
  11.6 8.5 %collective-permute-start.3 = (bf16[400,128]{1,0:T(8,128)(2,1)S(1)}, bf16[400,128]{1,0:T(8,128)(2,1)S(1)}, u32[]{:S(2)}, u32[]{:S(2)}) collective-permute-start(bf16[400,128]{1,0:T(8,128)(2,1)S(1)} %get-tuple-element.51), channel_id=1, source_target_pairs={{0,24},{8,16},{16,8},{24,0},{1,25},{9,17},{17,9},{25,1},{2,26},{10... | collective-permute-start | bytes 307208 | tf_op jit(solution)/shard_map/ppermute | solution.py:17
  12.9 7.4 %collective-permute-start.4 = (bf16[400,128]{1,0:T(8,128)(2,1)S(1)}, bf16[400,128]{1,0:T(8,128)(2,1)S(1)}, u32[]{:S(2)}, u32[]{:S(2)}) collective-permute-start(bf16[400,128]{1,0:T(8,128)(2,1)S(1)} %get-tuple-element.52), channel_id=1, source_target_pairs={{0,8},{8,0},{16,24},{24,16},{1,9},{9,1},{17,25},{25,17},{2,10},{10... | collective-permute-start | bytes 307208 | tf_op jit(solution)/shard_map/ppermute | solution.py:17
  20.5 4.7 %collective-permute-start.5 = (bf16[400,128]{1,0:T(8,128)(2,1)S(1)}, bf16[400,128]{1,0:T(8,128)(2,1)S(1)}, u32[]{:S(2)}, u32[]{:S(2)}) collective-permute-start(bf16[400,128]{1,0:T(8,128)(2,1)S(1)} %get-tuple-element.56), channel_id=1, source_target_pairs={{0,2},{1,3},{2,0},{3,1},{4,6},{5,7},{6,4},{7,5},{8,10},{9,11},{10,... | collective-permute-start | bytes 307208 | tf_op jit(solution)/shard_map/ppermute | solution.py:17
  23.2 9.6 %collective-permute-start.8 = (bf16[384,768]{1,0:T(8,128)(2,1)S(1)}, bf16[384,768]{1,0:T(8,128)(2,1)S(1)}, u32[]{:S(2)}, u32[]{:S(2)}) collective-permute-start(bf16[384,768]{1,0:T(8,128)(2,1)S(1)} %get-tuple-element.57), channel_id=1, source_target_pairs={{0,1},{1,0},{2,3},{3,2},{4,5},{5,4},{6,7},{7,6},{8,9},{9,8},{10,11... | collective-permute-start | bytes 1769480 | tf_op jit(solution)/shard_map/ppermute | solution.py:17
  25.5 4.7 %collective-permute-start.6 = (bf16[400,128]{1,0:T(8,128)(2,1)S(1)}, bf16[400,128]{1,0:T(8,128)(2,1)S(1)}, u32[]{:S(2)}, u32[]{:S(2)}) collective-permute-start(bf16[400,128]{1,0:T(8,128)(2,1)S(1)} %centre.1.own_ref), channel_id=1, source_target_pairs={{0,4},{4,0},{1,5},{5,1},{2,6},{6,2},{3,7},{7,3},{8,12},{12,8},{9,1... | collective-permute-start | bytes 307208 | tf_op jit(solution)/shard_map/ppermute | solution.py:17
  30.3 2.4 %collective-permute-start.10 = (bf16[128,1536]{1,0:T(8,128)(2,1)S(1)}, bf16[128,1536]{1,0:T(8,128)(2,1)S(1)}, u32[]{:S(2)}, u32[]{:S(2)}) collective-permute-start(bf16[128,1536]{1,0:T(8,128)(2,1)S(1)} %maps_pack.1.own_ref), channel_id=1, source_target_pairs={{0,1},{1,0},{2,3},{3,2},{4,5},{5,4},{6,7},{7,6},{8,9},{9,8},{10,11... | collective-permute-start | bytes 1179656 | tf_op jit(solution)/shard_map/ppermute | solution.py:17
  30.4 2.3 %collective-permute-start.7 = (bf16[800,128]{1,0:T(8,128)(2,1)S(1)}, bf16[800,128]{1,0:T(8,128)(2,1)S(1)}, u32[]{:S(2)}, u32[]{:S(2)}) collective-permute-start(bf16[800,128]{1,0:T(8,128)(2,1)S(1)} %join.1.refs_0_.dep_ref), channel_id=1, source_target_pairs={{0,1},{1,0},{2,3},{3,2},{4,5},{5,4},{6,7},{7,6},{8,9},{9,8},{10,11... | collective-permute-start | bytes 614408 | tf_op jit(solution)/shard_map/ppermute | solution.py:17
  31.1 20.3 %collective-permute-start.9 = (bf16[4,64,1536]{2,1,0:T(8,128)(2,1)S(1)}, bf16[4,64,1536]{2,1,0:T(8,128)(2,1)S(1)}, u32[]{:S(2)}, u32[]{:S(2)}) collective-permute-start(bf16[4,64,1536]{2,1,0:T(8,128)(2,1)S(1)} %image_pack.1), channel_id=1, source_target_pairs={{0,4},{4,0},{1,5},{5,1},{2,6},{6,2},{3,7},{7,3},{8,12},{12,8},{9,1... | collective-permute-start | bytes 2359304 | tf_op jit(solution)/shard_map/ppermute | solution.py:17
  33.9 19.3 %collective-permute-start.11 = (bf16[2,128,1536]{2,1,0:T(8,128)(2,1)S(1)}, bf16[2,128,1536]{2,1,0:T(8,128)(2,1)S(1)}, u32[]{:S(2)}, u32[]{:S(2)}) collective-permute-start(bf16[2,128,1536]{2,1,0:T(8,128)(2,1)S(1)} %maps_join.1.refs_0_), channel_id=1, source_target_pairs={{0,2},{1,3},{2,0},{3,1},{4,6},{5,7},{6,4},{7,5},{8,10},{9,11},{10,... | collective-permute-start | bytes 2359304 | tf_op jit(solution)/shard_map/ppermute | solution.py:17
  35.3 10.7 %collective-permute-start.13 = (bf16[400,128]{1,0:T(8,128)(2,1)S(1)}, bf16[400,128]{1,0:T(8,128)(2,1)S(1)}, u32[]{:S(2)}, u32[]{:S(2)}) collective-permute-start(bf16[400,128]{1,0:T(8,128)(2,1)S(1)} %get-tuple-element.62), channel_id=1, source_target_pairs={{0,16},{8,24},{16,0},{24,8},{1,17},{9,25},{17,1},{25,9},{2,18},{10... | collective-permute-start | bytes 307208 | tf_op jit(solution)/shard_map/ppermute | solution.py:17
  38.1 7.9 %collective-permute-start.14 = (bf16[400,128]{1,0:T(8,128)(2,1)S(1)}, bf16[400,128]{1,0:T(8,128)(2,1)S(1)}, u32[]{:S(2)}, u32[]{:S(2)}) collective-permute-start(bf16[400,128]{1,0:T(8,128)(2,1)S(1)} %get-tuple-element.63), channel_id=1, source_target_pairs={{0,24},{8,16},{16,8},{24,0},{1,25},{9,17},{17,9},{25,1},{2,26},{10... | collective-permute-start | bytes 307208 | tf_op jit(solution)/shard_map/ppermute | solution.py:17
  39.2 6.9 %collective-permute-start.15 = (bf16[400,128]{1,0:T(8,128)(2,1)S(1)}, bf16[400,128]{1,0:T(8,128)(2,1)S(1)}, u32[]{:S(2)}, u32[]{:S(2)}) collective-permute-start(bf16[400,128]{1,0:T(8,128)(2,1)S(1)} %get-tuple-element.64), channel_id=1, source_target_pairs={{0,8},{8,0},{16,24},{24,16},{1,9},{9,1},{17,25},{25,17},{2,10},{10... | collective-permute-start | bytes 307208 | tf_op jit(solution)/shard_map/ppermute | solution.py:17
  46.4 11.1 %collective-permute-start.16 = (bf16[64,768]{1,0:T(8,128)(2,1)S(1)}, bf16[64,768]{1,0:T(8,128)(2,1)S(1)}, u32[]{:S(2)}, u32[]{:S(2)}) collective-permute-start(bf16[64,768]{1,0:T(8,128)(2,1)S(1)} %finish.1.refs_0_), channel_id=1, source_target_pairs={{0,16},{8,24},{16,0},{24,8},{1,17},{9,25},{17,1},{25,9},{2,18},{10... | collective-permute-start | bytes 294920 | tf_op jit(solution)/shard_map/ppermute | solution.py:17
  50.1 7.4 %collective-permute-start.17 = (bf16[64,768]{1,0:T(8,128)(2,1)S(1)}, bf16[64,768]{1,0:T(8,128)(2,1)S(1)}, u32[]{:S(2)}, u32[]{:S(2)}) collective-permute-start(bf16[64,768]{1,0:T(8,128)(2,1)S(1)} %finish.1.refs_0_), channel_id=1, source_target_pairs={{0,24},{8,16},{16,8},{24,0},{1,25},{9,17},{17,9},{25,1},{2,26},{10... | collective-permute-start | bytes 294920 | tf_op jit(solution)/shard_map/ppermute | solution.py:17
  50.5 8.0 %collective-permute-start.18 = (bf16[64,768]{1,0:T(8,128)(2,1)S(1)}, bf16[64,768]{1,0:T(8,128)(2,1)S(1)}, u32[]{:S(2)}, u32[]{:S(2)}) collective-permute-start(bf16[64,768]{1,0:T(8,128)(2,1)S(1)} %finish.1.refs_0_), channel_id=1, source_target_pairs={{0,8},{8,0},{16,24},{24,16},{1,9},{9,1},{17,25},{25,17},{2,10},{10... | collective-permute-start | bytes 294920 | tf_op jit(solution)/shard_map/ppermute | solution.py:17
  53.5 5.1 %collective-permute-start.12 = (f32[2,64,64]{2,1,0:T(8,128)S(1)}, f32[2,64,64]{2,1,0:T(8,128)S(1)}, u32[]{:S(2)}, u32[]{:S(2)}) collective-permute-start(f32[2,64,64]{2,1,0:T(8,128)S(1)} %get-tuple-element.61.low_ref), channel_id=1, source_target_pairs={{0,4},{4,0},{1,5},{5,1},{2,6},{6,2},{3,7},{7,3},{8,12},{12,8},{9,1... | collective-permute-start | bytes 98312 | tf_op jit(solution)/shard_map/ppermute | solution.py:17
  60.0 4.2 %collective-permute-start.20 = (bf16[128,768]{1,0:T(8,128)(2,1)}, bf16[128,768]{1,0:T(8,128)(2,1)S(1)}, u32[]{:S(2)}, u32[]{:S(2)}) collective-permute-start(bf16[128,768]{1,0:T(8,128)(2,1)} %get-tuple-element.72), channel_id=1, source_target_pairs={{0,1},{1,0},{2,3},{3,2},{4,5},{5,4},{6,7},{7,6},{8,9},{9,8},{10,11... | collective-permute-start | bytes 589832 | tf_op jit(solution)/shard_map/ppermute | solution.py:17
  60.0 7.7 %collective-permute-start.22 = (bf16[128,768]{1,0:T(8,128)(2,1)S(1)}, bf16[128,768]{1,0:T(8,128)(2,1)S(1)}, u32[]{:S(2)}, u32[]{:S(2)}) collective-permute-start(bf16[128,768]{1,0:T(8,128)(2,1)S(1)} %get-tuple-element.75), channel_id=1, source_target_pairs={{0,2},{1,3},{2,0},{3,1},{4,6},{5,7},{6,4},{7,5},{8,10},{9,11},{10,... | collective-permute-start | bytes 589832 | tf_op jit(solution)/shard_map/ppermute | solution.py:17
  60.5 10.6 %collective-permute-start.24 = (bf16[128,768]{1,0:T(8,128)(2,1)S(1)}, bf16[128,768]{1,0:T(8,128)(2,1)S(1)}, u32[]{:S(2)}, u32[]{:S(2)}) collective-permute-start(bf16[128,768]{1,0:T(8,128)(2,1)S(1)} %get-tuple-element.78), channel_id=1, source_target_pairs={{0,3},{1,2},{2,1},{3,0},{4,7},{5,6},{6,5},{7,4},{8,11},{9,10},{10,... | collective-permute-start | bytes 589832 | tf_op jit(solution)/shard_map/ppermute | solution.py:17
  62.6 4.2 %collective-permute-start.19 = (bf16[64,384]{1,0:T(8,128)(2,1)S(1)}, bf16[64,384]{1,0:T(8,128)(2,1)S(1)}, u32[]{:S(2)}, u32[]{:S(2)}) collective-permute-start(bf16[64,384]{1,0:T(8,128)(2,1)S(1)} %get-tuple-element.71), channel_id=1, source_target_pairs={{0,4},{4,0},{1,5},{5,1},{2,6},{6,2},{3,7},{7,3},{8,12},{12,8},{9,1... | collective-permute-start | bytes 147464 | tf_op jit(solution)/shard_map/ppermute | solution.py:17
  64.6 6.5 %collective-permute-start.21 = (bf16[64,384]{1,0:T(8,128)(2,1)S(1)}, bf16[64,384]{1,0:T(8,128)(2,1)S(1)}, u32[]{:S(2)}, u32[]{:S(2)}) collective-permute-start(bf16[64,384]{1,0:T(8,128)(2,1)S(1)} %get-tuple-element.74), channel_id=1, source_target_pairs={{0,4},{4,0},{1,5},{5,1},{2,6},{6,2},{3,7},{7,3},{8,12},{12,8},{9,1... | collective-permute-start | bytes 147464 | tf_op jit(solution)/shard_map/ppermute | solution.py:17
  68.1 5.4 %collective-permute-start.23 = (bf16[64,384]{1,0:T(8,128)(2,1)S(1)}, bf16[64,384]{1,0:T(8,128)(2,1)S(1)}, u32[]{:S(2)}, u32[]{:S(2)}) collective-permute-start(bf16[64,384]{1,0:T(8,128)(2,1)S(1)} %get-tuple-element.77), channel_id=1, source_target_pairs={{0,4},{4,0},{1,5},{5,1},{2,6},{6,2},{3,7},{7,3},{8,12},{12,8},{9,1... | collective-permute-start | bytes 147464 | tf_op jit(solution)/shard_map/ppermute | solution.py:17
  71.5 4.2 %collective-permute-start.25 = (bf16[64,384]{1,0:T(8,128)(2,1)S(1)}, bf16[64,384]{1,0:T(8,128)(2,1)S(1)}, u32[]{:S(2)}, u32[]{:S(2)}) collective-permute-start(bf16[64,384]{1,0:T(8,128)(2,1)S(1)} %heads.8.refs_0_), channel_id=1, source_target_pairs={{0,4},{4,0},{1,5},{5,1},{2,6},{6,2},{3,7},{7,3},{8,12},{12,8},{9,1... | collective-permute-start | bytes 147464 | tf_op jit(solution)/shard_map/ppermute | solution.py:17
  (8 other events, 48.8 us)

commit v14 on v13

--- a/solution.py
+++ b/solution.py
@@ -846,7 +846,7 @@
     rows = call(
         functools.partial(choose_kernel, n_seq, n_enc),
         [struct((tokens, 2 * half)) for _ in range(n_req)],
-        (ids, low_other, text, *parts.values()),
+        (ids, image_values, text, *parts.values()),
         [SMEM, ANY] + [VMEM] * n_enc,
         name="choose",
     )

time: 76.7 us -> 76 us (level)
  no operation moved by 1% of the time
where the time goes in v14:
time: 76 us; the launch traced here: 75.8 us
  waiting for transfers between devices  33.1 us (44%)
  starting transfers between devices  30.6 us (40%)
  Pallas kernels  7.25 us (10%)
  local copies, waits for them, and re-layouts  3.28 us (4%)
  between operations  1.63 us (2%)
    ppermute x26, waiting for transfers between devices, swap(): return lax.ppermute(block, axis, [(i, i ^ step) for i in range(size)])  33.1 us
    ppermute x26, starting transfers between devices, swap(): return lax.ppermute(block, axis, [(i, i ^ step) for i in range(size)])  30.6 us
    pallas_call x21, Pallas kernels, call(): pl.pallas_call(kernel, out_shape=outs, in_specs=specs if specs is not Non...  7.25 us
    unnamed x28, local copies, waits for them, and re-layouts  3.11 us
  transfers between devices with their start and end apart: 26, of which 15 were waited for; matrix products, arithmetic and copies ran while one was open for 0% of the time, Pallas kernels for 6%

profile of v14, /device:TPU:0, one launch (start us, length us, event | category | flops | bytes accessed | tf_op | source)
XLA Modules:
  0.0 75.8 jit_solution(9555469750706380612)
XLA Ops:
  0.0 1.6 %copy-done.4 = bf16[256,3072]{1,0:T(8,128)(2,1)S(1)} copy-done((bf16[256,3072]{1,0:T(8,128)(2,1)S(1)}, bf16[256,3072]{1,0:T(8,128)(2,1)}, u32[]{:S(2)}) %copy-start.4) | copy-done | bytes 1572888
  1.6 0.8 %copy-done.8 = bf16[1,128,256]{2,1,0:T(8,128)(2,1)S(1)} copy-done((bf16[1,128,256]{2,1,0:T(8,128)(2,1)S(1)}, bf16[1,128,256]{2,1,0:T(8,128)(2,1)}, u32[]{:S(2)}) %copy-start.8) | copy-done | bytes 65560
  4.3 1.4 %collective-permute-done.got_ref = bf16[1552,128]{1,0:T(8,128)(2,1)S(1)} collective-permute-done((bf16[1552,128]{1,0:T(8,128)(2,1)S(1)}, bf16[1552,128]{1,0:T(8,128)(2,1)S(1)}, u32[]{:S(2)}, u32[]{:S(2)}) %collective-permute-start) | collective-permute-done | bytes 397344 | tf_op jit(solution)/shard_map/ppermute | solution.py:17
  6.0 2.9 %collective-permute-start.1 = (bf16[2,192,768]{2,1,0:T(8,128)(2,1)S(1)}, bf16[2,192,768]{2,1,0:T(8,128)(2,1)S(1)}, u32[]{:S(2)}, u32[]{:S(2)}) collective-permute-start(bf16[2,192,768]{2,1,0:T(8,128)(2,1)S(1)} %get-tuple-element.48), channel_id=1, source_target_pairs={{0,2},{1,3},{2,0},{3,1},{4,6},{5,7},{6,4},{7,5},{8,10},{9,11},{10,... | collective-permute-start | bytes 1769480 | tf_op jit(solution)/shard_map/ppermute | solution.py:17
  9.0 2.6 %collective-permute-start.2 = (bf16[400,128]{1,0:T(8,128)(2,1)S(1)}, bf16[400,128]{1,0:T(8,128)(2,1)S(1)}, u32[]{:S(2)}, u32[]{:S(2)}) collective-permute-start(bf16[400,128]{1,0:T(8,128)(2,1)S(1)} %get-tuple-element.50), channel_id=1, source_target_pairs={{0,16},{8,24},{16,0},{24,8},{1,17},{9,25},{17,1},{25,9},{2,18},{10... | collective-permute-start | bytes 307208 | tf_op jit(solution)/shard_map/ppermute | solution.py:17
  11.6 1.3 %collective-permute-start.3 = (bf16[400,128]{1,0:T(8,128)(2,1)S(1)}, bf16[400,128]{1,0:T(8,128)(2,1)S(1)}, u32[]{:S(2)}, u32[]{:S(2)}) collective-permute-start(bf16[400,128]{1,0:T(8,128)(2,1)S(1)} %get-tuple-element.51), channel_id=1, source_target_pairs={{0,24},{8,16},{16,8},{24,0},{1,25},{9,17},{17,9},{25,1},{2,26},{10... | collective-permute-start | bytes 307208 | tf_op jit(solution)/shard_map/ppermute | solution.py:17
  13.8 6.2 %collective-permute-done.2.refs_0_ = bf16[400,128]{1,0:T(8,128)(2,1)S(1)} collective-permute-done((bf16[400,128]{1,0:T(8,128)(2,1)S(1)}, bf16[400,128]{1,0:T(8,128)(2,1)S(1)}, u32[]{:S(2)}, u32[]{:S(2)}) %collective-permute-start.2) | collective-permute-done | bytes 102432 | tf_op jit(solution)/shard_map/ppermute | solution.py:17
  21.0 2.1 %collective-permute-done.1.got_ref = bf16[2,192,768]{2,1,0:T(8,128)(2,1)S(1)} collective-permute-done((bf16[2,192,768]{2,1,0:T(8,128)(2,1)S(1)}, bf16[2,192,768]{2,1,0:T(8,128)(2,1)S(1)}, u32[]{:S(2)}, u32[]{:S(2)}) %collective-permute-start.1) | collective-permute-done | bytes 589856 | tf_op jit(solution)/shard_map/ppermute | solution.py:17
  23.3 2.0 %collective-permute-done.5.got_ref = bf16[400,128]{1,0:T(8,128)(2,1)S(1)} collective-permute-done((bf16[400,128]{1,0:T(8,128)(2,1)S(1)}, bf16[400,128]{1,0:T(8,128)(2,1)S(1)}, u32[]{:S(2)}, u32[]{:S(2)}) %collective-permute-start.5) | collective-permute-done | bytes 102432 | tf_op jit(solution)/shard_map/ppermute | solution.py:17
  25.5 1.6 %collective-permute-start.6 = (bf16[400,128]{1,0:T(8,128)(2,1)S(1)}, bf16[400,128]{1,0:T(8,128)(2,1)S(1)}, u32[]{:S(2)}, u32[]{:S(2)}) collective-permute-start(bf16[400,128]{1,0:T(8,128)(2,1)S(1)} %centre.1.own_ref), channel_id=1, source_target_pairs={{0,4},{4,0},{1,5},{5,1},{2,6},{6,2},{3,7},{7,3},{8,12},{12,8},{9,1... | collective-permute-start | bytes 307208 | tf_op jit(solution)/shard_map/ppermute | solution.py:17
  27.0 3.2 %collective-permute-done.6.got_ref = bf16[400,128]{1,0:T(8,128)(2,1)S(1)} collective-permute-done((bf16[400,128]{1,0:T(8,128)(2,1)S(1)}, bf16[400,128]{1,0:T(8,128)(2,1)S(1)}, u32[]{:S(2)}, u32[]{:S(2)}) %collective-permute-start.6) | collective-permute-done | bytes 102432 | tf_op jit(solution)/shard_map/ppermute | solution.py:17
  31.1 1.6 %collective-permute-start.9 = (bf16[4,64,1536]{2,1,0:T(8,128)(2,1)S(1)}, bf16[4,64,1536]{2,1,0:T(8,128)(2,1)S(1)}, u32[]{:S(2)}, u32[]{:S(2)}) collective-permute-start(bf16[4,64,1536]{2,1,0:T(8,128)(2,1)S(1)} %image_pack.1), channel_id=1, source_target_pairs={{0,4},{4,0},{1,5},{5,1},{2,6},{6,2},{3,7},{7,3},{8,12},{12,8},{9,1... | collective-permute-start | bytes 2359304 | tf_op jit(solution)/shard_map/ppermute | solution.py:17
  32.8 1.2 %project.1 = (s32[4]{0:T(128)S(1)}, f32[400,128]{1,0:T(8,128)S(1)}, bf16[400,128]{1,0:T(8,128)(2,1)S(1)}, bf16[400,128]{1,0:T(8,128)(2,1)S(1)}, bf16[400,128]{1,0:T(8,128)(2,1)S(1)}) custom-call(bf16[800,128]{1,0:T(8,128)(2,1)S(1)} %join.1.refs_0_.dep_ref, bf16[800,128]{1,0:T(8,128)(2,1)S(1)} %collective-permute-done.7.refs_1_, ...), custom_call_target="tpu_custom_call" | custom-call | tf_op jit(solution)/shard_map/project/pallas_call | solution.py:280
  33.9 1.4 %collective-permute-start.11 = (bf16[2,128,1536]{2,1,0:T(8,128)(2,1)S(1)}, bf16[2,128,1536]{2,1,0:T(8,128)(2,1)S(1)}, u32[]{:S(2)}, u32[]{:S(2)}) collective-permute-start(bf16[2,128,1536]{2,1,0:T(8,128)(2,1)S(1)} %maps_join.1.refs_0_), channel_id=1, source_target_pairs={{0,2},{1,3},{2,0},{3,1},{4,6},{5,7},{6,4},{7,5},{8,10},{9,11},{10,... | collective-permute-start | bytes 2359304 | tf_op jit(solution)/shard_map/ppermute | solution.py:17
  35.3 2.8 %collective-permute-start.13 = (bf16[400,128]{1,0:T(8,128)(2,1)S(1)}, bf16[400,128]{1,0:T(8,128)(2,1)S(1)}, u32[]{:S(2)}, u32[]{:S(2)}) collective-permute-start(bf16[400,128]{1,0:T(8,128)(2,1)S(1)} %get-tuple-element.64), channel_id=1, source_target_pairs={{0,16},{8,24},{16,0},{24,8},{1,17},{9,25},{17,1},{25,9},{2,18},{10... | collective-permute-start | bytes 307208 | tf_op jit(solution)/shard_map/ppermute | solution.py:17
  38.1 1.1 %collective-permute-start.14 = (bf16[400,128]{1,0:T(8,128)(2,1)S(1)}, bf16[400,128]{1,0:T(8,128)(2,1)S(1)}, u32[]{:S(2)}, u32[]{:S(2)}) collective-permute-start(bf16[400,128]{1,0:T(8,128)(2,1)S(1)} %get-tuple-element.65), channel_id=1, source_target_pairs={{0,24},{8,16},{16,8},{24,0},{1,25},{9,17},{17,9},{25,1},{2,26},{10... | collective-permute-start | bytes 307208 | tf_op jit(solution)/shard_map/ppermute | solution.py:17
  39.5 6.6 %collective-permute-done.13.refs_0_ = bf16[400,128]{1,0:T(8,128)(2,1)S(1)} collective-permute-done((bf16[400,128]{1,0:T(8,128)(2,1)S(1)}, bf16[400,128]{1,0:T(8,128)(2,1)S(1)}, u32[]{:S(2)}, u32[]{:S(2)}) %collective-permute-start.13) | collective-permute-done | bytes 102432 | tf_op jit(solution)/shard_map/ppermute | solution.py:17
  46.4 3.7 %collective-permute-start.16 = (bf16[64,768]{1,0:T(8,128)(2,1)S(1)}, bf16[64,768]{1,0:T(8,128)(2,1)S(1)}, u32[]{:S(2)}, u32[]{:S(2)}) collective-permute-start(bf16[64,768]{1,0:T(8,128)(2,1)S(1)} %finish.1.refs_0_), channel_id=1, source_target_pairs={{0,16},{8,24},{16,0},{24,8},{1,17},{9,25},{17,1},{25,9},{2,18},{10... | collective-permute-start | bytes 294920 | tf_op jit(solution)/shard_map/ppermute | solution.py:17
  51.4 1.8 %collective-permute-done.11.refs_1_ = bf16[2,128,1536]{2,1,0:T(8,128)(2,1)S(1)} collective-permute-done((bf16[2,128,1536]{2,1,0:T(8,128)(2,1)S(1)}, bf16[2,128,1536]{2,1,0:T(8,128)(2,1)S(1)}, u32[]{:S(2)}, u32[]{:S(2)}) %collective-permute-start.11) | collective-permute-done | bytes 786464 | tf_op jit(solution)/shard_map/ppermute | solution.py:17
  53.5 1.5 %collective-permute-start.12 = (f32[2,64,64]{2,1,0:T(8,128)S(1)}, f32[2,64,64]{2,1,0:T(8,128)S(1)}, u32[]{:S(2)}, u32[]{:S(2)}) collective-permute-start(f32[2,64,64]{2,1,0:T(8,128)S(1)} %get-tuple-element.61.low_ref), channel_id=1, source_target_pairs={{0,4},{4,0},{1,5},{5,1},{2,6},{6,2},{3,7},{7,3},{8,12},{12,8},{9,1... | collective-permute-start | bytes 98312 | tf_op jit(solution)/shard_map/ppermute | solution.py:17
  55.0 2.8 %collective-permute-done.12.other_ref = f32[2,64,64]{2,1,0:T(8,128)S(1)} collective-permute-done((f32[2,64,64]{2,1,0:T(8,128)S(1)}, f32[2,64,64]{2,1,0:T(8,128)S(1)}, u32[]{:S(2)}, u32[]{:S(2)}) %collective-permute-start.12) | collective-permute-done | bytes 32800 | tf_op jit(solution)/shard_map/ppermute | solution.py:17
  58.5 0.7 choose.1
  59.4 0.9 %collective-permute-start.22 = (bf16[128,768]{1,0:T(8,128)(2,1)S(1)}, bf16[128,768]{1,0:T(8,128)(2,1)S(1)}, u32[]{:S(2)}, u32[]{:S(2)}) collective-permute-start(bf16[128,768]{1,0:T(8,128)(2,1)S(1)} %get-tuple-element.75), channel_id=1, source_target_pairs={{0,2},{1,3},{2,0},{3,1},{4,6},{5,7},{6,4},{7,5},{8,10},{9,11},{10,... | collective-permute-start | bytes 589832 | tf_op jit(solution)/shard_map/ppermute | solution.py:17
  60.3 0.9 %collective-permute-start.24 = (bf16[128,768]{1,0:T(8,128)(2,1)S(1)}, bf16[128,768]{1,0:T(8,128)(2,1)S(1)}, u32[]{:S(2)}, u32[]{:S(2)}) collective-permute-start(bf16[128,768]{1,0:T(8,128)(2,1)S(1)} %get-tuple-element.78), channel_id=1, source_target_pairs={{0,3},{1,2},{2,1},{3,0},{4,7},{5,6},{6,5},{7,4},{8,11},{9,10},{10,... | collective-permute-start | bytes 589832 | tf_op jit(solution)/shard_map/ppermute | solution.py:17
  61.7 1.6 %collective-permute-start.19 = (bf16[64,384]{1,0:T(8,128)(2,1)S(1)}, bf16[64,384]{1,0:T(8,128)(2,1)S(1)}, u32[]{:S(2)}, u32[]{:S(2)}) collective-permute-start(bf16[64,384]{1,0:T(8,128)(2,1)S(1)} %get-tuple-element.71), channel_id=1, source_target_pairs={{0,4},{4,0},{1,5},{5,1},{2,6},{6,2},{3,7},{7,3},{8,12},{12,8},{9,1... | collective-permute-start | bytes 147464 | tf_op jit(solution)/shard_map/ppermute | solution.py:17
  64.3 1.5 %collective-permute-done.19.refs_1_ = bf16[64,384]{1,0:T(8,128)(2,1)S(1)} collective-permute-done((bf16[64,384]{1,0:T(8,128)(2,1)S(1)}, bf16[64,384]{1,0:T(8,128)(2,1)S(1)}, u32[]{:S(2)}, u32[]{:S(2)}) %collective-permute-start.19) | collective-permute-done | bytes 49184 | tf_op jit(solution)/shard_map/ppermute | solution.py:17
  65.9 1.3 %collective-permute-done.22.text_ref = bf16[128,768]{1,0:T(8,128)(2,1)S(1)} collective-permute-done((bf16[128,768]{1,0:T(8,128)(2,1)S(1)}, bf16[128,768]{1,0:T(8,128)(2,1)S(1)}, u32[]{:S(2)}, u32[]{:S(2)}) %collective-permute-start.22) | collective-permute-done | bytes 196640 | tf_op jit(solution)/shard_map/ppermute | solution.py:17
  67.6 1.6 %collective-permute-start.23 = (bf16[64,384]{1,0:T(8,128)(2,1)S(1)}, bf16[64,384]{1,0:T(8,128)(2,1)S(1)}, u32[]{:S(2)}, u32[]{:S(2)}) collective-permute-start(bf16[64,384]{1,0:T(8,128)(2,1)S(1)} %get-tuple-element.77), channel_id=1, source_target_pairs={{0,4},{4,0},{1,5},{5,1},{2,6},{6,2},{3,7},{7,3},{8,12},{12,8},{9,1... | collective-permute-start | bytes 147464 | tf_op jit(solution)/shard_map/ppermute | solution.py:17
  69.2 1.3 %collective-permute-done.24.text_ref = bf16[128,768]{1,0:T(8,128)(2,1)S(1)} collective-permute-done((bf16[128,768]{1,0:T(8,128)(2,1)S(1)}, bf16[128,768]{1,0:T(8,128)(2,1)S(1)}, u32[]{:S(2)}, u32[]{:S(2)}) %collective-permute-start.24) | collective-permute-done | bytes 196640 | tf_op jit(solution)/shard_map/ppermute | solution.py:17
  70.9 1.6 %collective-permute-start.25 = (bf16[64,384]{1,0:T(8,128)(2,1)S(1)}, bf16[64,384]{1,0:T(8,128)(2,1)S(1)}, u32[]{:S(2)}, u32[]{:S(2)}) collective-permute-start(bf16[64,384]{1,0:T(8,128)(2,1)S(1)} %heads.8.refs_0_), channel_id=1, source_target_pairs={{0,4},{4,0},{1,5},{5,1},{2,6},{6,2},{3,7},{7,3},{8,12},{12,8},{9,1... | collective-permute-start | bytes 147464 | tf_op jit(solution)/shard_map/ppermute | solution.py:17
  72.9 2.1 %collective-permute-done.25.refs_7_ = bf16[64,384]{1,0:T(8,128)(2,1)S(1)} collective-permute-done((bf16[64,384]{1,0:T(8,128)(2,1)S(1)}, bf16[64,384]{1,0:T(8,128)(2,1)S(1)}, u32[]{:S(2)}, u32[]{:S(2)}) %collective-permute-start.25) | collective-permute-done | bytes 49184 | tf_op jit(solution)/shard_map/ppermute | solution.py:17
  75.0 0.8 %assemble.1 = bf16[64,3072]{1,0:T(8,128)(2,1)} custom-call(bf16[64,384]{1,0:T(8,128)(2,1)S(1)} %get-tuple-element.70.refs_0_, bf16[64,384]{1,0:T(8,128)(2,1)S(1)} %collective-permute-done.19.refs_1_, bf16[64,384]{1,0:T(8,128)(2,1)S(1)} %get-tuple-element.73.refs_0_.refs_2_, bf16[64,384]{1,0:T(8,128)(2,1)S(1)} %collective-permute-done.21.refs_1_.refs_3_, ...), custom_call_target="tpu_custom_call" | custom-call | tf_op jit(solution)/shard_map/assemble/pallas_call | solution.py:280
  (74 shorter events, 9.7 us)
Async XLA Ops:
  0.0 61.2 %copy-start = (s32[2,128]{1,0:T(2,128)S(1)}, s32[2,128]{1,0:T(2,128)}, u32[]{:S(2)}) copy-start(s32[2,128]{1,0:T(2,128)} %param.16) | copy-start | bytes 3076
  3.1 17.2 %copy-start.12 = (bf16[192]{0:T(256)(128)(2,1)S(1)}, bf16[192]{0:T(256)(128)(2,1)}, u32[]{:S(2)}) copy-start(bf16[192]{0:T(256)(128)(2,1)} %b_ref.1) | copy-start | bytes 1156
  3.1 17.3 %copy-start.9 = (bf16[1,192]{1,0:T(2,128)(2,1)S(1)}, bf16[1,192]{1,0:T(2,128)(2,1)}, u32[]{:S(2)}) copy-start(bf16[1,192]{1,0:T(2,128)(2,1)} %shift_ref.3) | copy-start | bytes 1156
  3.1 17.3 %copy-start.10 = (bf16[1,192]{1,0:T(2,128)(2,1)S(1)}, bf16[1,192]{1,0:T(2,128)(2,1)}, u32[]{:S(2)}) copy-start(bf16[1,192]{1,0:T(2,128)(2,1)} %scale_ref.1) | copy-start | bytes 1156
  3.8 1.9 %collective-permute-start = (bf16[1552,128]{1,0:T(8,128)(2,1)S(1)}, bf16[1552,128]{1,0:T(8,128)(2,1)S(1)}, u32[]{:S(2)}, u32[]{:S(2)}) collective-permute-start(bf16[1552,128]{1,0:T(8,128)(2,1)S(1)} %get-tuple-element.42), channel_id=1, source_target_pairs={{0,1},{1,0},{2,3},{3,2},{4,5},{5,4},{6,7},{7,6},{8,9},{9,8},{10,11... | collective-permute-start | bytes 1191944 | tf_op jit(solution)/shard_map/ppermute | solution.py:17
  6.0 24.2 %copy-start.6 = (bf16[1,3072,64]{1,2,0:T(8,128)(2,1)S(1)}, bf16[1,3072,64]{1,2,0:T(8,128)(2,1)}, u32[]{:S(2)}) copy-start(bf16[1,3072,64]{1,2,0:T(8,128)(2,1)} %param.25) | copy-start | bytes 1179652
  6.0 24.2 %copy-start.7 = (bf16[1,64,3072]{2,1,0:T(8,128)(2,1)S(1)}, bf16[1,64,3072]{2,1,0:T(8,128)(2,1)}, u32[]{:S(2)}) copy-start(bf16[1,64,3072]{2,1,0:T(8,128)(2,1)} %param.26) | copy-start | bytes 1179652
  6.0 17.1 %collective-permute-start.1 = (bf16[2,192,768]{2,1,0:T(8,128)(2,1)S(1)}, bf16[2,192,768]{2,1,0:T(8,128)(2,1)S(1)}, u32[]{:S(2)}, u32[]{:S(2)}) collective-permute-start(bf16[2,192,768]{2,1,0:T(8,128)(2,1)S(1)} %get-tuple-element.48), channel_id=1, source_target_pairs={{0,2},{1,3},{2,0},{3,1},{4,6},{5,7},{6,4},{7,5},{8,10},{9,11},{10,... | collective-permute-start | bytes 1769480 | tf_op jit(solution)/shard_map/ppermute | solution.py:17
  9.0 11.1 %collective-permute-start.2 = (bf16[400,128]{1,0:T(8,128)(2,1)S(1)}, bf16[400,128]{1,0:T(8,128)(2,1)S(1)}, u32[]{:S(2)}, u32[]{:S(2)}) collective-permute-start(bf16[400,128]{1,0:T(8,128)(2,1)S(1)} %get-tuple-element.50), channel_id=1, source_target_pairs={{0,16},{8,24},{16,0},{24,8},{1,17},{9,25},{17,1},{25,9},{2,18},{10... | collective-permute-start | bytes 307208 | tf_op jit(solution)/shard_map/ppermute | solution.py:17
  11.6 8.5 %collective-permute-start.3 = (bf16[400,128]{1,0:T(8,128)(2,1)S(1)}, bf16[400,128]{1,0:T(8,128)(2,1)S(1)}, u32[]{:S(2)}, u32[]{:S(2)}) collective-permute-start(bf16[400,128]{1,0:T(8,128)(2,1)S(1)} %get-tuple-element.51), channel_id=1, source_target_pairs={{0,24},{8,16},{16,8},{24,0},{1,25},{9,17},{17,9},{25,1},{2,26},{10... | collective-permute-start | bytes 307208 | tf_op jit(solution)/shard_map/ppermute | solution.py:17
  12.9 7.4 %collective-permute-start.4 = (bf16[400,128]{1,0:T(8,128)(2,1)S(1)}, bf16[400,128]{1,0:T(8,128)(2,1)S(1)}, u32[]{:S(2)}, u32[]{:S(2)}) collective-permute-start(bf16[400,128]{1,0:T(8,128)(2,1)S(1)} %get-tuple-element.52), channel_id=1, source_target_pairs={{0,8},{8,0},{16,24},{24,16},{1,9},{9,1},{17,25},{25,17},{2,10},{10... | collective-permute-start | bytes 307208 | tf_op jit(solution)/shard_map/ppermute | solution.py:17
  20.5 4.7 %collective-permute-start.5 = (bf16[400,128]{1,0:T(8,128)(2,1)S(1)}, bf16[400,128]{1,0:T(8,128)(2,1)S(1)}, u32[]{:S(2)}, u32[]{:S(2)}) collective-permute-start(bf16[400,128]{1,0:T(8,128)(2,1)S(1)} %get-tuple-element.56), channel_id=1, source_target_pairs={{0,2},{1,3},{2,0},{3,1},{4,6},{5,7},{6,4},{7,5},{8,10},{9,11},{10,... | collective-permute-start | bytes 307208 | tf_op jit(solution)/shard_map/ppermute | solution.py:17
  23.2 9.6 %collective-permute-start.8 = (bf16[384,768]{1,0:T(8,128)(2,1)S(1)}, bf16[384,768]{1,0:T(8,128)(2,1)S(1)}, u32[]{:S(2)}, u32[]{:S(2)}) collective-permute-start(bf16[384,768]{1,0:T(8,128)(2,1)S(1)} %get-tuple-element.57), channel_id=1, source_target_pairs={{0,1},{1,0},{2,3},{3,2},{4,5},{5,4},{6,7},{7,6},{8,9},{9,8},{10,11... | collective-permute-start | bytes 1769480 | tf_op jit(solution)/shard_map/ppermute | solution.py:17
  25.5 4.7 %collective-permute-start.6 = (bf16[400,128]{1,0:T(8,128)(2,1)S(1)}, bf16[400,128]{1,0:T(8,128)(2,1)S(1)}, u32[]{:S(2)}, u32[]{:S(2)}) collective-permute-start(bf16[400,128]{1,0:T(8,128)(2,1)S(1)} %centre.1.own_ref), channel_id=1, source_target_pairs={{0,4},{4,0},{1,5},{5,1},{2,6},{6,2},{3,7},{7,3},{8,12},{12,8},{9,1... | collective-permute-start | bytes 307208 | tf_op jit(solution)/shard_map/ppermute | solution.py:17
  30.3 2.4 %collective-permute-start.10 = (bf16[128,1536]{1,0:T(8,128)(2,1)S(1)}, bf16[128,1536]{1,0:T(8,128)(2,1)S(1)}, u32[]{:S(2)}, u32[]{:S(2)}) collective-permute-start(bf16[128,1536]{1,0:T(8,128)(2,1)S(1)} %maps_pack.1.own_ref), channel_id=1, source_target_pairs={{0,1},{1,0},{2,3},{3,2},{4,5},{5,4},{6,7},{7,6},{8,9},{9,8},{10,11... | collective-permute-start | bytes 1179656 | tf_op jit(solution)/shard_map/ppermute | solution.py:17
  30.4 2.3 %collective-permute-start.7 = (bf16[800,128]{1,0:T(8,128)(2,1)S(1)}, bf16[800,128]{1,0:T(8,128)(2,1)S(1)}, u32[]{:S(2)}, u32[]{:S(2)}) collective-permute-start(bf16[800,128]{1,0:T(8,128)(2,1)S(1)} %join.1.refs_0_.dep_ref), channel_id=1, source_target_pairs={{0,1},{1,0},{2,3},{3,2},{4,5},{5,4},{6,7},{7,6},{8,9},{9,8},{10,11... | collective-permute-start | bytes 614408 | tf_op jit(solution)/shard_map/ppermute | solution.py:17
  31.1 20.3 %collective-permute-start.9 = (bf16[4,64,1536]{2,1,0:T(8,128)(2,1)S(1)}, bf16[4,64,1536]{2,1,0:T(8,128)(2,1)S(1)}, u32[]{:S(2)}, u32[]{:S(2)}) collective-permute-start(bf16[4,64,1536]{2,1,0:T(8,128)(2,1)S(1)} %image_pack.1), channel_id=1, source_target_pairs={{0,4},{4,0},{1,5},{5,1},{2,6},{6,2},{3,7},{7,3},{8,12},{12,8},{9,1... | collective-permute-start | bytes 2359304 | tf_op jit(solution)/shard_map/ppermute | solution.py:17
  33.9 19.3 %collective-permute-start.11 = (bf16[2,128,1536]{2,1,0:T(8,128)(2,1)S(1)}, bf16[2,128,1536]{2,1,0:T(8,128)(2,1)S(1)}, u32[]{:S(2)}, u32[]{:S(2)}) collective-permute-start(bf16[2,128,1536]{2,1,0:T(8,128)(2,1)S(1)} %maps_join.1.refs_0_), channel_id=1, source_target_pairs={{0,2},{1,3},{2,0},{3,1},{4,6},{5,7},{6,4},{7,5},{8,10},{9,11},{10,... | collective-permute-start | bytes 2359304 | tf_op jit(solution)/shard_map/ppermute | solution.py:17
  35.3 10.7 %collective-permute-start.13 = (bf16[400,128]{1,0:T(8,128)(2,1)S(1)}, bf16[400,128]{1,0:T(8,128)(2,1)S(1)}, u32[]{:S(2)}, u32[]{:S(2)}) collective-permute-start(bf16[400,128]{1,0:T(8,128)(2,1)S(1)} %get-tuple-element.64), channel_id=1, source_target_pairs={{0,16},{8,24},{16,0},{24,8},{1,17},{9,25},{17,1},{25,9},{2,18},{10... | collective-permute-start | bytes 307208 | tf_op jit(solution)/shard_map/ppermute | solution.py:17
  38.1 7.9 %collective-permute-start.14 = (bf16[400,128]{1,0:T(8,128)(2,1)S(1)}, bf16[400,128]{1,0:T(8,128)(2,1)S(1)}, u32[]{:S(2)}, u32[]{:S(2)}) collective-permute-start(bf16[400,128]{1,0:T(8,128)(2,1)S(1)} %get-tuple-element.65), channel_id=1, source_target_pairs={{0,24},{8,16},{16,8},{24,0},{1,25},{9,17},{17,9},{25,1},{2,26},{10... | collective-permute-start | bytes 307208 | tf_op jit(solution)/shard_map/ppermute | solution.py:17
  39.2 6.9 %collective-permute-start.15 = (bf16[400,128]{1,0:T(8,128)(2,1)S(1)}, bf16[400,128]{1,0:T(8,128)(2,1)S(1)}, u32[]{:S(2)}, u32[]{:S(2)}) collective-permute-start(bf16[400,128]{1,0:T(8,128)(2,1)S(1)} %get-tuple-element.66), channel_id=1, source_target_pairs={{0,8},{8,0},{16,24},{24,16},{1,9},{9,1},{17,25},{25,17},{2,10},{10... | collective-permute-start | bytes 307208 | tf_op jit(solution)/shard_map/ppermute | solution.py:17
  46.4 11.7 %collective-permute-start.16 = (bf16[64,768]{1,0:T(8,128)(2,1)S(1)}, bf16[64,768]{1,0:T(8,128)(2,1)S(1)}, u32[]{:S(2)}, u32[]{:S(2)}) collective-permute-start(bf16[64,768]{1,0:T(8,128)(2,1)S(1)} %finish.1.refs_0_), channel_id=1, source_target_pairs={{0,16},{8,24},{16,0},{24,8},{1,17},{9,25},{17,1},{25,9},{2,18},{10... | collective-permute-start | bytes 294920 | tf_op jit(solution)/shard_map/ppermute | solution.py:17
  50.1 8.0 %collective-permute-start.17 = (bf16[64,768]{1,0:T(8,128)(2,1)S(1)}, bf16[64,768]{1,0:T(8,128)(2,1)S(1)}, u32[]{:S(2)}, u32[]{:S(2)}) collective-permute-start(bf16[64,768]{1,0:T(8,128)(2,1)S(1)} %finish.1.refs_0_), channel_id=1, source_target_pairs={{0,24},{8,16},{16,8},{24,0},{1,25},{9,17},{17,9},{25,1},{2,26},{10... | collective-permute-start | bytes 294920 | tf_op jit(solution)/shard_map/ppermute | solution.py:17
  50.5 8.0 %collective-permute-start.18 = (bf16[64,768]{1,0:T(8,128)(2,1)S(1)}, bf16[64,768]{1,0:T(8,128)(2,1)S(1)}, u32[]{:S(2)}, u32[]{:S(2)}) collective-permute-start(bf16[64,768]{1,0:T(8,128)(2,1)S(1)} %finish.1.refs_0_), channel_id=1, source_target_pairs={{0,8},{8,0},{16,24},{24,16},{1,9},{9,1},{17,25},{25,17},{2,10},{10... | collective-permute-start | bytes 294920 | tf_op jit(solution)/shard_map/ppermute | solution.py:17
  53.5 4.3 %collective-permute-start.12 = (f32[2,64,64]{2,1,0:T(8,128)S(1)}, f32[2,64,64]{2,1,0:T(8,128)S(1)}, u32[]{:S(2)}, u32[]{:S(2)}) collective-permute-start(f32[2,64,64]{2,1,0:T(8,128)S(1)} %get-tuple-element.61.low_ref), channel_id=1, source_target_pairs={{0,4},{4,0},{1,5},{5,1},{2,6},{6,2},{3,7},{7,3},{8,12},{12,8},{9,1... | collective-permute-start | bytes 98312 | tf_op jit(solution)/shard_map/ppermute | solution.py:17
  59.3 4.0 %collective-permute-start.20 = (bf16[128,768]{1,0:T(8,128)(2,1)S(1)}, bf16[128,768]{1,0:T(8,128)(2,1)S(1)}, u32[]{:S(2)}, u32[]{:S(2)}) collective-permute-start(bf16[128,768]{1,0:T(8,128)(2,1)S(1)} %get-tuple-element.72), channel_id=1, source_target_pairs={{0,1},{1,0},{2,3},{3,2},{4,5},{5,4},{6,7},{7,6},{8,9},{9,8},{10,11... | collective-permute-start | bytes 589832 | tf_op jit(solution)/shard_map/ppermute | solution.py:17
  59.4 7.8 %collective-permute-start.22 = (bf16[128,768]{1,0:T(8,128)(2,1)S(1)}, bf16[128,768]{1,0:T(8,128)(2,1)S(1)}, u32[]{:S(2)}, u32[]{:S(2)}) collective-permute-start(bf16[128,768]{1,0:T(8,128)(2,1)S(1)} %get-tuple-element.75), channel_id=1, source_target_pairs={{0,2},{1,3},{2,0},{3,1},{4,6},{5,7},{6,4},{7,5},{8,10},{9,11},{10,... | collective-permute-start | bytes 589832 | tf_op jit(solution)/shard_map/ppermute | solution.py:17
  60.3 10.2 %collective-permute-start.24 = (bf16[128,768]{1,0:T(8,128)(2,1)S(1)}, bf16[128,768]{1,0:T(8,128)(2,1)S(1)}, u32[]{:S(2)}, u32[]{:S(2)}) collective-permute-start(bf16[128,768]{1,0:T(8,128)(2,1)S(1)} %get-tuple-element.78), channel_id=1, source_target_pairs={{0,3},{1,2},{2,1},{3,0},{4,7},{5,6},{6,5},{7,4},{8,11},{9,10},{10,... | collective-permute-start | bytes 589832 | tf_op jit(solution)/shard_map/ppermute | solution.py:17
  61.7 4.2 %collective-permute-start.19 = (bf16[64,384]{1,0:T(8,128)(2,1)S(1)}, bf16[64,384]{1,0:T(8,128)(2,1)S(1)}, u32[]{:S(2)}, u32[]{:S(2)}) collective-permute-start(bf16[64,384]{1,0:T(8,128)(2,1)S(1)} %get-tuple-element.71), channel_id=1, source_target_pairs={{0,4},{4,0},{1,5},{5,1},{2,6},{6,2},{3,7},{7,3},{8,12},{12,8},{9,1... | collective-permute-start | bytes 147464 | tf_op jit(solution)/shard_map/ppermute | solution.py:17
  63.7 6.7 %collective-permute-start.21 = (bf16[64,384]{1,0:T(8,128)(2,1)S(1)}, bf16[64,384]{1,0:T(8,128)(2,1)S(1)}, u32[]{:S(2)}, u32[]{:S(2)}) collective-permute-start(bf16[64,384]{1,0:T(8,128)(2,1)S(1)} %get-tuple-element.74), channel_id=1, source_target_pairs={{0,4},{4,0},{1,5},{5,1},{2,6},{6,2},{3,7},{7,3},{8,12},{12,8},{9,1... | collective-permute-start | bytes 147464 | tf_op jit(solution)/shard_map/ppermute | solution.py:17
  67.6 5.3 %collective-permute-start.23 = (bf16[64,384]{1,0:T(8,128)(2,1)S(1)}, bf16[64,384]{1,0:T(8,128)(2,1)S(1)}, u32[]{:S(2)}, u32[]{:S(2)}) collective-permute-start(bf16[64,384]{1,0:T(8,128)(2,1)S(1)} %get-tuple-element.77), channel_id=1, source_target_pairs={{0,4},{4,0},{1,5},{5,1},{2,6},{6,2},{3,7},{7,3},{8,12},{12,8},{9,1... | collective-permute-start | bytes 147464 | tf_op jit(solution)/shard_map/ppermute | solution.py:17
  70.9 4.2 %collective-permute-start.25 = (bf16[64,384]{1,0:T(8,128)(2,1)S(1)}, bf16[64,384]{1,0:T(8,128)(2,1)S(1)}, u32[]{:S(2)}, u32[]{:S(2)}) collective-permute-start(bf16[64,384]{1,0:T(8,128)(2,1)S(1)} %heads.8.refs_0_), channel_id=1, source_target_pairs={{0,4},{4,0},{1,5},{5,1},{2,6},{6,2},{3,7},{7,3},{8,12},{12,8},{9,1... | collective-permute-start | bytes 147464 | tf_op jit(solution)/shard_map/ppermute | solution.py:17
  (8 other events, 48.8 us)

commit v15 on v14

--- a/solution.py
+++ b/solution.py
@@ -273,7 +273,7 @@
 
 
 def far_first(size):
-    return [k for k in range(2, size)] + [1]
+    return list(range(size - 1, 0, -1))
 
 
 def call(kernel, outs, ins, specs=None, scratch=(), name=None, out_specs=None, vmem=16):

time: 76 us -> 76.5 us (level)
  transfers between devices with their start and end apart: 26 -> 26, of which waited for: 15 -> 14; matrix products, arithmetic and copies ran while one was open for 0% -> 0% of each run, Pallas kernels for 6% -> 6%
where the time goes in v15:
time: 76.5 us; the launch traced here: 76.3 us
  waiting for transfers between devices  33.8 us (44%)
  starting transfers between devices  30.3 us (40%)
  Pallas kernels  7.25 us (9%)
  local copies, waits for them, and re-layouts  3.29 us (4%)
  between operations  1.64 us (2%)
    ppermute x26, waiting for transfers between devices, swap(): return lax.ppermute(block, axis, [(i, i ^ step) for i in range(size)])  33.8 us
    ppermute x26, starting transfers between devices, swap(): return lax.ppermute(block, axis, [(i, i ^ step) for i in range(size)])  30.3 us
    pallas_call x21, Pallas kernels, call(): pl.pallas_call(kernel, out_shape=outs, in_specs=specs if specs is not Non...  7.25 us
    unnamed x28, local copies, waits for them, and re-layouts  3.11 us
  transfers between devices with their start and end apart: 26, of which 14 were waited for; matrix products, arithmetic and copies ran while one was open for 0% of the time, Pallas kernels for 6%

profile of v15, /device:TPU:0, one launch (start us, length us, event | category | flops | bytes accessed | tf_op | source)
XLA Modules:
  0.0 76.3 jit_solution(17050066197940512638)
XLA Ops:
  0.0 1.6 %copy-done.4 = bf16[256,3072]{1,0:T(8,128)(2,1)S(1)} copy-done((bf16[256,3072]{1,0:T(8,128)(2,1)S(1)}, bf16[256,3072]{1,0:T(8,128)(2,1)}, u32[]{:S(2)}) %copy-start.4) | copy-done | bytes 1572888
  1.6 0.8 %copy-done.8 = bf16[1,128,256]{2,1,0:T(8,128)(2,1)S(1)} copy-done((bf16[1,128,256]{2,1,0:T(8,128)(2,1)S(1)}, bf16[1,128,256]{2,1,0:T(8,128)(2,1)}, u32[]{:S(2)}) %copy-start.8) | copy-done | bytes 65560
  4.3 1.4 %collective-permute-done.got_ref = bf16[1552,128]{1,0:T(8,128)(2,1)S(1)} collective-permute-done((bf16[1552,128]{1,0:T(8,128)(2,1)S(1)}, bf16[1552,128]{1,0:T(8,128)(2,1)S(1)}, u32[]{:S(2)}, u32[]{:S(2)}) %collective-permute-start) | collective-permute-done | bytes 397344 | tf_op jit(solution)/shard_map/ppermute | solution.py:17
  6.0 2.9 %collective-permute-start.1 = (bf16[2,192,768]{2,1,0:T(8,128)(2,1)S(1)}, bf16[2,192,768]{2,1,0:T(8,128)(2,1)S(1)}, u32[]{:S(2)}, u32[]{:S(2)}) collective-permute-start(bf16[2,192,768]{2,1,0:T(8,128)(2,1)S(1)} %get-tuple-element.48), channel_id=1, source_target_pairs={{0,2},{1,3},{2,0},{3,1},{4,6},{5,7},{6,4},{7,5},{8,10},{9,11},{10,... | collective-permute-start | bytes 1769480 | tf_op jit(solution)/shard_map/ppermute | solution.py:17
  9.0 3.6 %collective-permute-start.2 = (bf16[400,128]{1,0:T(8,128)(2,1)S(1)}, bf16[400,128]{1,0:T(8,128)(2,1)S(1)}, u32[]{:S(2)}, u32[]{:S(2)}) collective-permute-start(bf16[400,128]{1,0:T(8,128)(2,1)S(1)} %get-tuple-element.50), channel_id=1, source_target_pairs={{0,24},{8,16},{16,8},{24,0},{1,25},{9,17},{17,9},{25,1},{2,26},{10... | collective-permute-start | bytes 307208 | tf_op jit(solution)/shard_map/ppermute | solution.py:17
  12.6 0.8 %collective-permute-start.4 = (bf16[400,128]{1,0:T(8,128)(2,1)S(1)}, bf16[400,128]{1,0:T(8,128)(2,1)S(1)}, u32[]{:S(2)}, u32[]{:S(2)}) collective-permute-start(bf16[400,128]{1,0:T(8,128)(2,1)S(1)} %get-tuple-element.52), channel_id=1, source_target_pairs={{0,8},{8,0},{16,24},{24,16},{1,9},{9,1},{17,25},{25,17},{2,10},{10... | collective-permute-start | bytes 307208 | tf_op jit(solution)/shard_map/ppermute | solution.py:17
  14.0 2.5 %collective-permute-done.2.refs_0_ = bf16[400,128]{1,0:T(8,128)(2,1)S(1)} collective-permute-done((bf16[400,128]{1,0:T(8,128)(2,1)S(1)}, bf16[400,128]{1,0:T(8,128)(2,1)S(1)}, u32[]{:S(2)}, u32[]{:S(2)}) %collective-permute-start.2) | collective-permute-done | bytes 102432 | tf_op jit(solution)/shard_map/ppermute | solution.py:17
  16.5 4.7 %collective-permute-done.3.refs_1_ = bf16[400,128]{1,0:T(8,128)(2,1)S(1)} collective-permute-done((bf16[400,128]{1,0:T(8,128)(2,1)S(1)}, bf16[400,128]{1,0:T(8,128)(2,1)S(1)}, u32[]{:S(2)}, u32[]{:S(2)}) %collective-permute-start.3) | collective-permute-done | bytes 102432 | tf_op jit(solution)/shard_map/ppermute | solution.py:17
  22.8 3.4 %collective-permute-done.5.got_ref = bf16[400,128]{1,0:T(8,128)(2,1)S(1)} collective-permute-done((bf16[400,128]{1,0:T(8,128)(2,1)S(1)}, bf16[400,128]{1,0:T(8,128)(2,1)S(1)}, u32[]{:S(2)}, u32[]{:S(2)}) %collective-permute-start.5) | collective-permute-done | bytes 102432 | tf_op jit(solution)/shard_map/ppermute | solution.py:17
  26.4 1.6 %collective-permute-start.6 = (bf16[400,128]{1,0:T(8,128)(2,1)S(1)}, bf16[400,128]{1,0:T(8,128)(2,1)S(1)}, u32[]{:S(2)}, u32[]{:S(2)}) collective-permute-start(bf16[400,128]{1,0:T(8,128)(2,1)S(1)} %centre.1.own_ref), channel_id=1, source_target_pairs={{0,4},{4,0},{1,5},{5,1},{2,6},{6,2},{3,7},{7,3},{8,12},{12,8},{9,1... | collective-permute-start | bytes 307208 | tf_op jit(solution)/shard_map/ppermute | solution.py:17
  28.0 3.2 %collective-permute-done.6.got_ref = bf16[400,128]{1,0:T(8,128)(2,1)S(1)} collective-permute-done((bf16[400,128]{1,0:T(8,128)(2,1)S(1)}, bf16[400,128]{1,0:T(8,128)(2,1)S(1)}, u32[]{:S(2)}, u32[]{:S(2)}) %collective-permute-start.6) | collective-permute-done | bytes 102432 | tf_op jit(solution)/shard_map/ppermute | solution.py:17
  32.1 1.6 %collective-permute-start.9 = (bf16[4,64,1536]{2,1,0:T(8,128)(2,1)S(1)}, bf16[4,64,1536]{2,1,0:T(8,128)(2,1)S(1)}, u32[]{:S(2)}, u32[]{:S(2)}) collective-permute-start(bf16[4,64,1536]{2,1,0:T(8,128)(2,1)S(1)} %image_pack.1), channel_id=1, source_target_pairs={{0,4},{4,0},{1,5},{5,1},{2,6},{6,2},{3,7},{7,3},{8,12},{12,8},{9,1... | collective-permute-start | bytes 2359304 | tf_op jit(solution)/shard_map/ppermute | solution.py:17
  33.7 1.2 %project.1 = (s32[4]{0:T(128)S(1)}, f32[400,128]{1,0:T(8,128)S(1)}, bf16[400,128]{1,0:T(8,128)(2,1)S(1)}, bf16[400,128]{1,0:T(8,128)(2,1)S(1)}, bf16[400,128]{1,0:T(8,128)(2,1)S(1)}) custom-call(bf16[800,128]{1,0:T(8,128)(2,1)S(1)} %join.1.refs_0_.dep_ref, bf16[800,128]{1,0:T(8,128)(2,1)S(1)} %collective-permute-done.7.refs_1_, ...), custom_call_target="tpu_custom_call" | custom-call | tf_op jit(solution)/shard_map/project/pallas_call | solution.py:280
  35.4 3.5 %collective-permute-start.13 = (bf16[400,128]{1,0:T(8,128)(2,1)S(1)}, bf16[400,128]{1,0:T(8,128)(2,1)S(1)}, u32[]{:S(2)}, u32[]{:S(2)}) collective-permute-start(bf16[400,128]{1,0:T(8,128)(2,1)S(1)} %get-tuple-element.64), channel_id=1, source_target_pairs={{0,24},{8,16},{16,8},{24,0},{1,25},{9,17},{17,9},{25,1},{2,26},{10... | collective-permute-start | bytes 307208 | tf_op jit(solution)/shard_map/ppermute | solution.py:17
  38.9 0.9 %collective-permute-start.15 = (bf16[400,128]{1,0:T(8,128)(2,1)S(1)}, bf16[400,128]{1,0:T(8,128)(2,1)S(1)}, u32[]{:S(2)}, u32[]{:S(2)}) collective-permute-start(bf16[400,128]{1,0:T(8,128)(2,1)S(1)} %get-tuple-element.66), channel_id=1, source_target_pairs={{0,8},{8,0},{16,24},{24,16},{1,9},{9,1},{17,25},{25,17},{2,10},{10... | collective-permute-start | bytes 307208 | tf_op jit(solution)/shard_map/ppermute | solution.py:17
  39.9 3.1 %collective-permute-done.13.refs_0_ = bf16[400,128]{1,0:T(8,128)(2,1)S(1)} collective-permute-done((bf16[400,128]{1,0:T(8,128)(2,1)S(1)}, bf16[400,128]{1,0:T(8,128)(2,1)S(1)}, u32[]{:S(2)}, u32[]{:S(2)}) %collective-permute-start.13) | collective-permute-done | bytes 102432 | tf_op jit(solution)/shard_map/ppermute | solution.py:17
  43.0 4.2 %collective-permute-done.14.refs_1_ = bf16[400,128]{1,0:T(8,128)(2,1)S(1)} collective-permute-done((bf16[400,128]{1,0:T(8,128)(2,1)S(1)}, bf16[400,128]{1,0:T(8,128)(2,1)S(1)}, u32[]{:S(2)}, u32[]{:S(2)}) %collective-permute-start.14) | collective-permute-done | bytes 102432 | tf_op jit(solution)/shard_map/ppermute | solution.py:17
  47.4 2.5 %collective-permute-start.16 = (bf16[64,768]{1,0:T(8,128)(2,1)S(1)}, bf16[64,768]{1,0:T(8,128)(2,1)S(1)}, u32[]{:S(2)}, u32[]{:S(2)}) collective-permute-start(bf16[64,768]{1,0:T(8,128)(2,1)S(1)} %finish.1.refs_0_), channel_id=1, source_target_pairs={{0,24},{8,16},{16,8},{24,0},{1,25},{9,17},{17,9},{25,1},{2,26},{10... | collective-permute-start | bytes 294920 | tf_op jit(solution)/shard_map/ppermute | solution.py:17
  50.0 1.9 %collective-permute-start.18 = (bf16[64,768]{1,0:T(8,128)(2,1)S(1)}, bf16[64,768]{1,0:T(8,128)(2,1)S(1)}, u32[]{:S(2)}, u32[]{:S(2)}) collective-permute-start(bf16[64,768]{1,0:T(8,128)(2,1)S(1)} %finish.1.refs_0_), channel_id=1, source_target_pairs={{0,8},{8,0},{16,24},{24,16},{1,9},{9,1},{17,25},{25,17},{2,10},{10... | collective-permute-start | bytes 294920 | tf_op jit(solution)/shard_map/ppermute | solution.py:17
  52.6 1.6 %collective-permute-done.11.refs_1_ = bf16[2,128,1536]{2,1,0:T(8,128)(2,1)S(1)} collective-permute-done((bf16[2,128,1536]{2,1,0:T(8,128)(2,1)S(1)}, bf16[2,128,1536]{2,1,0:T(8,128)(2,1)S(1)}, u32[]{:S(2)}, u32[]{:S(2)}) %collective-permute-start.11) | collective-permute-done | bytes 786464 | tf_op jit(solution)/shard_map/ppermute | solution.py:17
  54.4 1.5 %collective-permute-start.12 = (f32[2,64,64]{2,1,0:T(8,128)S(1)}, f32[2,64,64]{2,1,0:T(8,128)S(1)}, u32[]{:S(2)}, u32[]{:S(2)}) collective-permute-start(f32[2,64,64]{2,1,0:T(8,128)S(1)} %get-tuple-element.61.low_ref), channel_id=1, source_target_pairs={{0,4},{4,0},{1,5},{5,1},{2,6},{6,2},{3,7},{7,3},{8,12},{12,8},{9,1... | collective-permute-start | bytes 98312 | tf_op jit(solution)/shard_map/ppermute | solution.py:17
  56.0 2.8 %collective-permute-done.12.other_ref = f32[2,64,64]{2,1,0:T(8,128)S(1)} collective-permute-done((f32[2,64,64]{2,1,0:T(8,128)S(1)}, f32[2,64,64]{2,1,0:T(8,128)S(1)}, u32[]{:S(2)}, u32[]{:S(2)}) %collective-permute-start.12) | collective-permute-done | bytes 32800 | tf_op jit(solution)/shard_map/ppermute | solution.py:17
  59.0 0.7 choose.1
  60.4 1.3 %collective-permute-start.24 = (bf16[128,768]{1,0:T(8,128)(2,1)S(1)}, bf16[128,768]{1,0:T(8,128)(2,1)S(1)}, u32[]{:S(2)}, u32[]{:S(2)}) collective-permute-start(bf16[128,768]{1,0:T(8,128)(2,1)S(1)} %get-tuple-element.78), channel_id=1, source_target_pairs={{0,3},{1,2},{2,1},{3,0},{4,7},{5,6},{6,5},{7,4},{8,11},{9,10},{10,... | collective-permute-start | bytes 589832 | tf_op jit(solution)/shard_map/ppermute | solution.py:17
  62.2 1.6 %collective-permute-start.19 = (bf16[64,384]{1,0:T(8,128)(2,1)S(1)}, bf16[64,384]{1,0:T(8,128)(2,1)S(1)}, u32[]{:S(2)}, u32[]{:S(2)}) collective-permute-start(bf16[64,384]{1,0:T(8,128)(2,1)S(1)} %get-tuple-element.71), channel_id=1, source_target_pairs={{0,4},{4,0},{1,5},{5,1},{2,6},{6,2},{3,7},{7,3},{8,12},{12,8},{9,1... | collective-permute-start | bytes 147464 | tf_op jit(solution)/shard_map/ppermute | solution.py:17
  64.8 1.5 %collective-permute-done.19.refs_1_ = bf16[64,384]{1,0:T(8,128)(2,1)S(1)} collective-permute-done((bf16[64,384]{1,0:T(8,128)(2,1)S(1)}, bf16[64,384]{1,0:T(8,128)(2,1)S(1)}, u32[]{:S(2)}, u32[]{:S(2)}) %collective-permute-start.19) | collective-permute-done | bytes 49184 | tf_op jit(solution)/shard_map/ppermute | solution.py:17
  66.3 1.3 %collective-permute-done.22.text_ref = bf16[128,768]{1,0:T(8,128)(2,1)S(1)} collective-permute-done((bf16[128,768]{1,0:T(8,128)(2,1)S(1)}, bf16[128,768]{1,0:T(8,128)(2,1)S(1)}, u32[]{:S(2)}, u32[]{:S(2)}) %collective-permute-start.22) | collective-permute-done | bytes 196640 | tf_op jit(solution)/shard_map/ppermute | solution.py:17
  68.1 1.6 %collective-permute-start.23 = (bf16[64,384]{1,0:T(8,128)(2,1)S(1)}, bf16[64,384]{1,0:T(8,128)(2,1)S(1)}, u32[]{:S(2)}, u32[]{:S(2)}) collective-permute-start(bf16[64,384]{1,0:T(8,128)(2,1)S(1)} %get-tuple-element.77), channel_id=1, source_target_pairs={{0,4},{4,0},{1,5},{5,1},{2,6},{6,2},{3,7},{7,3},{8,12},{12,8},{9,1... | collective-permute-start | bytes 147464 | tf_op jit(solution)/shard_map/ppermute | solution.py:17
  69.6 1.3 %collective-permute-done.24.text_ref = bf16[128,768]{1,0:T(8,128)(2,1)S(1)} collective-permute-done((bf16[128,768]{1,0:T(8,128)(2,1)S(1)}, bf16[128,768]{1,0:T(8,128)(2,1)S(1)}, u32[]{:S(2)}, u32[]{:S(2)}) %collective-permute-start.24) | collective-permute-done | bytes 196640 | tf_op jit(solution)/shard_map/ppermute | solution.py:17
  71.4 1.6 %collective-permute-start.25 = (bf16[64,384]{1,0:T(8,128)(2,1)S(1)}, bf16[64,384]{1,0:T(8,128)(2,1)S(1)}, u32[]{:S(2)}, u32[]{:S(2)}) collective-permute-start(bf16[64,384]{1,0:T(8,128)(2,1)S(1)} %heads.8.refs_0_), channel_id=1, source_target_pairs={{0,4},{4,0},{1,5},{5,1},{2,6},{6,2},{3,7},{7,3},{8,12},{12,8},{9,1... | collective-permute-start | bytes 147464 | tf_op jit(solution)/shard_map/ppermute | solution.py:17
  73.3 2.2 %collective-permute-done.25.refs_7_ = bf16[64,384]{1,0:T(8,128)(2,1)S(1)} collective-permute-done((bf16[64,384]{1,0:T(8,128)(2,1)S(1)}, bf16[64,384]{1,0:T(8,128)(2,1)S(1)}, u32[]{:S(2)}, u32[]{:S(2)}) %collective-permute-start.25) | collective-permute-done | bytes 49184 | tf_op jit(solution)/shard_map/ppermute | solution.py:17
  75.5 0.8 %assemble.1 = bf16[64,3072]{1,0:T(8,128)(2,1)} custom-call(bf16[64,384]{1,0:T(8,128)(2,1)S(1)} %get-tuple-element.70.refs_0_, bf16[64,384]{1,0:T(8,128)(2,1)S(1)} %collective-permute-done.19.refs_1_, bf16[64,384]{1,0:T(8,128)(2,1)S(1)} %get-tuple-element.73.refs_0_.refs_2_, bf16[64,384]{1,0:T(8,128)(2,1)S(1)} %collective-permute-done.21.refs_1_.refs_3_, ...), custom_call_target="tpu_custom_call" | custom-call | tf_op jit(solution)/shard_map/assemble/pallas_call | solution.py:280
  (74 shorter events, 9.6 us)
Async XLA Ops:
  0.0 61.7 %copy-start = (s32[2,128]{1,0:T(2,128)S(1)}, s32[2,128]{1,0:T(2,128)}, u32[]{:S(2)}) copy-start(s32[2,128]{1,0:T(2,128)} %param.16) | copy-start | bytes 3076
  3.1 18.2 %copy-start.12 = (bf16[192]{0:T(256)(128)(2,1)S(1)}, bf16[192]{0:T(256)(128)(2,1)}, u32[]{:S(2)}) copy-start(bf16[192]{0:T(256)(128)(2,1)} %b_ref.1) | copy-start | bytes 1156
  3.1 18.3 %copy-start.9 = (bf16[1,192]{1,0:T(2,128)(2,1)S(1)}, bf16[1,192]{1,0:T(2,128)(2,1)}, u32[]{:S(2)}) copy-start(bf16[1,192]{1,0:T(2,128)(2,1)} %shift_ref.3) | copy-start | bytes 1156
  3.1 18.3 %copy-start.10 = (bf16[1,192]{1,0:T(2,128)(2,1)S(1)}, bf16[1,192]{1,0:T(2,128)(2,1)}, u32[]{:S(2)}) copy-start(bf16[1,192]{1,0:T(2,128)(2,1)} %scale_ref.1) | copy-start | bytes 1156
  3.8 1.9 %collective-permute-start = (bf16[1552,128]{1,0:T(8,128)(2,1)S(1)}, bf16[1552,128]{1,0:T(8,128)(2,1)S(1)}, u32[]{:S(2)}, u32[]{:S(2)}) collective-permute-start(bf16[1552,128]{1,0:T(8,128)(2,1)S(1)} %get-tuple-element.42), channel_id=1, source_target_pairs={{0,1},{1,0},{2,3},{3,2},{4,5},{5,4},{6,7},{7,6},{8,9},{9,8},{10,11... | collective-permute-start | bytes 1191944 | tf_op jit(solution)/shard_map/ppermute | solution.py:17
  6.0 25.1 %copy-start.6 = (bf16[1,3072,64]{1,2,0:T(8,128)(2,1)S(1)}, bf16[1,3072,64]{1,2,0:T(8,128)(2,1)}, u32[]{:S(2)}) copy-start(bf16[1,3072,64]{1,2,0:T(8,128)(2,1)} %param.25) | copy-start | bytes 1179652
  6.0 25.1 %copy-start.7 = (bf16[1,64,3072]{2,1,0:T(8,128)(2,1)S(1)}, bf16[1,64,3072]{2,1,0:T(8,128)(2,1)}, u32[]{:S(2)}) copy-start(bf16[1,64,3072]{2,1,0:T(8,128)(2,1)} %param.26) | copy-start | bytes 1179652
  6.0 16.6 %collective-permute-start.1 = (bf16[2,192,768]{2,1,0:T(8,128)(2,1)S(1)}, bf16[2,192,768]{2,1,0:T(8,128)(2,1)S(1)}, u32[]{:S(2)}, u32[]{:S(2)}) collective-permute-start(bf16[2,192,768]{2,1,0:T(8,128)(2,1)S(1)} %get-tuple-element.48), channel_id=1, source_target_pairs={{0,2},{1,3},{2,0},{3,1},{4,6},{5,7},{6,4},{7,5},{8,10},{9,11},{10,... | collective-permute-start | bytes 1769480 | tf_op jit(solution)/shard_map/ppermute | solution.py:17
  9.0 7.5 %collective-permute-start.2 = (bf16[400,128]{1,0:T(8,128)(2,1)S(1)}, bf16[400,128]{1,0:T(8,128)(2,1)S(1)}, u32[]{:S(2)}, u32[]{:S(2)}) collective-permute-start(bf16[400,128]{1,0:T(8,128)(2,1)S(1)} %get-tuple-element.50), channel_id=1, source_target_pairs={{0,24},{8,16},{16,8},{24,0},{1,25},{9,17},{17,9},{25,1},{2,26},{10... | collective-permute-start | bytes 307208 | tf_op jit(solution)/shard_map/ppermute | solution.py:17
  12.6 8.6 %collective-permute-start.3 = (bf16[400,128]{1,0:T(8,128)(2,1)S(1)}, bf16[400,128]{1,0:T(8,128)(2,1)S(1)}, u32[]{:S(2)}, u32[]{:S(2)}) collective-permute-start(bf16[400,128]{1,0:T(8,128)(2,1)S(1)} %get-tuple-element.51), channel_id=1, source_target_pairs={{0,16},{8,24},{16,0},{24,8},{1,17},{9,25},{17,1},{25,9},{2,18},{10... | collective-permute-start | bytes 307208 | tf_op jit(solution)/shard_map/ppermute | solution.py:17
  12.6 8.6 %collective-permute-start.4 = (bf16[400,128]{1,0:T(8,128)(2,1)S(1)}, bf16[400,128]{1,0:T(8,128)(2,1)S(1)}, u32[]{:S(2)}, u32[]{:S(2)}) collective-permute-start(bf16[400,128]{1,0:T(8,128)(2,1)S(1)} %get-tuple-element.52), channel_id=1, source_target_pairs={{0,8},{8,0},{16,24},{24,16},{1,9},{9,1},{17,25},{25,17},{2,10},{10... | collective-permute-start | bytes 307208 | tf_op jit(solution)/shard_map/ppermute | solution.py:17
  21.5 4.7 %collective-permute-start.5 = (bf16[400,128]{1,0:T(8,128)(2,1)S(1)}, bf16[400,128]{1,0:T(8,128)(2,1)S(1)}, u32[]{:S(2)}, u32[]{:S(2)}) collective-permute-start(bf16[400,128]{1,0:T(8,128)(2,1)S(1)} %get-tuple-element.56), channel_id=1, source_target_pairs={{0,2},{1,3},{2,0},{3,1},{4,6},{5,7},{6,4},{7,5},{8,10},{9,11},{10,... | collective-permute-start | bytes 307208 | tf_op jit(solution)/shard_map/ppermute | solution.py:17
  22.7 11.0 %collective-permute-start.8 = (bf16[384,768]{1,0:T(8,128)(2,1)S(1)}, bf16[384,768]{1,0:T(8,128)(2,1)S(1)}, u32[]{:S(2)}, u32[]{:S(2)}) collective-permute-start(bf16[384,768]{1,0:T(8,128)(2,1)S(1)} %get-tuple-element.57), channel_id=1, source_target_pairs={{0,1},{1,0},{2,3},{3,2},{4,5},{5,4},{6,7},{7,6},{8,9},{9,8},{10,11... | collective-permute-start | bytes 1769480 | tf_op jit(solution)/shard_map/ppermute | solution.py:17
  26.4 4.7 %collective-permute-start.6 = (bf16[400,128]{1,0:T(8,128)(2,1)S(1)}, bf16[400,128]{1,0:T(8,128)(2,1)S(1)}, u32[]{:S(2)}, u32[]{:S(2)}) collective-permute-start(bf16[400,128]{1,0:T(8,128)(2,1)S(1)} %centre.1.own_ref), channel_id=1, source_target_pairs={{0,4},{4,0},{1,5},{5,1},{2,6},{6,2},{3,7},{7,3},{8,12},{12,8},{9,1... | collective-permute-start | bytes 307208 | tf_op jit(solution)/shard_map/ppermute | solution.py:17
  31.3 2.4 %collective-permute-start.10 = (bf16[128,1536]{1,0:T(8,128)(2,1)S(1)}, bf16[128,1536]{1,0:T(8,128)(2,1)S(1)}, u32[]{:S(2)}, u32[]{:S(2)}) collective-permute-start(bf16[128,1536]{1,0:T(8,128)(2,1)S(1)} %maps_pack.1.own_ref), channel_id=1, source_target_pairs={{0,1},{1,0},{2,3},{3,2},{4,5},{5,4},{6,7},{7,6},{8,9},{9,8},{10,11... | collective-permute-start | bytes 1179656 | tf_op jit(solution)/shard_map/ppermute | solution.py:17
  31.4 2.3 %collective-permute-start.7 = (bf16[800,128]{1,0:T(8,128)(2,1)S(1)}, bf16[800,128]{1,0:T(8,128)(2,1)S(1)}, u32[]{:S(2)}, u32[]{:S(2)}) collective-permute-start(bf16[800,128]{1,0:T(8,128)(2,1)S(1)} %join.1.refs_0_.dep_ref), channel_id=1, source_target_pairs={{0,1},{1,0},{2,3},{3,2},{4,5},{5,4},{6,7},{7,6},{8,9},{9,8},{10,11... | collective-permute-start | bytes 614408 | tf_op jit(solution)/shard_map/ppermute | solution.py:17
  32.1 20.5 %collective-permute-start.9 = (bf16[4,64,1536]{2,1,0:T(8,128)(2,1)S(1)}, bf16[4,64,1536]{2,1,0:T(8,128)(2,1)S(1)}, u32[]{:S(2)}, u32[]{:S(2)}) collective-permute-start(bf16[4,64,1536]{2,1,0:T(8,128)(2,1)S(1)} %image_pack.1), channel_id=1, source_target_pairs={{0,4},{4,0},{1,5},{5,1},{2,6},{6,2},{3,7},{7,3},{8,12},{12,8},{9,1... | collective-permute-start | bytes 2359304 | tf_op jit(solution)/shard_map/ppermute | solution.py:17
  34.9 19.3 %collective-permute-start.11 = (bf16[2,128,1536]{2,1,0:T(8,128)(2,1)S(1)}, bf16[2,128,1536]{2,1,0:T(8,128)(2,1)S(1)}, u32[]{:S(2)}, u32[]{:S(2)}) collective-permute-start(bf16[2,128,1536]{2,1,0:T(8,128)(2,1)S(1)} %maps_join.1.refs_0_), channel_id=1, source_target_pairs={{0,2},{1,3},{2,0},{3,1},{4,6},{5,7},{6,4},{7,5},{8,10},{9,11},{10,... | collective-permute-start | bytes 2359304 | tf_op jit(solution)/shard_map/ppermute | solution.py:17
  35.4 7.5 %collective-permute-start.13 = (bf16[400,128]{1,0:T(8,128)(2,1)S(1)}, bf16[400,128]{1,0:T(8,128)(2,1)S(1)}, u32[]{:S(2)}, u32[]{:S(2)}) collective-permute-start(bf16[400,128]{1,0:T(8,128)(2,1)S(1)} %get-tuple-element.64), channel_id=1, source_target_pairs={{0,24},{8,16},{16,8},{24,0},{1,25},{9,17},{17,9},{25,1},{2,26},{10... | collective-permute-start | bytes 307208 | tf_op jit(solution)/shard_map/ppermute | solution.py:17
  38.9 8.3 %collective-permute-start.14 = (bf16[400,128]{1,0:T(8,128)(2,1)S(1)}, bf16[400,128]{1,0:T(8,128)(2,1)S(1)}, u32[]{:S(2)}, u32[]{:S(2)}) collective-permute-start(bf16[400,128]{1,0:T(8,128)(2,1)S(1)} %get-tuple-element.65), channel_id=1, source_target_pairs={{0,16},{8,24},{16,0},{24,8},{1,17},{9,25},{17,1},{25,9},{2,18},{10... | collective-permute-start | bytes 307208 | tf_op jit(solution)/shard_map/ppermute | solution.py:17
  38.9 8.3 %collective-permute-start.15 = (bf16[400,128]{1,0:T(8,128)(2,1)S(1)}, bf16[400,128]{1,0:T(8,128)(2,1)S(1)}, u32[]{:S(2)}, u32[]{:S(2)}) collective-permute-start(bf16[400,128]{1,0:T(8,128)(2,1)S(1)} %get-tuple-element.66), channel_id=1, source_target_pairs={{0,8},{8,0},{16,24},{24,16},{1,9},{9,1},{17,25},{25,17},{2,10},{10... | collective-permute-start | bytes 307208 | tf_op jit(solution)/shard_map/ppermute | solution.py:17
  47.4 11.6 %collective-permute-start.16 = (bf16[64,768]{1,0:T(8,128)(2,1)S(1)}, bf16[64,768]{1,0:T(8,128)(2,1)S(1)}, u32[]{:S(2)}, u32[]{:S(2)}) collective-permute-start(bf16[64,768]{1,0:T(8,128)(2,1)S(1)} %finish.1.refs_0_), channel_id=1, source_target_pairs={{0,24},{8,16},{16,8},{24,0},{1,25},{9,17},{17,9},{25,1},{2,26},{10... | collective-permute-start | bytes 294920 | tf_op jit(solution)/shard_map/ppermute | solution.py:17
  50.0 9.0 %collective-permute-start.17 = (bf16[64,768]{1,0:T(8,128)(2,1)S(1)}, bf16[64,768]{1,0:T(8,128)(2,1)S(1)}, u32[]{:S(2)}, u32[]{:S(2)}) collective-permute-start(bf16[64,768]{1,0:T(8,128)(2,1)S(1)} %finish.1.refs_0_), channel_id=1, source_target_pairs={{0,16},{8,24},{16,0},{24,8},{1,17},{9,25},{17,1},{25,9},{2,18},{10... | collective-permute-start | bytes 294920 | tf_op jit(solution)/shard_map/ppermute | solution.py:17
  50.0 9.0 %collective-permute-start.18 = (bf16[64,768]{1,0:T(8,128)(2,1)S(1)}, bf16[64,768]{1,0:T(8,128)(2,1)S(1)}, u32[]{:S(2)}, u32[]{:S(2)}) collective-permute-start(bf16[64,768]{1,0:T(8,128)(2,1)S(1)} %finish.1.refs_0_), channel_id=1, source_target_pairs={{0,8},{8,0},{16,24},{24,16},{1,9},{9,1},{17,25},{25,17},{2,10},{10... | collective-permute-start | bytes 294920 | tf_op jit(solution)/shard_map/ppermute | solution.py:17
  54.4 4.3 %collective-permute-start.12 = (f32[2,64,64]{2,1,0:T(8,128)S(1)}, f32[2,64,64]{2,1,0:T(8,128)S(1)}, u32[]{:S(2)}, u32[]{:S(2)}) collective-permute-start(f32[2,64,64]{2,1,0:T(8,128)S(1)} %get-tuple-element.61.low_ref), channel_id=1, source_target_pairs={{0,4},{4,0},{1,5},{5,1},{2,6},{6,2},{3,7},{7,3},{8,12},{12,8},{9,1... | collective-permute-start | bytes 98312 | tf_op jit(solution)/shard_map/ppermute | solution.py:17
  59.8 4.0 %collective-permute-start.20 = (bf16[128,768]{1,0:T(8,128)(2,1)S(1)}, bf16[128,768]{1,0:T(8,128)(2,1)S(1)}, u32[]{:S(2)}, u32[]{:S(2)}) collective-permute-start(bf16[128,768]{1,0:T(8,128)(2,1)S(1)} %get-tuple-element.72), channel_id=1, source_target_pairs={{0,1},{1,0},{2,3},{3,2},{4,5},{5,4},{6,7},{7,6},{8,9},{9,8},{10,11... | collective-permute-start | bytes 589832 | tf_op jit(solution)/shard_map/ppermute | solution.py:17
  59.9 7.8 %collective-permute-start.22 = (bf16[128,768]{1,0:T(8,128)(2,1)S(1)}, bf16[128,768]{1,0:T(8,128)(2,1)S(1)}, u32[]{:S(2)}, u32[]{:S(2)}) collective-permute-start(bf16[128,768]{1,0:T(8,128)(2,1)S(1)} %get-tuple-element.75), channel_id=1, source_target_pairs={{0,2},{1,3},{2,0},{3,1},{4,6},{5,7},{6,4},{7,5},{8,10},{9,11},{10,... | collective-permute-start | bytes 589832 | tf_op jit(solution)/shard_map/ppermute | solution.py:17
  60.4 10.5 %collective-permute-start.24 = (bf16[128,768]{1,0:T(8,128)(2,1)S(1)}, bf16[128,768]{1,0:T(8,128)(2,1)S(1)}, u32[]{:S(2)}, u32[]{:S(2)}) collective-permute-start(bf16[128,768]{1,0:T(8,128)(2,1)S(1)} %get-tuple-element.78), channel_id=1, source_target_pairs={{0,3},{1,2},{2,1},{3,0},{4,7},{5,6},{6,5},{7,4},{8,11},{9,10},{10,... | collective-permute-start | bytes 589832 | tf_op jit(solution)/shard_map/ppermute | solution.py:17
  62.2 4.2 %collective-permute-start.19 = (bf16[64,384]{1,0:T(8,128)(2,1)S(1)}, bf16[64,384]{1,0:T(8,128)(2,1)S(1)}, u32[]{:S(2)}, u32[]{:S(2)}) collective-permute-start(bf16[64,384]{1,0:T(8,128)(2,1)S(1)} %get-tuple-element.71), channel_id=1, source_target_pairs={{0,4},{4,0},{1,5},{5,1},{2,6},{6,2},{3,7},{7,3},{8,12},{12,8},{9,1... | collective-permute-start | bytes 147464 | tf_op jit(solution)/shard_map/ppermute | solution.py:17
  64.2 6.8 %collective-permute-start.21 = (bf16[64,384]{1,0:T(8,128)(2,1)S(1)}, bf16[64,384]{1,0:T(8,128)(2,1)S(1)}, u32[]{:S(2)}, u32[]{:S(2)}) collective-permute-start(bf16[64,384]{1,0:T(8,128)(2,1)S(1)} %get-tuple-element.74), channel_id=1, source_target_pairs={{0,4},{4,0},{1,5},{5,1},{2,6},{6,2},{3,7},{7,3},{8,12},{12,8},{9,1... | collective-permute-start | bytes 147464 | tf_op jit(solution)/shard_map/ppermute | solution.py:17
  68.1 5.3 %collective-permute-start.23 = (bf16[64,384]{1,0:T(8,128)(2,1)S(1)}, bf16[64,384]{1,0:T(8,128)(2,1)S(1)}, u32[]{:S(2)}, u32[]{:S(2)}) collective-permute-start(bf16[64,384]{1,0:T(8,128)(2,1)S(1)} %get-tuple-element.77), channel_id=1, source_target_pairs={{0,4},{4,0},{1,5},{5,1},{2,6},{6,2},{3,7},{7,3},{8,12},{12,8},{9,1... | collective-permute-start | bytes 147464 | tf_op jit(solution)/shard_map/ppermute | solution.py:17
  71.4 4.2 %collective-permute-start.25 = (bf16[64,384]{1,0:T(8,128)(2,1)S(1)}, bf16[64,384]{1,0:T(8,128)(2,1)S(1)}, u32[]{:S(2)}, u32[]{:S(2)}) collective-permute-start(bf16[64,384]{1,0:T(8,128)(2,1)S(1)} %heads.8.refs_0_), channel_id=1, source_target_pairs={{0,4},{4,0},{1,5},{5,1},{2,6},{6,2},{3,7},{7,3},{8,12},{12,8},{9,1... | collective-permute-start | bytes 147464 | tf_op jit(solution)/shard_map/ppermute | solution.py:17
  (8 other events, 48.3 us)
